TPU v7x, 32 devices: a whole 2x2x4 slice. The times are simulated.
32 devices in a mesh: req: 32 (over z, y, x, core), kv: 1.
Axes of the slice: x: 2, y: 2, z: 4, core: 2. Of those that a mesh axis runs over, the one named last changes fastest.
Arguments:
- hidden: bfloat16 [256, 2048], P('req'), may hold values from -1.796875 to 1.796875
- queries: bfloat16 [256, 2048], P('req', 'kv'), may hold values from -30 to 30
- fresh_key_value: bfloat16 [256, 4, 256], P('req', 'kv'), may hold values from -6 to 6
- kv_pool: bfloat16 [3328, 32, 4, 256], P('req', None, 'kv'), may hold values from -6 to 6
- page_table: int32 [256, 20], P('req'), may hold values from 0 to 103, as said below
- lengths: int32 [256], P('req'), may hold values from 256 to 639, as said below
- out_weight: bfloat16 [2048, 2048], P('kv'), may hold values from -0.5 to 0.5
- norm_gain: bfloat16 [2048], replicated, may hold values from 0.099609375 to 1.8984375
- router_weight: bfloat16 [16, 2048], replicated, may hold values from -0.03125 to 0.03125
- expert_ids: int32 [256, 6], P('req'), may hold values from 0 to 15, all different within a row; in each aligned block of 8 rows (0 to 7, 8 to 15, ...) at most 4 rows name the same one
- expert_gate_up: bfloat16 [32, 2, 704, 2048], P('req', None, 'kv'), may hold values from -0.125 to 0.125
- expert_down: bfloat16 [32, 704, 2048], P('req', 'kv'), may hold values from -0.15625 to 0.15625
Outputs:
- out_hidden: bfloat16 [256, 2048], P('req')
- updated_pool: bfloat16 [3328, 32, 4, 256], P('req', None, 'kv')
- hidden_norms: float32 [256], P('req')
- max_logit: float32 [256], P('req')
Inputs may be any that keep to these rules, and one draw needn't show every extreme that they name: `page_table`: entries index the block of 104 pages of the request's own index of req. Requests of one index of req share their first pages, a common prompt of 8 or more pages; every other page is named by one request alone, and the page holding position lengths[r] is always one of request r's own. `lengths`: every request's length covers its shared prompt. `expert_ids`: within the 8 rows of one index of req, at most 4 rows name one expert, a bound that some block reaches of them.
All inputs are finite; a program needn't handle non-finite values.
Results may differ from a plain program's by a relative error of at most 0.015.
Values may be sent and summed in bfloat16 or wider, within the bound.
No kernel may reach another device: no remote copies, remote signals or barrier semaphores. Data moves between devices by JAX's collectives and lax.ppermute only.
A program may use at most 128 MiB of HBM per device.

v0:
```python
import math

import jax
import jax.numpy as jnp
from jax import lax
from jax.sharding import PartitionSpec as P


def body(
    hidden,
    queries,
    fresh_key_value,
    kv_pool,
    page_table,
    lengths,
    out_weight,
    norm_gain,
    router_weight,
    expert_ids,
    expert_gate_up,
    expert_down,
):
    req_dev = hidden.shape[0]
    model_width = hidden.shape[1]
    req_count = lax.axis_size("req")
    heads_kv = fresh_key_value.shape[1]
    head_dim = fresh_key_value.shape[2] // 2
    page_len = kv_pool.shape[1]
    max_pages = page_table.shape[1]
    slot_page = jnp.take_along_axis(page_table, (lengths // page_len)[:, None], axis=1)[:, 0]
    refreshed_pool = kv_pool.at[slot_page, lengths % page_len].set(fresh_key_value)
    collected_pages = refreshed_pool[page_table].reshape(
        req_dev, max_pages * page_len, heads_kv, 2 * head_dim
    )
    query_heads = queries.reshape(req_dev, heads_kv, -1, head_dim)
    scores = jnp.einsum(
        "rhgd,rphd->rhgp",
        query_heads,
        collected_pages[..., :head_dim],
        preferred_element_type=jnp.float32,
    ) / math.sqrt(head_dim)
    positions = jnp.arange(max_pages * page_len, dtype=jnp.int32)
    visible = positions[None, :] <= lengths[:, None]
    scores = jnp.where(visible[:, None, None, :], scores, -1e30)
    top_score = jnp.max(scores, axis=-1)
    exponent = jnp.exp(scores - top_score[..., None])
    denominator = jnp.sum(exponent, axis=-1)
    probs = exponent.astype(jnp.bfloat16)
    summed = jnp.einsum(
        "rhgp,rphd->rhgd",
        probs,
        collected_pages[..., head_dim:],
        preferred_element_type=jnp.float32,
    )
    attended = (summed / denominator[..., None]).astype(jnp.bfloat16).reshape(req_dev, -1)
    partial_proj = jnp.dot(attended, out_weight, preferred_element_type=jnp.float32)
    projected = lax.psum(partial_proj.astype(jnp.bfloat16), "kv").astype(jnp.float32)
    mixed_state = (hidden.astype(jnp.float32) + projected).astype(jnp.bfloat16)
    mixed_float = mixed_state.astype(jnp.float32)
    hidden_norms = jnp.sqrt(jnp.mean(mixed_float * mixed_float, axis=-1) + 1e-06)
    normed = (mixed_float / hidden_norms[:, None] * norm_gain.astype(jnp.float32)).astype(
        jnp.bfloat16
    )
    logits = jnp.dot(normed, router_weight.T, preferred_element_type=jnp.float32)
    max_logit = jnp.max(logits, axis=-1)
    experts = router_weight.shape[0]
    copies = req_count // experts
    chosen_count = expert_ids.shape[1]
    onehot = expert_ids[:, :, None] == jnp.arange(experts, dtype=jnp.int32)[None, None, :]
    picked = jnp.sum(jnp.where(onehot, logits[:, None, :], 0.0), axis=-1)
    exponent_gate = jnp.exp(picked)
    gate_weights = exponent_gate / jnp.sum(exponent_gate, axis=-1, keepdims=True)
    flat_hot = onehot.reshape(req_dev * chosen_count, experts)
    counts = jnp.cumsum(flat_hot.astype(jnp.int32), axis=0)
    slot_rank = (jnp.sum(jnp.where(flat_hot, counts, 0), axis=-1) - 1).reshape(
        req_dev, chosen_count
    )
    capacity = 2 * max(1, (req_dev * chosen_count + 2 * experts - 1) // (2 * experts))
    slot_index = expert_ids * capacity + slot_rank
    slot_count = experts * capacity
    assigned = slot_index[None, :, :] == jnp.arange(slot_count, dtype=jnp.int32)[:, None, None]
    dispatch_mat = jnp.sum(assigned.astype(jnp.float32), axis=-1).astype(jnp.bfloat16)
    outgoing = (
        jnp.dot(dispatch_mat, normed, preferred_element_type=jnp.float32)
        .astype(jnp.bfloat16)
        .reshape(experts, capacity, model_width)
    )
    spread = jnp.repeat(outgoing, copies, axis=0)
    combine_mat = jnp.sum(jnp.where(assigned, gate_weights[None, :, :], 0.0), axis=-1).T.reshape(
        req_dev, experts, capacity
    )
    gate_up = expert_gate_up[0]
    down_local = expert_down[0]
    arrived = lax.all_to_all(spread, "req", split_axis=0, concat_axis=0, tiled=True)
    rows = arrived.reshape(-1, model_width)
    gate_proj = jnp.einsum("rd,fd->rf", rows, gate_up[0], preferred_element_type=jnp.float32)
    up_proj = jnp.einsum("rd,fd->rf", rows, gate_up[1], preferred_element_type=jnp.float32)
    activated = (jax.nn.silu(gate_proj) * up_proj).astype(jnp.bfloat16)
    terms = jnp.dot(activated, down_local, preferred_element_type=jnp.float32)
    returned = lax.all_to_all(
        terms.reshape(arrived.shape[0], arrived.shape[1], model_width).astype(jnp.bfloat16),
        "req",
        split_axis=0,
        concat_axis=0,
        tiled=True,
    )
    pair_comb = jnp.repeat(combine_mat, copies, axis=1).reshape(req_dev, -1)
    partial_routed = jnp.dot(
        pair_comb,
        returned.reshape(-1, model_width).astype(jnp.float32),
        precision=lax.Precision.HIGHEST,
    )
    routed = lax.psum(partial_routed.astype(jnp.bfloat16), "kv").astype(jnp.float32)
    out_hidden = (mixed_float + routed).astype(jnp.bfloat16)
    return (out_hidden, refreshed_pool, hidden_norms, max_logit)


def solution(mesh):
    in_specs = (
        P("req", None),
        P("req", "kv"),
        P("req", "kv", None),
        P("req", None, "kv", None),
        P("req", None),
        P("req"),
        P("kv", None),
        P(),
        P(),
        P("req", None),
        P("req", None, "kv", None),
        P("req", "kv", None),
    )
    out_specs = (P("req", None), P("req", None, "kv", None), P("req"), P("req"))
    return jax.shard_map(body, mesh=mesh, in_specs=in_specs, out_specs=out_specs, check_vma=False)
```

profile of v0, /device:TPU:0, one launch (start us, length us, event | category | flops | bytes accessed | tf_op | source)
XLA Modules:
  0.0 116.3 jit_solution(18227233632624965626)
XLA Ops:
  0.6 0.0 copy-start
  0.6 0.0 copy-start.6
  0.7 0.0 copy-start.1
  0.7 0.0 copy-start.9
  0.7 0.0 copy-start.4
  0.7 11.8 %copy.82 = bf16[104,32,4,256]{3,2,1,0:T(4,128)(2,1)} copy(bf16[104,32,4,256]{3,2,1,0:T(4,128)(2,1)} %param.15) | data formatting | bytes 13631488
  12.5 0.0 copy-done.9
  12.5 0.1 iota_compare_fusion.3
  12.5 0.0 copy-done.4
  12.5 0.1 copy.49
  12.6 0.1 eq.37
  12.7 0.0 copy-done.1
  12.8 0.6 gather_fusion.1
  13.4 0.1 reshape.121
  13.5 0.0 copy-done.6
  13.5 2.0 %scatter_fusion = bf16[104,32,4,256]{3,2,1,0:T(4,128)(2,1)} fusion(bf16[104,32,4,256]{3,2,1,0:T(4,128)(2,1)} %copy.82, s32[8]{0:T(128)S(1)} %fusion.54, bf16[8,4,256]{2,1,0:T(4,128)(2,1)S(1)} %copy-done.6), kind=kCustom, calls=%fused_computation.2 | custom fusion | bytes 49216 | tf_op jit(solution)/shard_map/scatter | solution.py:31
  15.5 15.7 %gather_fusion = bf16[160,32,4,256]{3,2,1,0:T(4,128)(2,1)} fusion(bf16[104,32,4,256]{3,2,1,0:T(4,128)(2,1)} %scatter_fusion, s32[1024]{0:T(1024)S(1)} %pad_clamp_fusion), kind=kCustom, calls=%fused_computation | custom fusion | bytes 20972160 | tf_op jit(solution)/shard_map/gather | solution.py:32
  31.3 10.0 %copy.44 = bf16[160,32,4,256]{3,1,0,2:T(8,128)(2,1)} copy(bf16[160,32,4,256]{3,2,1,0:T(4,128)(2,1)} %gather_fusion) | data formatting | bytes 20971520 | tf_op jit(solution)/shard_map/gather | solution.py:32
  41.3 0.0 copy-start.10
  41.3 9.1 %fusion.55 = (bf16[8,640,4,128]{3,1,0,2:T(8,128)(2,1)}, bf16[8,640,4,128]{3,1,0,2:T(8,128)(2,1)}) fusion(bf16[8,640,4,256]{3,1,0,2:T(8,128)(2,1)} %bitcast.54), kind=kLoop, calls=%fused_computation.76 | loop fusion | bytes 20971520 | tf_op jit(solution)/shard_map/slice | solution.py:39
  50.5 0.0 copy-start.2
  50.5 0.0 copy-done.10
  50.5 0.0 copy-start.5
  50.5 4.4 %fusion.56 = (f32[8,4,4]{2,1,0:T(4,128)S(1)}, f32[8,4,4,640]{3,2,1,0:T(4,128)S(1)}) fusion(bf16[8,4,4,128]{3,0,2,1:T(8,128)(2,1)S(1)} %bitcast.59, bf16[8,640,4,128]{3,1,0,2:T(8,128)(2,1)} %get-tuple-element.6, pred[8,640]{1,0:T(8,128)(4,1)S(1)} %iota_compare_fusion.3), kind=kOutput, calls=%fused_computation.77 | convolution fusion | flops 21217152 | bytes 5608960 | tf_op jit(solution)/shard_map/rhgd,rphd->rhgp/dot_general | solution.py:36
  54.9 0.3 fusion.43
  55.2 0.0 copy-done.2
  55.2 1.0 fusion.40
  56.2 0.0 copy-start.7
  56.2 0.0 copy-start.3
  56.2 0.0 copy-done.5
  56.2 4.7 %multiply_reduce_fusion = (f32[8]{0:T(128)S(1)}, f32[8,2048]{1,0:T(8,128)S(1)}) fusion(bf16[8,2048]{1,0:T(8,128)(2,1)S(1)} %reshape.113, bf16[2048,2048]{1,0:T(8,128)(2,1)} %param.18, bf16[8,2048]{1,0:T(8,128)(2,1)S(1)} %copy-done.5), kind=kOutput, calls=%fused_computation.39 | convolution fusion | flops 67239928 | bytes 8519712 | tf_op jit(solution)/shard_map/dot_general | solution.py:56
  61.0 0.0 copy-done.7
  61.0 0.0 copy-start.8
  61.0 0.1 multiply_convert_fusion
  61.1 0.0 copy-done.3
  61.1 0.8 fusion.57
  61.8 0.1 select_reduce_fusion.1
  62.0 0.1 fusion.49
  62.1 0.1 reduce_window_sum.11
  62.2 0.2 select_reduce_fusion.2
  62.4 0.1 sub.22
  62.5 0.1 copy.48
  62.6 0.1 convert_reduce_fusion
  62.7 0.3 convolution_convert_fusion
  62.9 0.1 reshape.115
  63.0 0.2 broadcast_in_dim.81
  63.3 22.7 %all_to_all.10 = bf16[32,4,2048]{2,1,0:T(4,128)(2,1)S(1)} all-to-all(bf16[32,4,2048]{2,1,0:T(4,128)(2,1)S(1)} %bitcast.55), channel_id=1, replica_groups=mesh['req'=32,'kv'=1] {'req'}, dimensions={0} | all-to-all | bytes 1048576 | tf_op jit(solution)/shard_map/all_to_all | solution.py:94
  85.9 0.9 reshape.117
  86.8 2.9 %fusion.8 = f32[128,704]{0,1:T(8,128)S(1)} fusion(bf16[128,2048]{1,0:T(8,128)(2,1)} %reshape.117, bf16[1,2,704,2048]{3,2,1,0:T(8,128)(2,1)} %param.22), kind=kOutput, calls=%fused_computation.11 | convolution fusion | flops 369098752 | bytes 3768320 | tf_op jit(solution)/shard_map/rd,fd->rf/dot_general | solution.py:96
  89.7 2.9 %fusion.25 = bf16[128,704]{0,1:T(8,128)(2,1)S(1)} fusion(bf16[128,2048]{1,0:T(8,128)(2,1)} %reshape.117, bf16[1,2,704,2048]{3,2,1,0:T(8,128)(2,1)} %param.22, f32[128,704]{0,1:T(8,128)S(1)} %fusion.8), kind=kOutput, calls=%fused_computation.27 | convolution fusion | flops 369639424 | bytes 3948544 | tf_op jit(solution)/shard_map/rd,fd->rf/dot_general | solution.py:97
  92.7 0.0 copy-done.8
  92.7 0.1 copy.52
  92.8 0.1 dot_general.36
  92.9 0.0 copy-done
  92.9 0.6 fusion.12
  93.5 1.2 %copy.54 = bf16[32,4,2048]{2,1,0:T(4,128)(2,1)} copy(bf16[32,4,2048]{2,0,1:T(8,128)(2,1)S(1)} %fusion.12) | data formatting | bytes 1048576 | tf_op jit(solution)/shard_map/convert_element_type | solution.py:101
  94.7 3.1 %all-to-all-start.1 = ((bf16[32,4,2048]{2,1,0:T(4,128)(2,1)}), bf16[32,4,2048]{2,1,0:T(4,128)(2,1)S(1)}, u32[]{:S(2)}, u32[]{:S(2)}) async-start(bf16[32,4,2048]{2,1,0:T(4,128)(2,1)} %copy.54), calls=%async_computation.1 | async-start | bytes 1048576 | tf_op jit(solution)/shard_map/all_to_all | solution.py:100
  97.8 0.1 copy.51
  97.8 15.5 %all-to-all-done.1 = bf16[32,4,2048]{2,1,0:T(4,128)(2,1)S(1)} async-done(((bf16[32,4,2048]{2,1,0:T(4,128)(2,1)}), bf16[32,4,2048]{2,1,0:T(4,128)(2,1)S(1)}, u32[]{:S(2)}, u32[]{:S(2)}) %all-to-all-start.1) | async-done | bytes 524320 | tf_op jit(solution)/shard_map/all_to_all | solution.py:100
  113.3 0.9 reshape.118
  114.2 2.0 %fusion.17 = bf16[8,2048]{1,0:T(8,128)(2,1)} fusion(f32[8,2048]{1,0:T(8,128)S(1)} %get-tuple-element.11, f32[8,128]{0,1:T(8,128)S(1)} %bitcast.56, bf16[128,2048]{1,0:T(8,128)(2,1)} %reshape.118), kind=kOutput, calls=%fused_computation.20 | convolution fusion | flops 25231360 | bytes 626688 | tf_op jit(solution)/shard_map/dot_general | solution.py:108
  (15 shorter events, 0.2 us)
Async XLA Ops:
  0.6 92.2 %copy-start = (bf16[1,704,2048]{2,1,0:T(8,128)(2,1)S(1)}, bf16[1,704,2048]{2,1,0:T(8,128)(2,1)}, u32[]{:S(2)}) copy-start(bf16[1,704,2048]{2,1,0:T(8,128)(2,1)} %param.23) | copy-start | bytes 8650756
  0.6 12.9 %copy-start.6 = (bf16[8,4,256]{2,1,0:T(4,128)(2,1)S(1)}, bf16[8,4,256]{2,1,0:T(4,128)(2,1)}, u32[]{:S(2)}) copy-start(bf16[8,4,256]{2,1,0:T(4,128)(2,1)} %param.14) | copy-start | bytes 49156
  0.7 12.1 %copy-start.1 = (s32[8,20]{1,0:T(8,128)S(1)}, s32[8,20]{1,0:T(8,128)}, u32[]{:S(2)}) copy-start(s32[8,20]{1,0:T(8,128)} %param.16) | copy-start | bytes 1924
  0.7 11.8 %copy-start.9 = (s32[8]{0:T(128)S(1)}, s32[8]{0:T(128)}, u32[]{:S(2)}) copy-start(s32[8]{0:T(128)} %param.17) | copy-start | bytes 100
  0.7 11.9 %copy-start.4 = (s32[8,6]{1,0:T(8,128)S(1)}, s32[8,6]{1,0:T(8,128)}, u32[]{:S(2)}) copy-start(s32[8,6]{1,0:T(8,128)} %param.21) | copy-start | bytes 580
  41.3 9.1 %copy-start.10 = (bf16[8,2048]{1,0:T(8,128)(2,1)S(1)}, bf16[8,2048]{1,0:T(8,128)(2,1)}, u32[]{:S(2)}) copy-start(bf16[8,2048]{1,0:T(8,128)(2,1)} %param.13) | copy-start | bytes 98308
  50.5 4.7 %copy-start.2 = (bf16[8,640,4,128]{3,1,0,2:T(8,128)(2,1)S(1)}, bf16[8,640,4,128]{3,1,0,2:T(8,128)(2,1)}, u32[]{:S(2)}) copy-start(bf16[8,640,4,128]{3,1,0,2:T(8,128)(2,1)} %get-tuple-element.7) | copy-start | bytes 15728644
  50.5 5.8 %copy-start.5 = (bf16[8,2048]{1,0:T(8,128)(2,1)S(1)}, bf16[8,2048]{1,0:T(8,128)(2,1)}, u32[]{:S(2)}) copy-start(bf16[8,2048]{1,0:T(8,128)(2,1)} %param.12) | copy-start | bytes 98308
  56.2 4.8 %copy-start.7 = (bf16[2048]{0:T(1024)(128)(2,1)S(1)}, bf16[2048]{0:T(1024)(128)(2,1)}, u32[]{:S(2)}) copy-start(bf16[2048]{0:T(1024)(128)(2,1)} %param.19) | copy-start | bytes 12292
  56.2 4.9 %copy-start.3 = (bf16[16,2048]{1,0:T(8,128)(2,1)S(1)}, bf16[16,2048]{1,0:T(8,128)(2,1)}, u32[]{:S(2)}) copy-start(bf16[16,2048]{1,0:T(8,128)(2,1)} %param.20) | copy-start | bytes 196612
  61.0 31.7 %copy-start.8 = (f32[8]{0:T(128)}, f32[8]{0:T(128)S(1)}, u32[]{:S(2)}) copy-start(f32[8]{0:T(128)S(1)} %add_sqrt_fusion) | copy-start | bytes 100
  94.7 18.6 %all-to-all-start.1 = ((bf16[32,4,2048]{2,1,0:T(4,128)(2,1)}), bf16[32,4,2048]{2,1,0:T(4,128)(2,1)S(1)}, u32[]{:S(2)}, u32[]{:S(2)}) async-start(bf16[32,4,2048]{2,1,0:T(4,128)(2,1)} %copy.54), calls=%async_computation.1 | async-start | bytes 1048576 | tf_op jit(solution)/shard_map/all_to_all | solution.py:100
where the time goes:
time: 117 us; the launch traced here: 116 us
  local copies, waits for them, and re-layouts  53.5 us (46%)
  blocking collectives  22.7 us (19%)
  matrix products  19.6 us (17%)
  waiting for transfers between devices  15.5 us (13%)
  starting transfers between devices  3.08 us (3%)
    gather x2, local copies, waits for them, and re-layouts, body(): refreshed_pool[page_table]  25.8 us
    all_to_all x1, blocking collectives, body(): lax.all_to_all(spread, 'req', split_axis=0, concat_axis=0, tiled=True)  22.7 us
    all_to_all x1, waiting for transfers between devices, body(): lax.all_to_all(terms.reshape(arrived.shape[0], arrived.shape[1], model_wi...  15.5 us
    unnamed x25, local copies, waits for them, and re-layouts  11.9 us
    slice x1, local copies, waits for them, and re-layouts, body(): collected_pages[..., :head_dim]  9.14 us
    dot_general x1, matrix products, body(): jnp.dot(attended, out_weight, preferred_element_type=jnp.float32)  4.72 us
    dot_general x1, matrix products, body(): jnp.einsum('rhgd,rphd->rhgp', query_heads, collected_pages[..., :head_dim...  4.45 us
    all_to_all x1, starting transfers between devices, body(): lax.all_to_all(terms.reshape(arrived.shape[0], arrived.shape[1], model_wi...  3.08 us
  transfers between devices with their start and end apart: 1, of which 1 were waited for; matrix products, arithmetic and copies ran while one was open for 0% of the time, Pallas kernels for 0%

commit v1 on v0

--- a/solution.py
+++ b/solution.py
@@ -70,47 +70,27 @@
     picked = jnp.sum(jnp.where(onehot, logits[:, None, :], 0.0), axis=-1)
     exponent_gate = jnp.exp(picked)
     gate_weights = exponent_gate / jnp.sum(exponent_gate, axis=-1, keepdims=True)
-    flat_hot = onehot.reshape(req_dev * chosen_count, experts)
-    counts = jnp.cumsum(flat_hot.astype(jnp.int32), axis=0)
-    slot_rank = (jnp.sum(jnp.where(flat_hot, counts, 0), axis=-1) - 1).reshape(
-        req_dev, chosen_count
-    )
-    capacity = 2 * max(1, (req_dev * chosen_count + 2 * experts - 1) // (2 * experts))
-    slot_index = expert_ids * capacity + slot_rank
-    slot_count = experts * capacity
-    assigned = slot_index[None, :, :] == jnp.arange(slot_count, dtype=jnp.int32)[:, None, None]
-    dispatch_mat = jnp.sum(assigned.astype(jnp.float32), axis=-1).astype(jnp.bfloat16)
-    outgoing = (
-        jnp.dot(dispatch_mat, normed, preferred_element_type=jnp.float32)
-        .astype(jnp.bfloat16)
-        .reshape(experts, capacity, model_width)
-    )
-    spread = jnp.repeat(outgoing, copies, axis=0)
-    combine_mat = jnp.sum(jnp.where(assigned, gate_weights[None, :, :], 0.0), axis=-1).T.reshape(
-        req_dev, experts, capacity
-    )
+    combine = jnp.sum(jnp.where(onehot, gate_weights[:, :, None], 0.0), axis=1)
+    combine_hi = combine.astype(jnp.bfloat16)
+    combine_lo = (combine - combine_hi.astype(jnp.float32)).astype(jnp.bfloat16)
+    pad = jnp.zeros((req_dev, -(2 * experts) % 128), jnp.bfloat16)
+    payload = jnp.concatenate([normed, combine_hi, combine_lo, pad], axis=1)
+    gathered = lax.all_gather(payload, "req", axis=0, tiled=True)
+    rows = gathered[:, :model_width]
+    expert = lax.axis_index("req") // copies
+    weights = gathered[:, model_width:].astype(jnp.float32)
+    column = jnp.arange(weights.shape[1], dtype=jnp.int32)
+    chosen = ((column == expert) | (column == expert + experts)).astype(jnp.float32)
+    row_weight = jnp.sum(weights * chosen[None, :], axis=1)
     gate_up = expert_gate_up[0]
     down_local = expert_down[0]
-    arrived = lax.all_to_all(spread, "req", split_axis=0, concat_axis=0, tiled=True)
-    rows = arrived.reshape(-1, model_width)
     gate_proj = jnp.einsum("rd,fd->rf", rows, gate_up[0], preferred_element_type=jnp.float32)
     up_proj = jnp.einsum("rd,fd->rf", rows, gate_up[1], preferred_element_type=jnp.float32)
     activated = (jax.nn.silu(gate_proj) * up_proj).astype(jnp.bfloat16)
     terms = jnp.dot(activated, down_local, preferred_element_type=jnp.float32)
-    returned = lax.all_to_all(
-        terms.reshape(arrived.shape[0], arrived.shape[1], model_width).astype(jnp.bfloat16),
-        "req",
-        split_axis=0,
-        concat_axis=0,
-        tiled=True,
-    )
-    pair_comb = jnp.repeat(combine_mat, copies, axis=1).reshape(req_dev, -1)
-    partial_routed = jnp.dot(
-        pair_comb,
-        returned.reshape(-1, model_width).astype(jnp.float32),
-        precision=lax.Precision.HIGHEST,
-    )
-    routed = lax.psum(partial_routed.astype(jnp.bfloat16), "kv").astype(jnp.float32)
+    weighted = (terms * row_weight[:, None]).astype(jnp.bfloat16)
+    partial_routed = lax.psum_scatter(weighted, "req", scatter_dimension=0, tiled=True)
+    routed = lax.psum(partial_routed, "kv").astype(jnp.float32)
     out_hidden = (mixed_float + routed).astype(jnp.bfloat16)
     return (out_hidden, refreshed_pool, hidden_norms, max_logit)
 

time: 117 us -> 280 us (2.39)
  waiting for transfers between devices: 15.5 us -> 190 us
  blocking collectives: 22.7 us -> 0 us
  between operations: 0.9 us -> 14.3 us
  local copies, waits for them, and re-layouts: 53.5 us -> 50.3 us
  starting transfers between devices: 3.08 us -> 0.26 us
    reduce_scatter x0 -> x1, waiting for transfers between devices: none -> 134 us  [body(): lax.psum_scatter(weighted, 'req', scatter_dimension=0, tiled=True)]
    all_gather x0 -> x1, waiting for transfers between devices: none -> 56.5 us  [body(): gathered = lax.all_gather(payload, 'req', axis=0, tiled=True)]
    all_to_all x1 -> x0, blocking collectives: 22.7 us -> none  [body(): lax.all_to_all(spread, 'req', split_axis=0, concat_axis=0, tiled=True)]
    all_to_all x1 -> x0, waiting for transfers between devices: 15.5 us -> none  [body(): lax.all_to_all(terms.reshape(arrived.shape[0], arrived.shape[1], model_wi...]
    dot_general x1, matrix products: 0.58 us -> 6.61 us  [body(): terms = jnp.dot(activated, down_local, preferred_element_type=jnp.float32)]
    dot_general x3 -> x0, matrix products: 5.2 us -> none  [the longest x1 2.9 us: body(): jnp.einsum('rd,fd->rf', rows, gate_up[1], preferred_element_type=jnp.floa...]
    all_to_all x1 -> x0, starting transfers between devices: 3.08 us -> none  [body(): lax.all_to_all(terms.reshape(arrived.shape[0], arrived.shape[1], model_wi...]
  transfers between devices with their start and end apart: 1 -> 2, of which waited for: 1 -> 2; matrix products, arithmetic and copies ran while one was open for 0% -> 0% of each run, Pallas kernels for 0% -> 0%
where the time goes in v1:
time: 280 us
  waiting for transfers between devices  190 us (68%)
  local copies, waits for them, and re-layouts  50.3 us (18%)
  matrix products  21.5 us (8%)
  between operations  14.3 us (5%)
  other arithmetic  3.13 us (1%)
    reduce_scatter x1, waiting for transfers between devices, body(): lax.psum_scatter(weighted, 'req', scatter_dimension=0, tiled=True)  134 us
    all_gather x1, waiting for transfers between devices, body(): gathered = lax.all_gather(payload, 'req', axis=0, tiled=True)  56.5 us
    gather x2, local copies, waits for them, and re-layouts, body(): refreshed_pool[page_table]  25.8 us
    unnamed x25, local copies, waits for them, and re-layouts  11.9 us
    slice x1, local copies, waits for them, and re-layouts, body(): collected_pages[..., :head_dim]  9.14 us
    dot_general x1, matrix products, body(): terms = jnp.dot(activated, down_local, preferred_element_type=jnp.float32)  6.61 us
  transfers between devices with their start and end apart: 2, of which 2 were waited for; matrix products, arithmetic and copies ran while one was open for 0% of the time, Pallas kernels for 0%

profile of v1, /device:TPU:0, one launch (start us, length us, event | category | flops | bytes accessed | tf_op | source)
XLA Modules:
  0.0 279.8 jit_solution(8638930943442590355)
XLA Ops:
  7.2 0.0 copy-start
  7.2 0.0 copy-start.5
  7.2 0.0 copy-start.1
  7.2 0.0 copy-start.9
  7.2 0.0 all-gather.2.cloned.1.call-start
  7.3 11.8 %copy.52 = bf16[104,32,4,256]{3,2,1,0:T(4,128)(2,1)} copy(bf16[104,32,4,256]{3,2,1,0:T(4,128)(2,1)} %param.15) | data formatting | bytes 13631488
  19.0 0.0 copy-done.9
  19.0 0.1 iota_compare_fusion.1
  19.1 0.0 copy-done.1
  19.2 0.6 gather_fusion.1
  19.8 0.1 reshape.104
  19.9 0.0 copy-done.5
  19.9 2.0 scatter_fusion
  21.9 15.7 %gather_fusion = bf16[160,32,4,256]{3,2,1,0:T(4,128)(2,1)} fusion(bf16[104,32,4,256]{3,2,1,0:T(4,128)(2,1)} %scatter_fusion, s32[1024]{0:T(1024)S(1)} %pad_clamp_fusion), kind=kCustom, calls=%fused_computation | custom fusion | bytes 20972160 | tf_op jit(solution)/shard_map/gather | solution.py:32
  37.7 10.0 %copy.21 = bf16[160,32,4,256]{3,1,0,2:T(8,128)(2,1)} copy(bf16[160,32,4,256]{3,2,1,0:T(4,128)(2,1)} %gather_fusion) | data formatting | bytes 20971520 | tf_op jit(solution)/shard_map/gather | solution.py:32
  47.7 0.0 copy-start.10
  47.7 9.1 %fusion.60 = (bf16[8,640,4,128]{3,1,0,2:T(8,128)(2,1)}, bf16[8,640,4,128]{3,1,0,2:T(8,128)(2,1)}) fusion(bf16[8,640,4,256]{3,1,0,2:T(8,128)(2,1)} %bitcast.47), kind=kLoop, calls=%fused_computation.71 | loop fusion | bytes 20971520 | tf_op jit(solution)/shard_map/slice | solution.py:39
  56.9 0.0 copy-start.2
  56.9 0.0 copy-done.10
  56.9 4.4 %fusion.61 = (f32[8,4,4]{2,1,0:T(4,128)S(1)}, f32[8,4,4,640]{3,2,1,0:T(4,128)S(1)}) fusion(bf16[8,4,4,128]{3,0,2,1:T(8,128)(2,1)S(1)} %bitcast.48, bf16[8,640,4,128]{3,1,0,2:T(8,128)(2,1)} %get-tuple-element.6, pred[8,640]{1,0:T(8,128)(4,1)S(1)} %iota_compare_fusion.1), kind=kOutput, calls=%fused_computation.72 | convolution fusion | flops 21217152 | bytes 5608960 | tf_op jit(solution)/shard_map/rhgd,rphd->rhgp/dot_general | solution.py:36
  61.3 0.0 copy-start.4
  61.3 0.3 fusion.50
  61.6 0.0 copy-done.2
  61.6 1.0 fusion.40
  62.6 0.0 copy-start.6
  62.6 0.0 copy-start.7
  62.6 0.0 copy-start.3
  62.6 0.0 copy-done.4
  62.6 4.7 %multiply_reduce_fusion.1 = (f32[8]{0:T(128)S(1)}, f32[8,2048]{1,0:T(8,128)S(1)}) fusion(bf16[8,2048]{1,0:T(8,128)(2,1)S(1)} %reshape.101, bf16[2048,2048]{1,0:T(8,128)(2,1)} %param.18, bf16[8,2048]{1,0:T(8,128)(2,1)S(1)} %copy-done.4), kind=kOutput, calls=%fused_computation.39 | convolution fusion | flops 67239928 | bytes 8519712 | tf_op jit(solution)/shard_map/dot_general | solution.py:56
  67.4 0.0 copy-done.6
  67.4 0.0 copy-start.8
  67.4 0.0 copy-done.7
  67.4 0.1 copy.25
  67.5 0.1 multiply_convert_fusion
  67.6 0.0 copy-done.3
  67.6 0.8 fusion.62
  68.3 0.1 select_reduce_fusion.1
  68.5 0.1 select_reduce_fusion
  68.7 0.7 concatenate.7
  69.3 0.0 all-gather.2.cloned.1.call-update
  69.4 0.2 reduce-scatter.2.cloned.1.call-start
  69.6 56.5 %all-gather.2.cloned.1.call-done = bf16[256,2176]{1,0:T(8,128)(2,1)} async-done(((bf16[8,2176]{1,0:T(8,128)(2,1)}), bf16[256,2176]{1,0:T(8,128)(2,1)}) %all-gather.2.cloned.1.call-update) | async-done | bytes 1114128 | tf_op jit(solution)/shard_map/all_gather | solution.py:78
  126.2 4.0 %fusion.8 = f32[256,704]{0,1:T(8,128)} fusion(bf16[1,2,704,2048]{3,2,1,0:T(8,128)(2,1)} %param.22, bf16[256,2176]{1,0:T(8,128)(2,1)} %all-gather.2.cloned.1.call-done), kind=kOutput, calls=%fused_computation.11 | convolution fusion | flops 738197504 | bytes 4653056 | tf_op jit(solution)/shard_map/rd,fd->rf/dot_general | solution.py:87
  130.1 1.0 multiply_reduce_fusion
  131.1 0.0 copy-done
  131.1 6.6 %fusion.15 = bf16[256,2048]{1,0:T(8,128)(2,1)} fusion(bf16[1,704,2048]{2,1,0:T(8,128)(2,1)S(1)} %copy-done, f32[256]{0:T(256)S(1)} %multiply_reduce_fusion, bf16[1,2,704,2048]{3,2,1,0:T(8,128)(2,1)} %param.22, bf16[256,2176]{1,0:T(8,128)(2,1)} %all-gather.2.cloned.1.call-done, f32[256,704]{0,1:T(8,128)} %fusion.8), kind=kOutput, calls=%fused_computation.16 | convolution fusion | flops 1478524928 | bytes 8586240 | tf_op jit(solution)/shard_map/dot_general | solution.py:90
  137.7 0.0 copy-done.8
  137.7 0.0 reduce-scatter.2.cloned.1.call-update
  137.7 133.8 %reduce-scatter.2.cloned.1.call-done = bf16[8,2048]{1,0:T(8,128)(2,1)} async-done(((bf16[256,2048]{1,0:T(8,128)(2,1)}), bf16[8,2048]{1,0:T(8,128)(2,1)}) %reduce-scatter.2.cloned.1.call-update) | async-done | bytes 32784 | tf_op jit(solution)/shard_map/reduce_scatter | solution.py:92
  271.6 1.4 add_convert_fusion
  (15 shorter events, 0.1 us)
Async XLA Ops:
  7.2 123.9 %copy-start = (bf16[1,704,2048]{2,1,0:T(8,128)(2,1)S(1)}, bf16[1,704,2048]{2,1,0:T(8,128)(2,1)}, u32[]{:S(2)}) copy-start(bf16[1,704,2048]{2,1,0:T(8,128)(2,1)} %param.23) | copy-start | bytes 8650756
  7.2 12.7 %copy-start.5 = (bf16[8,4,256]{2,1,0:T(4,128)(2,1)S(1)}, bf16[8,4,256]{2,1,0:T(4,128)(2,1)}, u32[]{:S(2)}) copy-start(bf16[8,4,256]{2,1,0:T(4,128)(2,1)} %param.14) | copy-start | bytes 49156
  7.2 12.0 %copy-start.1 = (s32[8,20]{1,0:T(8,128)S(1)}, s32[8,20]{1,0:T(8,128)}, u32[]{:S(2)}) copy-start(s32[8,20]{1,0:T(8,128)} %param.16) | copy-start | bytes 1924
  7.2 11.8 %copy-start.9 = (s32[8]{0:T(128)S(1)}, s32[8]{0:T(128)}, u32[]{:S(2)}) copy-start(s32[8]{0:T(128)} %param.17) | copy-start | bytes 100
  7.2 119.0 %all-gather.2.cloned.1.call-start = ((), (), s32[]{:S(2)}) async-start(), calls=%async_computation.1 | async-start | bytes 1148928 | tf_op jit(solution)/shard_map/all_gather | solution.py:78
  47.7 9.1 %copy-start.10 = (bf16[8,2048]{1,0:T(8,128)(2,1)S(1)}, bf16[8,2048]{1,0:T(8,128)(2,1)}, u32[]{:S(2)}) copy-start(bf16[8,2048]{1,0:T(8,128)(2,1)} %param.13) | copy-start | bytes 98308
  56.9 4.7 %copy-start.2 = (bf16[8,640,4,128]{3,1,0,2:T(8,128)(2,1)S(1)}, bf16[8,640,4,128]{3,1,0,2:T(8,128)(2,1)}, u32[]{:S(2)}) copy-start(bf16[8,640,4,128]{3,1,0,2:T(8,128)(2,1)} %get-tuple-element.7) | copy-start | bytes 15728644
  61.3 1.3 copy-start.4
  62.6 4.8 %copy-start.6 = (bf16[2048]{0:T(1024)(128)(2,1)S(1)}, bf16[2048]{0:T(1024)(128)(2,1)}, u32[]{:S(2)}) copy-start(bf16[2048]{0:T(1024)(128)(2,1)} %param.19) | copy-start | bytes 12292
  62.6 4.8 %copy-start.7 = (s32[8,6]{1,0:T(8,128)S(1)}, s32[8,6]{1,0:T(8,128)}, u32[]{:S(2)}) copy-start(s32[8,6]{1,0:T(8,128)} %param.21) | copy-start | bytes 580
  62.6 5.0 %copy-start.3 = (bf16[16,2048]{1,0:T(8,128)(2,1)S(1)}, bf16[16,2048]{1,0:T(8,128)(2,1)}, u32[]{:S(2)}) copy-start(bf16[16,2048]{1,0:T(8,128)(2,1)} %param.20) | copy-start | bytes 196612
  67.4 70.3 %copy-start.8 = (f32[8]{0:T(128)}, f32[8]{0:T(128)S(1)}, u32[]{:S(2)}) copy-start(f32[8]{0:T(128)S(1)} %add_sqrt_fusion) | copy-start | bytes 100
  69.4 202.2 %reduce-scatter.2.cloned.1.call-start = ((), (), s32[]{:S(2)}) async-start(), calls=%async_computation.2 | async-start | bytes 1081344 | tf_op jit(solution)/shard_map/reduce_scatter | solution.py:92
Sparse Core Ops, SparseCore 0:
  69.5 56.6 all-gather.1
  137.9 133.6 reduce-scatter.1

commit v2 on v0

--- a/solution.py
+++ b/solution.py
@@ -85,28 +85,33 @@
         .astype(jnp.bfloat16)
         .reshape(experts, capacity, model_width)
     )
-    spread = jnp.repeat(outgoing, copies, axis=0)
-    combine_mat = jnp.sum(jnp.where(assigned, gate_weights[None, :, :], 0.0), axis=-1).T.reshape(
-        req_dev, experts, capacity
-    )
+    combine_mat = jnp.sum(jnp.where(assigned, gate_weights[None, :, :], 0.0), axis=-1).T
+    same_part = [list(range(part, req_count, copies)) for part in range(copies)]
+    swap = [(index, index ^ 1) for index in range(req_count)]
     gate_up = expert_gate_up[0]
     down_local = expert_down[0]
-    arrived = lax.all_to_all(spread, "req", split_axis=0, concat_axis=0, tiled=True)
-    rows = arrived.reshape(-1, model_width)
+    arrived = lax.all_to_all(
+        outgoing, "req", split_axis=0, concat_axis=0, tiled=True, axis_index_groups=same_part
+    )
+    partner = lax.ppermute(arrived, "req", swap)
+    rows = jnp.concatenate([arrived, partner], axis=0).reshape(-1, model_width)
     gate_proj = jnp.einsum("rd,fd->rf", rows, gate_up[0], preferred_element_type=jnp.float32)
     up_proj = jnp.einsum("rd,fd->rf", rows, gate_up[1], preferred_element_type=jnp.float32)
     activated = (jax.nn.silu(gate_proj) * up_proj).astype(jnp.bfloat16)
-    terms = jnp.dot(activated, down_local, preferred_element_type=jnp.float32)
+    terms = jnp.dot(activated, down_local, preferred_element_type=jnp.float32).astype(jnp.bfloat16)
+    own_terms, partner_terms = jnp.split(terms, 2, axis=0)
+    swapped = lax.ppermute(partner_terms, "req", swap)
+    expert_out = (own_terms.astype(jnp.float32) + swapped.astype(jnp.float32)).astype(jnp.bfloat16)
     returned = lax.all_to_all(
-        terms.reshape(arrived.shape[0], arrived.shape[1], model_width).astype(jnp.bfloat16),
+        expert_out.reshape(arrived.shape),
         "req",
         split_axis=0,
         concat_axis=0,
         tiled=True,
+        axis_index_groups=same_part,
     )
-    pair_comb = jnp.repeat(combine_mat, copies, axis=1).reshape(req_dev, -1)
     partial_routed = jnp.dot(
-        pair_comb,
+        combine_mat,
         returned.reshape(-1, model_width).astype(jnp.float32),
         precision=lax.Precision.HIGHEST,
     )

time: 117 us -> 111 us (0.949)
  waiting for transfers between devices: 15.5 us -> 2.38 us
  blocking collectives: 22.7 us -> 31.9 us
  starting transfers between devices: 3.08 us -> 0.21 us
  other arithmetic: 1.14 us -> 2.5 us
    all_to_all x1 -> x0, waiting for transfers between devices: 15.5 us -> none  [body(): lax.all_to_all(terms.reshape(arrived.shape[0], arrived.shape[1], model_wi...]
    all_to_all x1 -> x2, blocking collectives: 22.7 us -> 31.9 us  [the longest x1 18.2 us: body(): lax.all_to_all(outgoing, 'req', split_axis=0, concat_axis=0, tiled=True,...]
    all_to_all x1 -> x0, starting transfers between devices: 3.08 us -> none  [body(): lax.all_to_all(terms.reshape(arrived.shape[0], arrived.shape[1], model_wi...]
    ppermute x0 -> x2, waiting for transfers between devices: none -> 2.38 us  [the longest x1 1.53 us: body(): partner = lax.ppermute(arrived, 'req', swap)]
    convert_element_type x2 -> x0, local copies, waits for them, and re-layouts: 1.34 us -> none  [the longest x1 1.2 us: body(): terms.reshape(arrived.shape[0], arrived.shape[1], model_width)]
    unnamed x25 -> x27, local copies, waits for them, and re-layouts: 11.9 us -> 12.5 us
    dot_general x3 -> x2, matrix products: 5.52 us -> 5.01 us  [the longest x1 4.17 us: body(): jnp.dot(activated, down_local, preferred_element_type=jnp.float32)]
  transfers between devices with their start and end apart: 1 -> 2, of which waited for: 1 -> 2; matrix products, arithmetic and copies ran while one was open for 0% -> 0% of each run, Pallas kernels for 0% -> 0%
where the time goes in v2:
time: 111 us; the launch traced here: 110 us
  local copies, waits for them, and re-layouts  52.5 us (47%)
  blocking collectives  31.9 us (29%)
  matrix products  19.8 us (18%)
  other arithmetic  2.5 us (2%)
  waiting for transfers between devices  2.38 us (2%)
    gather x2, local copies, waits for them, and re-layouts, body(): refreshed_pool[page_table]  25.8 us
    all_to_all x1, blocking collectives, body(): lax.all_to_all(outgoing, 'req', split_axis=0, concat_axis=0, tiled=True,...  18.2 us
    all_to_all x1, blocking collectives, body(): lax.all_to_all(expert_out.reshape(arrived.shape), 'req', split_axis=0, co...  13.7 us
    unnamed x27, local copies, waits for them, and re-layouts  12.5 us
    slice x1, local copies, waits for them, and re-layouts, body(): collected_pages[..., :head_dim]  9.14 us
    dot_general x1, matrix products, body(): jnp.dot(attended, out_weight, preferred_element_type=jnp.float32)  4.72 us
    dot_general x1, matrix products, body(): jnp.einsum('rhgd,rphd->rhgp', query_heads, collected_pages[..., :head_dim...  4.45 us
    dot_general x1, matrix products, body(): jnp.dot(activated, down_local, preferred_element_type=jnp.float32)  4.17 us
  transfers between devices with their start and end apart: 2, of which 2 were waited for; matrix products, arithmetic and copies ran while one was open for 0% of the time, Pallas kernels for 0%

profile of v2, /device:TPU:0, one launch (start us, length us, event | category | flops | bytes accessed | tf_op | source)
XLA Modules:
  0.0 110.2 jit_solution(16901087671561987605)
XLA Ops:
  0.6 0.0 copy-start
  0.6 0.0 copy-start.7
  0.7 0.0 copy-start.1
  0.7 0.0 copy-start.10
  0.7 0.0 copy-start.5
  0.7 11.8 %copy.53 = bf16[104,32,4,256]{3,2,1,0:T(4,128)(2,1)} copy(bf16[104,32,4,256]{3,2,1,0:T(4,128)(2,1)} %param.15) | data formatting | bytes 13631488
  12.5 0.0 copy-done.10
  12.5 0.1 iota_compare_fusion.3
  12.5 0.0 copy-done.5
  12.5 0.1 copy.26
  12.6 0.1 eq.37
  12.7 0.0 copy-done.1
  12.8 0.6 gather_fusion.1
  13.4 0.1 reshape.115
  13.5 0.0 copy-done.7
  13.5 2.0 %scatter_fusion = bf16[104,32,4,256]{3,2,1,0:T(4,128)(2,1)} fusion(bf16[104,32,4,256]{3,2,1,0:T(4,128)(2,1)} %copy.53, s32[8]{0:T(128)S(1)} %fusion.52, bf16[8,4,256]{2,1,0:T(4,128)(2,1)S(1)} %copy-done.7), kind=kCustom, calls=%fused_computation.2 | custom fusion | bytes 49216 | tf_op jit(solution)/shard_map/scatter | solution.py:31
  15.5 15.7 %gather_fusion = bf16[160,32,4,256]{3,2,1,0:T(4,128)(2,1)} fusion(bf16[104,32,4,256]{3,2,1,0:T(4,128)(2,1)} %scatter_fusion, s32[1024]{0:T(1024)S(1)} %pad_clamp_fusion), kind=kCustom, calls=%fused_computation | custom fusion | bytes 20972160 | tf_op jit(solution)/shard_map/gather | solution.py:32
  31.3 10.0 %copy.21 = bf16[160,32,4,256]{3,1,0,2:T(8,128)(2,1)} copy(bf16[160,32,4,256]{3,2,1,0:T(4,128)(2,1)} %gather_fusion) | data formatting | bytes 20971520 | tf_op jit(solution)/shard_map/gather | solution.py:32
  41.3 0.0 copy-start.11
  41.3 9.1 %fusion.54 = (bf16[8,640,4,128]{3,1,0,2:T(8,128)(2,1)}, bf16[8,640,4,128]{3,1,0,2:T(8,128)(2,1)}) fusion(bf16[8,640,4,256]{3,1,0,2:T(8,128)(2,1)} %bitcast.49), kind=kLoop, calls=%fused_computation.78 | loop fusion | bytes 20971520 | tf_op jit(solution)/shard_map/slice | solution.py:39
  50.5 0.0 copy-start.2
  50.5 0.0 copy-done.11
  50.5 0.0 copy-start.6
  50.5 4.4 %fusion.55 = (f32[8,4,4]{2,1,0:T(4,128)S(1)}, f32[8,4,4,640]{3,2,1,0:T(4,128)S(1)}) fusion(bf16[8,4,4,128]{3,0,2,1:T(8,128)(2,1)S(1)} %bitcast.50, bf16[8,640,4,128]{3,1,0,2:T(8,128)(2,1)} %get-tuple-element.6, pred[8,640]{1,0:T(8,128)(4,1)S(1)} %iota_compare_fusion.3), kind=kOutput, calls=%fused_computation.79 | convolution fusion | flops 21217152 | bytes 5608960 | tf_op jit(solution)/shard_map/rhgd,rphd->rhgp/dot_general | solution.py:36
  54.9 0.3 fusion.37
  55.2 0.0 copy-done.2
  55.2 1.0 fusion.34
  56.2 0.0 copy-start.8
  56.2 0.0 copy-start.4
  56.2 0.0 copy-done.6
  56.2 4.7 %multiply_reduce_fusion = (f32[8]{0:T(128)S(1)}, f32[8,2048]{1,0:T(8,128)S(1)}) fusion(bf16[8,2048]{1,0:T(8,128)(2,1)S(1)} %reshape.108, bf16[2048,2048]{1,0:T(8,128)(2,1)} %param.18, bf16[8,2048]{1,0:T(8,128)(2,1)S(1)} %copy-done.6), kind=kOutput, calls=%fused_computation.40 | convolution fusion | flops 67239928 | bytes 8519712 | tf_op jit(solution)/shard_map/dot_general | solution.py:56
  61.0 0.0 copy-done.8
  61.0 0.0 copy-start.9
  61.0 0.1 multiply_convert_fusion.2
  61.1 0.0 copy-done.4
  61.1 0.8 fusion.56
  61.8 0.1 select_reduce_fusion.1
  62.0 0.1 fusion.47
  62.1 0.1 reduce_window_sum.11
  62.2 0.2 select_reduce_fusion.2
  62.4 0.1 sub.22
  62.5 0.1 copy.25
  62.6 0.1 convert_reduce_fusion
  62.7 0.3 convolution_convert_fusion
  62.9 0.1 reshape.109
  63.0 18.2 %all_to_all.10 = bf16[16,4,2048]{2,1,0:T(4,128)(2,1)S(1)} all-to-all(bf16[16,4,2048]{2,1,0:T(4,128)(2,1)S(1)} %reshape.109), channel_id=1, replica_groups={{0,2,4,6,8,10,12,14,16,18,20,22,24,26,28,30},{1,3,5,7,9,11,13,15,17,19,..., dimensions={0} | all-to-all | bytes 524288 | tf_op jit(solution)/shard_map/all_to_all | solution.py:93
  81.2 0.0 collective-permute-start
  81.2 1.5 %collective-permute-done = bf16[16,4,2048]{2,1,0:T(4,128)(2,1)S(1)} collective-permute-done((bf16[16,4,2048]{2,1,0:T(4,128)(2,1)S(1)}, bf16[16,4,2048]{2,1,0:T(4,128)(2,1)S(1)}, u32[]{:S(2)}, u32[]{:S(2)}) %collective-permute-start) | collective-permute-done | bytes 262176 | tf_op jit(solution)/shard_map/ppermute | solution.py:96
  82.7 0.3 pad_maximum_fusion
  83.1 0.9 reshape.110
  84.0 3.6 %fusion.6 = f32[128,704]{0,1:T(8,128)} fusion(bf16[128,2048]{1,0:T(8,128)(2,1)} %reshape.110, bf16[1,2,704,2048]{3,2,1,0:T(8,128)(2,1)} %param.22), kind=kOutput, calls=%fused_computation.9 | convolution fusion | flops 369098752 | bytes 3768320 | tf_op jit(solution)/shard_map/rd,fd->rf/dot_general | solution.py:99
  87.6 0.0 copy-done
  87.6 4.2 %fusion.12 = bf16[128,2048]{1,0:T(8,128)(2,1)S(1)} fusion(bf16[1,704,2048]{2,1,0:T(8,128)(2,1)S(1)} %copy-done, f32[128,704]{0,1:T(8,128)} %fusion.6, bf16[128,2048]{1,0:T(8,128)(2,1)} %reshape.110, bf16[1,2,704,2048]{3,2,1,0:T(8,128)(2,1)} %param.22), kind=kOutput, calls=%fused_computation.15 | convolution fusion | flops 739000320 | bytes 7176192 | tf_op jit(solution)/shard_map/dot_general | solution.py:101
  91.8 0.0 copy-done.9
  91.8 0.0 copy-start.3
  91.9 0.2 collective-permute-start.1
  92.1 0.5 copy-done.3
  92.6 0.8 collective-permute-done.1
  93.5 1.0 add_convert_fusion
  94.5 0.1 reshape.111
  94.6 13.7 %all_to_all.11 = bf16[16,4,2048]{2,1,0:T(4,128)(2,1)} all-to-all(bf16[16,4,2048]{2,1,0:T(4,128)(2,1)S(1)} %reshape.111), channel_id=1, replica_groups={{0,2,4,6,8,10,12,14,16,18,20,22,24,26,28,30},{1,3,5,7,9,11,13,15,17,19,..., dimensions={0} | all-to-all | bytes 524288 | tf_op jit(solution)/shard_map/all_to_all | solution.py:105
  108.3 1.0 reshape.112
  109.3 0.8 fusion.17
  (15 shorter events, 0.2 us)
Async XLA Ops:
  0.6 87.0 %copy-start = (bf16[1,704,2048]{2,1,0:T(8,128)(2,1)S(1)}, bf16[1,704,2048]{2,1,0:T(8,128)(2,1)}, u32[]{:S(2)}) copy-start(bf16[1,704,2048]{2,1,0:T(8,128)(2,1)} %param.23) | copy-start | bytes 8650756
  0.6 12.9 %copy-start.7 = (bf16[8,4,256]{2,1,0:T(4,128)(2,1)S(1)}, bf16[8,4,256]{2,1,0:T(4,128)(2,1)}, u32[]{:S(2)}) copy-start(bf16[8,4,256]{2,1,0:T(4,128)(2,1)} %param.14) | copy-start | bytes 49156
  0.7 12.1 %copy-start.1 = (s32[8,20]{1,0:T(8,128)S(1)}, s32[8,20]{1,0:T(8,128)}, u32[]{:S(2)}) copy-start(s32[8,20]{1,0:T(8,128)} %param.16) | copy-start | bytes 1924
  0.7 11.8 %copy-start.10 = (s32[8]{0:T(128)S(1)}, s32[8]{0:T(128)}, u32[]{:S(2)}) copy-start(s32[8]{0:T(128)} %param.17) | copy-start | bytes 100
  0.7 11.9 %copy-start.5 = (s32[8,6]{1,0:T(8,128)S(1)}, s32[8,6]{1,0:T(8,128)}, u32[]{:S(2)}) copy-start(s32[8,6]{1,0:T(8,128)} %param.21) | copy-start | bytes 580
  41.3 9.1 %copy-start.11 = (bf16[8,2048]{1,0:T(8,128)(2,1)S(1)}, bf16[8,2048]{1,0:T(8,128)(2,1)}, u32[]{:S(2)}) copy-start(bf16[8,2048]{1,0:T(8,128)(2,1)} %param.13) | copy-start | bytes 98308
  50.5 4.7 %copy-start.2 = (bf16[8,640,4,128]{3,1,0,2:T(8,128)(2,1)S(1)}, bf16[8,640,4,128]{3,1,0,2:T(8,128)(2,1)}, u32[]{:S(2)}) copy-start(bf16[8,640,4,128]{3,1,0,2:T(8,128)(2,1)} %get-tuple-element.7) | copy-start | bytes 15728644
  50.5 5.8 %copy-start.6 = (bf16[8,2048]{1,0:T(8,128)(2,1)S(1)}, bf16[8,2048]{1,0:T(8,128)(2,1)}, u32[]{:S(2)}) copy-start(bf16[8,2048]{1,0:T(8,128)(2,1)} %param.12) | copy-start | bytes 98308
  56.2 4.8 %copy-start.8 = (bf16[2048]{0:T(1024)(128)(2,1)S(1)}, bf16[2048]{0:T(1024)(128)(2,1)}, u32[]{:S(2)}) copy-start(bf16[2048]{0:T(1024)(128)(2,1)} %param.19) | copy-start | bytes 12292
  56.2 4.9 %copy-start.4 = (bf16[16,2048]{1,0:T(8,128)(2,1)S(1)}, bf16[16,2048]{1,0:T(8,128)(2,1)}, u32[]{:S(2)}) copy-start(bf16[16,2048]{1,0:T(8,128)(2,1)} %param.20) | copy-start | bytes 196612
  61.0 30.8 %copy-start.9 = (f32[8]{0:T(128)}, f32[8]{0:T(128)S(1)}, u32[]{:S(2)}) copy-start(f32[8]{0:T(128)S(1)} %add_sqrt_fusion) | copy-start | bytes 100
  81.2 1.5 %collective-permute-start = (bf16[16,4,2048]{2,1,0:T(4,128)(2,1)S(1)}, bf16[16,4,2048]{2,1,0:T(4,128)(2,1)S(1)}, u32[]{:S(2)}, u32[]{:S(2)}) collective-permute-start(bf16[16,4,2048]{2,1,0:T(4,128)(2,1)S(1)} %all_to_all.10), channel_id=1, source_target_pairs={{0,1},{1,0},{2,3},{3,2},{4,5},{5,4},{6,7},{7,6},{8,9},{9,8},{10,11... | collective-permute-start | bytes 786440 | tf_op jit(solution)/shard_map/ppermute | solution.py:96
  91.8 0.8 copy-start.3
  91.9 1.6 %collective-permute-start.1 = (bf16[64,2048]{1,0:T(8,128)(2,1)S(1)}, bf16[64,2048]{1,0:T(8,128)(2,1)S(1)}, u32[]{:S(2)}, u32[]{:S(2)}) collective-permute-start(bf16[64,2048]{1,0:T(8,128)(2,1)S(1)} %split.9), channel_id=1, source_target_pairs={{0,1},{1,0},{2,3},{3,2},{4,5},{5,4},{6,7},{7,6},{8,9},{9,8},{10,11... | collective-permute-start | bytes 786440 | tf_op jit(solution)/shard_map/ppermute | solution.py:103

commit v3 on v2

--- a/solution.py
+++ b/solution.py
@@ -76,7 +76,8 @@
         req_dev, chosen_count
     )
     capacity = 2 * max(1, (req_dev * chosen_count + 2 * experts - 1) // (2 * experts))
-    slot_index = expert_ids * capacity + slot_rank
+    chip = lax.axis_index("req") // copies
+    slot_index = (expert_ids ^ chip) * capacity + slot_rank
     slot_count = experts * capacity
     assigned = slot_index[None, :, :] == jnp.arange(slot_count, dtype=jnp.int32)[:, None, None]
     dispatch_mat = jnp.sum(assigned.astype(jnp.float32), axis=-1).astype(jnp.bfloat16)
@@ -86,12 +87,15 @@
         .reshape(experts, capacity, model_width)
     )
     combine_mat = jnp.sum(jnp.where(assigned, gate_weights[None, :, :], 0.0), axis=-1).T
-    same_part = [list(range(part, req_count, copies)) for part in range(copies)]
+    routes = [
+        [(index, index ^ (copies * step)) for index in range(req_count)] for step in range(experts)
+    ]
     swap = [(index, index ^ 1) for index in range(req_count)]
     gate_up = expert_gate_up[0]
     down_local = expert_down[0]
-    arrived = lax.all_to_all(
-        outgoing, "req", split_axis=0, concat_axis=0, tiled=True, axis_index_groups=same_part
+    arrived = jnp.stack(
+        [outgoing[0]]
+        + [lax.ppermute(outgoing[step], "req", routes[step]) for step in range(1, experts)]
     )
     partner = lax.ppermute(arrived, "req", swap)
     rows = jnp.concatenate([arrived, partner], axis=0).reshape(-1, model_width)
@@ -102,13 +106,10 @@
     own_terms, partner_terms = jnp.split(terms, 2, axis=0)
     swapped = lax.ppermute(partner_terms, "req", swap)
     expert_out = (own_terms.astype(jnp.float32) + swapped.astype(jnp.float32)).astype(jnp.bfloat16)
-    returned = lax.all_to_all(
-        expert_out.reshape(arrived.shape),
-        "req",
-        split_axis=0,
-        concat_axis=0,
-        tiled=True,
-        axis_index_groups=same_part,
+    leaving = expert_out.reshape(arrived.shape)
+    returned = jnp.stack(
+        [leaving[0]]
+        + [lax.ppermute(leaving[step], "req", routes[step]) for step in range(1, experts)]
     )
     partial_routed = jnp.dot(
         combine_mat,

time: 111 us -> 153 us (1.38)
  starting transfers between devices: 0.21 us -> 55.1 us
  blocking collectives: 31.9 us -> 0 us
  local copies, waits for them, and re-layouts: 52.5 us -> 63.9 us
  waiting for transfers between devices: 2.38 us -> 10.2 us
    ppermute x0 -> x30, starting transfers between devices: none -> 54.9 us  [the longest x15 27.8 us: body(): lax.ppermute(outgoing[step], 'req', routes[step])]
    all_to_all x2 -> x0, blocking collectives: 31.9 us -> none  [the longest x1 18.2 us: body(): lax.all_to_all(outgoing, 'req', split_axis=0, concat_axis=0, tiled=True,...]
    unnamed x27 -> x55, local copies, waits for them, and re-layouts: 12.5 us -> 21.3 us
    ppermute x0 -> x30, waiting for transfers between devices: none -> 7.29 us  [the longest x15 4.29 us: body(): lax.ppermute(outgoing[step], 'req', routes[step])]
  transfers between devices with their start and end apart: 2 -> 32, of which waited for: 2 -> 5; matrix products, arithmetic and copies ran while one was open for 0% -> 6% of each run, Pallas kernels for 0% -> 0%
where the time goes in v3:
time: 153 us
  local copies, waits for them, and re-layouts  63.9 us (42%)
  starting transfers between devices  55.1 us (36%)
  matrix products  20.6 us (13%)
  waiting for transfers between devices  10.2 us (7%)
  other arithmetic  2.15 us (1%)
    ppermute x15, starting transfers between devices, body(): lax.ppermute(outgoing[step], 'req', routes[step])  27.8 us
    ppermute x15, starting transfers between devices, body(): lax.ppermute(leaving[step], 'req', routes[step])  27.1 us
    gather x2, local copies, waits for them, and re-layouts, body(): refreshed_pool[page_table]  25.8 us
    unnamed x55, local copies, waits for them, and re-layouts  21.3 us
    slice x1, local copies, waits for them, and re-layouts, body(): collected_pages[..., :head_dim]  9.15 us
    dot_general x1, matrix products, body(): jnp.dot(activated, down_local, preferred_element_type=jnp.float32)  4.97 us
    dot_general x1, matrix products, body(): jnp.dot(attended, out_weight, preferred_element_type=jnp.float32)  4.69 us
    dot_general x1, matrix products, body(): jnp.einsum('rhgd,rphd->rhgp', query_heads, collected_pages[..., :head_dim...  4.45 us
  transfers between devices with their start and end apart: 32, of which 5 were waited for; matrix products, arithmetic and copies ran while one was open for 6% of the time, Pallas kernels for 0%

profile of v3, /device:TPU:0, one launch (start us, length us, event | category | flops | bytes accessed | tf_op | source)
XLA Modules:
  0.0 153.1 jit_solution(5297683701940851396)
XLA Ops:
  0.7 11.8 %copy.99 = bf16[104,32,4,256]{3,2,1,0:T(4,128)(2,1)} copy(bf16[104,32,4,256]{3,2,1,0:T(4,128)(2,1)} %param.15) | data formatting | bytes 13631488
  12.8 0.6 gather_fusion.1
  13.5 2.0 %scatter_fusion = bf16[104,32,4,256]{3,2,1,0:T(4,128)(2,1)} fusion(bf16[104,32,4,256]{3,2,1,0:T(4,128)(2,1)} %copy.99, s32[8]{0:T(128)S(1)} %fusion.52, bf16[8,4,256]{2,1,0:T(4,128)(2,1)S(1)} %copy-done.6), kind=kCustom, calls=%fused_computation.2 | custom fusion | bytes 49216 | tf_op jit(solution)/shard_map/scatter | solution.py:31
  15.5 15.8 %gather_fusion = bf16[160,32,4,256]{3,2,1,0:T(4,128)(2,1)} fusion(bf16[104,32,4,256]{3,2,1,0:T(4,128)(2,1)} %scatter_fusion, s32[1024]{0:T(1024)S(1)} %pad_clamp_fusion), kind=kCustom, calls=%fused_computation | custom fusion | bytes 20972160 | tf_op jit(solution)/shard_map/gather | solution.py:32
  31.3 10.1 %copy.21 = bf16[160,32,4,256]{3,1,0,2:T(8,128)(2,1)} copy(bf16[160,32,4,256]{3,2,1,0:T(4,128)(2,1)} %gather_fusion) | data formatting | bytes 20971520 | tf_op jit(solution)/shard_map/gather | solution.py:32
  41.4 9.2 %fusion.54 = (bf16[8,640,4,128]{3,1,0,2:T(8,128)(2,1)}, bf16[8,640,4,128]{3,1,0,2:T(8,128)(2,1)}) fusion(bf16[8,640,4,256]{3,1,0,2:T(8,128)(2,1)} %bitcast.134), kind=kLoop, calls=%fused_computation.128 | loop fusion | bytes 20971520 | tf_op jit(solution)/shard_map/slice | solution.py:39
  50.5 4.4 %fusion.57 = (f32[8,4,4]{2,1,0:T(4,128)S(1)}, f32[8,4,4,640]{3,2,1,0:T(4,128)S(1)}) fusion(bf16[8,4,4,128]{3,0,2,1:T(8,128)(2,1)S(1)} %bitcast.135, bf16[8,640,4,128]{3,1,0,2:T(8,128)(2,1)} %get-tuple-element.6, pred[8,640]{1,0:T(8,128)(4,1)S(1)} %iota_compare_fusion.3), kind=kOutput, calls=%fused_computation.131 | convolution fusion | flops 21217152 | bytes 5608960 | tf_op jit(solution)/shard_map/rhgd,rphd->rhgp/dot_general | solution.py:36
  55.0 0.3 fusion.37
  55.3 1.0 fusion.34
  56.5 0.2 select_reduce_fusion.2
  56.8 4.7 %multiply_reduce_fusion = (f32[8]{0:T(128)S(1)}, f32[8,2048]{1,0:T(8,128)S(1)}) fusion(bf16[8,2048]{1,0:T(8,128)(2,1)S(1)} %reshape.166, bf16[2048,2048]{1,0:T(8,128)(2,1)} %param.18, bf16[8,2048]{1,0:T(8,128)(2,1)S(1)} %copy-done.5), kind=kOutput, calls=%fused_computation.88 | convolution fusion | flops 67239928 | bytes 8519712 | tf_op jit(solution)/shard_map/dot_general | solution.py:56
  61.7 0.8 fusion.58
  62.7 0.3 convolution_convert_fusion
  63.1 3.0 %collective-permute-start = (bf16[4,2048]{1,0:T(4,128)(2,1)S(1)}, bf16[4,2048]{1,0:T(4,128)(2,1)S(1)}, u32[]{:S(2)}, u32[]{:S(2)}) collective-permute-start(bf16[4,2048]{1,0:T(4,128)(2,1)S(1)} %get-tuple-element.39), channel_id=1, source_target_pairs={{0,2},{1,3},{2,0},{3,1},{4,6},{5,7},{6,4},{7,5},{8,10},{9,11},{10,... | collective-permute-start | bytes 49160 | tf_op jit(solution)/shard_map/ppermute | solution.py:98
  66.1 1.5 collective-permute-start.1
  67.6 2.0 %collective-permute-start.3 = (bf16[4,2048]{1,0:T(4,128)(2,1)S(1)}, bf16[4,2048]{1,0:T(4,128)(2,1)S(1)}, u32[]{:S(2)}, u32[]{:S(2)}) collective-permute-start(bf16[4,2048]{1,0:T(4,128)(2,1)S(1)} %get-tuple-element.36), channel_id=1, source_target_pairs={{0,8},{1,9},{2,10},{3,11},{4,12},{5,13},{6,14},{7,15},{8,0},{9,1},... | collective-permute-start | bytes 49160 | tf_op jit(solution)/shard_map/ppermute | solution.py:98
  69.7 1.4 collective-permute-start.4
  71.0 0.6 constant_dynamic-update-slice_fusion.15
  71.7 2.5 %collective-permute-start.5 = (bf16[4,2048]{1,0:T(4,128)(2,1)S(1)}, bf16[4,2048]{1,0:T(4,128)(2,1)S(1)}, u32[]{:S(2)}, u32[]{:S(2)}) collective-permute-start(bf16[4,2048]{1,0:T(4,128)(2,1)S(1)} %get-tuple-element.34), channel_id=1, source_target_pairs={{0,12},{1,13},{2,14},{3,15},{4,8},{5,9},{6,10},{7,11},{8,4},{9,5},... | collective-permute-start | bytes 49160 | tf_op jit(solution)/shard_map/ppermute | solution.py:98
  74.2 0.6 constant_dynamic-update-slice_fusion.14
  74.8 0.6 constant_dynamic-update-slice_fusion.13
  75.4 2.9 %collective-permute-start.7 = (bf16[4,2048]{1,0:T(4,128)(2,1)S(1)}, bf16[4,2048]{1,0:T(4,128)(2,1)S(1)}, u32[]{:S(2)}, u32[]{:S(2)}) collective-permute-start(bf16[4,2048]{1,0:T(4,128)(2,1)S(1)} %get-tuple-element.32), channel_id=1, source_target_pairs={{0,16},{1,17},{2,18},{3,19},{4,20},{5,21},{6,22},{7,23},{8,24},{9,... | collective-permute-start | bytes 49160 | tf_op jit(solution)/shard_map/ppermute | solution.py:98
  78.4 0.6 constant_dynamic-update-slice_fusion.12
  79.0 1.3 collective-permute-start.8
  80.3 0.6 constant_dynamic-update-slice_fusion.11
  80.9 3.5 %collective-permute-start.9 = (bf16[4,2048]{1,0:T(4,128)(2,1)S(1)}, bf16[4,2048]{1,0:T(4,128)(2,1)S(1)}, u32[]{:S(2)}, u32[]{:S(2)}) collective-permute-start(bf16[4,2048]{1,0:T(4,128)(2,1)S(1)} %get-tuple-element.30), channel_id=1, source_target_pairs={{0,20},{1,21},{2,22},{3,23},{4,16},{5,17},{6,18},{7,19},{8,28},{9,... | collective-permute-start | bytes 49160 | tf_op jit(solution)/shard_map/ppermute | solution.py:98
  84.4 0.6 constant_dynamic-update-slice_fusion.10
  85.0 0.6 constant_dynamic-update-slice_fusion.9
  85.7 3.8 %collective-permute-start.11 = (bf16[4,2048]{1,0:T(4,128)(2,1)S(1)}, bf16[4,2048]{1,0:T(4,128)(2,1)S(1)}, u32[]{:S(2)}, u32[]{:S(2)}) collective-permute-start(bf16[4,2048]{1,0:T(4,128)(2,1)S(1)} %get-tuple-element.28), channel_id=1, source_target_pairs={{0,24},{1,25},{2,26},{3,27},{4,28},{5,29},{6,30},{7,31},{8,16},{9,... | collective-permute-start | bytes 49160 | tf_op jit(solution)/shard_map/ppermute | solution.py:98
  89.5 0.6 constant_dynamic-update-slice_fusion.8
  90.1 1.2 collective-permute-start.12
  91.3 0.6 constant_dynamic-update-slice_fusion.7
  91.9 4.6 %collective-permute-start.13 = (bf16[4,2048]{1,0:T(4,128)(2,1)S(1)}, bf16[4,2048]{1,0:T(4,128)(2,1)S(1)}, u32[]{:S(2)}, u32[]{:S(2)}) collective-permute-start(bf16[4,2048]{1,0:T(4,128)(2,1)S(1)} %get-tuple-element.26), channel_id=1, source_target_pairs={{0,28},{1,29},{2,30},{3,31},{4,24},{5,25},{6,26},{7,27},{8,20},{9,... | collective-permute-start | bytes 49160 | tf_op jit(solution)/shard_map/ppermute | solution.py:98
  96.5 0.6 constant_dynamic-update-slice_fusion.6
  97.1 0.6 constant_dynamic-update-slice_fusion.5
  97.7 0.6 constant_dynamic-update-slice_fusion.4
  98.3 0.6 constant_dynamic-update-slice_fusion.3
  98.9 0.6 constant_dynamic-update-slice_fusion.2
  99.5 0.6 constant_dynamic-update-slice_fusion.1
  100.2 4.3 %collective-permute-done.14 = bf16[4,2048]{1,0:T(4,128)(2,1)S(1)} collective-permute-done((bf16[4,2048]{1,0:T(4,128)(2,1)S(1)}, bf16[4,2048]{1,0:T(4,128)(2,1)S(1)}, u32[]{:S(2)}, u32[]{:S(2)}) %collective-permute-start.14) | collective-permute-done | bytes 16416 | tf_op jit(solution)/shard_map/ppermute | solution.py:98
  104.4 0.6 constant_dynamic-update-slice_fusion
  105.0 1.5 %collective-permute-done.15 = bf16[16,4,2048]{2,1,0:T(4,128)(2,1)S(1)} collective-permute-done((bf16[16,4,2048]{2,1,0:T(4,128)(2,1)S(1)}, bf16[16,4,2048]{2,1,0:T(4,128)(2,1)S(1)}, u32[]{:S(2)}, u32[]{:S(2)}) %collective-permute-start.15) | collective-permute-done | bytes 262176 | tf_op jit(solution)/shard_map/ppermute | solution.py:100
  106.6 0.8 constant_dynamic-update-slice_fusion.16
  107.4 2.0 %reshape.167 = bf16[128,2048]{1,0:T(8,128)(2,1)} reshape(bf16[32,4,2048]{2,1,0:T(4,128)(2,1)} %constant_dynamic-update-slice_fusion.16) | data formatting | bytes 1048576 | tf_op jit(solution)/shard_map/reshape | solution.py:101
  109.3 3.6 %fusion.6 = f32[128,704]{0,1:T(8,128)} fusion(bf16[128,2048]{1,0:T(8,128)(2,1)} %reshape.167, bf16[1,2,704,2048]{3,2,1,0:T(8,128)(2,1)} %param.22), kind=kOutput, calls=%fused_computation.9 | convolution fusion | flops 369098752 | bytes 3768320 | tf_op jit(solution)/shard_map/rd,fd->rf/dot_general | solution.py:103
  113.0 5.0 %fusion.12 = bf16[128,2048]{1,0:T(8,128)(2,1)} fusion(bf16[1,704,2048]{2,1,0:T(8,128)(2,1)S(1)} %copy-done, f32[128,704]{0,1:T(8,128)} %fusion.6, bf16[128,2048]{1,0:T(8,128)(2,1)} %reshape.167, bf16[1,2,704,2048]{3,2,1,0:T(8,128)(2,1)} %param.22), kind=kOutput, calls=%fused_computation.15 | convolution fusion | flops 739000320 | bytes 7176192 | tf_op jit(solution)/shard_map/dot_general | solution.py:105
  117.9 1.0 split.9
  118.9 0.2 collective-permute-start.16
  119.1 1.4 collective-permute-done.16
  120.5 1.0 add_convert_fusion
  121.6 0.6 collective-permute-start.17
  122.3 0.6 collective-permute-start.18
  122.8 2.4 %collective-permute-start.19 = (bf16[4,2048]{1,0:T(4,128)(2,1)S(1)}, bf16[4,2048]{1,0:T(4,128)(2,1)S(1)}, u32[]{:S(2)}, u32[]{:S(2)}) collective-permute-start(bf16[4,2048]{1,0:T(4,128)(2,1)S(1)} %get-tuple-element.20), channel_id=1, source_target_pairs={{0,6},{1,7},{2,4},{3,5},{4,2},{5,3},{6,0},{7,1},{8,14},{9,15},{10,... | collective-permute-start | bytes 49160 | tf_op jit(solution)/shard_map/ppermute | solution.py:112
  125.3 2.0 %collective-permute-start.21 = (bf16[4,2048]{1,0:T(4,128)(2,1)S(1)}, bf16[4,2048]{1,0:T(4,128)(2,1)S(1)}, u32[]{:S(2)}, u32[]{:S(2)}) collective-permute-start(bf16[4,2048]{1,0:T(4,128)(2,1)S(1)} %get-tuple-element.18), channel_id=1, source_target_pairs={{0,10},{1,11},{2,8},{3,9},{4,14},{5,15},{6,12},{7,13},{8,2},{9,3},... | collective-permute-start | bytes 49160 | tf_op jit(solution)/shard_map/ppermute | solution.py:112
  127.3 3.9 %collective-permute-start.23 = (bf16[4,2048]{1,0:T(4,128)(2,1)S(1)}, bf16[4,2048]{1,0:T(4,128)(2,1)S(1)}, u32[]{:S(2)}, u32[]{:S(2)}) collective-permute-start(bf16[4,2048]{1,0:T(4,128)(2,1)S(1)} %get-tuple-element.16), channel_id=1, source_target_pairs={{0,14},{1,15},{2,12},{3,13},{4,10},{5,11},{6,8},{7,9},{8,6},{9,7},... | collective-permute-start | bytes 49160 | tf_op jit(solution)/shard_map/ppermute | solution.py:112
  131.4 2.9 %collective-permute-start.25 = (bf16[4,2048]{1,0:T(4,128)(2,1)S(1)}, bf16[4,2048]{1,0:T(4,128)(2,1)S(1)}, u32[]{:S(2)}, u32[]{:S(2)}) collective-permute-start(bf16[4,2048]{1,0:T(4,128)(2,1)S(1)} %get-tuple-element.14), channel_id=1, source_target_pairs={{0,18},{1,19},{2,16},{3,17},{4,22},{5,23},{6,20},{7,21},{8,26},{9,... | collective-permute-start | bytes 49160 | tf_op jit(solution)/shard_map/ppermute | solution.py:112
  134.4 4.8 %collective-permute-start.27 = (bf16[4,2048]{1,0:T(4,128)(2,1)S(1)}, bf16[4,2048]{1,0:T(4,128)(2,1)S(1)}, u32[]{:S(2)}, u32[]{:S(2)}) collective-permute-start(bf16[4,2048]{1,0:T(4,128)(2,1)S(1)} %get-tuple-element.12), channel_id=1, source_target_pairs={{0,22},{1,23},{2,20},{3,21},{4,18},{5,19},{6,16},{7,17},{8,30},{9,... | collective-permute-start | bytes 49160 | tf_op jit(solution)/shard_map/ppermute | solution.py:112
  139.3 0.3 collective-permute-start.28
  139.6 3.6 %collective-permute-start.29 = (bf16[4,2048]{1,0:T(4,128)(2,1)S(1)}, bf16[4,2048]{1,0:T(4,128)(2,1)S(1)}, u32[]{:S(2)}, u32[]{:S(2)}) collective-permute-start(bf16[4,2048]{1,0:T(4,128)(2,1)S(1)} %get-tuple-element.10), channel_id=1, source_target_pairs={{0,26},{1,27},{2,24},{3,25},{4,30},{5,31},{6,28},{7,29},{8,18},{9,... | collective-permute-start | bytes 49160 | tf_op jit(solution)/shard_map/ppermute | solution.py:112
  143.2 1.5 collective-permute-start.30
  144.7 4.3 %collective-permute-start.31 = (bf16[4,2048]{1,0:T(4,128)(2,1)S(1)}, bf16[4,2048]{1,0:T(4,128)(2,1)S(1)}, u32[]{:S(2)}, u32[]{:S(2)}) collective-permute-start(bf16[4,2048]{1,0:T(4,128)(2,1)S(1)} %get-tuple-element.8), channel_id=1, source_target_pairs={{0,30},{1,31},{2,28},{3,29},{4,26},{5,27},{6,24},{7,25},{8,22},{9,... | collective-permute-start | bytes 49160 | tf_op jit(solution)/shard_map/ppermute | solution.py:112
  149.2 0.6 collective-permute-done.30
  149.8 2.4 %collective-permute-done.31 = bf16[4,2048]{1,0:T(4,128)(2,1)S(1)} collective-permute-done((bf16[4,2048]{1,0:T(4,128)(2,1)S(1)}, bf16[4,2048]{1,0:T(4,128)(2,1)S(1)}, u32[]{:S(2)}, u32[]{:S(2)}) %collective-permute-start.31) | collective-permute-done | bytes 16416 | tf_op jit(solution)/shard_map/ppermute | solution.py:112
  152.2 0.8 fusion.17
  (102 shorter events, 1.9 us)
Async XLA Ops:
  0.6 112.3 %copy-start = (bf16[1,704,2048]{2,1,0:T(8,128)(2,1)S(1)}, bf16[1,704,2048]{2,1,0:T(8,128)(2,1)}, u32[]{:S(2)}) copy-start(bf16[1,704,2048]{2,1,0:T(8,128)(2,1)} %param.23) | copy-start | bytes 8650756
  0.6 12.9 %copy-start.6 = (bf16[8,4,256]{2,1,0:T(4,128)(2,1)S(1)}, bf16[8,4,256]{2,1,0:T(4,128)(2,1)}, u32[]{:S(2)}) copy-start(bf16[8,4,256]{2,1,0:T(4,128)(2,1)} %param.14) | copy-start | bytes 49156
  0.7 12.1 %copy-start.1 = (s32[8,20]{1,0:T(8,128)S(1)}, s32[8,20]{1,0:T(8,128)}, u32[]{:S(2)}) copy-start(s32[8,20]{1,0:T(8,128)} %param.16) | copy-start | bytes 1924
  0.7 11.8 %copy-start.9 = (s32[8]{0:T(128)S(1)}, s32[8]{0:T(128)}, u32[]{:S(2)}) copy-start(s32[8]{0:T(128)} %param.17) | copy-start | bytes 100
  0.7 11.9 %copy-start.4 = (s32[8,6]{1,0:T(8,128)S(1)}, s32[8,6]{1,0:T(8,128)}, u32[]{:S(2)}) copy-start(s32[8,6]{1,0:T(8,128)} %param.21) | copy-start | bytes 580
  41.4 9.2 %copy-start.10 = (bf16[8,2048]{1,0:T(8,128)(2,1)S(1)}, bf16[8,2048]{1,0:T(8,128)(2,1)}, u32[]{:S(2)}) copy-start(bf16[8,2048]{1,0:T(8,128)(2,1)} %param.13) | copy-start | bytes 98308
  50.5 4.8 %copy-start.2 = (bf16[8,640,4,128]{3,1,0,2:T(8,128)(2,1)S(1)}, bf16[8,640,4,128]{3,1,0,2:T(8,128)(2,1)}, u32[]{:S(2)}) copy-start(bf16[8,640,4,128]{3,1,0,2:T(8,128)(2,1)} %get-tuple-element.7) | copy-start | bytes 15728644
  50.5 6.3 %copy-start.7 = (bf16[2048]{0:T(1024)(128)(2,1)S(1)}, bf16[2048]{0:T(1024)(128)(2,1)}, u32[]{:S(2)}) copy-start(bf16[2048]{0:T(1024)(128)(2,1)} %param.19) | copy-start | bytes 12292
  50.5 6.3 %copy-start.5 = (bf16[8,2048]{1,0:T(8,128)(2,1)S(1)}, bf16[8,2048]{1,0:T(8,128)(2,1)}, u32[]{:S(2)}) copy-start(bf16[8,2048]{1,0:T(8,128)(2,1)} %param.12) | copy-start | bytes 98308
  56.3 5.4 %copy-start.3 = (bf16[16,2048]{1,0:T(8,128)(2,1)S(1)}, bf16[16,2048]{1,0:T(8,128)(2,1)}, u32[]{:S(2)}) copy-start(bf16[16,2048]{1,0:T(8,128)(2,1)} %param.20) | copy-start | bytes 196612
  61.5 56.4 %copy-start.8 = (f32[8]{0:T(128)}, f32[8]{0:T(128)S(1)}, u32[]{:S(2)}) copy-start(f32[8]{0:T(128)S(1)} %add_sqrt_fusion) | copy-start | bytes 100
  63.1 8.6 %collective-permute-start = (bf16[4,2048]{1,0:T(4,128)(2,1)S(1)}, bf16[4,2048]{1,0:T(4,128)(2,1)S(1)}, u32[]{:S(2)}, u32[]{:S(2)}) collective-permute-start(bf16[4,2048]{1,0:T(4,128)(2,1)S(1)} %get-tuple-element.39), channel_id=1, source_target_pairs={{0,2},{1,3},{2,0},{3,1},{4,6},{5,7},{6,4},{7,5},{8,10},{9,11},{10,... | collective-permute-start | bytes 49160 | tf_op jit(solution)/shard_map/ppermute | solution.py:98
  66.1 8.7 %collective-permute-start.1 = (bf16[4,2048]{1,0:T(4,128)(2,1)S(1)}, bf16[4,2048]{1,0:T(4,128)(2,1)S(1)}, u32[]{:S(2)}, u32[]{:S(2)}) collective-permute-start(bf16[4,2048]{1,0:T(4,128)(2,1)S(1)} %get-tuple-element.38), channel_id=1, source_target_pairs={{0,4},{1,5},{2,6},{3,7},{4,0},{5,1},{6,2},{7,3},{8,12},{9,13},{10,... | collective-permute-start | bytes 49160 | tf_op jit(solution)/shard_map/ppermute | solution.py:98
  67.6 7.8 %collective-permute-start.2 = (bf16[4,2048]{1,0:T(4,128)(2,1)S(1)}, bf16[4,2048]{1,0:T(4,128)(2,1)S(1)}, u32[]{:S(2)}, u32[]{:S(2)}) collective-permute-start(bf16[4,2048]{1,0:T(4,128)(2,1)S(1)} %get-tuple-element.37), channel_id=1, source_target_pairs={{0,6},{1,7},{2,4},{3,5},{4,2},{5,3},{6,0},{7,1},{8,14},{9,15},{10,... | collective-permute-start | bytes 49160 | tf_op jit(solution)/shard_map/ppermute | solution.py:98
  67.6 11.4 %collective-permute-start.3 = (bf16[4,2048]{1,0:T(4,128)(2,1)S(1)}, bf16[4,2048]{1,0:T(4,128)(2,1)S(1)}, u32[]{:S(2)}, u32[]{:S(2)}) collective-permute-start(bf16[4,2048]{1,0:T(4,128)(2,1)S(1)} %get-tuple-element.36), channel_id=1, source_target_pairs={{0,8},{1,9},{2,10},{3,11},{4,12},{5,13},{6,14},{7,15},{8,0},{9,1},... | collective-permute-start | bytes 49160 | tf_op jit(solution)/shard_map/ppermute | solution.py:98
  69.7 11.2 %collective-permute-start.4 = (bf16[4,2048]{1,0:T(4,128)(2,1)S(1)}, bf16[4,2048]{1,0:T(4,128)(2,1)S(1)}, u32[]{:S(2)}, u32[]{:S(2)}) collective-permute-start(bf16[4,2048]{1,0:T(4,128)(2,1)S(1)} %get-tuple-element.35), channel_id=1, source_target_pairs={{0,10},{1,11},{2,8},{3,9},{4,14},{5,15},{6,12},{7,13},{8,2},{9,3},... | collective-permute-start | bytes 49160 | tf_op jit(solution)/shard_map/ppermute | solution.py:98
  71.7 13.4 %collective-permute-start.5 = (bf16[4,2048]{1,0:T(4,128)(2,1)S(1)}, bf16[4,2048]{1,0:T(4,128)(2,1)S(1)}, u32[]{:S(2)}, u32[]{:S(2)}) collective-permute-start(bf16[4,2048]{1,0:T(4,128)(2,1)S(1)} %get-tuple-element.34), channel_id=1, source_target_pairs={{0,12},{1,13},{2,14},{3,15},{4,8},{5,9},{6,10},{7,11},{8,4},{9,5},... | collective-permute-start | bytes 49160 | tf_op jit(solution)/shard_map/ppermute | solution.py:98
  74.8 10.8 %collective-permute-start.6 = (bf16[4,2048]{1,0:T(4,128)(2,1)S(1)}, bf16[4,2048]{1,0:T(4,128)(2,1)S(1)}, u32[]{:S(2)}, u32[]{:S(2)}) collective-permute-start(bf16[4,2048]{1,0:T(4,128)(2,1)S(1)} %get-tuple-element.33), channel_id=1, source_target_pairs={{0,14},{1,15},{2,12},{3,13},{4,10},{5,11},{6,8},{7,9},{8,6},{9,7},... | collective-permute-start | bytes 49160 | tf_op jit(solution)/shard_map/ppermute | solution.py:98
  75.4 14.7 %collective-permute-start.7 = (bf16[4,2048]{1,0:T(4,128)(2,1)S(1)}, bf16[4,2048]{1,0:T(4,128)(2,1)S(1)}, u32[]{:S(2)}, u32[]{:S(2)}) collective-permute-start(bf16[4,2048]{1,0:T(4,128)(2,1)S(1)} %get-tuple-element.32), channel_id=1, source_target_pairs={{0,16},{1,17},{2,18},{3,19},{4,20},{5,21},{6,22},{7,23},{8,24},{9,... | collective-permute-start | bytes 49160 | tf_op jit(solution)/shard_map/ppermute | solution.py:98
  79.0 12.9 %collective-permute-start.8 = (bf16[4,2048]{1,0:T(4,128)(2,1)S(1)}, bf16[4,2048]{1,0:T(4,128)(2,1)S(1)}, u32[]{:S(2)}, u32[]{:S(2)}) collective-permute-start(bf16[4,2048]{1,0:T(4,128)(2,1)S(1)} %get-tuple-element.31), channel_id=1, source_target_pairs={{0,18},{1,19},{2,16},{3,17},{4,22},{5,23},{6,20},{7,21},{8,26},{9,... | collective-permute-start | bytes 49160 | tf_op jit(solution)/shard_map/ppermute | solution.py:98
  80.9 16.2 %collective-permute-start.9 = (bf16[4,2048]{1,0:T(4,128)(2,1)S(1)}, bf16[4,2048]{1,0:T(4,128)(2,1)S(1)}, u32[]{:S(2)}, u32[]{:S(2)}) collective-permute-start(bf16[4,2048]{1,0:T(4,128)(2,1)S(1)} %get-tuple-element.30), channel_id=1, source_target_pairs={{0,20},{1,21},{2,22},{3,23},{4,16},{5,17},{6,18},{7,19},{8,28},{9,... | collective-permute-start | bytes 49160 | tf_op jit(solution)/shard_map/ppermute | solution.py:98
  85.0 12.6 %collective-permute-start.10 = (bf16[4,2048]{1,0:T(4,128)(2,1)S(1)}, bf16[4,2048]{1,0:T(4,128)(2,1)S(1)}, u32[]{:S(2)}, u32[]{:S(2)}) collective-permute-start(bf16[4,2048]{1,0:T(4,128)(2,1)S(1)} %get-tuple-element.29), channel_id=1, source_target_pairs={{0,22},{1,23},{2,20},{3,21},{4,18},{5,19},{6,16},{7,17},{8,30},{9,... | collective-permute-start | bytes 49160 | tf_op jit(solution)/shard_map/ppermute | solution.py:98
  85.7 12.7 %collective-permute-start.11 = (bf16[4,2048]{1,0:T(4,128)(2,1)S(1)}, bf16[4,2048]{1,0:T(4,128)(2,1)S(1)}, u32[]{:S(2)}, u32[]{:S(2)}) collective-permute-start(bf16[4,2048]{1,0:T(4,128)(2,1)S(1)} %get-tuple-element.28), channel_id=1, source_target_pairs={{0,24},{1,25},{2,26},{3,27},{4,28},{5,29},{6,30},{7,31},{8,16},{9,... | collective-permute-start | bytes 49160 | tf_op jit(solution)/shard_map/ppermute | solution.py:98
  90.1 8.8 %collective-permute-start.12 = (bf16[4,2048]{1,0:T(4,128)(2,1)S(1)}, bf16[4,2048]{1,0:T(4,128)(2,1)S(1)}, u32[]{:S(2)}, u32[]{:S(2)}) collective-permute-start(bf16[4,2048]{1,0:T(4,128)(2,1)S(1)} %get-tuple-element.27), channel_id=1, source_target_pairs={{0,26},{1,27},{2,24},{3,25},{4,30},{5,31},{6,28},{7,29},{8,18},{9,... | collective-permute-start | bytes 49160 | tf_op jit(solution)/shard_map/ppermute | solution.py:98
  91.9 7.6 %collective-permute-start.13 = (bf16[4,2048]{1,0:T(4,128)(2,1)S(1)}, bf16[4,2048]{1,0:T(4,128)(2,1)S(1)}, u32[]{:S(2)}, u32[]{:S(2)}) collective-permute-start(bf16[4,2048]{1,0:T(4,128)(2,1)S(1)} %get-tuple-element.26), channel_id=1, source_target_pairs={{0,28},{1,29},{2,30},{3,31},{4,24},{5,25},{6,26},{7,27},{8,20},{9,... | collective-permute-start | bytes 49160 | tf_op jit(solution)/shard_map/ppermute | solution.py:98
  97.1 7.3 %collective-permute-start.14 = (bf16[4,2048]{1,0:T(4,128)(2,1)S(1)}, bf16[4,2048]{1,0:T(4,128)(2,1)S(1)}, u32[]{:S(2)}, u32[]{:S(2)}) collective-permute-start(bf16[4,2048]{1,0:T(4,128)(2,1)S(1)} %get-tuple-element.25), channel_id=1, source_target_pairs={{0,30},{1,31},{2,28},{3,29},{4,26},{5,27},{6,24},{7,25},{8,22},{9,... | collective-permute-start | bytes 49160 | tf_op jit(solution)/shard_map/ppermute | solution.py:98
  105.0 1.5 %collective-permute-start.15 = (bf16[16,4,2048]{2,1,0:T(4,128)(2,1)S(1)}, bf16[16,4,2048]{2,1,0:T(4,128)(2,1)S(1)}, u32[]{:S(2)}, u32[]{:S(2)}) collective-permute-start(bf16[16,4,2048]{2,1,0:T(4,128)(2,1)S(1)} %get-tuple-element.40), channel_id=1, source_target_pairs={{0,1},{1,0},{2,3},{3,2},{4,5},{5,4},{6,7},{7,6},{8,9},{9,8},{10,11... | collective-permute-start | bytes 786440 | tf_op jit(solution)/shard_map/ppermute | solution.py:100
  118.9 1.6 %collective-permute-start.16 = (bf16[64,2048]{1,0:T(8,128)(2,1)S(1)}, bf16[64,2048]{1,0:T(8,128)(2,1)S(1)}, u32[]{:S(2)}, u32[]{:S(2)}) collective-permute-start(bf16[64,2048]{1,0:T(8,128)(2,1)S(1)} %split.9), channel_id=1, source_target_pairs={{0,1},{1,0},{2,3},{3,2},{4,5},{5,4},{6,7},{7,6},{8,9},{9,8},{10,11... | collective-permute-start | bytes 786440 | tf_op jit(solution)/shard_map/ppermute | solution.py:107
  121.6 5.6 %collective-permute-start.17 = (bf16[4,2048]{1,0:T(4,128)(2,1)S(1)}, bf16[4,2048]{1,0:T(4,128)(2,1)S(1)}, u32[]{:S(2)}, u32[]{:S(2)}) collective-permute-start(bf16[4,2048]{1,0:T(4,128)(2,1)S(1)} %get-tuple-element.22), channel_id=1, source_target_pairs={{0,2},{1,3},{2,0},{3,1},{4,6},{5,7},{6,4},{7,5},{8,10},{9,11},{10,... | collective-permute-start | bytes 49160 | tf_op jit(solution)/shard_map/ppermute | solution.py:112
  122.3 5.0 %collective-permute-start.18 = (bf16[4,2048]{1,0:T(4,128)(2,1)S(1)}, bf16[4,2048]{1,0:T(4,128)(2,1)S(1)}, u32[]{:S(2)}, u32[]{:S(2)}) collective-permute-start(bf16[4,2048]{1,0:T(4,128)(2,1)S(1)} %get-tuple-element.21), channel_id=1, source_target_pairs={{0,4},{1,5},{2,6},{3,7},{4,0},{5,1},{6,2},{7,3},{8,12},{9,13},{10,... | collective-permute-start | bytes 49160 | tf_op jit(solution)/shard_map/ppermute | solution.py:112
  122.8 8.4 %collective-permute-start.19 = (bf16[4,2048]{1,0:T(4,128)(2,1)S(1)}, bf16[4,2048]{1,0:T(4,128)(2,1)S(1)}, u32[]{:S(2)}, u32[]{:S(2)}) collective-permute-start(bf16[4,2048]{1,0:T(4,128)(2,1)S(1)} %get-tuple-element.20), channel_id=1, source_target_pairs={{0,6},{1,7},{2,4},{3,5},{4,2},{5,3},{6,0},{7,1},{8,14},{9,15},{10,... | collective-permute-start | bytes 49160 | tf_op jit(solution)/shard_map/ppermute | solution.py:112
  125.3 6.1 %collective-permute-start.20 = (bf16[4,2048]{1,0:T(4,128)(2,1)S(1)}, bf16[4,2048]{1,0:T(4,128)(2,1)S(1)}, u32[]{:S(2)}, u32[]{:S(2)}) collective-permute-start(bf16[4,2048]{1,0:T(4,128)(2,1)S(1)} %get-tuple-element.19), channel_id=1, source_target_pairs={{0,8},{1,9},{2,10},{3,11},{4,12},{5,13},{6,14},{7,15},{8,0},{9,1},... | collective-permute-start | bytes 49160 | tf_op jit(solution)/shard_map/ppermute | solution.py:112
  125.3 9.0 %collective-permute-start.21 = (bf16[4,2048]{1,0:T(4,128)(2,1)S(1)}, bf16[4,2048]{1,0:T(4,128)(2,1)S(1)}, u32[]{:S(2)}, u32[]{:S(2)}) collective-permute-start(bf16[4,2048]{1,0:T(4,128)(2,1)S(1)} %get-tuple-element.18), channel_id=1, source_target_pairs={{0,10},{1,11},{2,8},{3,9},{4,14},{5,15},{6,12},{7,13},{8,2},{9,3},... | collective-permute-start | bytes 49160 | tf_op jit(solution)/shard_map/ppermute | solution.py:112
  127.3 7.2 %collective-permute-start.22 = (bf16[4,2048]{1,0:T(4,128)(2,1)S(1)}, bf16[4,2048]{1,0:T(4,128)(2,1)S(1)}, u32[]{:S(2)}, u32[]{:S(2)}) collective-permute-start(bf16[4,2048]{1,0:T(4,128)(2,1)S(1)} %get-tuple-element.17), channel_id=1, source_target_pairs={{0,12},{1,13},{2,14},{3,15},{4,8},{5,9},{6,10},{7,11},{8,4},{9,5},... | collective-permute-start | bytes 49160 | tf_op jit(solution)/shard_map/ppermute | solution.py:112
  127.3 11.9 %collective-permute-start.23 = (bf16[4,2048]{1,0:T(4,128)(2,1)S(1)}, bf16[4,2048]{1,0:T(4,128)(2,1)S(1)}, u32[]{:S(2)}, u32[]{:S(2)}) collective-permute-start(bf16[4,2048]{1,0:T(4,128)(2,1)S(1)} %get-tuple-element.16), channel_id=1, source_target_pairs={{0,14},{1,15},{2,12},{3,13},{4,10},{5,11},{6,8},{7,9},{8,6},{9,7},... | collective-permute-start | bytes 49160 | tf_op jit(solution)/shard_map/ppermute | solution.py:112
  131.3 8.3 %collective-permute-start.24 = (bf16[4,2048]{1,0:T(4,128)(2,1)S(1)}, bf16[4,2048]{1,0:T(4,128)(2,1)S(1)}, u32[]{:S(2)}, u32[]{:S(2)}) collective-permute-start(bf16[4,2048]{1,0:T(4,128)(2,1)S(1)} %get-tuple-element.15), channel_id=1, source_target_pairs={{0,16},{1,17},{2,18},{3,19},{4,20},{5,21},{6,22},{7,23},{8,24},{9,... | collective-permute-start | bytes 49160 | tf_op jit(solution)/shard_map/ppermute | solution.py:112
  131.4 11.9 %collective-permute-start.25 = (bf16[4,2048]{1,0:T(4,128)(2,1)S(1)}, bf16[4,2048]{1,0:T(4,128)(2,1)S(1)}, u32[]{:S(2)}, u32[]{:S(2)}) collective-permute-start(bf16[4,2048]{1,0:T(4,128)(2,1)S(1)} %get-tuple-element.14), channel_id=1, source_target_pairs={{0,18},{1,19},{2,16},{3,17},{4,22},{5,23},{6,20},{7,21},{8,26},{9,... | collective-permute-start | bytes 49160 | tf_op jit(solution)/shard_map/ppermute | solution.py:112
  134.3 10.4 %collective-permute-start.26 = (bf16[4,2048]{1,0:T(4,128)(2,1)S(1)}, bf16[4,2048]{1,0:T(4,128)(2,1)S(1)}, u32[]{:S(2)}, u32[]{:S(2)}) collective-permute-start(bf16[4,2048]{1,0:T(4,128)(2,1)S(1)} %get-tuple-element.13), channel_id=1, source_target_pairs={{0,20},{1,21},{2,22},{3,23},{4,16},{5,17},{6,18},{7,19},{8,28},{9,... | collective-permute-start | bytes 49160 | tf_op jit(solution)/shard_map/ppermute | solution.py:112
  134.4 14.6 %collective-permute-start.27 = (bf16[4,2048]{1,0:T(4,128)(2,1)S(1)}, bf16[4,2048]{1,0:T(4,128)(2,1)S(1)}, u32[]{:S(2)}, u32[]{:S(2)}) collective-permute-start(bf16[4,2048]{1,0:T(4,128)(2,1)S(1)} %get-tuple-element.12), channel_id=1, source_target_pairs={{0,22},{1,23},{2,20},{3,21},{4,18},{5,19},{6,16},{7,17},{8,30},{9,... | collective-permute-start | bytes 49160 | tf_op jit(solution)/shard_map/ppermute | solution.py:112
  139.3 9.8 %collective-permute-start.28 = (bf16[4,2048]{1,0:T(4,128)(2,1)S(1)}, bf16[4,2048]{1,0:T(4,128)(2,1)S(1)}, u32[]{:S(2)}, u32[]{:S(2)}) collective-permute-start(bf16[4,2048]{1,0:T(4,128)(2,1)S(1)} %get-tuple-element.11), channel_id=1, source_target_pairs={{0,24},{1,25},{2,26},{3,27},{4,28},{5,29},{6,30},{7,31},{8,16},{9,... | collective-permute-start | bytes 49160 | tf_op jit(solution)/shard_map/ppermute | solution.py:112
  139.6 9.5 %collective-permute-start.29 = (bf16[4,2048]{1,0:T(4,128)(2,1)S(1)}, bf16[4,2048]{1,0:T(4,128)(2,1)S(1)}, u32[]{:S(2)}, u32[]{:S(2)}) collective-permute-start(bf16[4,2048]{1,0:T(4,128)(2,1)S(1)} %get-tuple-element.10), channel_id=1, source_target_pairs={{0,26},{1,27},{2,24},{3,25},{4,30},{5,31},{6,28},{7,29},{8,18},{9,... | collective-permute-start | bytes 49160 | tf_op jit(solution)/shard_map/ppermute | solution.py:112
  143.2 6.5 %collective-permute-start.30 = (bf16[4,2048]{1,0:T(4,128)(2,1)S(1)}, bf16[4,2048]{1,0:T(4,128)(2,1)S(1)}, u32[]{:S(2)}, u32[]{:S(2)}) collective-permute-start(bf16[4,2048]{1,0:T(4,128)(2,1)S(1)} %get-tuple-element.9), channel_id=1, source_target_pairs={{0,28},{1,29},{2,30},{3,31},{4,24},{5,25},{6,26},{7,27},{8,20},{9,... | collective-permute-start | bytes 49160 | tf_op jit(solution)/shard_map/ppermute | solution.py:112
  144.7 7.4 %collective-permute-start.31 = (bf16[4,2048]{1,0:T(4,128)(2,1)S(1)}, bf16[4,2048]{1,0:T(4,128)(2,1)S(1)}, u32[]{:S(2)}, u32[]{:S(2)}) collective-permute-start(bf16[4,2048]{1,0:T(4,128)(2,1)S(1)} %get-tuple-element.8), channel_id=1, source_target_pairs={{0,30},{1,31},{2,28},{3,29},{4,26},{5,27},{6,24},{7,25},{8,22},{9,... | collective-permute-start | bytes 49160 | tf_op jit(solution)/shard_map/ppermute | solution.py:112

commit v4 on v1

v4 whole, which is shorter than its diff:
```python
import functools
import math

import jax
import jax.numpy as jnp
from jax import lax
from jax.experimental import pallas as pl
from jax.experimental.pallas import tpu as pltpu
from jax.sharding import PartitionSpec as P

BF16 = jnp.bfloat16
F32 = jnp.float32
NT = (((1,), (1,)), ((), ()))
NN = (((1,), (0,)), ((), ()))
SLAB = 16
MIB = 1 << 20


def dot(a, b, dims=NN, precision=None):
    return lax.dot_general(a, b, dims, precision=precision, preferred_element_type=F32)


def iota(shape, dim):
    return lax.broadcasted_iota(jnp.int32, shape, dim)


def pool_loads(pool, keys, values, sems):
    half = keys.shape[-1]
    return [
        pltpu.make_async_copy(pool.at[:, :, :, pl.ds(i * half, half)], kept, sems.at[i])
        for i, kept in enumerate((keys, values))
    ]


def attend(table, lengths, q_ref, fresh, weight, pool, new_pool, keys, values, kept_weight, qs, att, sems):
    requests, max_pages = table.shape
    pages, page_len, heads_kv, head_dim = keys.shape
    heads = q_ref.shape[1] // head_dim
    group = heads // heads_kv
    page_rows = page_len * heads_kv
    loads = pool_loads(pool, keys, values, sems)
    weight_load = pltpu.make_async_copy(weight, kept_weight, sems.at[2])
    for copy in loads:
        copy.start()
    weight_load.start()
    for h in range(heads):
        qs[pl.ds(h * requests, requests), :] = q_ref[:, pl.ds(h * head_dim, head_dim)].astype(F32)
    for copy in loads:
        copy.wait()
    for r in range(requests):
        page = table[r, lengths[r] // page_len]
        slot = lengths[r] % page_len
        row = fresh[r]
        keys[page, slot] = row[:, :head_dim]
        values[page, slot] = row[:, head_dim:]
    stores = [
        pltpu.make_async_copy(kept, new_pool.at[:, :, :, pl.ds(i * head_dim, head_dim)], sems.at[3 + i])
        for i, kept in enumerate((keys, values))
    ]
    for copy in stores:
        copy.start()
    key_pages = keys.reshape(pages, page_rows, head_dim)
    value_pages = values.reshape(pages, page_rows, head_dim)
    columns = max_pages * page_rows
    lane = iota((heads, columns), 1)
    own_head = lane % heads_kv == iota((heads, columns), 0) // group
    position = lane // heads_kv
    for r in range(requests):
        chosen = [table[r, j] for j in range(max_pages)]
        query = qs[pl.ds(r, heads, stride=requests), :].astype(BF16)
        gathered = jnp.concatenate([key_pages[page] for page in chosen], axis=0)
        scores = dot(query, gathered, NT) * (1.0 / math.sqrt(head_dim))
        scores = jnp.where(own_head & (position <= lengths[r]), scores, -1e30)
        top = jnp.max(scores, axis=1, keepdims=True)
        exponent = jnp.exp(scores - top)
        denominator = jnp.sum(exponent, axis=1, keepdims=True)
        gathered = jnp.concatenate([value_pages[page] for page in chosen], axis=0)
        summed = dot(exponent.astype(BF16), gathered)
        att[pl.ds(r, heads, stride=requests), :] = summed / denominator
    attended = jnp.concatenate(
        [att[pl.ds(h * requests, requests), :] for h in range(heads)], axis=1
    ).astype(BF16)
    weight_load.wait()
    projected = dot(attended, kept_weight[...])
    for copy in stores:
        copy.wait()
    return projected


def route(projected, hidden, gain, router, ids, mixed_ref, norms_ref, top_ref, slabs_ref, comb_ref, capacity):
    requests, width = hidden.shape
    experts = router.shape[0]
    parts = SLAB // capacity
    piece = width // parts
    slab_rows = experts * SLAB
    mixed = (hidden[...].astype(F32) + projected).astype(BF16)
    mixed_ref[...] = mixed
    mixed = mixed.astype(F32)
    norms = jnp.sqrt(jnp.mean(mixed * mixed, axis=1, keepdims=True) + 1e-06)
    norms_ref[...] = norms
    normed = (mixed / norms * gain[...].astype(F32)).astype(BF16)
    logits = dot(normed, router[...], NT)
    top_ref[...] = jnp.max(logits, axis=1, keepdims=True)
    column = iota((requests, experts), 1)
    named = column < 0
    for k in range(ids.shape[1]):
        named = named | (ids[:, k : k + 1] == column)
    weights = jnp.where(named, jnp.exp(logits), 0.0)
    weights = weights / jnp.sum(weights, axis=1, keepdims=True)
    earlier = (iota((requests, requests), 1) < iota((requests, requests), 0)).astype(F32)
    rank = dot(earlier, named.astype(F32))
    place = jnp.where(named, rank, -1.0)
    normed = normed.astype(F32)
    stacked = jnp.concatenate([normed[:, p * piece : (p + 1) * piece] for p in range(parts)], axis=0)
    places = jnp.concatenate([place] * parts, axis=0)
    shape = (slab_rows, parts * requests)
    inner = iota(shape, 0) % SLAB
    spread = (iota((slab_rows, experts), 0) // SLAB == iota((slab_rows, experts), 1)).astype(F32)
    picks = (dot(spread, places, NT) == (inner // parts).astype(F32)) & (
        inner % parts == iota(shape, 1) // requests
    )
    slabs_ref[...] = dot(picks.astype(BF16), stacked.astype(BF16)).astype(BF16)
    shape = (experts, slab_rows)
    spread = (iota(shape, 1) // SLAB == iota(shape, 0)).astype(F32)
    inner = iota((requests, slab_rows), 1) % SLAB
    comb_ref[...] = jnp.where(
        dot(place, spread) == (inner // parts).astype(F32),
        dot(weights, spread, precision=lax.Precision.HIGHEST),
        0.0,
    )


def attend_route_kernel(capacity, table, lengths, q_ref, fresh, hidden, gain, router, ids, weight, pool,
                        new_pool, mixed, norms, top, slabs, comb, *scratch):
    projected = attend(table, lengths, q_ref, fresh, weight, pool, new_pool, *scratch)
    route(projected, hidden, gain, router, ids, mixed, norms, top, slabs, comb, capacity)


def attend_kernel(table, lengths, q_ref, fresh, weight, pool, new_pool, projected, *scratch):
    projected[...] = attend(table, lengths, q_ref, fresh, weight, pool, new_pool, *scratch)


def route_kernel(capacity, projected, hidden, gain, router, ids, mixed, norms, top, slabs, comb):
    route(projected[...], hidden, gain, router, ids, mixed, norms, top, slabs, comb, capacity)


def unit_chunks(units):
    return [(start, min(256, units - start)) for start in range(0, units, 256)]


def expert_kernel(capacity, own, partner, gate_up, down, own_out, partner_out, kept_up, kept_down, rows, total, sems):
    units, width = kept_down.shape
    parts = SLAB // capacity
    loads = []
    for i, (start, size) in enumerate(unit_chunks(units)):
        span = pl.ds(start, size)
        loads.append((
            pltpu.make_async_copy(gate_up.at[0, :, span, :], kept_up.at[:, span, :], sems.at[2 * i]),
            pltpu.make_async_copy(down.at[0, span, :], kept_down.at[span, :], sems.at[2 * i + 1]),
        ))
        for copy in loads[-1]:
            copy.start()
    block = 128
    each = block // parts
    shape = (block, block)
    sort = (iota(shape, 1) == iota(shape, 0) % each * parts + iota(shape, 0) // each).astype(BF16)
    row = 0
    for source in (own, partner):
        for start in range(0, source.shape[0], block):
            sorted_rows = dot(sort, source[pl.ds(start, block), :]).astype(BF16)
            rows[pl.ds(row, each), :] = jnp.concatenate(
                [sorted_rows[p * each : (p + 1) * each] for p in range(parts)], axis=1
            )
            row += each
    arrived = rows[...]
    for i, (start, size) in enumerate(unit_chunks(units)):
        span = pl.ds(start, size)
        for copy in loads[i]:
            copy.wait()
        gate = dot(arrived, kept_up[0, span, :], NT)
        up = dot(arrived, kept_up[1, span, :], NT)
        activated = (gate / (1.0 + jnp.exp(-gate)) * up).astype(BF16)
        term = dot(activated, kept_down[span, :])
        if i == 0:
            total[...] = term
        else:
            total[...] += term
    kept = own_out.shape[0]
    own_out[...] = total[pl.ds(0, kept), :].astype(BF16)
    partner_out[...] = total[pl.ds(kept, kept), :].astype(BF16)


def merge_kernel(capacity, own, partner, slabs):
    parts = SLAB // capacity
    block = 128
    each = block // parts
    piece = slabs.shape[1]
    shape = (block, block)
    unsort = (iota(shape, 0) == iota(shape, 1) % each * parts + iota(shape, 1) // each).astype(BF16)
    for i in range(slabs.shape[0] // block):
        span = pl.ds(i * each, each)
        summed = (own[span, :].astype(F32) + partner[span, :].astype(F32)).astype(BF16)
        stacked = jnp.concatenate([summed[:, p * piece : (p + 1) * piece] for p in range(parts)], axis=0)
        slabs[pl.ds(i * block, block), :] = dot(unsort, stacked).astype(BF16)


def gather_terms(comb, slabs, capacity):
    parts = SLAB // capacity
    requests = comb.shape[0]
    weights = comb[...]
    pieces = []
    for _ in range(3):
        piece = weights.astype(BF16).astype(F32)
        weights = weights - piece
        pieces.append(piece)
    part = iota(comb.shape, 1) % parts
    stacked = jnp.concatenate(
        [jnp.where(part == p, piece, 0.0) for p in range(parts) for piece in pieces], axis=0
    ).astype(BF16)
    terms = dot(stacked, slabs[...])
    return jnp.concatenate(
        [
            sum(terms[(3 * p + i) * requests : (3 * p + i + 1) * requests] for i in range(3))
            for p in range(parts)
        ],
        axis=1,
    )


def combine_kernel(capacity, comb, slabs, mixed, out):
    out[...] = (mixed[...].astype(F32) + gather_terms(comb, slabs, capacity)).astype(BF16)


def gather_kernel(capacity, comb, slabs, out):
    out[...] = gather_terms(comb, slabs, capacity).astype(BF16)


def vmem(count):
    return [pl.BlockSpec(memory_space=pltpu.VMEM)] * count


def anywhere(count):
    return [pl.BlockSpec(memory_space=pl.ANY)] * count


def scalars(count):
    return [pl.BlockSpec(memory_space=pltpu.SMEM)] * count


def like(shape, dtype=BF16):
    return jax.ShapeDtypeStruct(shape, dtype)


def body(
    hidden,
    queries,
    fresh_key_value,
    kv_pool,
    page_table,
    lengths,
    out_weight,
    norm_gain,
    router_weight,
    expert_ids,
    expert_gate_up,
    expert_down,
):
    requests, width = hidden.shape
    req_count, kv_count = lax.axis_size("req"), lax.axis_size("kv")
    pages, page_len, heads_kv, pair_dim = kv_pool.shape
    head_dim = pair_dim // 2
    heads = queries.shape[1] // head_dim
    experts = router_weight.shape[0]
    copies = req_count // experts
    chosen = expert_ids.shape[1]
    capacity = 2 * max(1, (requests * chosen + 2 * experts - 1) // (2 * experts))
    parts = SLAB // capacity
    piece = width // parts
    slab_rows = experts * SLAB
    gain = norm_gain.reshape(1, width)

    attend_scratch = [
        pltpu.VMEM((pages, page_len, heads_kv, head_dim), BF16),
        pltpu.VMEM((pages, page_len, heads_kv, head_dim), BF16),
        pltpu.VMEM(out_weight.shape, BF16),
        pltpu.VMEM((heads * requests, head_dim), F32),
        pltpu.VMEM((heads * requests, head_dim), F32),
        pltpu.SemaphoreType.DMA((5,)),
    ]
    routed_shapes = [
        like((requests, width)),
        like((requests, 1), F32),
        like((requests, 1), F32),
        like((slab_rows, piece)),
        like((requests, slab_rows), F32),
    ]
    attend_params = pltpu.CompilerParams(vmem_limit_bytes=32 * MIB)
    if kv_count == 1:
        new_pool, mixed, norms, top, slabs, comb = pl.pallas_call(
            functools.partial(attend_route_kernel, capacity),
            out_shape=[like(kv_pool.shape)] + routed_shapes,
            in_specs=scalars(2) + vmem(6) + anywhere(2),
            out_specs=anywhere(1) + vmem(5),
            scratch_shapes=attend_scratch,
            compiler_params=attend_params,
        )(page_table, lengths, queries, fresh_key_value, hidden, gain, router_weight, expert_ids,
          out_weight, kv_pool)
    else:
        new_pool, projected = pl.pallas_call(
            attend_kernel,
            out_shape=[like(kv_pool.shape), like((requests, width), F32)],
            in_specs=scalars(2) + vmem(2) + anywhere(2),
            out_specs=anywhere(1) + vmem(1),
            scratch_shapes=attend_scratch,
            compiler_params=attend_params,
        )(page_table, lengths, queries, fresh_key_value, out_weight, kv_pool)
        projected = lax.psum(projected, "kv")
        mixed, norms, top, slabs, comb = pl.pallas_call(
            functools.partial(route_kernel, capacity),
            out_shape=routed_shapes,
            in_specs=vmem(5),
            out_specs=vmem(5),
        )(projected, hidden, gain, router_weight, expert_ids)

    same_part = [list(range(part, req_count, copies)) for part in range(copies)]
    swap = [(index, index ^ 1) for index in range(req_count)]

    def exchange(array):
        array = array.reshape(experts, SLAB, piece)
        array = lax.all_to_all(
            array, "req", split_axis=0, concat_axis=0, tiled=True, axis_index_groups=same_part
        )
        return array.reshape(slab_rows, piece)

    arrived = exchange(slabs)
    partner = lax.ppermute(arrived, "req", swap)
    units = expert_down.shape[1]
    kept = experts * capacity
    own_terms, partner_terms = pl.pallas_call(
        functools.partial(expert_kernel, capacity),
        out_shape=[like((kept, width))] * 2,
        in_specs=vmem(2) + anywhere(2),
        out_specs=vmem(2),
        scratch_shapes=[
            pltpu.VMEM((2, units, width), BF16),
            pltpu.VMEM((units, width), BF16),
            pltpu.VMEM((2 * kept, width), BF16),
            pltpu.VMEM((2 * kept, width), F32),
            pltpu.SemaphoreType.DMA((2 * len(unit_chunks(units)),)),
        ],
        compiler_params=pltpu.CompilerParams(vmem_limit_bytes=32 * MIB),
    )(arrived, partner, expert_gate_up, expert_down)
    swapped = lax.ppermute(partner_terms, "req", swap)
    leaving = pl.pallas_call(
        functools.partial(merge_kernel, capacity),
        out_shape=like((slab_rows, piece)),
        in_specs=vmem(2),
        out_specs=pl.BlockSpec(memory_space=pltpu.VMEM),
    )(own_terms, swapped)
    returned = exchange(leaving)
    if kv_count == 1:
        out_hidden = pl.pallas_call(
            functools.partial(combine_kernel, capacity),
            out_shape=like((requests, width)),
            in_specs=vmem(3),
            out_specs=pl.BlockSpec(memory_space=pltpu.VMEM),
        )(comb, returned, mixed)
    else:
        routed = pl.pallas_call(
            functools.partial(gather_kernel, capacity),
            out_shape=like((requests, width)),
            in_specs=vmem(2),
            out_specs=pl.BlockSpec(memory_space=pltpu.VMEM),
        )(comb, returned)
        routed = lax.psum(routed, "kv").astype(F32)
        out_hidden = (mixed.astype(F32) + routed).astype(BF16)
    return out_hidden, new_pool, norms.reshape(requests), top.reshape(requests)


def solution(mesh):
    in_specs = (
        P("req", None),
        P("req", "kv"),
        P("req", "kv", None),
        P("req", None, "kv", None),
        P("req", None),
        P("req"),
        P("kv", None),
        P(),
        P(),
        P("req", None),
        P("req", None, "kv", None),
        P("req", "kv", None),
    )
    out_specs = (P("req", None), P("req", None, "kv", None), P("req"), P("req"))
    return jax.shard_map(body, mesh=mesh, in_specs=in_specs, out_specs=out_specs, check_vma=False)
```

time: 280 us -> 68.8 us (0.25)
  waiting for transfers between devices: 190 us -> 12.1 us
  local copies, waits for them, and re-layouts: 50.3 us -> 14.2 us
  matrix products: 21.5 us -> 0 us
  Pallas kernels: 0 us -> 18.2 us
  blocking collectives: 0 us -> 18 us
  between operations: 14.3 us -> 0.71 us
  starting transfers between devices: 0.26 us -> 3.68 us
    reduce_scatter x1 -> x0, waiting for transfers between devices: 134 us -> none  [body(): lax.psum_scatter(weighted, 'req', scatter_dimension=0, tiled=True)]
    all_gather x1 -> x0, waiting for transfers between devices: 56.5 us -> none  [body(): gathered = lax.all_gather(payload, 'req', axis=0, tiled=True)]
    gather x3 -> x0, local copies, waits for them, and re-layouts: 26.4 us -> none  [the longest x2 25.8 us: body(): refreshed_pool[page_table]]
    dot_general x6 -> x0, matrix products: 21.5 us -> none  [the longest x1 6.61 us: body(): terms = jnp.dot(activated, down_local, preferred_element_type=jnp.float32)]
    pallas_call x0 -> x4, Pallas kernels: none -> 18.2 us  [the longest x1 10.7 us: body(): pl.pallas_call(functools.partial(attend_route_kernel, capacity), out_shap...]
    all_to_all x0 -> x1, blocking collectives: none -> 18 us  [exchange(): lax.all_to_all(array, 'req', split_axis=0, concat_axis=0, tiled=True, axi...]
    slice x1 -> x0, local copies, waits for them, and re-layouts: 9.14 us -> none  [body(): collected_pages[..., :head_dim]]
    all_to_all x0 -> x1, waiting for transfers between devices: none -> 9.12 us  [exchange(): lax.all_to_all(array, 'req', split_axis=0, concat_axis=0, tiled=True, axi...]
  transfers between devices with their start and end apart: 2 -> 3, of which waited for: 2 -> 3; matrix products, arithmetic and copies ran while one was open for 0% -> 2% of each run, Pallas kernels for 0% -> 0%
where the time goes in v4:
time: 68.8 us; the launch traced here: 68.1 us
  Pallas kernels  18.2 us (26%)
  blocking collectives  18 us (26%)
  local copies, waits for them, and re-layouts  14.2 us (21%)
  waiting for transfers between devices  12.1 us (18%)
  starting transfers between devices  3.68 us (5%)
  other arithmetic  1.25 us (2%)
  between operations  0.71 us (1%)
    all_to_all x1, blocking collectives, exchange(): lax.all_to_all(array, 'req', split_axis=0, concat_axis=0, tiled=True, axi...  18 us
    unnamed x32, local copies, waits for them, and re-layouts  13.5 us
    pallas_call x1, Pallas kernels, body(): pl.pallas_call(functools.partial(attend_route_kernel, capacity), out_shap...  10.7 us
    all_to_all x1, waiting for transfers between devices, exchange(): lax.all_to_all(array, 'req', split_axis=0, concat_axis=0, tiled=True, axi...  9.12 us
    pallas_call x1, Pallas kernels, body(): pl.pallas_call(functools.partial(expert_kernel, capacity), out_shape=[lik...  3.77 us
    all_to_all x1, starting transfers between devices, exchange(): lax.all_to_all(array, 'req', split_axis=0, concat_axis=0, tiled=True, axi...  3.55 us
    pallas_call x1, Pallas kernels, body(): pl.pallas_call(functools.partial(merge_kernel, capacity), out_shape=like(...  1.97 us
    pallas_call x1, Pallas kernels, body(): pl.pallas_call(functools.partial(combine_kernel, capacity), out_shape=lik...  1.75 us
  transfers between devices with their start and end apart: 3, of which 3 were waited for; matrix products, arithmetic and copies ran while one was open for 2% of the time, Pallas kernels for 0%

profile of v4, /device:TPU:0, one launch (start us, length us, event | category | flops | bytes accessed | tf_op | source)
XLA Modules:
  0.0 68.1 jit_solution(16399490855153709457)
XLA Ops:
  0.6 0.7 %reshape.29.gain = bf16[1,2048]{1,0:T(2,128)(2,1)S(1)} reshape(bf16[2048]{0:T(1024)(128)(2,1)} %param.19) | data formatting | bytes 8192 | tf_op jit(solution)/shard_map/reshape | solution.py:280
  1.3 0.0 copy-start
  1.3 3.4 %copy-done = bf16[2048,2048]{1,0:T(8,128)(2,1)S(1)} copy-done((bf16[2048,2048]{1,0:T(8,128)(2,1)S(1)}, bf16[2048,2048]{1,0:T(8,128)(2,1)}, u32[]{:S(2)}) %copy-start) | copy-done | bytes 8388632
  4.7 0.0 copy-start.1
  4.7 2.9 %copy-done.1 = bf16[104,32,4,256]{3,2,1,0:T(4,128)(2,1)S(1)} copy-done((bf16[104,32,4,256]{3,2,1,0:T(4,128)(2,1)S(1)}, bf16[104,32,4,256]{3,2,1,0:T(4,128)(2,1)}, u32[]{:S(2)}) %copy-start.1) | copy-done | bytes 6815768
  7.6 0.0 copy-start.5
  7.6 0.8 %copy-done.5 = bf16[16,2048]{1,0:T(8,128)(2,1)S(1)} copy-done((bf16[16,2048]{1,0:T(8,128)(2,1)S(1)}, bf16[16,2048]{1,0:T(8,128)(2,1)}, u32[]{:S(2)}) %copy-start.5) | copy-done | bytes 65560
  8.5 0.0 copy-start.6
  8.5 0.8 %copy-done.6 = bf16[8,2048]{1,0:T(8,128)(2,1)S(1)} copy-done((bf16[8,2048]{1,0:T(8,128)(2,1)S(1)}, bf16[8,2048]{1,0:T(8,128)(2,1)}, u32[]{:S(2)}) %copy-start.6) | copy-done | bytes 32792
  9.2 0.0 copy-start.7
  9.2 0.8 %copy-done.7 = bf16[8,2048]{1,0:T(8,128)(2,1)S(1)} copy-done((bf16[8,2048]{1,0:T(8,128)(2,1)S(1)}, bf16[8,2048]{1,0:T(8,128)(2,1)}, u32[]{:S(2)}) %copy-start.7) | copy-done | bytes 32792
  10.0 0.0 copy-start.9
  10.0 0.7 %copy-done.9 = bf16[8,4,256]{2,1,0:T(4,128)(2,1)S(1)} copy-done((bf16[8,4,256]{2,1,0:T(4,128)(2,1)S(1)}, bf16[8,4,256]{2,1,0:T(4,128)(2,1)}, u32[]{:S(2)}) %copy-start.9) | copy-done | bytes 16408
  10.7 0.0 copy-start.11
  10.7 0.7 %copy-done.11 = s32[8,20]{1,0:T(8,128)S(1)} copy-done((s32[8,20]{1,0:T(8,128)S(1)}, s32[8,20]{1,0:T(8,128)}, u32[]{:S(2)}) %copy-start.11) | copy-done | bytes 664
  11.4 0.0 copy-start.12
  11.4 0.7 %copy-done.12 = s32[8,6]{1,0:T(8,128)S(1)} copy-done((s32[8,6]{1,0:T(8,128)S(1)}, s32[8,6]{1,0:T(8,128)}, u32[]{:S(2)}) %copy-start.12) | copy-done | bytes 216
  12.1 0.0 copy-start.13
  12.1 0.7 copy-done.13
  12.7 0.0 copy-start.2
  12.7 0.0 copy-start.3
  12.8 10.7 %shard_map.147 = (bf16[104,32,4,256]{3,2,1,0:T(4,128)(2,1)}, bf16[8,2048]{1,0:T(8,128)(2,1)S(1)}, f32[8,1]{1,0:T(8,128)S(1)}, f32[8,1]{1,0:T(8,128)S(1)}, bf16[2...) custom-call(s32[8,20]{1,0:T(8,128)S(1)} %copy-done.11, s32[8]{0:T(128)S(1)} %copy-done.13, bf16[8,2048]{1,0:T(8,128)(2,1)S(1)} %copy-done.6, ...), custom_call_target="tpu_custom_call" | custom-call | tf_op jit(solution)/shard_map/pallas_call | solution.py:299
  23.5 0.0 copy-start.8
  23.5 0.0 copy-start.10
  23.5 18.0 %all_to_all.10 = bf16[16,16,512]{2,1,0:T(8,128)(2,1)S(1)} all-to-all(bf16[16,16,512]{2,1,0:T(8,128)(2,1)S(1)} %bitcast.6), channel_id=1, replica_groups={{0,2,4,6,8,10,12,14,16,18,20,22,24,26,28,30},{1,3,5,7,9,11,13,15,17,19,..., dimensions={0} | all-to-all | bytes 524288 | tf_op jit(solution)/shard_map/all_to_all | solution.py:330
  41.5 0.0 collective-permute-start
  41.5 1.5 %collective-permute-done.partner = bf16[256,512]{1,0:T(8,128)(2,1)S(1)} collective-permute-done((bf16[256,512]{1,0:T(8,128)(2,1)S(1)}, bf16[256,512]{1,0:T(8,128)(2,1)S(1)}, u32[]{:S(2)}, u32[]{:S(2)}) %collective-permute-start) | collective-permute-done | bytes 262176 | tf_op jit(solution)/shard_map/ppermute | solution.py:336
  43.0 0.0 copy-done.2
  43.0 0.0 copy-done.3
  43.0 3.8 %shard_map.148 = (bf16[64,2048]{1,0:T(8,128)(2,1)S(1)}, bf16[64,2048]{1,0:T(8,128)(2,1)S(1)}) custom-call(bf16[256,512]{1,0:T(8,128)(2,1)S(1)} %bitcast.5, bf16[256,512]{1,0:T(8,128)(2,1)S(1)} %collective-permute-done.partner, bf16[1,2,704,2048]{3,2,1,0:T(8,128)(2,1)S(1)} %copy-done.2, bf16[1,704,2048]{2,1,0:T(8,128)(2,1)S(1)} %copy-done.3), custom_call_target="tpu_custom_call" | custom-call | tf_op jit(solution)/shard_map/pallas_call | solution.py:339
  46.8 0.0 copy-done.8
  46.8 0.0 copy-start.4
  46.8 0.7 %copy-done.4 = bf16[64,2048]{1,0:T(8,128)(2,1)} copy-done((bf16[64,2048]{1,0:T(8,128)(2,1)}, bf16[64,2048]{1,0:T(8,128)(2,1)S(1)}, u32[]{:S(2)}) %copy-start.4) | copy-done | bytes 262168
  47.5 0.0 copy-done.10
  47.5 0.1 collective-permute-start.1
  47.6 1.4 %collective-permute-done.1.partner = bf16[64,2048]{1,0:T(8,128)(2,1)S(1)} collective-permute-done((bf16[64,2048]{1,0:T(8,128)(2,1)S(1)}, bf16[64,2048]{1,0:T(8,128)(2,1)S(1)}, u32[]{:S(2)}, u32[]{:S(2)}) %collective-permute-start.1) | collective-permute-done | bytes 262176 | tf_op jit(solution)/shard_map/ppermute | solution.py:353
  49.0 0.0 copy-start.15
  49.0 0.7 %copy-done.15 = bf16[64,2048]{1,0:T(8,128)(2,1)} copy-done((bf16[64,2048]{1,0:T(8,128)(2,1)}, bf16[64,2048]{1,0:T(8,128)(2,1)S(1)}, u32[]{:S(2)}) %copy-start.15) | copy-done | bytes 262168
  49.7 2.0 %shard_map.149 = bf16[256,512]{1,0:T(8,128)(2,1)} custom-call(bf16[64,2048]{1,0:T(8,128)(2,1)} %copy-done.4, bf16[64,2048]{1,0:T(8,128)(2,1)} %copy-done.15), custom_call_target="tpu_custom_call" | custom-call | tf_op jit(solution)/shard_map/pallas_call | solution.py:354
  51.7 3.5 %all-to-all-start.1 = ((bf16[16,16,512]{2,1,0:T(8,128)(2,1)}), bf16[16,16,512]{2,1,0:T(8,128)(2,1)S(1)}, u32[]{:S(2)}, u32[]{:S(2)}) async-start(bf16[16,16,512]{2,1,0:T(8,128)(2,1)} %bitcast.7), calls=%async_computation.1 | async-start | bytes 524288 | tf_op jit(solution)/shard_map/all_to_all | solution.py:330
  55.2 0.6 reduce
  55.9 0.6 reduce.1
  56.5 9.1 %all-to-all-done.1 = bf16[16,16,512]{2,1,0:T(8,128)(2,1)S(1)} async-done(((bf16[16,16,512]{2,1,0:T(8,128)(2,1)}), bf16[16,16,512]{2,1,0:T(8,128)(2,1)S(1)}, u32[]{:S(2)}, u32[]{:S(2)}) %all-to-all-start.1) | async-done | bytes 262176 | tf_op jit(solution)/shard_map/all_to_all | solution.py:330
  65.6 0.0 copy-start.14
  65.6 0.7 %copy-done.14 = bf16[16,16,512]{2,1,0:T(8,128)(2,1)} copy-done((bf16[16,16,512]{2,1,0:T(8,128)(2,1)}, bf16[16,16,512]{2,1,0:T(8,128)(2,1)S(1)}, u32[]{:S(2)}) %copy-start.14) | copy-done | bytes 262168
  66.3 1.7 %shard_map.150 = bf16[8,2048]{1,0:T(8,128)(2,1)} custom-call(f32[8,256]{1,0:T(8,128)} %copy-done.10, bf16[256,512]{1,0:T(8,128)(2,1)} %bitcast.8, bf16[8,2048]{1,0:T(8,128)(2,1)} %copy-done.8), custom_call_target="tpu_custom_call" | custom-call | tf_op jit(solution)/shard_map/pallas_call | solution.py:362
Async XLA Ops:
  1.3 3.4 %copy-start = (bf16[2048,2048]{1,0:T(8,128)(2,1)S(1)}, bf16[2048,2048]{1,0:T(8,128)(2,1)}, u32[]{:S(2)}) copy-start(bf16[2048,2048]{1,0:T(8,128)(2,1)} %weight.1) | copy-start | bytes 25165828
  4.7 2.9 %copy-start.1 = (bf16[104,32,4,256]{3,2,1,0:T(4,128)(2,1)S(1)}, bf16[104,32,4,256]{3,2,1,0:T(4,128)(2,1)}, u32[]{:S(2)}) copy-start(bf16[104,32,4,256]{3,2,1,0:T(4,128)(2,1)} %pool.1) | copy-start | bytes 20447236
  7.6 0.8 %copy-start.5 = (bf16[16,2048]{1,0:T(8,128)(2,1)S(1)}, bf16[16,2048]{1,0:T(8,128)(2,1)}, u32[]{:S(2)}) copy-start(bf16[16,2048]{1,0:T(8,128)(2,1)} %router.1) | copy-start | bytes 196612
  8.5 0.8 %copy-start.6 = (bf16[8,2048]{1,0:T(8,128)(2,1)S(1)}, bf16[8,2048]{1,0:T(8,128)(2,1)}, u32[]{:S(2)}) copy-start(bf16[8,2048]{1,0:T(8,128)(2,1)} %q_ref.1) | copy-start | bytes 98308
  9.2 0.8 %copy-start.7 = (bf16[8,2048]{1,0:T(8,128)(2,1)S(1)}, bf16[8,2048]{1,0:T(8,128)(2,1)}, u32[]{:S(2)}) copy-start(bf16[8,2048]{1,0:T(8,128)(2,1)} %hidden.1) | copy-start | bytes 98308
  10.0 0.7 %copy-start.9 = (bf16[8,4,256]{2,1,0:T(4,128)(2,1)S(1)}, bf16[8,4,256]{2,1,0:T(4,128)(2,1)}, u32[]{:S(2)}) copy-start(bf16[8,4,256]{2,1,0:T(4,128)(2,1)} %fresh.1) | copy-start | bytes 49156
  10.7 0.7 %copy-start.11 = (s32[8,20]{1,0:T(8,128)S(1)}, s32[8,20]{1,0:T(8,128)}, u32[]{:S(2)}) copy-start(s32[8,20]{1,0:T(8,128)} %table.1) | copy-start | bytes 1924
  11.4 0.7 %copy-start.12 = (s32[8,6]{1,0:T(8,128)S(1)}, s32[8,6]{1,0:T(8,128)}, u32[]{:S(2)}) copy-start(s32[8,6]{1,0:T(8,128)} %ids.1) | copy-start | bytes 580
  12.1 0.7 copy-start.13
  12.7 30.3 %copy-start.2 = (bf16[1,2,704,2048]{3,2,1,0:T(8,128)(2,1)S(1)}, bf16[1,2,704,2048]{3,2,1,0:T(8,128)(2,1)}, u32[]{:S(2)}) copy-start(bf16[1,2,704,2048]{3,2,1,0:T(8,128)(2,1)} %gate_up.1) | copy-start | bytes 17301508
  12.7 30.3 %copy-start.3 = (bf16[1,704,2048]{2,1,0:T(8,128)(2,1)S(1)}, bf16[1,704,2048]{2,1,0:T(8,128)(2,1)}, u32[]{:S(2)}) copy-start(bf16[1,704,2048]{2,1,0:T(8,128)(2,1)} %down.1) | copy-start | bytes 8650756
  23.5 23.3 %copy-start.8 = (bf16[8,2048]{1,0:T(8,128)(2,1)}, bf16[8,2048]{1,0:T(8,128)(2,1)S(1)}, u32[]{:S(2)}) copy-start(bf16[8,2048]{1,0:T(8,128)(2,1)S(1)} %get-tuple-element.16.mixed) | copy-start | bytes 98308
  23.5 24.0 %copy-start.10 = (f32[8,256]{1,0:T(8,128)}, f32[8,256]{1,0:T(8,128)S(1)}, u32[]{:S(2)}) copy-start(f32[8,256]{1,0:T(8,128)S(1)} %get-tuple-element.12.comb) | copy-start | bytes 24580
  41.5 1.5 %collective-permute-start = (bf16[256,512]{1,0:T(8,128)(2,1)S(1)}, bf16[256,512]{1,0:T(8,128)(2,1)S(1)}, u32[]{:S(2)}, u32[]{:S(2)}) collective-permute-start(bf16[256,512]{1,0:T(8,128)(2,1)S(1)} %bitcast.4), channel_id=1, source_target_pairs={{0,1},{1,0},{2,3},{3,2},{4,5},{5,4},{6,7},{7,6},{8,9},{9,8},{10,11... | collective-permute-start | bytes 786440 | tf_op jit(solution)/shard_map/ppermute | solution.py:336
  46.8 0.7 %copy-start.4 = (bf16[64,2048]{1,0:T(8,128)(2,1)}, bf16[64,2048]{1,0:T(8,128)(2,1)S(1)}, u32[]{:S(2)}) copy-start(bf16[64,2048]{1,0:T(8,128)(2,1)S(1)} %get-tuple-element.14.own) | copy-start | bytes 786436
  47.5 1.5 %collective-permute-start.1 = (bf16[64,2048]{1,0:T(8,128)(2,1)S(1)}, bf16[64,2048]{1,0:T(8,128)(2,1)S(1)}, u32[]{:S(2)}, u32[]{:S(2)}) collective-permute-start(bf16[64,2048]{1,0:T(8,128)(2,1)S(1)} %get-tuple-element.15), channel_id=1, source_target_pairs={{0,1},{1,0},{2,3},{3,2},{4,5},{5,4},{6,7},{7,6},{8,9},{9,8},{10,11... | collective-permute-start | bytes 786440 | tf_op jit(solution)/shard_map/ppermute | solution.py:353
  49.0 0.7 %copy-start.15 = (bf16[64,2048]{1,0:T(8,128)(2,1)}, bf16[64,2048]{1,0:T(8,128)(2,1)S(1)}, u32[]{:S(2)}) copy-start(bf16[64,2048]{1,0:T(8,128)(2,1)S(1)} %collective-permute-done.1.partner) | copy-start | bytes 786436
  51.7 13.9 %all-to-all-start.1 = ((bf16[16,16,512]{2,1,0:T(8,128)(2,1)}), bf16[16,16,512]{2,1,0:T(8,128)(2,1)S(1)}, u32[]{:S(2)}, u32[]{:S(2)}) async-start(bf16[16,16,512]{2,1,0:T(8,128)(2,1)} %bitcast.7), calls=%async_computation.1 | async-start | bytes 524288 | tf_op jit(solution)/shard_map/all_to_all | solution.py:330
  65.6 0.7 %copy-start.14 = (bf16[16,16,512]{2,1,0:T(8,128)(2,1)}, bf16[16,16,512]{2,1,0:T(8,128)(2,1)S(1)}, u32[]{:S(2)}) copy-start(bf16[16,16,512]{2,1,0:T(8,128)(2,1)S(1)} %all-to-all-done.1) | copy-start | bytes 786436

commit v5 on v4

--- a/solution.py
+++ b/solution.py
@@ -24,41 +24,41 @@
     return lax.broadcasted_iota(jnp.int32, shape, dim)
 
 
-def pool_loads(pool, keys, values, sems):
-    half = keys.shape[-1]
-    return [
-        pltpu.make_async_copy(pool.at[:, :, :, pl.ds(i * half, half)], kept, sems.at[i])
-        for i, kept in enumerate((keys, values))
-    ]
-
-
-def attend(table, lengths, q_ref, fresh, weight, pool, new_pool, keys, values, kept_weight, qs, att, sems):
+def copies(pairs, sems, first=0):
+    return [pltpu.make_async_copy(src, dst, sems.at[first + i]) for i, (src, dst) in enumerate(pairs)]
+
+
+def attend(refs, new_pool, scratch):
+    small, (keys, values, kept_weight, qs, att, probs, sums, sems) = scratch
+    table, lengths, q_ref, fresh = small[:4]
     requests, max_pages = table.shape
     pages, page_len, heads_kv, head_dim = keys.shape
     heads = q_ref.shape[1] // head_dim
     group = heads // heads_kv
     page_rows = page_len * heads_kv
-    loads = pool_loads(pool, keys, values, sems)
-    weight_load = pltpu.make_async_copy(weight, kept_weight, sems.at[2])
+    pool, weight = refs[-2:]
+
+    def half(array, i):
+        return array.at[:, :, :, pl.ds(i * head_dim, head_dim)]
+
+    loads = copies(list(zip(refs[:4], small[:4])), sems)
+    key_load, value_load, weight_load = copies(
+        [(half(pool, 0), keys), (half(pool, 1), values), (weight, kept_weight)], sems, 4
+    )
+    later = copies(list(zip(refs[4:-2], small[4:])), sems, 9)
+    for copy in loads + [key_load, value_load] + later + [weight_load]:
+        copy.start()
     for copy in loads:
-        copy.start()
-    weight_load.start()
+        copy.wait()
     for h in range(heads):
         qs[pl.ds(h * requests, requests), :] = q_ref[:, pl.ds(h * head_dim, head_dim)].astype(F32)
-    for copy in loads:
-        copy.wait()
-    for r in range(requests):
-        page = table[r, lengths[r] // page_len]
-        slot = lengths[r] % page_len
-        row = fresh[r]
-        keys[page, slot] = row[:, :head_dim]
-        values[page, slot] = row[:, head_dim:]
-    stores = [
-        pltpu.make_async_copy(kept, new_pool.at[:, :, :, pl.ds(i * head_dim, head_dim)], sems.at[3 + i])
-        for i, kept in enumerate((keys, values))
-    ]
-    for copy in stores:
-        copy.start()
+    spots = [(table[r, lengths[r] // page_len], lengths[r] % page_len) for r in range(requests)]
+    key_store, value_store = copies([(keys, half(new_pool, 0)), (values, half(new_pool, 1))], sems, 7)
+
+    key_load.wait()
+    for r, (page, slot) in enumerate(spots):
+        keys[page, slot] = fresh[r][:, :head_dim]
+    key_store.start()
     key_pages = keys.reshape(pages, page_rows, head_dim)
     value_pages = values.reshape(pages, page_rows, head_dim)
     columns = max_pages * page_rows
@@ -66,23 +66,27 @@
     own_head = lane % heads_kv == iota((heads, columns), 0) // group
     position = lane // heads_kv
     for r in range(requests):
-        chosen = [table[r, j] for j in range(max_pages)]
         query = qs[pl.ds(r, heads, stride=requests), :].astype(BF16)
-        gathered = jnp.concatenate([key_pages[page] for page in chosen], axis=0)
+        gathered = jnp.concatenate([key_pages[table[r, j]] for j in range(max_pages)], axis=0)
         scores = dot(query, gathered, NT) * (1.0 / math.sqrt(head_dim))
         scores = jnp.where(own_head & (position <= lengths[r]), scores, -1e30)
-        top = jnp.max(scores, axis=1, keepdims=True)
-        exponent = jnp.exp(scores - top)
-        denominator = jnp.sum(exponent, axis=1, keepdims=True)
-        gathered = jnp.concatenate([value_pages[page] for page in chosen], axis=0)
-        summed = dot(exponent.astype(BF16), gathered)
-        att[pl.ds(r, heads, stride=requests), :] = summed / denominator
+        exponent = jnp.exp(scores - jnp.max(scores, axis=1, keepdims=True))
+        sums[r] = jnp.broadcast_to(jnp.sum(exponent, axis=1, keepdims=True), (heads, head_dim))
+        probs[r] = exponent.astype(BF16)
+
+    value_load.wait()
+    for r, (page, slot) in enumerate(spots):
+        values[page, slot] = fresh[r][:, head_dim:]
+    value_store.start()
+    for r in range(requests):
+        gathered = jnp.concatenate([value_pages[table[r, j]] for j in range(max_pages)], axis=0)
+        att[pl.ds(r, heads, stride=requests), :] = dot(probs[r], gathered) / sums[r]
     attended = jnp.concatenate(
         [att[pl.ds(h * requests, requests), :] for h in range(heads)], axis=1
     ).astype(BF16)
     weight_load.wait()
     projected = dot(attended, kept_weight[...])
-    for copy in stores:
+    for copy in later + [key_store, value_store]:
         copy.wait()
     return projected
 
@@ -98,7 +102,7 @@
     mixed = mixed.astype(F32)
     norms = jnp.sqrt(jnp.mean(mixed * mixed, axis=1, keepdims=True) + 1e-06)
     norms_ref[...] = norms
-    normed = (mixed / norms * gain[...].astype(F32)).astype(BF16)
+    normed = (mixed / norms * gain[...].astype(F32).reshape(1, width)).astype(BF16)
     logits = dot(normed, router[...], NT)
     top_ref[...] = jnp.max(logits, axis=1, keepdims=True)
     column = iota((requests, experts), 1)
@@ -130,14 +134,17 @@
     )
 
 
-def attend_route_kernel(capacity, table, lengths, q_ref, fresh, hidden, gain, router, ids, weight, pool,
-                        new_pool, mixed, norms, top, slabs, comb, *scratch):
-    projected = attend(table, lengths, q_ref, fresh, weight, pool, new_pool, *scratch)
+def attend_route_kernel(capacity, *refs):
+    new_pool, mixed, norms, top, slabs, comb = refs[10:16]
+    small, scratch = refs[16:24], refs[24:]
+    projected = attend(refs[:10], new_pool, (small, scratch))
+    hidden, gain, router, ids = small[4:]
     route(projected, hidden, gain, router, ids, mixed, norms, top, slabs, comb, capacity)
 
 
-def attend_kernel(table, lengths, q_ref, fresh, weight, pool, new_pool, projected, *scratch):
-    projected[...] = attend(table, lengths, q_ref, fresh, weight, pool, new_pool, *scratch)
+def attend_kernel(*refs):
+    new_pool, projected = refs[6:8]
+    projected[...] = attend(refs[:6], new_pool, (refs[8:12], refs[12:]))
 
 
 def route_kernel(capacity, projected, hidden, gain, router, ids, mixed, norms, top, slabs, comb):
@@ -243,8 +250,8 @@
     return [pl.BlockSpec(memory_space=pl.ANY)] * count
 
 
-def scalars(count):
-    return [pl.BlockSpec(memory_space=pltpu.SMEM)] * count
+def in_hbm(count):
+    return [pl.BlockSpec(memory_space=pltpu.HBM)] * count
 
 
 def like(shape, dtype=BF16):
@@ -277,7 +284,6 @@
     parts = SLAB // capacity
     piece = width // parts
     slab_rows = experts * SLAB
-    gain = norm_gain.reshape(1, width)
 
     attend_scratch = [
         pltpu.VMEM((pages, page_len, heads_kv, head_dim), BF16),
@@ -285,8 +291,16 @@
         pltpu.VMEM(out_weight.shape, BF16),
         pltpu.VMEM((heads * requests, head_dim), F32),
         pltpu.VMEM((heads * requests, head_dim), F32),
-        pltpu.SemaphoreType.DMA((5,)),
+        pltpu.VMEM((requests, heads, page_table.shape[1] * page_len * heads_kv), BF16),
+        pltpu.VMEM((requests, heads, head_dim), F32),
+        pltpu.SemaphoreType.DMA((13,)),
     ]
+
+    def small(*arrays):
+        return [pltpu.VMEM(array.shape, array.dtype) for array in arrays]
+
+    inputs = [pltpu.SMEM(page_table.shape, jnp.int32), pltpu.SMEM(lengths.shape, jnp.int32)]
+    inputs += small(queries, fresh_key_value)
     routed_shapes = [
         like((requests, width)),
         like((requests, 1), F32),
@@ -299,28 +313,28 @@
         new_pool, mixed, norms, top, slabs, comb = pl.pallas_call(
             functools.partial(attend_route_kernel, capacity),
             out_shape=[like(kv_pool.shape)] + routed_shapes,
-            in_specs=scalars(2) + vmem(6) + anywhere(2),
-            out_specs=anywhere(1) + vmem(5),
-            scratch_shapes=attend_scratch,
+            in_specs=in_hbm(10),
+            out_specs=in_hbm(1) + vmem(5),
+            scratch_shapes=inputs + small(hidden, norm_gain, router_weight, expert_ids) + attend_scratch,
             compiler_params=attend_params,
-        )(page_table, lengths, queries, fresh_key_value, hidden, gain, router_weight, expert_ids,
-          out_weight, kv_pool)
+        )(page_table, lengths, queries, fresh_key_value, hidden, norm_gain, router_weight, expert_ids,
+          kv_pool, out_weight)
     else:
         new_pool, projected = pl.pallas_call(
             attend_kernel,
             out_shape=[like(kv_pool.shape), like((requests, width), F32)],
-            in_specs=scalars(2) + vmem(2) + anywhere(2),
-            out_specs=anywhere(1) + vmem(1),
-            scratch_shapes=attend_scratch,
+            in_specs=in_hbm(6),
+            out_specs=in_hbm(1) + vmem(1),
+            scratch_shapes=inputs + attend_scratch,
             compiler_params=attend_params,
-        )(page_table, lengths, queries, fresh_key_value, out_weight, kv_pool)
+        )(page_table, lengths, queries, fresh_key_value, kv_pool, out_weight)
         projected = lax.psum(projected, "kv")
         mixed, norms, top, slabs, comb = pl.pallas_call(
             functools.partial(route_kernel, capacity),
             out_shape=routed_shapes,
             in_specs=vmem(5),
             out_specs=vmem(5),
-        )(projected, hidden, gain, router_weight, expert_ids)
+        )(projected, hidden, norm_gain, router_weight, expert_ids)
 
     same_part = [list(range(part, req_count, copies)) for part in range(copies)]
     swap = [(index, index ^ 1) for index in range(req_count)]
@@ -356,6 +370,7 @@
         out_shape=like((slab_rows, piece)),
         in_specs=vmem(2),
         out_specs=pl.BlockSpec(memory_space=pltpu.VMEM),
+        compiler_params=pltpu.CompilerParams(vmem_limit_bytes=8 * MIB),
     )(own_terms, swapped)
     returned = exchange(leaving)
     if kv_count == 1:
@@ -364,6 +379,7 @@
             out_shape=like((requests, width)),
             in_specs=vmem(3),
             out_specs=pl.BlockSpec(memory_space=pltpu.VMEM),
+            compiler_params=pltpu.CompilerParams(vmem_limit_bytes=8 * MIB),
         )(comb, returned, mixed)
     else:
         routed = pl.pallas_call(

time: 68.8 us -> 62.5 us (0.908)
  Pallas kernels: 18.2 us -> 14 us
  local copies, waits for them, and re-layouts: 14.2 us -> 12.1 us
    pallas_call x1, Pallas kernels: 10.7 us -> 8.47 us  [body(): pl.pallas_call(functools.partial(attend_route_kernel, capacity), out_shap...]
    unnamed x32 -> x24, local copies, waits for them, and re-layouts: 13.5 us -> 12.1 us
    pallas_call x1, Pallas kernels: 1.97 us -> 0.94 us  [body(): pl.pallas_call(functools.partial(merge_kernel, capacity), out_shape=like(...]
    pallas_call x1, Pallas kernels: 1.75 us -> 0.8 us  [body(): pl.pallas_call(functools.partial(combine_kernel, capacity), out_shape=lik...]
    reshape x1 -> x0, local copies, waits for them, and re-layouts: 0.69 us -> none  [body(): gain = norm_gain.reshape(1, width)]
where the time goes in v5:
time: 62.5 us; the launch traced here: 61.8 us
  blocking collectives  18 us (29%)
  Pallas kernels  14 us (22%)
  local copies, waits for them, and re-layouts  12.1 us (19%)
  waiting for transfers between devices  12.1 us (19%)
  starting transfers between devices  3.75 us (6%)
  other arithmetic  1.25 us (2%)
  between operations  0.68 us (1%)
    all_to_all x1, blocking collectives, exchange(): lax.all_to_all(array, 'req', split_axis=0, concat_axis=0, tiled=True, axi...  18 us
    unnamed x24, local copies, waits for them, and re-layouts  12.1 us
    all_to_all x1, waiting for transfers between devices, exchange(): lax.all_to_all(array, 'req', split_axis=0, concat_axis=0, tiled=True, axi...  9.13 us
    pallas_call x1, Pallas kernels, body(): pl.pallas_call(functools.partial(attend_route_kernel, capacity), out_shap...  8.47 us
    pallas_call x1, Pallas kernels, body(): pl.pallas_call(functools.partial(expert_kernel, capacity), out_shape=[lik...  3.77 us
    all_to_all x1, starting transfers between devices, exchange(): lax.all_to_all(array, 'req', split_axis=0, concat_axis=0, tiled=True, axi...  3.55 us
    ppermute x1, waiting for transfers between devices, body(): partner = lax.ppermute(arrived, 'req', swap)  1.53 us
    ppermute x1, waiting for transfers between devices, body(): swapped = lax.ppermute(partner_terms, 'req', swap)  1.4 us
  transfers between devices with their start and end apart: 3, of which 3 were waited for; matrix products, arithmetic and copies ran while one was open for 2% of the time, Pallas kernels for 0%

profile of v5, /device:TPU:0, one launch (start us, length us, event | category | flops | bytes accessed | tf_op | source)
XLA Modules:
  0.0 61.8 jit_solution(10588263351340493725)
XLA Ops:
  0.6 0.0 copy-start
  0.6 3.4 %copy-done = bf16[2048,2048]{1,0:T(8,128)(2,1)S(1)} copy-done((bf16[2048,2048]{1,0:T(8,128)(2,1)S(1)}, bf16[2048,2048]{1,0:T(8,128)(2,1)}, u32[]{:S(2)}) %copy-start) | copy-done | bytes 8388632
  4.0 0.0 copy-start.1
  4.0 2.9 %copy-done.1 = bf16[104,32,4,256]{3,2,1,0:T(4,128)(2,1)S(1)} copy-done((bf16[104,32,4,256]{3,2,1,0:T(4,128)(2,1)S(1)}, bf16[104,32,4,256]{3,2,1,0:T(4,128)(2,1)}, u32[]{:S(2)}) %copy-start.1) | copy-done | bytes 6815768
  7.0 0.0 copy-start.4
  7.0 0.8 %copy-done.4 = bf16[16,2048]{1,0:T(8,128)(2,1)S(1)} copy-done((bf16[16,2048]{1,0:T(8,128)(2,1)S(1)}, bf16[16,2048]{1,0:T(8,128)(2,1)}, u32[]{:S(2)}) %copy-start.4) | copy-done | bytes 65560
  7.8 0.0 copy-start.5
  7.8 0.8 %copy-done.5 = bf16[8,2048]{1,0:T(8,128)(2,1)S(1)} copy-done((bf16[8,2048]{1,0:T(8,128)(2,1)S(1)}, bf16[8,2048]{1,0:T(8,128)(2,1)}, u32[]{:S(2)}) %copy-start.5) | copy-done | bytes 32792
  8.6 0.0 copy-start.6
  8.6 0.8 %copy-done.6 = bf16[8,2048]{1,0:T(8,128)(2,1)S(1)} copy-done((bf16[8,2048]{1,0:T(8,128)(2,1)S(1)}, bf16[8,2048]{1,0:T(8,128)(2,1)}, u32[]{:S(2)}) %copy-start.6) | copy-done | bytes 32792
  9.3 0.0 copy-start.7
  9.3 0.7 %copy-done.7 = bf16[8,4,256]{2,1,0:T(4,128)(2,1)S(1)} copy-done((bf16[8,4,256]{2,1,0:T(4,128)(2,1)S(1)}, bf16[8,4,256]{2,1,0:T(4,128)(2,1)}, u32[]{:S(2)}) %copy-start.7) | copy-done | bytes 16408
  10.0 0.0 copy-start.8
  10.0 0.7 %copy-done.8 = s32[8,20]{1,0:T(8,128)S(1)} copy-done((s32[8,20]{1,0:T(8,128)S(1)}, s32[8,20]{1,0:T(8,128)}, u32[]{:S(2)}) %copy-start.8) | copy-done | bytes 664
  10.7 0.0 copy-start.9
  10.7 0.7 %copy-done.9 = bf16[2048]{0:T(1024)(128)(2,1)S(1)} copy-done((bf16[2048]{0:T(1024)(128)(2,1)S(1)}, bf16[2048]{0:T(1024)(128)(2,1)}, u32[]{:S(2)}) %copy-start.9) | copy-done | bytes 4120
  11.4 0.0 copy-start.10
  11.4 0.7 %copy-done.10 = s32[8,6]{1,0:T(8,128)S(1)} copy-done((s32[8,6]{1,0:T(8,128)S(1)}, s32[8,6]{1,0:T(8,128)}, u32[]{:S(2)}) %copy-start.10) | copy-done | bytes 216
  12.1 0.0 copy-start.11
  12.1 0.7 %copy-done.11 = s32[8]{0:T(128)S(1)} copy-done((s32[8]{0:T(128)S(1)}, s32[8]{0:T(128)}, u32[]{:S(2)}) %copy-start.11) | copy-done | bytes 56
  12.7 0.0 copy-start.2
  12.7 0.0 copy-start.3
  12.7 8.5 %shard_map.147 = (bf16[104,32,4,256]{3,2,1,0:T(4,128)(2,1)}, bf16[8,2048]{1,0:T(8,128)(2,1)S(1)}, f32[8,1]{1,0:T(8,128)S(1)}, f32[8,1]{1,0:T(8,128)S(1)}, bf16[2...) custom-call(s32[8,20]{1,0:T(8,128)S(1)} %copy-done.8, s32[8]{0:T(128)S(1)} %copy-done.11, bf16[8,2048]{1,0:T(8,128)(2,1)S(1)} %copy-done.5, ...), custom_call_target="tpu_custom_call" | custom-call | tf_op jit(solution)/shard_map/pallas_call | solution.py:313
  21.2 18.0 %all_to_all.10 = bf16[16,16,512]{2,1,0:T(8,128)(2,1)S(1)} all-to-all(bf16[16,16,512]{2,1,0:T(8,128)(2,1)S(1)} %bitcast.7), channel_id=1, replica_groups={{0,2,4,6,8,10,12,14,16,18,20,22,24,26,28,30},{1,3,5,7,9,11,13,15,17,19,..., dimensions={0} | all-to-all | bytes 524288 | tf_op jit(solution)/shard_map/all_to_all | solution.py:344
  39.2 0.0 collective-permute-start
  39.2 1.5 %collective-permute-done.partner = bf16[256,512]{1,0:T(8,128)(2,1)S(1)} collective-permute-done((bf16[256,512]{1,0:T(8,128)(2,1)S(1)}, bf16[256,512]{1,0:T(8,128)(2,1)S(1)}, u32[]{:S(2)}, u32[]{:S(2)}) %collective-permute-start) | collective-permute-done | bytes 262176 | tf_op jit(solution)/shard_map/ppermute | solution.py:350
  40.7 0.0 copy-done.2
  40.8 0.0 copy-done.3
  40.8 3.8 %shard_map.148 = (bf16[64,2048]{1,0:T(8,128)(2,1)S(1)}, bf16[64,2048]{1,0:T(8,128)(2,1)S(1)}) custom-call(bf16[256,512]{1,0:T(8,128)(2,1)S(1)} %bitcast.5, bf16[256,512]{1,0:T(8,128)(2,1)S(1)} %collective-permute-done.partner, bf16[1,2,704,2048]{3,2,1,0:T(8,128)(2,1)S(1)} %copy-done.2, bf16[1,704,2048]{2,1,0:T(8,128)(2,1)S(1)} %copy-done.3), custom_call_target="tpu_custom_call" | custom-call | tf_op jit(solution)/shard_map/pallas_call | solution.py:353
  44.5 0.2 collective-permute-start.1
  44.7 1.4 %collective-permute-done.1.partner = bf16[64,2048]{1,0:T(8,128)(2,1)S(1)} collective-permute-done((bf16[64,2048]{1,0:T(8,128)(2,1)S(1)}, bf16[64,2048]{1,0:T(8,128)(2,1)S(1)}, u32[]{:S(2)}, u32[]{:S(2)}) %collective-permute-start.1) | collective-permute-done | bytes 262176 | tf_op jit(solution)/shard_map/ppermute | solution.py:367
  46.1 0.9 %shard_map.149 = bf16[256,512]{1,0:T(8,128)(2,1)} custom-call(bf16[64,2048]{1,0:T(8,128)(2,1)S(1)} %get-tuple-element.14.own, bf16[64,2048]{1,0:T(8,128)(2,1)S(1)} %collective-permute-done.1.partner), custom_call_target="tpu_custom_call" | custom-call | tf_op jit(solution)/shard_map/pallas_call | solution.py:368
  47.1 3.5 %all-to-all-start.1 = ((bf16[16,16,512]{2,1,0:T(8,128)(2,1)}), bf16[16,16,512]{2,1,0:T(8,128)(2,1)S(1)}, u32[]{:S(2)}, u32[]{:S(2)}) async-start(bf16[16,16,512]{2,1,0:T(8,128)(2,1)} %bitcast.2), calls=%async_computation.1 | async-start | bytes 524288 | tf_op jit(solution)/shard_map/all_to_all | solution.py:344
  50.6 0.6 %reduce = f32[8]{0:T(128)} reduce(f32[8,1]{1,0:T(8,128)S(1)} %get-tuple-element.18, f32[]{:T(128)} %constant.9), dimensions={1}, to_apply=%get-tuple-element.18.reduce_sub_computation | reduce | bytes 68 | tf_op jit(solution)/shard_map/pallas_call | solution.py:313
  51.2 0.6 %reduce.1 = f32[8]{0:T(128)} reduce(f32[8,1]{1,0:T(8,128)S(1)} %get-tuple-element.19, f32[]{:T(128)} %constant.9), dimensions={1}, to_apply=%get-tuple-element.19.reduce_sub_computation | reduce | bytes 68 | tf_op jit(solution)/shard_map/pallas_call | solution.py:313
  51.9 9.1 %all-to-all-done.1 = bf16[16,16,512]{2,1,0:T(8,128)(2,1)S(1)} async-done(((bf16[16,16,512]{2,1,0:T(8,128)(2,1)}), bf16[16,16,512]{2,1,0:T(8,128)(2,1)S(1)}, u32[]{:S(2)}, u32[]{:S(2)}) %all-to-all-start.1) | async-done | bytes 262176 | tf_op jit(solution)/shard_map/all_to_all | solution.py:344
  61.0 0.8 %shard_map.150 = bf16[8,2048]{1,0:T(8,128)(2,1)} custom-call(f32[8,256]{1,0:T(8,128)S(1)} %get-tuple-element.12.comb, bf16[256,512]{1,0:T(8,128)(2,1)S(1)} %bitcast.6, bf16[8,2048]{1,0:T(8,128)(2,1)S(1)} %get-tuple-element.16.mixed), custom_call_target="tpu_custom_call" | custom-call | tf_op jit(solution)/shard_map/pallas_call | solution.py:377
Async XLA Ops:
  0.6 3.4 %copy-start = (bf16[2048,2048]{1,0:T(8,128)(2,1)S(1)}, bf16[2048,2048]{1,0:T(8,128)(2,1)}, u32[]{:S(2)}) copy-start(bf16[2048,2048]{1,0:T(8,128)(2,1)} %refs_9_.1) | copy-start | bytes 25165828
  4.0 2.9 %copy-start.1 = (bf16[104,32,4,256]{3,2,1,0:T(4,128)(2,1)S(1)}, bf16[104,32,4,256]{3,2,1,0:T(4,128)(2,1)}, u32[]{:S(2)}) copy-start(bf16[104,32,4,256]{3,2,1,0:T(4,128)(2,1)} %refs_8_.1) | copy-start | bytes 20447236
  7.0 0.8 %copy-start.4 = (bf16[16,2048]{1,0:T(8,128)(2,1)S(1)}, bf16[16,2048]{1,0:T(8,128)(2,1)}, u32[]{:S(2)}) copy-start(bf16[16,2048]{1,0:T(8,128)(2,1)} %refs_6_.1) | copy-start | bytes 196612
  7.8 0.8 %copy-start.5 = (bf16[8,2048]{1,0:T(8,128)(2,1)S(1)}, bf16[8,2048]{1,0:T(8,128)(2,1)}, u32[]{:S(2)}) copy-start(bf16[8,2048]{1,0:T(8,128)(2,1)} %refs_2_.1) | copy-start | bytes 98308
  8.6 0.8 %copy-start.6 = (bf16[8,2048]{1,0:T(8,128)(2,1)S(1)}, bf16[8,2048]{1,0:T(8,128)(2,1)}, u32[]{:S(2)}) copy-start(bf16[8,2048]{1,0:T(8,128)(2,1)} %refs_4_.1) | copy-start | bytes 98308
  9.3 0.7 %copy-start.7 = (bf16[8,4,256]{2,1,0:T(4,128)(2,1)S(1)}, bf16[8,4,256]{2,1,0:T(4,128)(2,1)}, u32[]{:S(2)}) copy-start(bf16[8,4,256]{2,1,0:T(4,128)(2,1)} %refs_3_.1) | copy-start | bytes 49156
  10.0 0.7 %copy-start.8 = (s32[8,20]{1,0:T(8,128)S(1)}, s32[8,20]{1,0:T(8,128)}, u32[]{:S(2)}) copy-start(s32[8,20]{1,0:T(8,128)} %refs_0_.1) | copy-start | bytes 1924
  10.7 0.7 %copy-start.9 = (bf16[2048]{0:T(1024)(128)(2,1)S(1)}, bf16[2048]{0:T(1024)(128)(2,1)}, u32[]{:S(2)}) copy-start(bf16[2048]{0:T(1024)(128)(2,1)} %refs_5_.1) | copy-start | bytes 12292
  11.4 0.7 %copy-start.10 = (s32[8,6]{1,0:T(8,128)S(1)}, s32[8,6]{1,0:T(8,128)}, u32[]{:S(2)}) copy-start(s32[8,6]{1,0:T(8,128)} %refs_7_.1) | copy-start | bytes 580
  12.1 0.7 %copy-start.11 = (s32[8]{0:T(128)S(1)}, s32[8]{0:T(128)}, u32[]{:S(2)}) copy-start(s32[8]{0:T(128)} %refs_1_.1) | copy-start | bytes 100
  12.7 28.0 %copy-start.2 = (bf16[1,2,704,2048]{3,2,1,0:T(8,128)(2,1)S(1)}, bf16[1,2,704,2048]{3,2,1,0:T(8,128)(2,1)}, u32[]{:S(2)}) copy-start(bf16[1,2,704,2048]{3,2,1,0:T(8,128)(2,1)} %gate_up.1) | copy-start | bytes 17301508
  12.7 28.0 %copy-start.3 = (bf16[1,704,2048]{2,1,0:T(8,128)(2,1)S(1)}, bf16[1,704,2048]{2,1,0:T(8,128)(2,1)}, u32[]{:S(2)}) copy-start(bf16[1,704,2048]{2,1,0:T(8,128)(2,1)} %down.1) | copy-start | bytes 8650756
  39.2 1.5 %collective-permute-start = (bf16[256,512]{1,0:T(8,128)(2,1)S(1)}, bf16[256,512]{1,0:T(8,128)(2,1)S(1)}, u32[]{:S(2)}, u32[]{:S(2)}) collective-permute-start(bf16[256,512]{1,0:T(8,128)(2,1)S(1)} %bitcast.4), channel_id=1, source_target_pairs={{0,1},{1,0},{2,3},{3,2},{4,5},{5,4},{6,7},{7,6},{8,9},{9,8},{10,11... | collective-permute-start | bytes 786440 | tf_op jit(solution)/shard_map/ppermute | solution.py:350
  44.5 1.6 %collective-permute-start.1 = (bf16[64,2048]{1,0:T(8,128)(2,1)S(1)}, bf16[64,2048]{1,0:T(8,128)(2,1)S(1)}, u32[]{:S(2)}, u32[]{:S(2)}) collective-permute-start(bf16[64,2048]{1,0:T(8,128)(2,1)S(1)} %get-tuple-element.15), channel_id=1, source_target_pairs={{0,1},{1,0},{2,3},{3,2},{4,5},{5,4},{6,7},{7,6},{8,9},{9,8},{10,11... | collective-permute-start | bytes 786440 | tf_op jit(solution)/shard_map/ppermute | solution.py:367
  47.1 13.9 %all-to-all-start.1 = ((bf16[16,16,512]{2,1,0:T(8,128)(2,1)}), bf16[16,16,512]{2,1,0:T(8,128)(2,1)S(1)}, u32[]{:S(2)}, u32[]{:S(2)}) async-start(bf16[16,16,512]{2,1,0:T(8,128)(2,1)} %bitcast.2), calls=%async_computation.1 | async-start | bytes 524288 | tf_op jit(solution)/shard_map/all_to_all | solution.py:344

commit v6 on v5

--- a/solution.py
+++ b/solution.py
@@ -29,14 +29,14 @@
 
 
 def attend(refs, new_pool, scratch):
-    small, (keys, values, kept_weight, qs, att, probs, sums, sems) = scratch
+    small, (kept_up, kept_down, keys, values, kept_weight, qs, att, probs, sums, sems) = scratch
     table, lengths, q_ref, fresh = small[:4]
     requests, max_pages = table.shape
     pages, page_len, heads_kv, head_dim = keys.shape
     heads = q_ref.shape[1] // head_dim
     group = heads // heads_kv
     page_rows = page_len * heads_kv
-    pool, weight = refs[-2:]
+    pool, weight, gate_up, down = refs[-4:]
 
     def half(array, i):
         return array.at[:, :, :, pl.ds(i * head_dim, head_dim)]
@@ -45,8 +45,8 @@
     key_load, value_load, weight_load = copies(
         [(half(pool, 0), keys), (half(pool, 1), values), (weight, kept_weight)], sems, 4
     )
-    later = copies(list(zip(refs[4:-2], small[4:])), sems, 9)
-    for copy in loads + [key_load, value_load] + later + [weight_load]:
+    later = copies([(gate_up.at[0], kept_up), (down.at[0], kept_down)] + list(zip(refs[4:-4], small[4:])), sems, 9)
+    for copy in loads + [key_load, value_load] + later[2:] + [weight_load] + later[:2]:
         copy.start()
     for copy in loads:
         copy.wait()
@@ -135,16 +135,16 @@
 
 
 def attend_route_kernel(capacity, *refs):
-    new_pool, mixed, norms, top, slabs, comb = refs[10:16]
-    small, scratch = refs[16:24], refs[24:]
-    projected = attend(refs[:10], new_pool, (small, scratch))
+    inputs, (new_pool, kept_up, kept_down, mixed, norms, top, slabs, comb) = refs[:12], refs[12:20]
+    small, scratch = refs[20:28], refs[28:]
+    projected = attend(inputs, new_pool, (small, (kept_up, kept_down) + scratch))
     hidden, gain, router, ids = small[4:]
     route(projected, hidden, gain, router, ids, mixed, norms, top, slabs, comb, capacity)
 
 
 def attend_kernel(*refs):
-    new_pool, projected = refs[6:8]
-    projected[...] = attend(refs[:6], new_pool, (refs[8:12], refs[12:]))
+    new_pool, kept_up, kept_down, projected = refs[8:12]
+    projected[...] = attend(refs[:8], new_pool, (refs[12:16], (kept_up, kept_down) + refs[16:]))
 
 
 def route_kernel(capacity, projected, hidden, gain, router, ids, mixed, norms, top, slabs, comb):
@@ -155,18 +155,9 @@
     return [(start, min(256, units - start)) for start in range(0, units, 256)]
 
 
-def expert_kernel(capacity, own, partner, gate_up, down, own_out, partner_out, kept_up, kept_down, rows, total, sems):
-    units, width = kept_down.shape
-    parts = SLAB // capacity
-    loads = []
-    for i, (start, size) in enumerate(unit_chunks(units)):
-        span = pl.ds(start, size)
-        loads.append((
-            pltpu.make_async_copy(gate_up.at[0, :, span, :], kept_up.at[:, span, :], sems.at[2 * i]),
-            pltpu.make_async_copy(down.at[0, span, :], kept_down.at[span, :], sems.at[2 * i + 1]),
-        ))
-        for copy in loads[-1]:
-            copy.start()
+def expert_kernel(capacity, own, partner, gate_up, down, own_out, partner_out, rows, total):
+    units, width = down.shape
+    parts = SLAB // capacity
     block = 128
     each = block // parts
     shape = (block, block)
@@ -182,12 +173,10 @@
     arrived = rows[...]
     for i, (start, size) in enumerate(unit_chunks(units)):
         span = pl.ds(start, size)
-        for copy in loads[i]:
-            copy.wait()
-        gate = dot(arrived, kept_up[0, span, :], NT)
-        up = dot(arrived, kept_up[1, span, :], NT)
+        gate = dot(arrived, gate_up[0, span, :], NT)
+        up = dot(arrived, gate_up[1, span, :], NT)
         activated = (gate / (1.0 + jnp.exp(-gate)) * up).astype(BF16)
-        term = dot(activated, kept_down[span, :])
+        term = dot(activated, down[span, :])
         if i == 0:
             total[...] = term
         else:
@@ -246,12 +235,12 @@
     return [pl.BlockSpec(memory_space=pltpu.VMEM)] * count
 
 
-def anywhere(count):
-    return [pl.BlockSpec(memory_space=pl.ANY)] * count
-
-
 def in_hbm(count):
     return [pl.BlockSpec(memory_space=pltpu.HBM)] * count
+
+
+def pinned(*arrays):
+    return [pltpu.with_memory_space_constraint(array, pltpu.HBM) for array in arrays]
 
 
 def like(shape, dtype=BF16):
@@ -293,7 +282,7 @@
         pltpu.VMEM((heads * requests, head_dim), F32),
         pltpu.VMEM((requests, heads, page_table.shape[1] * page_len * heads_kv), BF16),
         pltpu.VMEM((requests, heads, head_dim), F32),
-        pltpu.SemaphoreType.DMA((13,)),
+        pltpu.SemaphoreType.DMA((15,)),
     ]
 
     def small(*arrays):
@@ -301,6 +290,7 @@
 
     inputs = [pltpu.SMEM(page_table.shape, jnp.int32), pltpu.SMEM(lengths.shape, jnp.int32)]
     inputs += small(queries, fresh_key_value)
+    kept_shapes = [like(array) for array in (kv_pool.shape, expert_gate_up.shape[1:], expert_down.shape[1:])]
     routed_shapes = [
         like((requests, width)),
         like((requests, 1), F32),
@@ -310,24 +300,24 @@
     ]
     attend_params = pltpu.CompilerParams(vmem_limit_bytes=32 * MIB)
     if kv_count == 1:
-        new_pool, mixed, norms, top, slabs, comb = pl.pallas_call(
+        new_pool, kept_up, kept_down, mixed, norms, top, slabs, comb = pl.pallas_call(
             functools.partial(attend_route_kernel, capacity),
-            out_shape=[like(kv_pool.shape)] + routed_shapes,
-            in_specs=in_hbm(10),
-            out_specs=in_hbm(1) + vmem(5),
+            out_shape=kept_shapes + routed_shapes,
+            in_specs=in_hbm(12),
+            out_specs=in_hbm(1) + vmem(7),
             scratch_shapes=inputs + small(hidden, norm_gain, router_weight, expert_ids) + attend_scratch,
             compiler_params=attend_params,
-        )(page_table, lengths, queries, fresh_key_value, hidden, norm_gain, router_weight, expert_ids,
-          kv_pool, out_weight)
+        )(*pinned(page_table, lengths, queries, fresh_key_value, hidden, norm_gain, router_weight, expert_ids,
+                  kv_pool, out_weight, expert_gate_up, expert_down))
     else:
-        new_pool, projected = pl.pallas_call(
+        new_pool, kept_up, kept_down, projected = pl.pallas_call(
             attend_kernel,
-            out_shape=[like(kv_pool.shape), like((requests, width), F32)],
-            in_specs=in_hbm(6),
-            out_specs=in_hbm(1) + vmem(1),
+            out_shape=kept_shapes + [like((requests, width), F32)],
+            in_specs=in_hbm(8),
+            out_specs=in_hbm(1) + vmem(3),
             scratch_shapes=inputs + attend_scratch,
             compiler_params=attend_params,
-        )(page_table, lengths, queries, fresh_key_value, kv_pool, out_weight)
+        )(*pinned(page_table, lengths, queries, fresh_key_value, kv_pool, out_weight, expert_gate_up, expert_down))
         projected = lax.psum(projected, "kv")
         mixed, norms, top, slabs, comb = pl.pallas_call(
             functools.partial(route_kernel, capacity),
@@ -348,22 +338,15 @@
 
     arrived = exchange(slabs)
     partner = lax.ppermute(arrived, "req", swap)
-    units = expert_down.shape[1]
     kept = experts * capacity
     own_terms, partner_terms = pl.pallas_call(
         functools.partial(expert_kernel, capacity),
         out_shape=[like((kept, width))] * 2,
-        in_specs=vmem(2) + anywhere(2),
+        in_specs=vmem(4),
         out_specs=vmem(2),
-        scratch_shapes=[
-            pltpu.VMEM((2, units, width), BF16),
-            pltpu.VMEM((units, width), BF16),
-            pltpu.VMEM((2 * kept, width), BF16),
-            pltpu.VMEM((2 * kept, width), F32),
-            pltpu.SemaphoreType.DMA((2 * len(unit_chunks(units)),)),
-        ],
-        compiler_params=pltpu.CompilerParams(vmem_limit_bytes=32 * MIB),
-    )(arrived, partner, expert_gate_up, expert_down)
+        scratch_shapes=[pltpu.VMEM((2 * kept, width), BF16), pltpu.VMEM((2 * kept, width), F32)],
+        compiler_params=pltpu.CompilerParams(vmem_limit_bytes=28 * MIB),
+    )(arrived, partner, kept_up, kept_down)
     swapped = lax.ppermute(partner_terms, "req", swap)
     leaving = pl.pallas_call(
         functools.partial(merge_kernel, capacity),

time: 62.5 us -> 51.8 us (0.83)
  local copies, waits for them, and re-layouts: 12.1 us -> 0 us
  Pallas kernels: 14 us -> 15.8 us
    unnamed x24 -> x0, local copies, waits for them, and re-layouts: 12.1 us -> none
    pallas_call x1, Pallas kernels: 8.47 us -> 11.1 us  [body(): pl.pallas_call(functools.partial(attend_route_kernel, capacity), out_shap...]
    pallas_call x1, Pallas kernels: 3.77 us -> 2.92 us  [body(): pl.pallas_call(functools.partial(expert_kernel, capacity), out_shape=[lik...]
where the time goes in v6:
time: 51.8 us; the launch traced here: 51.5 us
  blocking collectives  18 us (35%)
  Pallas kernels  15.8 us (31%)
  waiting for transfers between devices  12.1 us (23%)
  starting transfers between devices  3.74 us (7%)
  other arithmetic  1.25 us (2%)
  between operations  0.66 us (1%)
    all_to_all x1, blocking collectives, exchange(): lax.all_to_all(array, 'req', split_axis=0, concat_axis=0, tiled=True, axi...  18 us
    pallas_call x1, Pallas kernels, body(): pl.pallas_call(functools.partial(attend_route_kernel, capacity), out_shap...  11.1 us
    all_to_all x1, waiting for transfers between devices, exchange(): lax.all_to_all(array, 'req', split_axis=0, concat_axis=0, tiled=True, axi...  9.13 us
    all_to_all x1, starting transfers between devices, exchange(): lax.all_to_all(array, 'req', split_axis=0, concat_axis=0, tiled=True, axi...  3.54 us
    pallas_call x1, Pallas kernels, body(): pl.pallas_call(functools.partial(expert_kernel, capacity), out_shape=[lik...  2.92 us
    ppermute x1, waiting for transfers between devices, body(): partner = lax.ppermute(arrived, 'req', swap)  1.53 us
    ppermute x1, waiting for transfers between devices, body(): swapped = lax.ppermute(partner_terms, 'req', swap)  1.4 us
    pallas_call x2, other arithmetic, body(): pl.pallas_call(functools.partial(attend_route_kernel, capacity), out_shap...  1.25 us
  transfers between devices with their start and end apart: 3, of which 3 were waited for; matrix products, arithmetic and copies ran while one was open for 2% of the time, Pallas kernels for 0%

profile of v6, /device:TPU:0, one launch (start us, length us, event | category | flops | bytes accessed | tf_op | source)
XLA Modules:
  0.0 51.5 jit_solution(12552232916268216904)
XLA Ops:
  0.6 11.1 %shard_map.147 = (bf16[104,32,4,256]{3,2,1,0:T(4,128)(2,1)}, bf16[2,704,2048]{2,1,0:T(8,128)(2,1)S(1)}, bf16[704,2048]{1,0:T(8,128)(2,1)S(1)}, bf16[8,2048]{1,0:...) custom-call(s32[8,20]{1,0:T(8,128)} %refs_0_.1, ...), custom_call_target="tpu_custom_call" | custom-call | tf_op jit(solution)/shard_map/pallas_call | solution.py:303
  11.8 18.0 %all_to_all.10 = bf16[16,16,512]{2,1,0:T(8,128)(2,1)S(1)} all-to-all(bf16[16,16,512]{2,1,0:T(8,128)(2,1)S(1)} %bitcast.7), channel_id=1, replica_groups={{0,2,4,6,8,10,12,14,16,18,20,22,24,26,28,30},{1,3,5,7,9,11,13,15,17,19,..., dimensions={0} | all-to-all | bytes 524288 | tf_op jit(solution)/shard_map/all_to_all | solution.py:334
  29.8 0.0 collective-permute-start
  29.8 1.5 %collective-permute-done.partner = bf16[256,512]{1,0:T(8,128)(2,1)S(1)} collective-permute-done((bf16[256,512]{1,0:T(8,128)(2,1)S(1)}, bf16[256,512]{1,0:T(8,128)(2,1)S(1)}, u32[]{:S(2)}, u32[]{:S(2)}) %collective-permute-start) | collective-permute-done | bytes 262176 | tf_op jit(solution)/shard_map/ppermute | solution.py:340
  31.3 2.9 %shard_map.148 = (bf16[64,2048]{1,0:T(8,128)(2,1)S(1)}, bf16[64,2048]{1,0:T(8,128)(2,1)S(1)}) custom-call(bf16[256,512]{1,0:T(8,128)(2,1)S(1)} %bitcast.5, bf16[256,512]{1,0:T(8,128)(2,1)S(1)} %collective-permute-done.partner, bf16[2,704,2048]{2,1,0:T(8,128)(2,1)S(1)} %get-tuple-element.16.gate_up, bf16[704,2048]{1,0:T(8,128)(2,1)S(1)} %get-tuple-element.17.down), custom_call_target="tpu_custom_call" | custom-call | tf_op jit(solution)/shard_map/pallas_call | solution.py:342
  34.2 0.2 collective-permute-start.1
  34.4 1.4 %collective-permute-done.1.partner = bf16[64,2048]{1,0:T(8,128)(2,1)S(1)} collective-permute-done((bf16[64,2048]{1,0:T(8,128)(2,1)S(1)}, bf16[64,2048]{1,0:T(8,128)(2,1)S(1)}, u32[]{:S(2)}, u32[]{:S(2)}) %collective-permute-start.1) | collective-permute-done | bytes 262176 | tf_op jit(solution)/shard_map/ppermute | solution.py:350
  35.8 0.9 %shard_map.149 = bf16[256,512]{1,0:T(8,128)(2,1)} custom-call(bf16[64,2048]{1,0:T(8,128)(2,1)S(1)} %get-tuple-element.18.own, bf16[64,2048]{1,0:T(8,128)(2,1)S(1)} %collective-permute-done.1.partner), custom_call_target="tpu_custom_call" | custom-call | tf_op jit(solution)/shard_map/pallas_call | solution.py:351
  36.8 3.5 %all-to-all-start.1 = ((bf16[16,16,512]{2,1,0:T(8,128)(2,1)}), bf16[16,16,512]{2,1,0:T(8,128)(2,1)S(1)}, u32[]{:S(2)}, u32[]{:S(2)}) async-start(bf16[16,16,512]{2,1,0:T(8,128)(2,1)} %bitcast.2), calls=%async_computation.1 | async-start | bytes 524288 | tf_op jit(solution)/shard_map/all_to_all | solution.py:334
  40.3 0.6 %reduce = f32[8]{0:T(128)} reduce(f32[8,1]{1,0:T(8,128)S(1)} %get-tuple-element.22, f32[]{:T(128)} %constant.9), dimensions={1}, to_apply=%get-tuple-element.22.reduce_sub_computation | reduce | bytes 68 | tf_op jit(solution)/shard_map/pallas_call | solution.py:303
  40.9 0.6 %reduce.1 = f32[8]{0:T(128)} reduce(f32[8,1]{1,0:T(8,128)S(1)} %get-tuple-element.23, f32[]{:T(128)} %constant.9), dimensions={1}, to_apply=%get-tuple-element.23.reduce_sub_computation | reduce | bytes 68 | tf_op jit(solution)/shard_map/pallas_call | solution.py:303
  41.6 9.1 %all-to-all-done.1 = bf16[16,16,512]{2,1,0:T(8,128)(2,1)S(1)} async-done(((bf16[16,16,512]{2,1,0:T(8,128)(2,1)}), bf16[16,16,512]{2,1,0:T(8,128)(2,1)S(1)}, u32[]{:S(2)}, u32[]{:S(2)}) %all-to-all-start.1) | async-done | bytes 262176 | tf_op jit(solution)/shard_map/all_to_all | solution.py:334
  50.7 0.8 %shard_map.150 = bf16[8,2048]{1,0:T(8,128)(2,1)} custom-call(f32[8,256]{1,0:T(8,128)S(1)} %get-tuple-element.14.comb, bf16[256,512]{1,0:T(8,128)(2,1)S(1)} %bitcast.6, bf16[8,2048]{1,0:T(8,128)(2,1)S(1)} %get-tuple-element.20.mixed), custom_call_target="tpu_custom_call" | custom-call | tf_op jit(solution)/shard_map/pallas_call | solution.py:360
Async XLA Ops:
  29.8 1.5 %collective-permute-start = (bf16[256,512]{1,0:T(8,128)(2,1)S(1)}, bf16[256,512]{1,0:T(8,128)(2,1)S(1)}, u32[]{:S(2)}, u32[]{:S(2)}) collective-permute-start(bf16[256,512]{1,0:T(8,128)(2,1)S(1)} %bitcast.4), channel_id=1, source_target_pairs={{0,1},{1,0},{2,3},{3,2},{4,5},{5,4},{6,7},{7,6},{8,9},{9,8},{10,11... | collective-permute-start | bytes 786440 | tf_op jit(solution)/shard_map/ppermute | solution.py:340
  34.2 1.6 %collective-permute-start.1 = (bf16[64,2048]{1,0:T(8,128)(2,1)S(1)}, bf16[64,2048]{1,0:T(8,128)(2,1)S(1)}, u32[]{:S(2)}, u32[]{:S(2)}) collective-permute-start(bf16[64,2048]{1,0:T(8,128)(2,1)S(1)} %get-tuple-element.19), channel_id=1, source_target_pairs={{0,1},{1,0},{2,3},{3,2},{4,5},{5,4},{6,7},{7,6},{8,9},{9,8},{10,11... | collective-permute-start | bytes 786440 | tf_op jit(solution)/shard_map/ppermute | solution.py:350
  36.8 13.9 %all-to-all-start.1 = ((bf16[16,16,512]{2,1,0:T(8,128)(2,1)}), bf16[16,16,512]{2,1,0:T(8,128)(2,1)S(1)}, u32[]{:S(2)}, u32[]{:S(2)}) async-start(bf16[16,16,512]{2,1,0:T(8,128)(2,1)} %bitcast.2), calls=%async_computation.1 | async-start | bytes 524288 | tf_op jit(solution)/shard_map/all_to_all | solution.py:334

commit v7 on v6

--- a/solution.py
+++ b/solution.py
@@ -28,37 +28,36 @@
     return [pltpu.make_async_copy(src, dst, sems.at[first + i]) for i, (src, dst) in enumerate(pairs)]
 
 
-def attend(refs, new_pool, scratch):
-    small, (kept_up, kept_down, keys, values, kept_weight, qs, att, probs, sums, sems) = scratch
+def pool_half(array, i):
+    head_dim = array.shape[3] // 2
+    return array.at[:, :, :, pl.ds(i * head_dim, head_dim)]
+
+
+def attend(refs, keys, values, scratch):
+    small, (kept_weight, qs, att, probs, sums, sems) = scratch
     table, lengths, q_ref, fresh = small[:4]
     requests, max_pages = table.shape
     pages, page_len, heads_kv, head_dim = keys.shape
     heads = q_ref.shape[1] // head_dim
     group = heads // heads_kv
     page_rows = page_len * heads_kv
-    pool, weight, gate_up, down = refs[-4:]
-
-    def half(array, i):
-        return array.at[:, :, :, pl.ds(i * head_dim, head_dim)]
-
+    pool, weight = refs[-2:]
     loads = copies(list(zip(refs[:4], small[:4])), sems)
     key_load, value_load, weight_load = copies(
-        [(half(pool, 0), keys), (half(pool, 1), values), (weight, kept_weight)], sems, 4
-    )
-    later = copies([(gate_up.at[0], kept_up), (down.at[0], kept_down)] + list(zip(refs[4:-4], small[4:])), sems, 9)
-    for copy in loads + [key_load, value_load] + later[2:] + [weight_load] + later[:2]:
+        [(pool_half(pool, 0), keys), (pool_half(pool, 1), values), (weight, kept_weight)], sems, 4
+    )
+    later = copies(list(zip(refs[4:-2], small[4:])), sems, 7)
+    for copy in loads + [key_load, value_load] + later + [weight_load]:
         copy.start()
     for copy in loads:
         copy.wait()
     for h in range(heads):
         qs[pl.ds(h * requests, requests), :] = q_ref[:, pl.ds(h * head_dim, head_dim)].astype(F32)
     spots = [(table[r, lengths[r] // page_len], lengths[r] % page_len) for r in range(requests)]
-    key_store, value_store = copies([(keys, half(new_pool, 0)), (values, half(new_pool, 1))], sems, 7)
 
     key_load.wait()
     for r, (page, slot) in enumerate(spots):
         keys[page, slot] = fresh[r][:, :head_dim]
-    key_store.start()
     key_pages = keys.reshape(pages, page_rows, head_dim)
     value_pages = values.reshape(pages, page_rows, head_dim)
     columns = max_pages * page_rows
@@ -77,7 +76,6 @@
     value_load.wait()
     for r, (page, slot) in enumerate(spots):
         values[page, slot] = fresh[r][:, head_dim:]
-    value_store.start()
     for r in range(requests):
         gathered = jnp.concatenate([value_pages[table[r, j]] for j in range(max_pages)], axis=0)
         att[pl.ds(r, heads, stride=requests), :] = dot(probs[r], gathered) / sums[r]
@@ -86,7 +84,7 @@
     ).astype(BF16)
     weight_load.wait()
     projected = dot(attended, kept_weight[...])
-    for copy in later + [key_store, value_store]:
+    for copy in later:
         copy.wait()
     return projected
 
@@ -135,16 +133,32 @@
 
 
 def attend_route_kernel(capacity, *refs):
-    inputs, (new_pool, kept_up, kept_down, mixed, norms, top, slabs, comb) = refs[:12], refs[12:20]
-    small, scratch = refs[20:28], refs[28:]
-    projected = attend(inputs, new_pool, (small, (kept_up, kept_down) + scratch))
+    inputs, (keys, values, mixed, norms, top, slabs, comb) = refs[:10], refs[10:17]
+    small, scratch = refs[17:25], refs[25:]
+    projected = attend(inputs, keys, values, (small, scratch))
     hidden, gain, router, ids = small[4:]
     route(projected, hidden, gain, router, ids, mixed, norms, top, slabs, comb, capacity)
 
 
 def attend_kernel(*refs):
-    new_pool, kept_up, kept_down, projected = refs[8:12]
-    projected[...] = attend(refs[:8], new_pool, (refs[12:16], (kept_up, kept_down) + refs[16:]))
+    keys, values, projected = refs[6:9]
+    projected[...] = attend(refs[:6], keys, values, (refs[9:13], refs[13:]))
+
+
+def store_kernel(keys, values, gate_up, down, new_pool, kept_up, kept_down, sems):
+    moves = copies(
+        [
+            (gate_up.at[0], kept_up),
+            (down.at[0], kept_down),
+            (keys, pool_half(new_pool, 0)),
+            (values, pool_half(new_pool, 1)),
+        ],
+        sems,
+    )
+    for copy in moves:
+        copy.start()
+    for copy in moves:
+        copy.wait()
 
 
 def route_kernel(capacity, projected, hidden, gain, router, ids, mixed, norms, top, slabs, comb):
@@ -275,14 +289,12 @@
     slab_rows = experts * SLAB
 
     attend_scratch = [
-        pltpu.VMEM((pages, page_len, heads_kv, head_dim), BF16),
-        pltpu.VMEM((pages, page_len, heads_kv, head_dim), BF16),
         pltpu.VMEM(out_weight.shape, BF16),
         pltpu.VMEM((heads * requests, head_dim), F32),
         pltpu.VMEM((heads * requests, head_dim), F32),
         pltpu.VMEM((requests, heads, page_table.shape[1] * page_len * heads_kv), BF16),
         pltpu.VMEM((requests, heads, head_dim), F32),
-        pltpu.SemaphoreType.DMA((15,)),
+        pltpu.SemaphoreType.DMA((11,)),
     ]
 
     def small(*arrays):
@@ -290,7 +302,7 @@
 
     inputs = [pltpu.SMEM(page_table.shape, jnp.int32), pltpu.SMEM(lengths.shape, jnp.int32)]
     inputs += small(queries, fresh_key_value)
-    kept_shapes = [like(array) for array in (kv_pool.shape, expert_gate_up.shape[1:], expert_down.shape[1:])]
+    kept_shapes = [like((pages, page_len, heads_kv, head_dim))] * 2
     routed_shapes = [
         like((requests, width)),
         like((requests, 1), F32),
@@ -300,24 +312,24 @@
     ]
     attend_params = pltpu.CompilerParams(vmem_limit_bytes=32 * MIB)
     if kv_count == 1:
-        new_pool, kept_up, kept_down, mixed, norms, top, slabs, comb = pl.pallas_call(
+        keys, values, mixed, norms, top, slabs, comb = pl.pallas_call(
             functools.partial(attend_route_kernel, capacity),
             out_shape=kept_shapes + routed_shapes,
-            in_specs=in_hbm(12),
-            out_specs=in_hbm(1) + vmem(7),
+            in_specs=in_hbm(10),
+            out_specs=vmem(7),
             scratch_shapes=inputs + small(hidden, norm_gain, router_weight, expert_ids) + attend_scratch,
             compiler_params=attend_params,
         )(*pinned(page_table, lengths, queries, fresh_key_value, hidden, norm_gain, router_weight, expert_ids,
-                  kv_pool, out_weight, expert_gate_up, expert_down))
+                  kv_pool, out_weight))
     else:
-        new_pool, kept_up, kept_down, projected = pl.pallas_call(
+        keys, values, projected = pl.pallas_call(
             attend_kernel,
             out_shape=kept_shapes + [like((requests, width), F32)],
-            in_specs=in_hbm(8),
-            out_specs=in_hbm(1) + vmem(3),
+            in_specs=in_hbm(6),
+            out_specs=vmem(3),
             scratch_shapes=inputs + attend_scratch,
             compiler_params=attend_params,
-        )(*pinned(page_table, lengths, queries, fresh_key_value, kv_pool, out_weight, expert_gate_up, expert_down))
+        )(*pinned(page_table, lengths, queries, fresh_key_value, kv_pool, out_weight))
         projected = lax.psum(projected, "kv")
         mixed, norms, top, slabs, comb = pl.pallas_call(
             functools.partial(route_kernel, capacity),
@@ -325,6 +337,17 @@
             in_specs=vmem(5),
             out_specs=vmem(5),
         )(projected, hidden, norm_gain, router_weight, expert_ids)
+
+    stored = kv_pool.size + expert_gate_up.size + expert_down.size
+    new_pool, kept_up, kept_down = pl.pallas_call(
+        store_kernel,
+        out_shape=[like(array) for array in (kv_pool.shape, expert_gate_up.shape[1:], expert_down.shape[1:])],
+        in_specs=vmem(2) + in_hbm(2),
+        out_specs=in_hbm(1) + vmem(2),
+        scratch_shapes=[pltpu.SemaphoreType.DMA((4,))],
+        compiler_params=pltpu.CompilerParams(vmem_limit_bytes=24 * MIB),
+        cost_estimate=pl.CostEstimate(flops=0, bytes_accessed=4 * stored, transcendentals=0),
+    )(keys, values, *pinned(expert_gate_up, expert_down))
 
     same_part = [list(range(part, req_count, copies)) for part in range(copies)]
     swap = [(index, index ^ 1) for index in range(req_count)]

time: 51.8 us -> 52.9 us (1.021)
  Pallas kernels: 15.8 us -> 18 us
  waiting for transfers between devices: 12.1 us -> 10.5 us
    pallas_call x0 -> x1, Pallas kernels: none -> 6.01 us  [body(): pl.pallas_call(store_kernel, out_shape=[like(array) for array in (kv_pool...]
    pallas_call x1, Pallas kernels: 11.1 us -> 7.38 us  [body(): pl.pallas_call(functools.partial(attend_route_kernel, capacity), out_shap...]
    ppermute x1, waiting for transfers between devices: 1.53 us -> 0.01 us  [body(): partner = lax.ppermute(arrived, 'req', swap)]
  transfers between devices with their start and end apart: 3 -> 3, of which waited for: 3 -> 2; matrix products, arithmetic and copies ran while one was open for 2% -> 2% of each run, Pallas kernels for 0% -> 11%
where the time goes in v7:
time: 52.9 us; the launch traced here: 52.6 us
  Pallas kernels  18 us (34%)
  blocking collectives  18 us (34%)
  waiting for transfers between devices  10.5 us (20%)
  starting transfers between devices  4.13 us (8%)
  other arithmetic  1.25 us (2%)
  between operations  0.68 us (1%)
    all_to_all x1, blocking collectives, exchange(): lax.all_to_all(array, 'req', split_axis=0, concat_axis=0, tiled=True, axi...  18 us
    all_to_all x1, waiting for transfers between devices, exchange(): lax.all_to_all(array, 'req', split_axis=0, concat_axis=0, tiled=True, axi...  9.36 us
    pallas_call x1, Pallas kernels, body(): pl.pallas_call(functools.partial(attend_route_kernel, capacity), out_shap...  7.38 us
    pallas_call x1, Pallas kernels, body(): pl.pallas_call(store_kernel, out_shape=[like(array) for array in (kv_pool...  6.01 us
    all_to_all x1, starting transfers between devices, exchange(): lax.all_to_all(array, 'req', split_axis=0, concat_axis=0, tiled=True, axi...  3.55 us
    pallas_call x1, Pallas kernels, body(): pl.pallas_call(functools.partial(expert_kernel, capacity), out_shape=[lik...  2.92 us
    pallas_call x2, other arithmetic, body(): pl.pallas_call(functools.partial(attend_route_kernel, capacity), out_shap...  1.25 us
    ppermute x1, waiting for transfers between devices, body(): swapped = lax.ppermute(partner_terms, 'req', swap)  1.16 us
  transfers between devices with their start and end apart: 3, of which 2 were waited for; matrix products, arithmetic and copies ran while one was open for 2% of the time, Pallas kernels for 11%

profile of v7, /device:TPU:0, one launch (start us, length us, event | category | flops | bytes accessed | tf_op | source)
XLA Modules:
  0.0 52.6 jit_solution(14891263204250326627)
XLA Ops:
  0.6 7.4 %shard_map.147 = (bf16[104,32,4,128]{3,2,1,0:T(4,128)(2,1)S(1)}, bf16[104,32,4,128]{3,2,1,0:T(4,128)(2,1)S(1)}, bf16[8,2048]{1,0:T(8,128)(2,1)S(1)}, f32[8,1]{1,...) custom-call(s32[8,20]{1,0:T(8,128)} %refs_0_.1, s32[8]{0:T(128)} %refs_1_.1, ...), custom_call_target="tpu_custom_call" | custom-call | tf_op jit(solution)/shard_map/pallas_call | solution.py:315
  8.0 18.0 %all_to_all.10 = bf16[16,16,512]{2,1,0:T(8,128)(2,1)S(1)} all-to-all(bf16[16,16,512]{2,1,0:T(8,128)(2,1)S(1)} %bitcast.7), channel_id=1, replica_groups={{0,2,4,6,8,10,12,14,16,18,20,22,24,26,28,30},{1,3,5,7,9,11,13,15,17,19,..., dimensions={0} | all-to-all | bytes 524288 | tf_op jit(solution)/shard_map/all_to_all | solution.py:357
  26.0 0.0 collective-permute-start
  26.0 6.0 %shard_map.148 = (bf16[104,32,4,256]{3,2,1,0:T(4,128)(2,1)}, bf16[2,704,2048]{2,1,0:T(8,128)(2,1)S(1)}, bf16[704,2048]{1,0:T(8,128)(2,1)S(1)}) custom-call(bf16[104,32,4,128]{3,2,1,0:T(4,128)(2,1)S(1)} %get-tuple-element.18.keys, bf16[104,32,4,128]{3,2,1,0:T(4,128)(2,1)S(1)} %get-tuple-element.19.values, bf16[1,2,704,2048]{3,2,1,0:T(8,128)(2,1)} %gate_up.1, ...), custom_call_target="tpu_custom_call" | custom-call | bytes 30932992 | tf_op jit(solution)/shard_map/pallas_call | solution.py:342
  32.0 0.0 collective-permute-done.partner
  32.0 2.9 %shard_map.149 = (bf16[64,2048]{1,0:T(8,128)(2,1)S(1)}, bf16[64,2048]{1,0:T(8,128)(2,1)S(1)}) custom-call(bf16[256,512]{1,0:T(8,128)(2,1)S(1)} %bitcast.5, bf16[256,512]{1,0:T(8,128)(2,1)S(1)} %collective-permute-done.partner, bf16[2,704,2048]{2,1,0:T(8,128)(2,1)S(1)} %get-tuple-element.20.gate_up, bf16[704,2048]{1,0:T(8,128)(2,1)S(1)} %get-tuple-element.21.down), custom_call_target="tpu_custom_call" | custom-call | tf_op jit(solution)/shard_map/pallas_call | solution.py:365
  35.0 0.6 %collective-permute-start.1 = (bf16[64,2048]{1,0:T(8,128)(2,1)S(1)}, bf16[64,2048]{1,0:T(8,128)(2,1)S(1)}, u32[]{:S(2)}, u32[]{:S(2)}) collective-permute-start(bf16[64,2048]{1,0:T(8,128)(2,1)S(1)} %get-tuple-element.23), channel_id=1, source_target_pairs={{0,1},{1,0},{2,3},{3,2},{4,5},{5,4},{6,7},{7,6},{8,9},{9,8},{10,11... | collective-permute-start | bytes 786440 | tf_op jit(solution)/shard_map/ppermute | solution.py:373
  35.5 1.2 %collective-permute-done.1.partner = bf16[64,2048]{1,0:T(8,128)(2,1)S(1)} collective-permute-done((bf16[64,2048]{1,0:T(8,128)(2,1)S(1)}, bf16[64,2048]{1,0:T(8,128)(2,1)S(1)}, u32[]{:S(2)}, u32[]{:S(2)}) %collective-permute-start.1) | collective-permute-done | bytes 262176 | tf_op jit(solution)/shard_map/ppermute | solution.py:373
  36.7 0.9 %shard_map.150 = bf16[256,512]{1,0:T(8,128)(2,1)} custom-call(bf16[64,2048]{1,0:T(8,128)(2,1)S(1)} %get-tuple-element.22.own, bf16[64,2048]{1,0:T(8,128)(2,1)S(1)} %collective-permute-done.1.partner), custom_call_target="tpu_custom_call" | custom-call | tf_op jit(solution)/shard_map/pallas_call | solution.py:374
  37.6 3.5 %all-to-all-start.1 = ((bf16[16,16,512]{2,1,0:T(8,128)(2,1)}), bf16[16,16,512]{2,1,0:T(8,128)(2,1)S(1)}, u32[]{:S(2)}, u32[]{:S(2)}) async-start(bf16[16,16,512]{2,1,0:T(8,128)(2,1)} %bitcast.2), calls=%async_computation.1 | async-start | bytes 524288 | tf_op jit(solution)/shard_map/all_to_all | solution.py:357
  41.2 0.6 %reduce = f32[8]{0:T(128)} reduce(f32[8,1]{1,0:T(8,128)S(1)} %get-tuple-element.26, f32[]{:T(128)} %constant.9), dimensions={1}, to_apply=%get-tuple-element.26.reduce_sub_computation | reduce | bytes 68 | tf_op jit(solution)/shard_map/pallas_call | solution.py:315
  41.8 0.6 %reduce.1 = f32[8]{0:T(128)} reduce(f32[8,1]{1,0:T(8,128)S(1)} %get-tuple-element.27, f32[]{:T(128)} %constant.9), dimensions={1}, to_apply=%get-tuple-element.27.reduce_sub_computation | reduce | bytes 68 | tf_op jit(solution)/shard_map/pallas_call | solution.py:315
  42.4 9.4 %all-to-all-done.1 = bf16[16,16,512]{2,1,0:T(8,128)(2,1)S(1)} async-done(((bf16[16,16,512]{2,1,0:T(8,128)(2,1)}), bf16[16,16,512]{2,1,0:T(8,128)(2,1)S(1)}, u32[]{:S(2)}, u32[]{:S(2)}) %all-to-all-start.1) | async-done | bytes 262176 | tf_op jit(solution)/shard_map/all_to_all | solution.py:357
  51.8 0.8 %shard_map.151 = bf16[8,2048]{1,0:T(8,128)(2,1)} custom-call(f32[8,256]{1,0:T(8,128)S(1)} %get-tuple-element.16.comb, bf16[256,512]{1,0:T(8,128)(2,1)S(1)} %bitcast.6, bf16[8,2048]{1,0:T(8,128)(2,1)S(1)} %get-tuple-element.24.mixed), custom_call_target="tpu_custom_call" | custom-call | tf_op jit(solution)/shard_map/pallas_call | solution.py:383
Async XLA Ops:
  26.0 6.0 %collective-permute-start = (bf16[256,512]{1,0:T(8,128)(2,1)S(1)}, bf16[256,512]{1,0:T(8,128)(2,1)S(1)}, u32[]{:S(2)}, u32[]{:S(2)}) collective-permute-start(bf16[256,512]{1,0:T(8,128)(2,1)S(1)} %bitcast.4), channel_id=1, source_target_pairs={{0,1},{1,0},{2,3},{3,2},{4,5},{5,4},{6,7},{7,6},{8,9},{9,8},{10,11... | collective-permute-start | bytes 786440 | tf_op jit(solution)/shard_map/ppermute | solution.py:363
  35.0 1.7 %collective-permute-start.1 = (bf16[64,2048]{1,0:T(8,128)(2,1)S(1)}, bf16[64,2048]{1,0:T(8,128)(2,1)S(1)}, u32[]{:S(2)}, u32[]{:S(2)}) collective-permute-start(bf16[64,2048]{1,0:T(8,128)(2,1)S(1)} %get-tuple-element.23), channel_id=1, source_target_pairs={{0,1},{1,0},{2,3},{3,2},{4,5},{5,4},{6,7},{7,6},{8,9},{9,8},{10,11... | collective-permute-start | bytes 786440 | tf_op jit(solution)/shard_map/ppermute | solution.py:373
  37.6 14.2 %all-to-all-start.1 = ((bf16[16,16,512]{2,1,0:T(8,128)(2,1)}), bf16[16,16,512]{2,1,0:T(8,128)(2,1)S(1)}, u32[]{:S(2)}, u32[]{:S(2)}) async-start(bf16[16,16,512]{2,1,0:T(8,128)(2,1)} %bitcast.2), calls=%async_computation.1 | async-start | bytes 524288 | tf_op jit(solution)/shard_map/all_to_all | solution.py:357

commit v8 on v7

--- a/solution.py
+++ b/solution.py
@@ -169,47 +169,35 @@
     return [(start, min(256, units - start)) for start in range(0, units, 256)]
 
 
-def expert_kernel(capacity, own, partner, gate_up, down, own_out, partner_out, rows, total):
-    units, width = down.shape
+def expert_kernel(capacity, arrived, own_up, own_down, other_up, other_down, slabs, rows, total):
     parts = SLAB // capacity
+    piece = slabs.shape[1]
     block = 128
     each = block // parts
+    blocks = slabs.shape[0] // block
     shape = (block, block)
-    sort = (iota(shape, 1) == iota(shape, 0) % each * parts + iota(shape, 0) // each).astype(BF16)
-    row = 0
-    for source in (own, partner):
-        for start in range(0, source.shape[0], block):
-            sorted_rows = dot(sort, source[pl.ds(start, block), :]).astype(BF16)
-            rows[pl.ds(row, each), :] = jnp.concatenate(
-                [sorted_rows[p * each : (p + 1) * each] for p in range(parts)], axis=1
-            )
-            row += each
-    arrived = rows[...]
-    for i, (start, size) in enumerate(unit_chunks(units)):
-        span = pl.ds(start, size)
-        gate = dot(arrived, gate_up[0, span, :], NT)
-        up = dot(arrived, gate_up[1, span, :], NT)
-        activated = (gate / (1.0 + jnp.exp(-gate)) * up).astype(BF16)
-        term = dot(activated, down[span, :])
-        if i == 0:
-            total[...] = term
-        else:
-            total[...] += term
-    kept = own_out.shape[0]
-    own_out[...] = total[pl.ds(0, kept), :].astype(BF16)
-    partner_out[...] = total[pl.ds(kept, kept), :].astype(BF16)
-
-
-def merge_kernel(capacity, own, partner, slabs):
-    parts = SLAB // capacity
-    block = 128
-    each = block // parts
-    piece = slabs.shape[1]
-    shape = (block, block)
-    unsort = (iota(shape, 0) == iota(shape, 1) % each * parts + iota(shape, 1) // each).astype(BF16)
-    for i in range(slabs.shape[0] // block):
-        span = pl.ds(i * each, each)
-        summed = (own[span, :].astype(F32) + partner[span, :].astype(F32)).astype(BF16)
+    slab_row, sorted_row = iota(shape, 1), iota(shape, 0)
+    sort = (slab_row == sorted_row % each * parts + sorted_row // each).astype(BF16)
+    for i in range(blocks):
+        sorted_rows = dot(sort, arrived[pl.ds(i * block, block), :]).astype(BF16)
+        rows[pl.ds(i * each, each), :] = jnp.concatenate(
+            [sorted_rows[p * each : (p + 1) * each] for p in range(parts)], axis=1
+        )
+    states = rows[...]
+    first = True
+    for gate_up, down in ((own_up, own_down), (other_up.at[0], other_down.at[0])):
+        for start, size in unit_chunks(down.shape[0]):
+            span = pl.ds(start, size)
+            gate = dot(states, gate_up[0, span, :], NT)
+            up = dot(states, gate_up[1, span, :], NT)
+            activated = (gate / (1.0 + jnp.exp(-gate)) * up).astype(BF16)
+            term = dot(activated, down[span, :])
+            total[...] = term if first else total[...] + term
+            first = False
+    slab_row, sorted_row = iota(shape, 0), iota(shape, 1)
+    unsort = (slab_row == sorted_row % each * parts + sorted_row // each).astype(BF16)
+    for i in range(blocks):
+        summed = total[pl.ds(i * each, each), :].astype(BF16)
         stacked = jnp.concatenate([summed[:, p * piece : (p + 1) * piece] for p in range(parts)], axis=0)
         slabs[pl.ds(i * block, block), :] = dot(unsort, stacked).astype(BF16)
 
@@ -288,6 +276,11 @@
     piece = width // parts
     slab_rows = experts * SLAB
 
+    same_part = [list(range(part, req_count, copies)) for part in range(copies)]
+    swap = [(index, index ^ 1) for index in range(req_count)]
+    other_up = lax.ppermute(expert_gate_up, "req", swap)
+    other_down = lax.ppermute(expert_down, "req", swap)
+
     attend_scratch = [
         pltpu.VMEM(out_weight.shape, BF16),
         pltpu.VMEM((heads * requests, head_dim), F32),
@@ -310,7 +303,7 @@
         like((slab_rows, piece)),
         like((requests, slab_rows), F32),
     ]
-    attend_params = pltpu.CompilerParams(vmem_limit_bytes=32 * MIB)
+    attend_params = pltpu.CompilerParams(vmem_limit_bytes=20 * MIB)
     if kv_count == 1:
         keys, values, mixed, norms, top, slabs, comb = pl.pallas_call(
             functools.partial(attend_route_kernel, capacity),
@@ -345,12 +338,9 @@
         in_specs=vmem(2) + in_hbm(2),
         out_specs=in_hbm(1) + vmem(2),
         scratch_shapes=[pltpu.SemaphoreType.DMA((4,))],
-        compiler_params=pltpu.CompilerParams(vmem_limit_bytes=24 * MIB),
+        compiler_params=pltpu.CompilerParams(vmem_limit_bytes=4 * MIB),
         cost_estimate=pl.CostEstimate(flops=0, bytes_accessed=4 * stored, transcendentals=0),
     )(keys, values, *pinned(expert_gate_up, expert_down))
-
-    same_part = [list(range(part, req_count, copies)) for part in range(copies)]
-    swap = [(index, index ^ 1) for index in range(req_count)]
 
     def exchange(array):
         array = array.reshape(experts, SLAB, piece)
@@ -360,24 +350,15 @@
         return array.reshape(slab_rows, piece)
 
     arrived = exchange(slabs)
-    partner = lax.ppermute(arrived, "req", swap)
     kept = experts * capacity
-    own_terms, partner_terms = pl.pallas_call(
+    leaving = pl.pallas_call(
         functools.partial(expert_kernel, capacity),
-        out_shape=[like((kept, width))] * 2,
-        in_specs=vmem(4),
-        out_specs=vmem(2),
-        scratch_shapes=[pltpu.VMEM((2 * kept, width), BF16), pltpu.VMEM((2 * kept, width), F32)],
-        compiler_params=pltpu.CompilerParams(vmem_limit_bytes=28 * MIB),
-    )(arrived, partner, kept_up, kept_down)
-    swapped = lax.ppermute(partner_terms, "req", swap)
-    leaving = pl.pallas_call(
-        functools.partial(merge_kernel, capacity),
         out_shape=like((slab_rows, piece)),
-        in_specs=vmem(2),
+        in_specs=vmem(5),
         out_specs=pl.BlockSpec(memory_space=pltpu.VMEM),
-        compiler_params=pltpu.CompilerParams(vmem_limit_bytes=8 * MIB),
-    )(own_terms, swapped)
+        scratch_shapes=[pltpu.VMEM((kept, width), BF16), pltpu.VMEM((kept, width), F32)],
+        compiler_params=pltpu.CompilerParams(vmem_limit_bytes=12 * MIB),
+    )(arrived, kept_up, kept_down, other_up, other_down)
     returned = exchange(leaving)
     if kv_count == 1:
         out_hidden = pl.pallas_call(

time: 52.9 us -> 63.4 us (1.20)
  blocking collectives: 18 us -> 0 us
  local copies, waits for them, and re-layouts: 0 us -> 12.9 us
  starting transfers between devices: 4.13 us -> 15.8 us
  Pallas kernels: 18 us -> 24 us
  waiting for transfers between devices: 10.5 us -> 8.3 us
    all_to_all x1 -> x0, blocking collectives: 18 us -> none  [exchange(): lax.all_to_all(array, 'req', split_axis=0, concat_axis=0, tiled=True, axi...]
    unnamed x0 -> x14, local copies, waits for them, and re-layouts: none -> 12.9 us
    all_to_all x1 -> x2, starting transfers between devices: 3.55 us -> 15.2 us  [exchange(): lax.all_to_all(array, 'req', split_axis=0, concat_axis=0, tiled=True, axi...]
    pallas_call x2 -> x1, Pallas kernels: 3.84 us -> 9.8 us  [body(): pl.pallas_call(functools.partial(expert_kernel, capacity), out_shape=like...]
    ppermute x2, waiting for transfers between devices: 1.16 us -> 0.01 us  [the longest x1 0.01 us: body(): other_down = lax.ppermute(expert_down, 'req', swap)]
    all_to_all x1 -> x2, waiting for transfers between devices: 9.36 us -> 8.3 us  [exchange(): lax.all_to_all(array, 'req', split_axis=0, concat_axis=0, tiled=True, axi...]
  transfers between devices with their start and end apart: 3 -> 4, of which waited for: 2 -> 1; matrix products, arithmetic and copies ran while one was open for 2% -> 2% of each run, Pallas kernels for 11% -> 21%
where the time goes in v8:
time: 63.4 us; the launch traced here: 63 us
  Pallas kernels  24 us (38%)
  starting transfers between devices  15.8 us (25%)
  local copies, waits for them, and re-layouts  12.9 us (20%)
  waiting for transfers between devices  8.3 us (13%)
  other arithmetic  1.25 us (2%)
  between operations  0.71 us (1%)
    all_to_all x2, starting transfers between devices, exchange(): lax.all_to_all(array, 'req', split_axis=0, concat_axis=0, tiled=True, axi...  15.2 us
    unnamed x14, local copies, waits for them, and re-layouts  12.9 us
    pallas_call x1, Pallas kernels, body(): pl.pallas_call(functools.partial(expert_kernel, capacity), out_shape=like...  9.8 us
    all_to_all x2, waiting for transfers between devices, exchange(): lax.all_to_all(array, 'req', split_axis=0, concat_axis=0, tiled=True, axi...  8.3 us
    pallas_call x1, Pallas kernels, body(): pl.pallas_call(functools.partial(attend_route_kernel, capacity), out_shap...  7.37 us
    pallas_call x1, Pallas kernels, body(): pl.pallas_call(store_kernel, out_shape=[like(array) for array in (kv_pool...  6.01 us
  transfers between devices with their start and end apart: 4, of which 1 were waited for; matrix products, arithmetic and copies ran while one was open for 2% of the time, Pallas kernels for 21%

profile of v8, /device:TPU:0, one launch (start us, length us, event | category | flops | bytes accessed | tf_op | source)
XLA Modules:
  0.0 63.0 jit_solution(4598871111136886308)
XLA Ops:
  0.6 0.5 collective-permute-start
  1.2 0.1 collective-permute-start.1
  1.2 7.4 %shard_map.147 = (bf16[104,32,4,128]{3,2,1,0:T(4,128)(2,1)S(1)}, bf16[104,32,4,128]{3,2,1,0:T(4,128)(2,1)S(1)}, bf16[8,2048]{1,0:T(8,128)(2,1)S(1)}, f32[8,1]{1,...) custom-call(s32[8,20]{1,0:T(8,128)} %refs_0_.1, s32[8]{0:T(128)} %refs_1_.1, ...), custom_call_target="tpu_custom_call" | custom-call | tf_op jit(solution)/shard_map/pallas_call | solution.py:308
  8.6 0.0 copy-start.2
  8.6 1.7 %copy-done.2 = bf16[104,32,4,128]{3,2,1,0:T(4,128)(2,1)} copy-done((bf16[104,32,4,128]{3,2,1,0:T(4,128)(2,1)}, bf16[104,32,4,128]{3,2,1,0:T(4,128)(2,1)S(1)}, u32[]{:S(2)}) %copy-start.2) | copy-done | bytes 3407896
  10.4 0.0 copy-start.6
  10.4 0.7 %copy-done.6 = bf16[256,512]{1,0:T(8,128)(2,1)} copy-done((bf16[256,512]{1,0:T(8,128)(2,1)}, bf16[256,512]{1,0:T(8,128)(2,1)S(1)}, u32[]{:S(2)}) %copy-start.6) | copy-done | bytes 262168
  11.1 8.3 %all-to-all-start = ((bf16[16,16,512]{2,1,0:T(8,128)(2,1)}), bf16[16,16,512]{2,1,0:T(8,128)(2,1)}, u32[]{:S(2)}, u32[]{:S(2)}) async-start(bf16[16,16,512]{2,1,0:T(8,128)(2,1)} %bitcast.5), calls=%async_computation | async-start | bytes 524288 | tf_op jit(solution)/shard_map/all_to_all | solution.py:347
  19.4 0.0 copy-start.3
  19.4 2.0 %copy-done.3 = bf16[104,32,4,128]{3,2,1,0:T(4,128)(2,1)S(1)} copy-done((bf16[104,32,4,128]{3,2,1,0:T(4,128)(2,1)S(1)}, bf16[104,32,4,128]{3,2,1,0:T(4,128)(2,1)}, u32[]{:S(2)}) %copy-start.3) | copy-done | bytes 3407896
  21.4 6.0 %shard_map.148 = (bf16[104,32,4,256]{3,2,1,0:T(4,128)(2,1)}, bf16[2,704,2048]{2,1,0:T(8,128)(2,1)S(1)}, bf16[704,2048]{1,0:T(8,128)(2,1)S(1)}) custom-call(bf16[104,32,4,128]{3,2,1,0:T(4,128)(2,1)S(1)} %get-tuple-element.16.keys, bf16[104,32,4,128]{3,2,1,0:T(4,128)(2,1)S(1)} %copy-done.3, bf16[1,2,704,2048]{3,2,1,0:T(8,128)(2,1)} %gate_up.1, ...), custom_call_target="tpu_custom_call" | custom-call | bytes 30932992 | tf_op jit(solution)/shard_map/pallas_call | solution.py:335
  27.4 0.0 copy-start
  27.4 2.5 %copy-done = bf16[2,704,2048]{2,1,0:T(8,128)(2,1)} copy-done((bf16[2,704,2048]{2,1,0:T(8,128)(2,1)}, bf16[2,704,2048]{2,1,0:T(8,128)(2,1)S(1)}, u32[]{:S(2)}) %copy-start) | copy-done | bytes 5767192
  29.9 0.0 copy-start.4
  29.9 1.5 %copy-done.4 = bf16[704,2048]{1,0:T(8,128)(2,1)} copy-done((bf16[704,2048]{1,0:T(8,128)(2,1)}, bf16[704,2048]{1,0:T(8,128)(2,1)S(1)}, u32[]{:S(2)}) %copy-start.4) | copy-done | bytes 2883608
  31.5 0.0 all-to-all-done
  31.5 0.0 collective-permute-done.1.other_down
  31.5 0.0 collective-permute-done.other_up
  31.5 0.0 copy-start.1
  31.5 2.6 %copy-done.1 = bf16[2,704,2048]{2,1,0:T(8,128)(2,1)S(1)} copy-done((bf16[2,704,2048]{2,1,0:T(8,128)(2,1)S(1)}, bf16[2,704,2048]{2,1,0:T(8,128)(2,1)}, u32[]{:S(2)}) %copy-start.1) | copy-done | bytes 5767192
  34.1 0.0 copy-start.5
  34.1 1.8 %copy-done.5 = bf16[704,2048]{1,0:T(8,128)(2,1)S(1)} copy-done((bf16[704,2048]{1,0:T(8,128)(2,1)S(1)}, bf16[704,2048]{1,0:T(8,128)(2,1)}, u32[]{:S(2)}) %copy-start.5) | copy-done | bytes 2883608
  35.9 9.8 %shard_map.149 = bf16[256,512]{1,0:T(8,128)(2,1)} custom-call(bf16[256,512]{1,0:T(8,128)(2,1)} %bitcast.1.arrived, bf16[2,704,2048]{2,1,0:T(8,128)(2,1)S(1)} %copy-done.1, bf16[704,2048]{1,0:T(8,128)(2,1)S(1)} %copy-done.5, bf16[1,2,704,2048]{3,2,1,0:T(8,128)(2,1)} %collective-permute-done.other_up, bf16[1,704,2048]{2,1,0:T(8,128)(2,1)} %collective-permute-done.1.other_down), custom_call_target="tpu_custom_call" | custom-call | tf_op jit(solution)/shard_map/pallas_call | solution.py:354
  45.8 6.9 %all-to-all-start.1 = ((bf16[16,16,512]{2,1,0:T(8,128)(2,1)}), bf16[16,16,512]{2,1,0:T(8,128)(2,1)S(1)}, u32[]{:S(2)}, u32[]{:S(2)}) async-start(bf16[16,16,512]{2,1,0:T(8,128)(2,1)} %bitcast.2), calls=%async_computation.1 | async-start | bytes 524288 | tf_op jit(solution)/shard_map/all_to_all | solution.py:347
  52.6 0.6 reduce
  53.3 0.6 reduce.1
  53.9 8.3 %all-to-all-done.1 = bf16[16,16,512]{2,1,0:T(8,128)(2,1)S(1)} async-done(((bf16[16,16,512]{2,1,0:T(8,128)(2,1)}), bf16[16,16,512]{2,1,0:T(8,128)(2,1)S(1)}, u32[]{:S(2)}, u32[]{:S(2)}) %all-to-all-start.1) | async-done | bytes 262176 | tf_op jit(solution)/shard_map/all_to_all | solution.py:347
  62.2 0.8 %shard_map.150 = bf16[8,2048]{1,0:T(8,128)(2,1)} custom-call(f32[8,256]{1,0:T(8,128)S(1)} %get-tuple-element.14.comb, bf16[256,512]{1,0:T(8,128)(2,1)S(1)} %bitcast.4, bf16[8,2048]{1,0:T(8,128)(2,1)S(1)} %get-tuple-element.20.mixed), custom_call_target="tpu_custom_call" | custom-call | tf_op jit(solution)/shard_map/pallas_call | solution.py:364
Async XLA Ops:
  0.6 30.9 %collective-permute-start = (bf16[1,2,704,2048]{3,2,1,0:T(8,128)(2,1)}, bf16[1,2,704,2048]{3,2,1,0:T(8,128)(2,1)}, u32[]{:S(2)}, u32[]{:S(2)}) collective-permute-start(bf16[1,2,704,2048]{3,2,1,0:T(8,128)(2,1)} %gate_up.1), channel_id=1, source_target_pairs={{0,1},{1,0},{2,3},{3,2},{4,5},{5,4},{6,7},{7,6},{8,9},{9,8},{10,11... | collective-permute-start | bytes 17301512 | tf_op jit(solution)/shard_map/ppermute | solution.py:281
  1.2 30.3 %collective-permute-start.1 = (bf16[1,704,2048]{2,1,0:T(8,128)(2,1)}, bf16[1,704,2048]{2,1,0:T(8,128)(2,1)}, u32[]{:S(2)}, u32[]{:S(2)}) collective-permute-start(bf16[1,704,2048]{2,1,0:T(8,128)(2,1)} %down.1), channel_id=1, source_target_pairs={{0,1},{1,0},{2,3},{3,2},{4,5},{5,4},{6,7},{7,6},{8,9},{9,8},{10,11... | collective-permute-start | bytes 8650760 | tf_op jit(solution)/shard_map/ppermute | solution.py:282
  8.6 1.8 %copy-start.2 = (bf16[104,32,4,128]{3,2,1,0:T(4,128)(2,1)}, bf16[104,32,4,128]{3,2,1,0:T(4,128)(2,1)S(1)}, u32[]{:S(2)}) copy-start(bf16[104,32,4,128]{3,2,1,0:T(4,128)(2,1)S(1)} %get-tuple-element.17.values) | copy-start | bytes 10223620
  10.4 0.7 %copy-start.6 = (bf16[256,512]{1,0:T(8,128)(2,1)}, bf16[256,512]{1,0:T(8,128)(2,1)S(1)}, u32[]{:S(2)}) copy-start(bf16[256,512]{1,0:T(8,128)(2,1)S(1)} %get-tuple-element.15) | copy-start | bytes 786436
  11.1 20.4 %all-to-all-start = ((bf16[16,16,512]{2,1,0:T(8,128)(2,1)}), bf16[16,16,512]{2,1,0:T(8,128)(2,1)}, u32[]{:S(2)}, u32[]{:S(2)}) async-start(bf16[16,16,512]{2,1,0:T(8,128)(2,1)} %bitcast.5), calls=%async_computation | async-start | bytes 524288 | tf_op jit(solution)/shard_map/all_to_all | solution.py:347
  19.4 2.0 %copy-start.3 = (bf16[104,32,4,128]{3,2,1,0:T(4,128)(2,1)S(1)}, bf16[104,32,4,128]{3,2,1,0:T(4,128)(2,1)}, u32[]{:S(2)}) copy-start(bf16[104,32,4,128]{3,2,1,0:T(4,128)(2,1)} %copy-done.2) | copy-start | bytes 10223620
  27.4 2.5 %copy-start = (bf16[2,704,2048]{2,1,0:T(8,128)(2,1)}, bf16[2,704,2048]{2,1,0:T(8,128)(2,1)S(1)}, u32[]{:S(2)}) copy-start(bf16[2,704,2048]{2,1,0:T(8,128)(2,1)S(1)} %get-tuple-element.18.own_up) | copy-start | bytes 17301508
  29.9 1.5 %copy-start.4 = (bf16[704,2048]{1,0:T(8,128)(2,1)}, bf16[704,2048]{1,0:T(8,128)(2,1)S(1)}, u32[]{:S(2)}) copy-start(bf16[704,2048]{1,0:T(8,128)(2,1)S(1)} %get-tuple-element.19.own_down) | copy-start | bytes 8650756
  31.5 2.6 %copy-start.1 = (bf16[2,704,2048]{2,1,0:T(8,128)(2,1)S(1)}, bf16[2,704,2048]{2,1,0:T(8,128)(2,1)}, u32[]{:S(2)}) copy-start(bf16[2,704,2048]{2,1,0:T(8,128)(2,1)} %copy-done) | copy-start | bytes 17301508
  34.1 1.8 %copy-start.5 = (bf16[704,2048]{1,0:T(8,128)(2,1)S(1)}, bf16[704,2048]{1,0:T(8,128)(2,1)}, u32[]{:S(2)}) copy-start(bf16[704,2048]{1,0:T(8,128)(2,1)} %copy-done.4) | copy-start | bytes 8650756
  45.8 16.4 %all-to-all-start.1 = ((bf16[16,16,512]{2,1,0:T(8,128)(2,1)}), bf16[16,16,512]{2,1,0:T(8,128)(2,1)S(1)}, u32[]{:S(2)}, u32[]{:S(2)}) async-start(bf16[16,16,512]{2,1,0:T(8,128)(2,1)} %bitcast.2), calls=%async_computation.1 | async-start | bytes 524288 | tf_op jit(solution)/shard_map/all_to_all | solution.py:347

commit v9 on v8

--- a/solution.py
+++ b/solution.py
@@ -89,7 +89,7 @@
     return projected
 
 
-def route(projected, hidden, gain, router, ids, mixed_ref, norms_ref, top_ref, slabs_ref, comb_ref, capacity):
+def route(projected, hidden, gain, router, ids, mixed_ref, norms_ref, top_ref, slabs_ref, comb_ref, capacity, leave=None):
     requests, width = hidden.shape
     experts = router.shape[0]
     parts = SLAB // capacity
@@ -122,6 +122,8 @@
         inner % parts == iota(shape, 1) // requests
     )
     slabs_ref[...] = dot(picks.astype(BF16), stacked.astype(BF16)).astype(BF16)
+    if leave is not None:
+        leave()
     shape = (experts, slab_rows)
     spread = (iota(shape, 1) // SLAB == iota(shape, 0)).astype(F32)
     inner = iota((requests, slab_rows), 1) % SLAB
@@ -133,31 +135,36 @@
 
 
 def attend_route_kernel(capacity, *refs):
-    inputs, (keys, values, mixed, norms, top, slabs, comb) = refs[:10], refs[10:17]
-    small, scratch = refs[17:25], refs[25:]
-    projected = attend(inputs, keys, values, (small, scratch))
+    inputs, (mixed, norms, top, slabs, comb) = refs[:10], refs[10:15]
+    small, scratch = refs[15:23], refs[23:]
+    keys, values, kept_slabs = scratch[:3]
+    projected = attend(inputs, keys, values, (small, scratch[3:]))
     hidden, gain, router, ids = small[4:]
-    route(projected, hidden, gain, router, ids, mixed, norms, top, slabs, comb, capacity)
+    leave = pltpu.make_async_copy(kept_slabs, slabs, scratch[-1].at[0])
+    route(projected, hidden, gain, router, ids, mixed, norms, top, kept_slabs, comb, capacity, leave.start)
+    leave.wait()
 
 
 def attend_kernel(*refs):
-    keys, values, projected = refs[6:9]
-    projected[...] = attend(refs[:6], keys, values, (refs[9:13], refs[13:]))
-
-
-def store_kernel(keys, values, gate_up, down, new_pool, kept_up, kept_down, sems):
-    moves = copies(
-        [
-            (gate_up.at[0], kept_up),
-            (down.at[0], kept_down),
-            (keys, pool_half(new_pool, 0)),
-            (values, pool_half(new_pool, 1)),
-        ],
-        sems,
-    )
-    for copy in moves:
+    attended, scratch = refs[6], refs[11:]
+    attended[...] = attend(refs[:6], scratch[0], scratch[1], (refs[7:11], scratch[2:]))
+
+
+def refresh_kernel(table, lengths, fresh, after, pool, new_pool, kept, sems):
+    pages, page_len = kept.shape[:2]
+    step = -(-pages // 4)
+    spans = [pl.ds(start, min(step, pages - start)) for start in range(0, pages, step)]
+    loads = copies([(pool.at[span], kept.at[span]) for span in spans], sems)
+    stores = copies([(kept.at[span], new_pool.at[span]) for span in spans], sems, len(spans))
+    for copy in loads:
         copy.start()
-    for copy in moves:
+    for copy in loads:
+        copy.wait()
+    for r in range(table.shape[0]):
+        kept[table[r, lengths[r] // page_len], lengths[r] % page_len] = fresh[r]
+    for copy in stores:
+        copy.start()
+    for copy in stores:
         copy.wait()
 
 
@@ -169,7 +176,27 @@
     return [(start, min(256, units - start)) for start in range(0, units, 256)]
 
 
-def expert_kernel(capacity, arrived, own_up, own_down, other_up, other_down, slabs, rows, total):
+def expert_kernel(capacity, arrived, own_up, own_down, other_up, other_down, slabs,
+                  slab_rows, kept_up, kept_down, rows, total, sems):
+    units = kept_down.shape[1]
+    arrive = pltpu.make_async_copy(arrived, slab_rows, sems.at[0])
+    arrive.start()
+    chunks = []
+    for half, (gate_up, down) in enumerate(((own_up, own_down), (other_up, other_down))):
+        for start, size in unit_chunks(units):
+            span = pl.ds(start, size)
+            chunks.append((half, span, copies(
+                [
+                    (gate_up.at[0, :, span, :], kept_up.at[half, :, span, :]),
+                    (down.at[0, span, :], kept_down.at[half, span, :]),
+                ],
+                sems,
+                1 + 2 * len(chunks),
+            )))
+    for _, _, loads in chunks:
+        for copy in loads:
+            copy.start()
+    arrive.wait()
     parts = SLAB // capacity
     piece = slabs.shape[1]
     block = 128
@@ -179,21 +206,19 @@
     slab_row, sorted_row = iota(shape, 1), iota(shape, 0)
     sort = (slab_row == sorted_row % each * parts + sorted_row // each).astype(BF16)
     for i in range(blocks):
-        sorted_rows = dot(sort, arrived[pl.ds(i * block, block), :]).astype(BF16)
+        sorted_rows = dot(sort, slab_rows[pl.ds(i * block, block), :]).astype(BF16)
         rows[pl.ds(i * each, each), :] = jnp.concatenate(
             [sorted_rows[p * each : (p + 1) * each] for p in range(parts)], axis=1
         )
     states = rows[...]
-    first = True
-    for gate_up, down in ((own_up, own_down), (other_up.at[0], other_down.at[0])):
-        for start, size in unit_chunks(down.shape[0]):
-            span = pl.ds(start, size)
-            gate = dot(states, gate_up[0, span, :], NT)
-            up = dot(states, gate_up[1, span, :], NT)
-            activated = (gate / (1.0 + jnp.exp(-gate)) * up).astype(BF16)
-            term = dot(activated, down[span, :])
-            total[...] = term if first else total[...] + term
-            first = False
+    for i, (half, span, loads) in enumerate(chunks):
+        for copy in loads:
+            copy.wait()
+        gate = dot(states, kept_up[half, 0, span, :], NT)
+        up = dot(states, kept_up[half, 1, span, :], NT)
+        activated = (gate / (1.0 + jnp.exp(-gate)) * up).astype(BF16)
+        term = dot(activated, kept_down[half, span, :])
+        total[...] = term if i == 0 else total[...] + term
     slab_row, sorted_row = iota(shape, 0), iota(shape, 1)
     unsort = (slab_row == sorted_row % each * parts + sorted_row // each).astype(BF16)
     for i in range(blocks):
@@ -235,6 +260,10 @@
 
 def vmem(count):
     return [pl.BlockSpec(memory_space=pltpu.VMEM)] * count
+
+
+def scalars(count):
+    return [pl.BlockSpec(memory_space=pltpu.SMEM)] * count
 
 
 def in_hbm(count):
@@ -282,6 +311,8 @@
     other_down = lax.ppermute(expert_down, "req", swap)
 
     attend_scratch = [
+        pltpu.VMEM((pages, page_len, heads_kv, head_dim), BF16),
+        pltpu.VMEM((pages, page_len, heads_kv, head_dim), BF16),
         pltpu.VMEM(out_weight.shape, BF16),
         pltpu.VMEM((heads * requests, head_dim), F32),
         pltpu.VMEM((heads * requests, head_dim), F32),
@@ -295,7 +326,6 @@
 
     inputs = [pltpu.SMEM(page_table.shape, jnp.int32), pltpu.SMEM(lengths.shape, jnp.int32)]
     inputs += small(queries, fresh_key_value)
-    kept_shapes = [like((pages, page_len, heads_kv, head_dim))] * 2
     routed_shapes = [
         like((requests, width)),
         like((requests, 1), F32),
@@ -303,23 +333,24 @@
         like((slab_rows, piece)),
         like((requests, slab_rows), F32),
     ]
-    attend_params = pltpu.CompilerParams(vmem_limit_bytes=20 * MIB)
+    attend_params = pltpu.CompilerParams(vmem_limit_bytes=24 * MIB)
     if kv_count == 1:
-        keys, values, mixed, norms, top, slabs, comb = pl.pallas_call(
+        attend_scratch.insert(2, pltpu.VMEM((slab_rows, piece), BF16))
+        mixed, norms, top, slabs, comb = pl.pallas_call(
             functools.partial(attend_route_kernel, capacity),
-            out_shape=kept_shapes + routed_shapes,
+            out_shape=routed_shapes,
             in_specs=in_hbm(10),
-            out_specs=vmem(7),
+            out_specs=vmem(3) + in_hbm(1) + vmem(1),
             scratch_shapes=inputs + small(hidden, norm_gain, router_weight, expert_ids) + attend_scratch,
             compiler_params=attend_params,
         )(*pinned(page_table, lengths, queries, fresh_key_value, hidden, norm_gain, router_weight, expert_ids,
                   kv_pool, out_weight))
     else:
-        keys, values, projected = pl.pallas_call(
+        projected = pl.pallas_call(
             attend_kernel,
-            out_shape=kept_shapes + [like((requests, width), F32)],
+            out_shape=like((requests, width), F32),
             in_specs=in_hbm(6),
-            out_specs=vmem(3),
+            out_specs=pl.BlockSpec(memory_space=pltpu.VMEM),
             scratch_shapes=inputs + attend_scratch,
             compiler_params=attend_params,
         )(*pinned(page_table, lengths, queries, fresh_key_value, kv_pool, out_weight))
@@ -331,16 +362,15 @@
             out_specs=vmem(5),
         )(projected, hidden, norm_gain, router_weight, expert_ids)
 
-    stored = kv_pool.size + expert_gate_up.size + expert_down.size
-    new_pool, kept_up, kept_down = pl.pallas_call(
-        store_kernel,
-        out_shape=[like(array) for array in (kv_pool.shape, expert_gate_up.shape[1:], expert_down.shape[1:])],
-        in_specs=vmem(2) + in_hbm(2),
-        out_specs=in_hbm(1) + vmem(2),
-        scratch_shapes=[pltpu.SemaphoreType.DMA((4,))],
-        compiler_params=pltpu.CompilerParams(vmem_limit_bytes=4 * MIB),
-        cost_estimate=pl.CostEstimate(flops=0, bytes_accessed=4 * stored, transcendentals=0),
-    )(keys, values, *pinned(expert_gate_up, expert_down))
+    new_pool = pl.pallas_call(
+        refresh_kernel,
+        out_shape=like(kv_pool.shape),
+        in_specs=scalars(2) + vmem(1) + in_hbm(2),
+        out_specs=pl.BlockSpec(memory_space=pltpu.HBM),
+        scratch_shapes=[pltpu.VMEM(kv_pool.shape, BF16), pltpu.SemaphoreType.DMA((8,))],
+        compiler_params=pltpu.CompilerParams(vmem_limit_bytes=12 * MIB),
+        cost_estimate=pl.CostEstimate(flops=0, bytes_accessed=8 * kv_pool.size, transcendentals=0),
+    )(page_table, lengths, fresh_key_value, top, *pinned(kv_pool))
 
     def exchange(array):
         array = array.reshape(experts, SLAB, piece)
@@ -351,14 +381,23 @@
 
     arrived = exchange(slabs)
     kept = experts * capacity
+    units = expert_down.shape[1]
+    chunk_count = 2 * len(unit_chunks(units))
     leaving = pl.pallas_call(
         functools.partial(expert_kernel, capacity),
         out_shape=like((slab_rows, piece)),
-        in_specs=vmem(5),
+        in_specs=in_hbm(5),
         out_specs=pl.BlockSpec(memory_space=pltpu.VMEM),
-        scratch_shapes=[pltpu.VMEM((kept, width), BF16), pltpu.VMEM((kept, width), F32)],
-        compiler_params=pltpu.CompilerParams(vmem_limit_bytes=12 * MIB),
-    )(arrived, kept_up, kept_down, other_up, other_down)
+        scratch_shapes=[
+            pltpu.VMEM((slab_rows, piece), BF16),
+            pltpu.VMEM((2, 2, units, width), BF16),
+            pltpu.VMEM((2, units, width), BF16),
+            pltpu.VMEM((kept, width), BF16),
+            pltpu.VMEM((kept, width), F32),
+            pltpu.SemaphoreType.DMA((1 + 2 * chunk_count,)),
+        ],
+        compiler_params=pltpu.CompilerParams(vmem_limit_bytes=28 * MIB),
+    )(arrived, *pinned(expert_gate_up, expert_down), other_up, other_down)
     returned = exchange(leaving)
     if kv_count == 1:
         out_hidden = pl.pallas_call(

time: 63.4 us -> 49.3 us (0.78)
  blocking collectives: 0 us -> 18.2 us
  local copies, waits for them, and re-layouts: 12.9 us -> 0.02 us
  starting transfers between devices: 15.8 us -> 4.16 us
  waiting for transfers between devices: 8.3 us -> 1.53 us
  Pallas kernels: 24 us -> 23.1 us
    all_to_all x0 -> x1, blocking collectives: none -> 18.2 us  [exchange(): lax.all_to_all(array, 'req', split_axis=0, concat_axis=0, tiled=True, axi...]
    unnamed x14 -> x6, local copies, waits for them, and re-layouts: 12.9 us -> 0.02 us
    all_to_all x2 -> x1, starting transfers between devices: 15.2 us -> 3.56 us  [exchange(): lax.all_to_all(array, 'req', split_axis=0, concat_axis=0, tiled=True, axi...]
    all_to_all x2 -> x1, waiting for transfers between devices: 8.3 us -> 1.53 us  [exchange(): lax.all_to_all(array, 'req', split_axis=0, concat_axis=0, tiled=True, axi...]
    pallas_call x1, Pallas kernels: 9.8 us -> 8.22 us  [body(): pl.pallas_call(functools.partial(expert_kernel, capacity), out_shape=like...]
  transfers between devices with their start and end apart: 4 -> 3, of which waited for: 1 -> 1; matrix products, arithmetic and copies ran while one was open for 2% -> 3% of each run, Pallas kernels for 21% -> 29%
where the time goes in v9:
time: 49.3 us; the launch traced here: 48.9 us
  Pallas kernels  23.1 us (47%)
  blocking collectives  18.2 us (37%)
  starting transfers between devices  4.16 us (8%)
  waiting for transfers between devices  1.53 us (3%)
  other arithmetic  1.25 us (3%)
  between operations  0.71 us (1%)
    all_to_all x1, blocking collectives, exchange(): lax.all_to_all(array, 'req', split_axis=0, concat_axis=0, tiled=True, axi...  18.2 us
    pallas_call x1, Pallas kernels, body(): pl.pallas_call(functools.partial(expert_kernel, capacity), out_shape=like...  8.22 us
    pallas_call x1, Pallas kernels, body(): pl.pallas_call(functools.partial(attend_route_kernel, capacity), out_shap...  7.51 us
    pallas_call x1, Pallas kernels, body(): pl.pallas_call(refresh_kernel, out_shape=like(kv_pool.shape), in_specs=sc...  6.54 us
    all_to_all x1, starting transfers between devices, exchange(): lax.all_to_all(array, 'req', split_axis=0, concat_axis=0, tiled=True, axi...  3.56 us
    all_to_all x1, waiting for transfers between devices, exchange(): lax.all_to_all(array, 'req', split_axis=0, concat_axis=0, tiled=True, axi...  1.53 us
    pallas_call x2, other arithmetic, body(): pl.pallas_call(functools.partial(attend_route_kernel, capacity), out_shap...  1.25 us
  transfers between devices with their start and end apart: 3, of which 1 were waited for; matrix products, arithmetic and copies ran while one was open for 3% of the time, Pallas kernels for 29%

profile of v9, /device:TPU:0, one launch (start us, length us, event | category | flops | bytes accessed | tf_op | source)
XLA Modules:
  0.0 48.9 jit_solution(8767364314868847294)
XLA Ops:
  0.6 0.5 %collective-permute-start = (bf16[1,2,704,2048]{3,2,1,0:T(8,128)(2,1)}, bf16[1,2,704,2048]{3,2,1,0:T(8,128)(2,1)S(1)}, u32[]{:S(2)}, u32[]{:S(2)}) collective-permute-start(bf16[1,2,704,2048]{3,2,1,0:T(8,128)(2,1)} %own_up.1), channel_id=1, source_target_pairs={{0,1},{1,0},{2,3},{3,2},{4,5},{5,4},{6,7},{7,6},{8,9},{9,8},{10,11... | collective-permute-start | bytes 17301512 | tf_op jit(solution)/shard_map/ppermute | solution.py:310
  1.2 0.1 collective-permute-start.1
  1.2 7.5 %shard_map.147 = (bf16[8,2048]{1,0:T(8,128)(2,1)S(1)}, f32[8,1]{1,0:T(8,128)S(1)}, f32[8,1]{1,0:T(8,128)S(1)}, bf16[256,512]{1,0:T(8,128)(2,1)S(1)}, f32[8,256]{1,0:T(8,128)S(1)}) custom-call(s32[8,20]{1,0:T(8,128)} %table.1, s32[8]{0:T(128)} %lengths.1, bf16[8,2048]{1,0:T(8,128)(2,1)} %refs_2_.1, bf16[8,4,256]{2,1,0:T(4,128)(2,1)} %fresh.1, ...), custom_call_target="tpu_custom_call" | custom-call | tf_op jit(solution)/shard_map/pallas_call | solution.py:339
  8.8 18.2 %all_to_all.10 = bf16[16,16,512]{2,1,0:T(8,128)(2,1)S(1)} all-to-all(bf16[16,16,512]{2,1,0:T(8,128)(2,1)S(1)} %bitcast.6), channel_id=1, replica_groups={{0,2,4,6,8,10,12,14,16,18,20,22,24,26,28,30},{1,3,5,7,9,11,13,15,17,19,..., dimensions={0} | all-to-all | bytes 524288 | tf_op jit(solution)/shard_map/all_to_all | solution.py:377
  27.0 0.0 collective-permute-done.1.other_down
  27.0 0.0 collective-permute-done.other_up
  27.0 0.0 copy-start
  27.0 0.0 copy-start.1
  27.0 0.0 copy-start.2
  27.0 8.2 %shard_map.148 = bf16[256,512]{1,0:T(8,128)(2,1)} custom-call(bf16[256,512]{1,0:T(8,128)(2,1)S(1)} %bitcast.4, bf16[1,2,704,2048]{3,2,1,0:T(8,128)(2,1)} %own_up.1, bf16[1,704,2048]{2,1,0:T(8,128)(2,1)} %own_down.1, bf16[1,2,704,2048]{3,2,1,0:T(8,128)(2,1)S(1)} %collective-permute-done.other_up, bf16[1,704,2048]{2,1,0:T(8,128)(2,1)S(1)} %collective-permute-done.1.other_down), custom_call_target="tpu_custom_call" | custom-call | tf_op jit(solution)/shard_map/pallas_call | solution.py:386
  35.2 3.6 %all-to-all-start.1 = ((bf16[16,16,512]{2,1,0:T(8,128)(2,1)}), bf16[16,16,512]{2,1,0:T(8,128)(2,1)S(1)}, u32[]{:S(2)}, u32[]{:S(2)}) async-start(bf16[16,16,512]{2,1,0:T(8,128)(2,1)} %bitcast.2), calls=%async_computation.1 | async-start | bytes 524288 | tf_op jit(solution)/shard_map/all_to_all | solution.py:377
  38.8 0.0 copy-done
  38.8 0.0 copy-done.1
  38.8 0.0 copy-done.2
  38.8 6.5 %shard_map.150 = bf16[104,32,4,256]{3,2,1,0:T(4,128)(2,1)} custom-call(s32[8,20]{1,0:T(8,128)S(1)} %copy-done.1, s32[8]{0:T(128)S(1)} %copy-done.2, bf16[8,4,256]{2,1,0:T(4,128)(2,1)S(1)} %copy-done, f32[8,1]{1,0:T(8,128)S(1)} %get-tuple-element.12.after, bf16[104,32,4,256]{3,2,1,0:T(4,128)(2,1)} %pool.1), custom_call_target="tpu_custom_call" | custom-call | bytes 27262976 | tf_op jit(solution)/shard_map/pallas_call | solution.py:365
  45.4 0.6 %reduce.1 = f32[8]{0:T(128)} reduce(f32[8,1]{1,0:T(8,128)S(1)} %get-tuple-element.12.after, f32[]{:T(128)} %constant.9), dimensions={1}, to_apply=%get-tuple-element.12.reduce_sub_computation | reduce | bytes 68 | tf_op jit(solution)/shard_map/pallas_call | solution.py:339
  46.0 0.6 %reduce = f32[8]{0:T(128)} reduce(f32[8,1]{1,0:T(8,128)S(1)} %get-tuple-element.13, f32[]{:T(128)} %constant.9), dimensions={1}, to_apply=%get-tuple-element.13.reduce_sub_computation | reduce | bytes 68 | tf_op jit(solution)/shard_map/pallas_call | solution.py:339
  46.6 1.5 %all-to-all-done.1 = bf16[16,16,512]{2,1,0:T(8,128)(2,1)S(1)} async-done(((bf16[16,16,512]{2,1,0:T(8,128)(2,1)}), bf16[16,16,512]{2,1,0:T(8,128)(2,1)S(1)}, u32[]{:S(2)}, u32[]{:S(2)}) %all-to-all-start.1) | async-done | bytes 262176 | tf_op jit(solution)/shard_map/all_to_all | solution.py:377
  48.1 0.8 %shard_map.149 = bf16[8,2048]{1,0:T(8,128)(2,1)} custom-call(f32[8,256]{1,0:T(8,128)S(1)} %get-tuple-element.9.comb, bf16[256,512]{1,0:T(8,128)(2,1)S(1)} %bitcast.5, bf16[8,2048]{1,0:T(8,128)(2,1)S(1)} %get-tuple-element.11.mixed), custom_call_target="tpu_custom_call" | custom-call | tf_op jit(solution)/shard_map/pallas_call | solution.py:403
Async XLA Ops:
  0.6 26.3 %collective-permute-start = (bf16[1,2,704,2048]{3,2,1,0:T(8,128)(2,1)}, bf16[1,2,704,2048]{3,2,1,0:T(8,128)(2,1)S(1)}, u32[]{:S(2)}, u32[]{:S(2)}) collective-permute-start(bf16[1,2,704,2048]{3,2,1,0:T(8,128)(2,1)} %own_up.1), channel_id=1, source_target_pairs={{0,1},{1,0},{2,3},{3,2},{4,5},{5,4},{6,7},{7,6},{8,9},{9,8},{10,11... | collective-permute-start | bytes 17301512 | tf_op jit(solution)/shard_map/ppermute | solution.py:310
  1.2 25.8 %collective-permute-start.1 = (bf16[1,704,2048]{2,1,0:T(8,128)(2,1)}, bf16[1,704,2048]{2,1,0:T(8,128)(2,1)S(1)}, u32[]{:S(2)}, u32[]{:S(2)}) collective-permute-start(bf16[1,704,2048]{2,1,0:T(8,128)(2,1)} %own_down.1), channel_id=1, source_target_pairs={{0,1},{1,0},{2,3},{3,2},{4,5},{5,4},{6,7},{7,6},{8,9},{9,8},{10,11... | collective-permute-start | bytes 8650760 | tf_op jit(solution)/shard_map/ppermute | solution.py:311
  27.0 11.8 %copy-start = (bf16[8,4,256]{2,1,0:T(4,128)(2,1)S(1)}, bf16[8,4,256]{2,1,0:T(4,128)(2,1)}, u32[]{:S(2)}) copy-start(bf16[8,4,256]{2,1,0:T(4,128)(2,1)} %fresh.1) | copy-start | bytes 49156
  27.0 11.8 %copy-start.1 = (s32[8,20]{1,0:T(8,128)S(1)}, s32[8,20]{1,0:T(8,128)}, u32[]{:S(2)}) copy-start(s32[8,20]{1,0:T(8,128)} %table.1) | copy-start | bytes 1924
  27.0 11.8 %copy-start.2 = (s32[8]{0:T(128)S(1)}, s32[8]{0:T(128)}, u32[]{:S(2)}) copy-start(s32[8]{0:T(128)} %lengths.1) | copy-start | bytes 100
  35.2 12.9 %all-to-all-start.1 = ((bf16[16,16,512]{2,1,0:T(8,128)(2,1)}), bf16[16,16,512]{2,1,0:T(8,128)(2,1)S(1)}, u32[]{:S(2)}, u32[]{:S(2)}) async-start(bf16[16,16,512]{2,1,0:T(8,128)(2,1)} %bitcast.2), calls=%async_computation.1 | async-start | bytes 524288 | tf_op jit(solution)/shard_map/all_to_all | solution.py:377

commit v10 on v9

--- a/solution.py
+++ b/solution.py
@@ -178,22 +178,18 @@
 
 def expert_kernel(capacity, arrived, own_up, own_down, other_up, other_down, slabs,
                   slab_rows, kept_up, kept_down, rows, total, sems):
-    units = kept_down.shape[1]
+    units = kept_down.shape[0]
     arrive = pltpu.make_async_copy(arrived, slab_rows, sems.at[0])
     arrive.start()
     chunks = []
-    for half, (gate_up, down) in enumerate(((own_up, own_down), (other_up, other_down))):
-        for start, size in unit_chunks(units):
-            span = pl.ds(start, size)
-            chunks.append((half, span, copies(
-                [
-                    (gate_up.at[0, :, span, :], kept_up.at[half, :, span, :]),
-                    (down.at[0, span, :], kept_down.at[half, span, :]),
-                ],
-                sems,
-                1 + 2 * len(chunks),
-            )))
-    for _, _, loads in chunks:
+    for i, (start, size) in enumerate(unit_chunks(units)):
+        span = pl.ds(start, size)
+        chunks.append((span, copies(
+            [(own_up.at[0, :, span, :], kept_up.at[:, span, :]), (own_down.at[0, span, :], kept_down.at[span, :])],
+            sems,
+            1 + 2 * i,
+        )))
+    for _, loads in chunks:
         for copy in loads:
             copy.start()
     arrive.wait()
@@ -211,13 +207,15 @@
             [sorted_rows[p * each : (p + 1) * each] for p in range(parts)], axis=1
         )
     states = rows[...]
-    for i, (half, span, loads) in enumerate(chunks):
+    steps = [(other_up.at[0], other_down.at[0], span, []) for span, _ in chunks]
+    steps += [(kept_up, kept_down, span, loads) for span, loads in chunks]
+    for i, (gate_up, down, span, loads) in enumerate(steps):
         for copy in loads:
             copy.wait()
-        gate = dot(states, kept_up[half, 0, span, :], NT)
-        up = dot(states, kept_up[half, 1, span, :], NT)
+        gate = dot(states, gate_up[0, span, :], NT)
+        up = dot(states, gate_up[1, span, :], NT)
         activated = (gate / (1.0 + jnp.exp(-gate)) * up).astype(BF16)
-        term = dot(activated, kept_down[half, span, :])
+        term = dot(activated, down[span, :])
         total[...] = term if i == 0 else total[...] + term
     slab_row, sorted_row = iota(shape, 0), iota(shape, 1)
     unsort = (slab_row == sorted_row % each * parts + sorted_row // each).astype(BF16)
@@ -382,21 +380,20 @@
     arrived = exchange(slabs)
     kept = experts * capacity
     units = expert_down.shape[1]
-    chunk_count = 2 * len(unit_chunks(units))
     leaving = pl.pallas_call(
         functools.partial(expert_kernel, capacity),
         out_shape=like((slab_rows, piece)),
-        in_specs=in_hbm(5),
+        in_specs=in_hbm(3) + vmem(2),
         out_specs=pl.BlockSpec(memory_space=pltpu.VMEM),
         scratch_shapes=[
             pltpu.VMEM((slab_rows, piece), BF16),
-            pltpu.VMEM((2, 2, units, width), BF16),
             pltpu.VMEM((2, units, width), BF16),
+            pltpu.VMEM((units, width), BF16),
             pltpu.VMEM((kept, width), BF16),
             pltpu.VMEM((kept, width), F32),
-            pltpu.SemaphoreType.DMA((1 + 2 * chunk_count,)),
+            pltpu.SemaphoreType.DMA((1 + 2 * len(unit_chunks(units)),)),
         ],
-        compiler_params=pltpu.CompilerParams(vmem_limit_bytes=28 * MIB),
+        compiler_params=pltpu.CompilerParams(vmem_limit_bytes=20 * MIB),
     )(arrived, *pinned(expert_gate_up, expert_down), other_up, other_down)
     returned = exchange(leaving)
     if kv_count == 1:

time: 49.3 us -> 47.4 us (0.961)
  Pallas kernels: 23.1 us -> 21.2 us
    pallas_call x1, Pallas kernels: 8.22 us -> 6.37 us  [body(): pl.pallas_call(functools.partial(expert_kernel, capacity), out_shape=like...]
  transfers between devices with their start and end apart: 3 -> 3, of which waited for: 1 -> 1; matrix products, arithmetic and copies ran while one was open for 3% -> 3% of each run, Pallas kernels for 29% -> 30%
where the time goes in v10:
time: 47.4 us; the launch traced here: 47.1 us
  Pallas kernels  21.2 us (45%)
  blocking collectives  18.2 us (38%)
  starting transfers between devices  4.16 us (9%)
  waiting for transfers between devices  1.54 us (3%)
  other arithmetic  1.25 us (3%)
  between operations  0.71 us (1%)
    all_to_all x1, blocking collectives, exchange(): lax.all_to_all(array, 'req', split_axis=0, concat_axis=0, tiled=True, axi...  18.2 us
    pallas_call x1, Pallas kernels, body(): pl.pallas_call(functools.partial(attend_route_kernel, capacity), out_shap...  7.51 us
    pallas_call x1, Pallas kernels, body(): pl.pallas_call(refresh_kernel, out_shape=like(kv_pool.shape), in_specs=sc...  6.54 us
    pallas_call x1, Pallas kernels, body(): pl.pallas_call(functools.partial(expert_kernel, capacity), out_shape=like...  6.37 us
    all_to_all x1, starting transfers between devices, exchange(): lax.all_to_all(array, 'req', split_axis=0, concat_axis=0, tiled=True, axi...  3.56 us
    all_to_all x1, waiting for transfers between devices, exchange(): lax.all_to_all(array, 'req', split_axis=0, concat_axis=0, tiled=True, axi...  1.53 us
    pallas_call x2, other arithmetic, body(): pl.pallas_call(functools.partial(attend_route_kernel, capacity), out_shap...  1.25 us
  transfers between devices with their start and end apart: 3, of which 1 were waited for; matrix products, arithmetic and copies ran while one was open for 3% of the time, Pallas kernels for 30%

profile of v10, /device:TPU:0, one launch (start us, length us, event | category | flops | bytes accessed | tf_op | source)
XLA Modules:
  0.0 47.1 jit_solution(5615817940062378490)
XLA Ops:
  0.6 0.5 %collective-permute-start = (bf16[1,2,704,2048]{3,2,1,0:T(8,128)(2,1)}, bf16[1,2,704,2048]{3,2,1,0:T(8,128)(2,1)S(1)}, u32[]{:S(2)}, u32[]{:S(2)}) collective-permute-start(bf16[1,2,704,2048]{3,2,1,0:T(8,128)(2,1)} %own_up.1), channel_id=1, source_target_pairs={{0,1},{1,0},{2,3},{3,2},{4,5},{5,4},{6,7},{7,6},{8,9},{9,8},{10,11... | collective-permute-start | bytes 17301512 | tf_op jit(solution)/shard_map/ppermute | solution.py:308
  1.2 0.1 collective-permute-start.1
  1.2 7.5 %shard_map.147 = (bf16[8,2048]{1,0:T(8,128)(2,1)S(1)}, f32[8,1]{1,0:T(8,128)S(1)}, f32[8,1]{1,0:T(8,128)S(1)}, bf16[256,512]{1,0:T(8,128)(2,1)S(1)}, f32[8,256]{1,0:T(8,128)S(1)}) custom-call(s32[8,20]{1,0:T(8,128)} %table.1, s32[8]{0:T(128)} %lengths.1, bf16[8,2048]{1,0:T(8,128)(2,1)} %refs_2_.1, bf16[8,4,256]{2,1,0:T(4,128)(2,1)} %fresh.1, ...), custom_call_target="tpu_custom_call" | custom-call | tf_op jit(solution)/shard_map/pallas_call | solution.py:337
  8.8 18.2 %all_to_all.10 = bf16[16,16,512]{2,1,0:T(8,128)(2,1)S(1)} all-to-all(bf16[16,16,512]{2,1,0:T(8,128)(2,1)S(1)} %bitcast.6), channel_id=1, replica_groups={{0,2,4,6,8,10,12,14,16,18,20,22,24,26,28,30},{1,3,5,7,9,11,13,15,17,19,..., dimensions={0} | all-to-all | bytes 524288 | tf_op jit(solution)/shard_map/all_to_all | solution.py:375
  27.0 0.0 collective-permute-done.1.other_down
  27.0 0.0 collective-permute-done.other_up
  27.0 0.0 copy-start
  27.0 0.0 copy-start.1
  27.0 0.0 copy-start.2
  27.0 6.4 %shard_map.148 = bf16[256,512]{1,0:T(8,128)(2,1)} custom-call(bf16[256,512]{1,0:T(8,128)(2,1)S(1)} %bitcast.4, bf16[1,2,704,2048]{3,2,1,0:T(8,128)(2,1)} %own_up.1, bf16[1,704,2048]{2,1,0:T(8,128)(2,1)} %own_down.1, bf16[1,2,704,2048]{3,2,1,0:T(8,128)(2,1)S(1)} %collective-permute-done.other_up, bf16[1,704,2048]{2,1,0:T(8,128)(2,1)S(1)} %collective-permute-done.1.other_down), custom_call_target="tpu_custom_call" | custom-call | tf_op jit(solution)/shard_map/pallas_call | solution.py:383
  33.4 3.6 %all-to-all-start.1 = ((bf16[16,16,512]{2,1,0:T(8,128)(2,1)}), bf16[16,16,512]{2,1,0:T(8,128)(2,1)S(1)}, u32[]{:S(2)}, u32[]{:S(2)}) async-start(bf16[16,16,512]{2,1,0:T(8,128)(2,1)} %bitcast.2), calls=%async_computation.1 | async-start | bytes 524288 | tf_op jit(solution)/shard_map/all_to_all | solution.py:375
  36.9 0.0 copy-done
  36.9 0.0 copy-done.1
  37.0 0.0 copy-done.2
  37.0 6.5 %shard_map.150 = bf16[104,32,4,256]{3,2,1,0:T(4,128)(2,1)} custom-call(s32[8,20]{1,0:T(8,128)S(1)} %copy-done.1, s32[8]{0:T(128)S(1)} %copy-done.2, bf16[8,4,256]{2,1,0:T(4,128)(2,1)S(1)} %copy-done, f32[8,1]{1,0:T(8,128)S(1)} %get-tuple-element.12.after, bf16[104,32,4,256]{3,2,1,0:T(4,128)(2,1)} %pool.1), custom_call_target="tpu_custom_call" | custom-call | bytes 27262976 | tf_op jit(solution)/shard_map/pallas_call | solution.py:363
  43.5 0.6 %reduce.1 = f32[8]{0:T(128)} reduce(f32[8,1]{1,0:T(8,128)S(1)} %get-tuple-element.12.after, f32[]{:T(128)} %constant.9), dimensions={1}, to_apply=%get-tuple-element.12.reduce_sub_computation | reduce | bytes 68 | tf_op jit(solution)/shard_map/pallas_call | solution.py:337
  44.1 0.6 %reduce = f32[8]{0:T(128)} reduce(f32[8,1]{1,0:T(8,128)S(1)} %get-tuple-element.13, f32[]{:T(128)} %constant.9), dimensions={1}, to_apply=%get-tuple-element.13.reduce_sub_computation | reduce | bytes 68 | tf_op jit(solution)/shard_map/pallas_call | solution.py:337
  44.8 1.5 %all-to-all-done.1 = bf16[16,16,512]{2,1,0:T(8,128)(2,1)S(1)} async-done(((bf16[16,16,512]{2,1,0:T(8,128)(2,1)}), bf16[16,16,512]{2,1,0:T(8,128)(2,1)S(1)}, u32[]{:S(2)}, u32[]{:S(2)}) %all-to-all-start.1) | async-done | bytes 262176 | tf_op jit(solution)/shard_map/all_to_all | solution.py:375
  46.3 0.8 %shard_map.149 = bf16[8,2048]{1,0:T(8,128)(2,1)} custom-call(f32[8,256]{1,0:T(8,128)S(1)} %get-tuple-element.9.comb, bf16[256,512]{1,0:T(8,128)(2,1)S(1)} %bitcast.5, bf16[8,2048]{1,0:T(8,128)(2,1)S(1)} %get-tuple-element.11.mixed), custom_call_target="tpu_custom_call" | custom-call | tf_op jit(solution)/shard_map/pallas_call | solution.py:400
Async XLA Ops:
  0.6 26.3 %collective-permute-start = (bf16[1,2,704,2048]{3,2,1,0:T(8,128)(2,1)}, bf16[1,2,704,2048]{3,2,1,0:T(8,128)(2,1)S(1)}, u32[]{:S(2)}, u32[]{:S(2)}) collective-permute-start(bf16[1,2,704,2048]{3,2,1,0:T(8,128)(2,1)} %own_up.1), channel_id=1, source_target_pairs={{0,1},{1,0},{2,3},{3,2},{4,5},{5,4},{6,7},{7,6},{8,9},{9,8},{10,11... | collective-permute-start | bytes 17301512 | tf_op jit(solution)/shard_map/ppermute | solution.py:308
  1.2 25.8 %collective-permute-start.1 = (bf16[1,704,2048]{2,1,0:T(8,128)(2,1)}, bf16[1,704,2048]{2,1,0:T(8,128)(2,1)S(1)}, u32[]{:S(2)}, u32[]{:S(2)}) collective-permute-start(bf16[1,704,2048]{2,1,0:T(8,128)(2,1)} %own_down.1), channel_id=1, source_target_pairs={{0,1},{1,0},{2,3},{3,2},{4,5},{5,4},{6,7},{7,6},{8,9},{9,8},{10,11... | collective-permute-start | bytes 8650760 | tf_op jit(solution)/shard_map/ppermute | solution.py:309
  27.0 10.0 %copy-start = (bf16[8,4,256]{2,1,0:T(4,128)(2,1)S(1)}, bf16[8,4,256]{2,1,0:T(4,128)(2,1)}, u32[]{:S(2)}) copy-start(bf16[8,4,256]{2,1,0:T(4,128)(2,1)} %fresh.1) | copy-start | bytes 49156
  27.0 10.0 %copy-start.1 = (s32[8,20]{1,0:T(8,128)S(1)}, s32[8,20]{1,0:T(8,128)}, u32[]{:S(2)}) copy-start(s32[8,20]{1,0:T(8,128)} %table.1) | copy-start | bytes 1924
  27.0 10.0 %copy-start.2 = (s32[8]{0:T(128)S(1)}, s32[8]{0:T(128)}, u32[]{:S(2)}) copy-start(s32[8]{0:T(128)} %lengths.1) | copy-start | bytes 100
  33.4 12.9 %all-to-all-start.1 = ((bf16[16,16,512]{2,1,0:T(8,128)(2,1)}), bf16[16,16,512]{2,1,0:T(8,128)(2,1)S(1)}, u32[]{:S(2)}, u32[]{:S(2)}) async-start(bf16[16,16,512]{2,1,0:T(8,128)(2,1)} %bitcast.2), calls=%async_computation.1 | async-start | bytes 524288 | tf_op jit(solution)/shard_map/all_to_all | solution.py:375

commit v11 on v10

--- a/solution.py
+++ b/solution.py
@@ -95,6 +95,12 @@
     parts = SLAB // capacity
     piece = width // parts
     slab_rows = experts * SLAB
+    backwards = lax.axis_index("req") % 2 == 1
+
+    def slab_expert(shape, dim):
+        slab = iota(shape, dim) // SLAB
+        return jnp.where(backwards, experts - 1 - slab, slab)
+
     mixed = (hidden[...].astype(F32) + projected).astype(BF16)
     mixed_ref[...] = mixed
     mixed = mixed.astype(F32)
@@ -117,7 +123,7 @@
     places = jnp.concatenate([place] * parts, axis=0)
     shape = (slab_rows, parts * requests)
     inner = iota(shape, 0) % SLAB
-    spread = (iota((slab_rows, experts), 0) // SLAB == iota((slab_rows, experts), 1)).astype(F32)
+    spread = (slab_expert((slab_rows, experts), 0) == iota((slab_rows, experts), 1)).astype(F32)
     picks = (dot(spread, places, NT) == (inner // parts).astype(F32)) & (
         inner % parts == iota(shape, 1) // requests
     )
@@ -125,7 +131,7 @@
     if leave is not None:
         leave()
     shape = (experts, slab_rows)
-    spread = (iota(shape, 1) // SLAB == iota(shape, 0)).astype(F32)
+    spread = (slab_expert(shape, 1) == iota(shape, 0)).astype(F32)
     inner = iota((requests, slab_rows), 1) % SLAB
     comb_ref[...] = jnp.where(
         dot(place, spread) == (inner // parts).astype(F32),
@@ -177,22 +183,19 @@
 
 
 def expert_kernel(capacity, arrived, own_up, own_down, other_up, other_down, slabs,
-                  slab_rows, kept_up, kept_down, rows, total, sems):
+                  kept_up, kept_down, rows, total, sems):
     units = kept_down.shape[0]
-    arrive = pltpu.make_async_copy(arrived, slab_rows, sems.at[0])
-    arrive.start()
     chunks = []
     for i, (start, size) in enumerate(unit_chunks(units)):
         span = pl.ds(start, size)
         chunks.append((span, copies(
             [(own_up.at[0, :, span, :], kept_up.at[:, span, :]), (own_down.at[0, span, :], kept_down.at[span, :])],
             sems,
-            1 + 2 * i,
+            2 * i,
         )))
     for _, loads in chunks:
         for copy in loads:
             copy.start()
-    arrive.wait()
     parts = SLAB // capacity
     piece = slabs.shape[1]
     block = 128
@@ -202,7 +205,7 @@
     slab_row, sorted_row = iota(shape, 1), iota(shape, 0)
     sort = (slab_row == sorted_row % each * parts + sorted_row // each).astype(BF16)
     for i in range(blocks):
-        sorted_rows = dot(sort, slab_rows[pl.ds(i * block, block), :]).astype(BF16)
+        sorted_rows = dot(sort, arrived[pl.ds(i * block, block), :]).astype(BF16)
         rows[pl.ds(i * each, each), :] = jnp.concatenate(
             [sorted_rows[p * each : (p + 1) * each] for p in range(parts)], axis=1
         )
@@ -303,7 +306,7 @@
     piece = width // parts
     slab_rows = experts * SLAB
 
-    same_part = [list(range(part, req_count, copies)) for part in range(copies)]
+    same_part = [list(range(part, req_count, copies))[:: -1 if part % 2 else 1] for part in range(copies)]
     swap = [(index, index ^ 1) for index in range(req_count)]
     other_up = lax.ppermute(expert_gate_up, "req", swap)
     other_down = lax.ppermute(expert_down, "req", swap)
@@ -383,15 +386,14 @@
     leaving = pl.pallas_call(
         functools.partial(expert_kernel, capacity),
         out_shape=like((slab_rows, piece)),
-        in_specs=in_hbm(3) + vmem(2),
+        in_specs=vmem(1) + in_hbm(2) + vmem(2),
         out_specs=pl.BlockSpec(memory_space=pltpu.VMEM),
         scratch_shapes=[
-            pltpu.VMEM((slab_rows, piece), BF16),
             pltpu.VMEM((2, units, width), BF16),
             pltpu.VMEM((units, width), BF16),
             pltpu.VMEM((kept, width), BF16),
             pltpu.VMEM((kept, width), F32),
-            pltpu.SemaphoreType.DMA((1 + 2 * len(unit_chunks(units)),)),
+            pltpu.SemaphoreType.DMA((2 * len(unit_chunks(units)),)),
         ],
         compiler_params=pltpu.CompilerParams(vmem_limit_bytes=20 * MIB),
     )(arrived, *pinned(expert_gate_up, expert_down), other_up, other_down)

time: 47.4 us -> 48.3 us (1.019)
  starting transfers between devices: 4.16 us -> 6 us
  Pallas kernels: 21.2 us -> 22.8 us
  blocking collectives: 18.2 us -> 16.6 us
  waiting for transfers between devices: 1.54 us -> 0.68 us
    all_to_all x1, starting transfers between devices: 3.56 us -> 5.4 us  [exchange(): lax.all_to_all(array, 'req', split_axis=0, concat_axis=0, tiled=True, axi...]
    all_to_all x1, blocking collectives: 18.2 us -> 16.6 us  [exchange(): lax.all_to_all(array, 'req', split_axis=0, concat_axis=0, tiled=True, axi...]
    pallas_call x1, Pallas kernels: 6.37 us -> 7.9 us  [body(): pl.pallas_call(functools.partial(expert_kernel, capacity), out_shape=like...]
    all_to_all x1, waiting for transfers between devices: 1.53 us -> 0.67 us  [exchange(): lax.all_to_all(array, 'req', split_axis=0, concat_axis=0, tiled=True, axi...]
  transfers between devices with their start and end apart: 3 -> 3, of which waited for: 1 -> 1; matrix products, arithmetic and copies ran while one was open for 3% -> 3% of each run, Pallas kernels for 30% -> 29%
where the time goes in v11:
time: 48.3 us; the launch traced here: 48 us
  Pallas kernels  22.8 us (47%)
  blocking collectives  16.6 us (34%)
  starting transfers between devices  6 us (12%)
  other arithmetic  1.25 us (3%)
  between operations  0.71 us (1%)
  waiting for transfers between devices  0.68 us (1%)
    all_to_all x1, blocking collectives, exchange(): lax.all_to_all(array, 'req', split_axis=0, concat_axis=0, tiled=True, axi...  16.6 us
    pallas_call x1, Pallas kernels, body(): pl.pallas_call(functools.partial(expert_kernel, capacity), out_shape=like...  7.9 us
    pallas_call x1, Pallas kernels, body(): pl.pallas_call(functools.partial(attend_route_kernel, capacity), out_shap...  7.52 us
    pallas_call x1, Pallas kernels, body(): pl.pallas_call(refresh_kernel, out_shape=like(kv_pool.shape), in_specs=sc...  6.54 us
    all_to_all x1, starting transfers between devices, exchange(): lax.all_to_all(array, 'req', split_axis=0, concat_axis=0, tiled=True, axi...  5.4 us
    pallas_call x2, other arithmetic, body(): pl.pallas_call(functools.partial(attend_route_kernel, capacity), out_shap...  1.25 us
  transfers between devices with their start and end apart: 3, of which 1 were waited for; matrix products, arithmetic and copies ran while one was open for 3% of the time, Pallas kernels for 29%

profile of v11, /device:TPU:0, one launch (start us, length us, event | category | flops | bytes accessed | tf_op | source)
XLA Modules:
  0.0 48.0 jit_solution(10116137270432762354)
XLA Ops:
  0.6 0.5 %collective-permute-start = (bf16[1,2,704,2048]{3,2,1,0:T(8,128)(2,1)}, bf16[1,2,704,2048]{3,2,1,0:T(8,128)(2,1)S(1)}, u32[]{:S(2)}, u32[]{:S(2)}) collective-permute-start(bf16[1,2,704,2048]{3,2,1,0:T(8,128)(2,1)} %own_up.1), channel_id=1, source_target_pairs={{0,1},{1,0},{2,3},{3,2},{4,5},{5,4},{6,7},{7,6},{8,9},{9,8},{10,11... | collective-permute-start | bytes 17301512 | tf_op jit(solution)/shard_map/ppermute | solution.py:311
  1.2 0.1 collective-permute-start.1
  1.2 7.5 %shard_map.147 = (bf16[8,2048]{1,0:T(8,128)(2,1)S(1)}, f32[8,1]{1,0:T(8,128)S(1)}, f32[8,1]{1,0:T(8,128)S(1)}, bf16[256,512]{1,0:T(8,128)(2,1)S(1)}, f32[8,256]{1,0:T(8,128)S(1)}) custom-call(s32[8,20]{1,0:T(8,128)} %table.1, s32[8]{0:T(128)} %lengths.1, bf16[8,2048]{1,0:T(8,128)(2,1)} %refs_2_.1, bf16[8,4,256]{2,1,0:T(4,128)(2,1)} %fresh.1, ...), custom_call_target="tpu_custom_call" | custom-call | tf_op jit(solution)/shard_map/pallas_call | solution.py:340
  8.8 16.6 %all_to_all.10 = bf16[16,16,512]{2,1,0:T(8,128)(2,1)S(1)} all-to-all(bf16[16,16,512]{2,1,0:T(8,128)(2,1)S(1)} %bitcast.6), channel_id=1, replica_groups={{0,2,4,6,8,10,12,14,16,18,20,22,24,26,28,30},{31,29,27,25,23,21,19,17,1..., dimensions={0} | all-to-all | bytes 524288 | tf_op jit(solution)/shard_map/all_to_all | solution.py:378
  25.3 0.0 collective-permute-done.1.other_down
  25.4 0.0 collective-permute-done.other_up
  25.4 0.0 copy-start
  25.4 0.0 copy-start.1
  25.4 0.0 copy-start.2
  25.4 7.9 %shard_map.148 = bf16[256,512]{1,0:T(8,128)(2,1)} custom-call(bf16[256,512]{1,0:T(8,128)(2,1)S(1)} %bitcast.4, bf16[1,2,704,2048]{3,2,1,0:T(8,128)(2,1)} %own_up.1, bf16[1,704,2048]{2,1,0:T(8,128)(2,1)} %own_down.1, bf16[1,2,704,2048]{3,2,1,0:T(8,128)(2,1)S(1)} %collective-permute-done.other_up, bf16[1,704,2048]{2,1,0:T(8,128)(2,1)S(1)} %collective-permute-done.1.other_down), custom_call_target="tpu_custom_call" | custom-call | tf_op jit(solution)/shard_map/pallas_call | solution.py:386
  33.3 5.4 %all-to-all-start.1 = ((bf16[16,16,512]{2,1,0:T(8,128)(2,1)}), bf16[16,16,512]{2,1,0:T(8,128)(2,1)S(1)}, u32[]{:S(2)}, u32[]{:S(2)}) async-start(bf16[16,16,512]{2,1,0:T(8,128)(2,1)} %bitcast.2), calls=%async_computation.1 | async-start | bytes 524288 | tf_op jit(solution)/shard_map/all_to_all | solution.py:378
  38.7 0.0 copy-done
  38.7 0.0 copy-done.1
  38.7 0.0 copy-done.2
  38.7 6.5 %shard_map.150 = bf16[104,32,4,256]{3,2,1,0:T(4,128)(2,1)} custom-call(s32[8,20]{1,0:T(8,128)S(1)} %copy-done.1, s32[8]{0:T(128)S(1)} %copy-done.2, bf16[8,4,256]{2,1,0:T(4,128)(2,1)S(1)} %copy-done, f32[8,1]{1,0:T(8,128)S(1)} %get-tuple-element.12.after, bf16[104,32,4,256]{3,2,1,0:T(4,128)(2,1)} %pool.1), custom_call_target="tpu_custom_call" | custom-call | bytes 27262976 | tf_op jit(solution)/shard_map/pallas_call | solution.py:366
  45.3 0.6 %reduce.1 = f32[8]{0:T(128)} reduce(f32[8,1]{1,0:T(8,128)S(1)} %get-tuple-element.12.after, f32[]{:T(128)} %constant.9), dimensions={1}, to_apply=%get-tuple-element.12.reduce_sub_computation | reduce | bytes 68 | tf_op jit(solution)/shard_map/pallas_call | solution.py:340
  45.9 0.6 %reduce = f32[8]{0:T(128)} reduce(f32[8,1]{1,0:T(8,128)S(1)} %get-tuple-element.13, f32[]{:T(128)} %constant.9), dimensions={1}, to_apply=%get-tuple-element.13.reduce_sub_computation | reduce | bytes 68 | tf_op jit(solution)/shard_map/pallas_call | solution.py:340
  46.5 0.7 %all-to-all-done.1 = bf16[16,16,512]{2,1,0:T(8,128)(2,1)S(1)} async-done(((bf16[16,16,512]{2,1,0:T(8,128)(2,1)}), bf16[16,16,512]{2,1,0:T(8,128)(2,1)S(1)}, u32[]{:S(2)}, u32[]{:S(2)}) %all-to-all-start.1) | async-done | bytes 262176 | tf_op jit(solution)/shard_map/all_to_all | solution.py:378
  47.2 0.8 %shard_map.149 = bf16[8,2048]{1,0:T(8,128)(2,1)} custom-call(f32[8,256]{1,0:T(8,128)S(1)} %get-tuple-element.9.comb, bf16[256,512]{1,0:T(8,128)(2,1)S(1)} %bitcast.5, bf16[8,2048]{1,0:T(8,128)(2,1)S(1)} %get-tuple-element.11.mixed), custom_call_target="tpu_custom_call" | custom-call | tf_op jit(solution)/shard_map/pallas_call | solution.py:402
Async XLA Ops:
  0.6 24.7 %collective-permute-start = (bf16[1,2,704,2048]{3,2,1,0:T(8,128)(2,1)}, bf16[1,2,704,2048]{3,2,1,0:T(8,128)(2,1)S(1)}, u32[]{:S(2)}, u32[]{:S(2)}) collective-permute-start(bf16[1,2,704,2048]{3,2,1,0:T(8,128)(2,1)} %own_up.1), channel_id=1, source_target_pairs={{0,1},{1,0},{2,3},{3,2},{4,5},{5,4},{6,7},{7,6},{8,9},{9,8},{10,11... | collective-permute-start | bytes 17301512 | tf_op jit(solution)/shard_map/ppermute | solution.py:311
  1.2 24.2 %collective-permute-start.1 = (bf16[1,704,2048]{2,1,0:T(8,128)(2,1)}, bf16[1,704,2048]{2,1,0:T(8,128)(2,1)S(1)}, u32[]{:S(2)}, u32[]{:S(2)}) collective-permute-start(bf16[1,704,2048]{2,1,0:T(8,128)(2,1)} %own_down.1), channel_id=1, source_target_pairs={{0,1},{1,0},{2,3},{3,2},{4,5},{5,4},{6,7},{7,6},{8,9},{9,8},{10,11... | collective-permute-start | bytes 8650760 | tf_op jit(solution)/shard_map/ppermute | solution.py:312
  25.4 13.3 %copy-start = (bf16[8,4,256]{2,1,0:T(4,128)(2,1)S(1)}, bf16[8,4,256]{2,1,0:T(4,128)(2,1)}, u32[]{:S(2)}) copy-start(bf16[8,4,256]{2,1,0:T(4,128)(2,1)} %fresh.1) | copy-start | bytes 49156
  25.4 13.4 %copy-start.1 = (s32[8,20]{1,0:T(8,128)S(1)}, s32[8,20]{1,0:T(8,128)}, u32[]{:S(2)}) copy-start(s32[8,20]{1,0:T(8,128)} %table.1) | copy-start | bytes 1924
  25.4 13.4 %copy-start.2 = (s32[8]{0:T(128)S(1)}, s32[8]{0:T(128)}, u32[]{:S(2)}) copy-start(s32[8]{0:T(128)} %lengths.1) | copy-start | bytes 100
  33.3 13.9 %all-to-all-start.1 = ((bf16[16,16,512]{2,1,0:T(8,128)(2,1)}), bf16[16,16,512]{2,1,0:T(8,128)(2,1)S(1)}, u32[]{:S(2)}, u32[]{:S(2)}) async-start(bf16[16,16,512]{2,1,0:T(8,128)(2,1)} %bitcast.2), calls=%async_computation.1 | async-start | bytes 524288 | tf_op jit(solution)/shard_map/all_to_all | solution.py:378

commit v12 on v10

--- a/solution.py
+++ b/solution.py
@@ -12,6 +12,7 @@
 F32 = jnp.float32
 NT = (((1,), (1,)), ((), ()))
 NN = (((1,), (0,)), ((), ()))
+SHARED_PAGES = 8
 SLAB = 16
 MIB = 1 << 20
 
@@ -64,10 +65,17 @@
     lane = iota((heads, columns), 1)
     own_head = lane % heads_kv == iota((heads, columns), 0) // group
     position = lane // heads_kv
+    shared_columns = SHARED_PAGES * page_rows
+
+    def pages_of(array, r, first, last):
+        return jnp.concatenate([array[table[r, j]] for j in range(first, last)], axis=0)
+
+    query = [qs[pl.ds(r, heads, stride=requests), :] for r in range(requests)]
+    shared = dot(jnp.concatenate(query, axis=0).astype(BF16), pages_of(key_pages, 0, 0, SHARED_PAGES), NT)
     for r in range(requests):
-        query = qs[pl.ds(r, heads, stride=requests), :].astype(BF16)
-        gathered = jnp.concatenate([key_pages[table[r, j]] for j in range(max_pages)], axis=0)
-        scores = dot(query, gathered, NT) * (1.0 / math.sqrt(head_dim))
+        own = dot(query[r].astype(BF16), pages_of(key_pages, r, SHARED_PAGES, max_pages), NT)
+        scores = jnp.concatenate([shared[r * heads : (r + 1) * heads], own], axis=1)
+        scores = scores * (1.0 / math.sqrt(head_dim))
         scores = jnp.where(own_head & (position <= lengths[r]), scores, -1e30)
         exponent = jnp.exp(scores - jnp.max(scores, axis=1, keepdims=True))
         sums[r] = jnp.broadcast_to(jnp.sum(exponent, axis=1, keepdims=True), (heads, head_dim))
@@ -76,9 +84,13 @@
     value_load.wait()
     for r, (page, slot) in enumerate(spots):
         values[page, slot] = fresh[r][:, head_dim:]
+    shared = dot(
+        probs[:, :, :shared_columns].reshape(requests * heads, shared_columns),
+        pages_of(value_pages, 0, 0, SHARED_PAGES),
+    )
     for r in range(requests):
-        gathered = jnp.concatenate([value_pages[table[r, j]] for j in range(max_pages)], axis=0)
-        att[pl.ds(r, heads, stride=requests), :] = dot(probs[r], gathered) / sums[r]
+        own = dot(probs[r, :, shared_columns:], pages_of(value_pages, r, SHARED_PAGES, max_pages))
+        att[pl.ds(r, heads, stride=requests), :] = (shared[r * heads : (r + 1) * heads] + own) / sums[r]
     attended = jnp.concatenate(
         [att[pl.ds(h * requests, requests), :] for h in range(heads)], axis=1
     ).astype(BF16)
@@ -95,6 +107,12 @@
     parts = SLAB // capacity
     piece = width // parts
     slab_rows = experts * SLAB
+    backwards = lax.axis_index("req") % 2 == 0
+
+    def slab_expert(shape, dim):
+        slab = iota(shape, dim) // SLAB
+        return jnp.where(backwards, experts - 1 - slab, slab)
+
     mixed = (hidden[...].astype(F32) + projected).astype(BF16)
     mixed_ref[...] = mixed
     mixed = mixed.astype(F32)
@@ -117,7 +135,7 @@
     places = jnp.concatenate([place] * parts, axis=0)
     shape = (slab_rows, parts * requests)
     inner = iota(shape, 0) % SLAB
-    spread = (iota((slab_rows, experts), 0) // SLAB == iota((slab_rows, experts), 1)).astype(F32)
+    spread = (slab_expert((slab_rows, experts), 0) == iota((slab_rows, experts), 1)).astype(F32)
     picks = (dot(spread, places, NT) == (inner // parts).astype(F32)) & (
         inner % parts == iota(shape, 1) // requests
     )
@@ -125,7 +143,7 @@
     if leave is not None:
         leave()
     shape = (experts, slab_rows)
-    spread = (iota(shape, 1) // SLAB == iota(shape, 0)).astype(F32)
+    spread = (slab_expert(shape, 1) == iota(shape, 0)).astype(F32)
     inner = iota((requests, slab_rows), 1) % SLAB
     comb_ref[...] = jnp.where(
         dot(place, spread) == (inner // parts).astype(F32),
@@ -303,7 +321,7 @@
     piece = width // parts
     slab_rows = experts * SLAB
 
-    same_part = [list(range(part, req_count, copies)) for part in range(copies)]
+    same_part = [list(range(part, req_count, copies))[:: 1 if part % 2 else -1] for part in range(copies)]
     swap = [(index, index ^ 1) for index in range(req_count)]
     other_up = lax.ppermute(expert_gate_up, "req", swap)
     other_down = lax.ppermute(expert_down, "req", swap)

time: 47.4 us -> 48 us (1.013)
  starting transfers between devices: 4.16 us -> 7.7 us
  waiting for transfers between devices: 1.54 us -> 0.01 us
  blocking collectives: 18.2 us -> 16.8 us
    all_to_all x1, starting transfers between devices: 3.56 us -> 7.1 us  [exchange(): lax.all_to_all(array, 'req', split_axis=0, concat_axis=0, tiled=True, axi...]
    all_to_all x1, waiting for transfers between devices: 1.53 us -> 0.01 us  [exchange(): lax.all_to_all(array, 'req', split_axis=0, concat_axis=0, tiled=True, axi...]
    all_to_all x1, blocking collectives: 18.2 us -> 16.8 us  [exchange(): lax.all_to_all(array, 'req', split_axis=0, concat_axis=0, tiled=True, axi...]
  transfers between devices with their start and end apart: 3 -> 3, of which waited for: 1 -> 0; matrix products, arithmetic and copies ran while one was open for 3% -> 3% of each run, Pallas kernels for 30% -> 30%
where the time goes in v12:
time: 48 us; the launch traced here: 47.6 us
  Pallas kernels  21.2 us (44%)
  blocking collectives  16.8 us (35%)
  starting transfers between devices  7.7 us (16%)
  other arithmetic  1.25 us (3%)
  between operations  0.7 us (1%)
    all_to_all x1, blocking collectives, exchange(): lax.all_to_all(array, 'req', split_axis=0, concat_axis=0, tiled=True, axi...  16.8 us
    pallas_call x1, Pallas kernels, body(): pl.pallas_call(functools.partial(attend_route_kernel, capacity), out_shap...  7.52 us
    all_to_all x1, starting transfers between devices, exchange(): lax.all_to_all(array, 'req', split_axis=0, concat_axis=0, tiled=True, axi...  7.1 us
    pallas_call x1, Pallas kernels, body(): pl.pallas_call(refresh_kernel, out_shape=like(kv_pool.shape), in_specs=sc...  6.54 us
    pallas_call x1, Pallas kernels, body(): pl.pallas_call(functools.partial(expert_kernel, capacity), out_shape=like...  6.37 us
    pallas_call x2, other arithmetic, body(): pl.pallas_call(functools.partial(attend_route_kernel, capacity), out_shap...  1.25 us
  transfers between devices with their start and end apart: 3, of which 0 were waited for; matrix products, arithmetic and copies ran while one was open for 3% of the time, Pallas kernels for 30%

profile of v12, /device:TPU:0, one launch (start us, length us, event | category | flops | bytes accessed | tf_op | source)
XLA Modules:
  0.0 47.6 jit_solution(13163282147571351124)
XLA Ops:
  0.6 0.5 %collective-permute-start = (bf16[1,2,704,2048]{3,2,1,0:T(8,128)(2,1)}, bf16[1,2,704,2048]{3,2,1,0:T(8,128)(2,1)S(1)}, u32[]{:S(2)}, u32[]{:S(2)}) collective-permute-start(bf16[1,2,704,2048]{3,2,1,0:T(8,128)(2,1)} %own_up.1), channel_id=1, source_target_pairs={{0,1},{1,0},{2,3},{3,2},{4,5},{5,4},{6,7},{7,6},{8,9},{9,8},{10,11... | collective-permute-start | bytes 17301512 | tf_op jit(solution)/shard_map/ppermute | solution.py:326
  1.2 0.1 collective-permute-start.1
  1.2 7.5 %shard_map.147 = (bf16[8,2048]{1,0:T(8,128)(2,1)S(1)}, f32[8,1]{1,0:T(8,128)S(1)}, f32[8,1]{1,0:T(8,128)S(1)}, bf16[256,512]{1,0:T(8,128)(2,1)S(1)}, f32[8,256]{1,0:T(8,128)S(1)}) custom-call(s32[8,20]{1,0:T(8,128)} %table.1, s32[8]{0:T(128)} %lengths.1, bf16[8,2048]{1,0:T(8,128)(2,1)} %refs_2_.1, bf16[8,4,256]{2,1,0:T(4,128)(2,1)} %fresh.1, ...), custom_call_target="tpu_custom_call" | custom-call | tf_op jit(solution)/shard_map/pallas_call | solution.py:355
  8.8 16.8 %all_to_all.10 = bf16[16,16,512]{2,1,0:T(8,128)(2,1)S(1)} all-to-all(bf16[16,16,512]{2,1,0:T(8,128)(2,1)S(1)} %bitcast.6), channel_id=1, replica_groups={{30,28,26,24,22,20,18,16,14,12,10,8,6,4,2,0},{1,3,5,7,9,11,13,15,17,19,..., dimensions={0} | all-to-all | bytes 524288 | tf_op jit(solution)/shard_map/all_to_all | solution.py:393
  25.5 0.0 collective-permute-done.1.other_down
  25.5 0.0 collective-permute-done.other_up
  25.5 0.0 copy-start
  25.5 0.0 copy-start.1
  25.5 0.0 copy-start.2
  25.6 6.4 %shard_map.148 = bf16[256,512]{1,0:T(8,128)(2,1)} custom-call(bf16[256,512]{1,0:T(8,128)(2,1)S(1)} %bitcast.4, bf16[1,2,704,2048]{3,2,1,0:T(8,128)(2,1)} %own_up.1, bf16[1,704,2048]{2,1,0:T(8,128)(2,1)} %own_down.1, bf16[1,2,704,2048]{3,2,1,0:T(8,128)(2,1)S(1)} %collective-permute-done.other_up, bf16[1,704,2048]{2,1,0:T(8,128)(2,1)S(1)} %collective-permute-done.1.other_down), custom_call_target="tpu_custom_call" | custom-call | tf_op jit(solution)/shard_map/pallas_call | solution.py:401
  31.9 7.1 %all-to-all-start.1 = ((bf16[16,16,512]{2,1,0:T(8,128)(2,1)}), bf16[16,16,512]{2,1,0:T(8,128)(2,1)S(1)}, u32[]{:S(2)}, u32[]{:S(2)}) async-start(bf16[16,16,512]{2,1,0:T(8,128)(2,1)} %bitcast.2), calls=%async_computation.1 | async-start | bytes 524288 | tf_op jit(solution)/shard_map/all_to_all | solution.py:393
  39.0 0.0 copy-done
  39.0 0.0 copy-done.1
  39.0 0.0 copy-done.2
  39.1 6.5 %shard_map.150 = bf16[104,32,4,256]{3,2,1,0:T(4,128)(2,1)} custom-call(s32[8,20]{1,0:T(8,128)S(1)} %copy-done.1, s32[8]{0:T(128)S(1)} %copy-done.2, bf16[8,4,256]{2,1,0:T(4,128)(2,1)S(1)} %copy-done, f32[8,1]{1,0:T(8,128)S(1)} %get-tuple-element.12.after, bf16[104,32,4,256]{3,2,1,0:T(4,128)(2,1)} %pool.1), custom_call_target="tpu_custom_call" | custom-call | bytes 27262976 | tf_op jit(solution)/shard_map/pallas_call | solution.py:381
  45.6 0.6 %reduce.1 = f32[8]{0:T(128)} reduce(f32[8,1]{1,0:T(8,128)S(1)} %get-tuple-element.12.after, f32[]{:T(128)} %constant.9), dimensions={1}, to_apply=%get-tuple-element.12.reduce_sub_computation | reduce | bytes 68 | tf_op jit(solution)/shard_map/pallas_call | solution.py:355
  46.2 0.6 %reduce = f32[8]{0:T(128)} reduce(f32[8,1]{1,0:T(8,128)S(1)} %get-tuple-element.13, f32[]{:T(128)} %constant.9), dimensions={1}, to_apply=%get-tuple-element.13.reduce_sub_computation | reduce | bytes 68 | tf_op jit(solution)/shard_map/pallas_call | solution.py:355
  46.9 0.0 all-to-all-done.1
  46.9 0.8 %shard_map.149 = bf16[8,2048]{1,0:T(8,128)(2,1)} custom-call(f32[8,256]{1,0:T(8,128)S(1)} %get-tuple-element.9.comb, bf16[256,512]{1,0:T(8,128)(2,1)S(1)} %bitcast.5, bf16[8,2048]{1,0:T(8,128)(2,1)S(1)} %get-tuple-element.11.mixed), custom_call_target="tpu_custom_call" | custom-call | tf_op jit(solution)/shard_map/pallas_call | solution.py:418
Async XLA Ops:
  0.6 24.9 %collective-permute-start = (bf16[1,2,704,2048]{3,2,1,0:T(8,128)(2,1)}, bf16[1,2,704,2048]{3,2,1,0:T(8,128)(2,1)S(1)}, u32[]{:S(2)}, u32[]{:S(2)}) collective-permute-start(bf16[1,2,704,2048]{3,2,1,0:T(8,128)(2,1)} %own_up.1), channel_id=1, source_target_pairs={{0,1},{1,0},{2,3},{3,2},{4,5},{5,4},{6,7},{7,6},{8,9},{9,8},{10,11... | collective-permute-start | bytes 17301512 | tf_op jit(solution)/shard_map/ppermute | solution.py:326
  1.2 24.4 %collective-permute-start.1 = (bf16[1,704,2048]{2,1,0:T(8,128)(2,1)}, bf16[1,704,2048]{2,1,0:T(8,128)(2,1)S(1)}, u32[]{:S(2)}, u32[]{:S(2)}) collective-permute-start(bf16[1,704,2048]{2,1,0:T(8,128)(2,1)} %own_down.1), channel_id=1, source_target_pairs={{0,1},{1,0},{2,3},{3,2},{4,5},{5,4},{6,7},{7,6},{8,9},{9,8},{10,11... | collective-permute-start | bytes 8650760 | tf_op jit(solution)/shard_map/ppermute | solution.py:327
  25.5 13.5 %copy-start = (bf16[8,4,256]{2,1,0:T(4,128)(2,1)S(1)}, bf16[8,4,256]{2,1,0:T(4,128)(2,1)}, u32[]{:S(2)}) copy-start(bf16[8,4,256]{2,1,0:T(4,128)(2,1)} %fresh.1) | copy-start | bytes 49156
  25.5 13.5 %copy-start.1 = (s32[8,20]{1,0:T(8,128)S(1)}, s32[8,20]{1,0:T(8,128)}, u32[]{:S(2)}) copy-start(s32[8,20]{1,0:T(8,128)} %table.1) | copy-start | bytes 1924
  25.5 13.5 %copy-start.2 = (s32[8]{0:T(128)S(1)}, s32[8]{0:T(128)}, u32[]{:S(2)}) copy-start(s32[8]{0:T(128)} %lengths.1) | copy-start | bytes 100
  31.9 14.9 %all-to-all-start.1 = ((bf16[16,16,512]{2,1,0:T(8,128)(2,1)}), bf16[16,16,512]{2,1,0:T(8,128)(2,1)S(1)}, u32[]{:S(2)}, u32[]{:S(2)}) async-start(bf16[16,16,512]{2,1,0:T(8,128)(2,1)} %bitcast.2), calls=%async_computation.1 | async-start | bytes 524288 | tf_op jit(solution)/shard_map/all_to_all | solution.py:393

commit v13 on v10

--- a/solution.py
+++ b/solution.py
@@ -47,10 +47,12 @@
         [(pool_half(pool, 0), keys), (pool_half(pool, 1), values), (weight, kept_weight)], sems, 4
     )
     later = copies(list(zip(refs[4:-2], small[4:])), sems, 7)
-    for copy in loads + [key_load, value_load] + later + [weight_load]:
+    for copy in loads + [key_load]:
         copy.start()
     for copy in loads:
         copy.wait()
+    for copy in [value_load, weight_load] + later:
+        copy.start()
     for h in range(heads):
         qs[pl.ds(h * requests, requests), :] = q_ref[:, pl.ds(h * head_dim, head_dim)].astype(F32)
     spots = [(table[r, lengths[r] // page_len], lengths[r] % page_len) for r in range(requests)]
@@ -89,7 +91,12 @@
     return projected
 
 
-def route(projected, hidden, gain, router, ids, mixed_ref, norms_ref, top_ref, slabs_ref, comb_ref, capacity, leave=None):
+def as_row(column):
+    shape = (column.shape[0],) * 2
+    return jnp.sum(jnp.where(iota(shape, 0) == iota(shape, 1), column, 0.0), axis=0, keepdims=True)
+
+
+def route(projected, hidden, gain, router, ids, mixed_ref, norms_ref, top_ref, slabs_ref, comb_ref, capacity):
     requests, width = hidden.shape
     experts = router.shape[0]
     parts = SLAB // capacity
@@ -99,10 +106,10 @@
     mixed_ref[...] = mixed
     mixed = mixed.astype(F32)
     norms = jnp.sqrt(jnp.mean(mixed * mixed, axis=1, keepdims=True) + 1e-06)
-    norms_ref[...] = norms
+    norms_ref[...] = as_row(norms)
     normed = (mixed / norms * gain[...].astype(F32).reshape(1, width)).astype(BF16)
     logits = dot(normed, router[...], NT)
-    top_ref[...] = jnp.max(logits, axis=1, keepdims=True)
+    top_ref[...] = as_row(jnp.max(logits, axis=1, keepdims=True))
     column = iota((requests, experts), 1)
     named = column < 0
     for k in range(ids.shape[1]):
@@ -122,8 +129,6 @@
         inner % parts == iota(shape, 1) // requests
     )
     slabs_ref[...] = dot(picks.astype(BF16), stacked.astype(BF16)).astype(BF16)
-    if leave is not None:
-        leave()
     shape = (experts, slab_rows)
     spread = (iota(shape, 1) // SLAB == iota(shape, 0)).astype(F32)
     inner = iota((requests, slab_rows), 1) % SLAB
@@ -135,37 +140,16 @@
 
 
 def attend_route_kernel(capacity, *refs):
-    inputs, (mixed, norms, top, slabs, comb) = refs[:10], refs[10:15]
-    small, scratch = refs[15:23], refs[23:]
-    keys, values, kept_slabs = scratch[:3]
-    projected = attend(inputs, keys, values, (small, scratch[3:]))
+    inputs, (keys, values, mixed, norms, top, slabs, comb) = refs[:10], refs[10:17]
+    small, scratch = refs[17:25], refs[25:]
+    projected = attend(inputs, keys, values, (small, scratch))
     hidden, gain, router, ids = small[4:]
-    leave = pltpu.make_async_copy(kept_slabs, slabs, scratch[-1].at[0])
-    route(projected, hidden, gain, router, ids, mixed, norms, top, kept_slabs, comb, capacity, leave.start)
-    leave.wait()
+    route(projected, hidden, gain, router, ids, mixed, norms, top, slabs, comb, capacity)
 
 
 def attend_kernel(*refs):
-    attended, scratch = refs[6], refs[11:]
-    attended[...] = attend(refs[:6], scratch[0], scratch[1], (refs[7:11], scratch[2:]))
-
-
-def refresh_kernel(table, lengths, fresh, after, pool, new_pool, kept, sems):
-    pages, page_len = kept.shape[:2]
-    step = -(-pages // 4)
-    spans = [pl.ds(start, min(step, pages - start)) for start in range(0, pages, step)]
-    loads = copies([(pool.at[span], kept.at[span]) for span in spans], sems)
-    stores = copies([(kept.at[span], new_pool.at[span]) for span in spans], sems, len(spans))
-    for copy in loads:
-        copy.start()
-    for copy in loads:
-        copy.wait()
-    for r in range(table.shape[0]):
-        kept[table[r, lengths[r] // page_len], lengths[r] % page_len] = fresh[r]
-    for copy in stores:
-        copy.start()
-    for copy in stores:
-        copy.wait()
+    keys, values, projected = refs[6:9]
+    projected[...] = attend(refs[:6], keys, values, (refs[9:13], refs[13:]))
 
 
 def route_kernel(capacity, projected, hidden, gain, router, ids, mixed, norms, top, slabs, comb):
@@ -176,7 +160,7 @@
     return [(start, min(256, units - start)) for start in range(0, units, 256)]
 
 
-def expert_kernel(capacity, arrived, own_up, own_down, other_up, other_down, slabs,
+def expert_kernel(capacity, arrived, own_up, own_down, other_up, other_down, keys, values, slabs, new_pool,
                   slab_rows, kept_up, kept_down, rows, total, sems):
     units = kept_down.shape[0]
     arrive = pltpu.make_async_copy(arrived, slab_rows, sems.at[0])
@@ -189,9 +173,11 @@
             sems,
             1 + 2 * i,
         )))
-    for _, loads in chunks:
-        for copy in loads:
-            copy.start()
+    stores = copies(
+        [(keys, pool_half(new_pool, 0)), (values, pool_half(new_pool, 1))], sems, 1 + 2 * len(chunks)
+    )
+    for copy in [copy for _, loads in chunks for copy in loads] + stores:
+        copy.start()
     arrive.wait()
     parts = SLAB // capacity
     piece = slabs.shape[1]
@@ -223,6 +209,8 @@
         summed = total[pl.ds(i * each, each), :].astype(BF16)
         stacked = jnp.concatenate([summed[:, p * piece : (p + 1) * piece] for p in range(parts)], axis=0)
         slabs[pl.ds(i * block, block), :] = dot(unsort, stacked).astype(BF16)
+    for copy in stores:
+        copy.wait()
 
 
 def gather_terms(comb, slabs, capacity):
@@ -258,10 +246,6 @@
 
 def vmem(count):
     return [pl.BlockSpec(memory_space=pltpu.VMEM)] * count
-
-
-def scalars(count):
-    return [pl.BlockSpec(memory_space=pltpu.SMEM)] * count
 
 
 def in_hbm(count):
@@ -309,8 +293,6 @@
     other_down = lax.ppermute(expert_down, "req", swap)
 
     attend_scratch = [
-        pltpu.VMEM((pages, page_len, heads_kv, head_dim), BF16),
-        pltpu.VMEM((pages, page_len, heads_kv, head_dim), BF16),
         pltpu.VMEM(out_weight.shape, BF16),
         pltpu.VMEM((heads * requests, head_dim), F32),
         pltpu.VMEM((heads * requests, head_dim), F32),
@@ -324,31 +306,31 @@
 
     inputs = [pltpu.SMEM(page_table.shape, jnp.int32), pltpu.SMEM(lengths.shape, jnp.int32)]
     inputs += small(queries, fresh_key_value)
+    kept_shapes = [like((pages, page_len, heads_kv, head_dim))] * 2
     routed_shapes = [
         like((requests, width)),
-        like((requests, 1), F32),
-        like((requests, 1), F32),
+        like((1, requests), F32),
+        like((1, requests), F32),
         like((slab_rows, piece)),
         like((requests, slab_rows), F32),
     ]
     attend_params = pltpu.CompilerParams(vmem_limit_bytes=24 * MIB)
     if kv_count == 1:
-        attend_scratch.insert(2, pltpu.VMEM((slab_rows, piece), BF16))
-        mixed, norms, top, slabs, comb = pl.pallas_call(
+        keys, values, mixed, norms, top, slabs, comb = pl.pallas_call(
             functools.partial(attend_route_kernel, capacity),
-            out_shape=routed_shapes,
+            out_shape=kept_shapes + routed_shapes,
             in_specs=in_hbm(10),
-            out_specs=vmem(3) + in_hbm(1) + vmem(1),
+            out_specs=vmem(7),
             scratch_shapes=inputs + small(hidden, norm_gain, router_weight, expert_ids) + attend_scratch,
             compiler_params=attend_params,
         )(*pinned(page_table, lengths, queries, fresh_key_value, hidden, norm_gain, router_weight, expert_ids,
                   kv_pool, out_weight))
     else:
-        projected = pl.pallas_call(
+        keys, values, projected = pl.pallas_call(
             attend_kernel,
-            out_shape=like((requests, width), F32),
+            out_shape=kept_shapes + [like((requests, width), F32)],
             in_specs=in_hbm(6),
-            out_specs=pl.BlockSpec(memory_space=pltpu.VMEM),
+            out_specs=vmem(3),
             scratch_shapes=inputs + attend_scratch,
             compiler_params=attend_params,
         )(*pinned(page_table, lengths, queries, fresh_key_value, kv_pool, out_weight))
@@ -360,16 +342,6 @@
             out_specs=vmem(5),
         )(projected, hidden, norm_gain, router_weight, expert_ids)
 
-    new_pool = pl.pallas_call(
-        refresh_kernel,
-        out_shape=like(kv_pool.shape),
-        in_specs=scalars(2) + vmem(1) + in_hbm(2),
-        out_specs=pl.BlockSpec(memory_space=pltpu.HBM),
-        scratch_shapes=[pltpu.VMEM(kv_pool.shape, BF16), pltpu.SemaphoreType.DMA((8,))],
-        compiler_params=pltpu.CompilerParams(vmem_limit_bytes=12 * MIB),
-        cost_estimate=pl.CostEstimate(flops=0, bytes_accessed=8 * kv_pool.size, transcendentals=0),
-    )(page_table, lengths, fresh_key_value, top, *pinned(kv_pool))
-
     def exchange(array):
         array = array.reshape(experts, SLAB, piece)
         array = lax.all_to_all(
@@ -380,21 +352,21 @@
     arrived = exchange(slabs)
     kept = experts * capacity
     units = expert_down.shape[1]
-    leaving = pl.pallas_call(
+    leaving, new_pool = pl.pallas_call(
         functools.partial(expert_kernel, capacity),
-        out_shape=like((slab_rows, piece)),
-        in_specs=in_hbm(3) + vmem(2),
-        out_specs=pl.BlockSpec(memory_space=pltpu.VMEM),
+        out_shape=[like((slab_rows, piece)), like(kv_pool.shape)],
+        in_specs=in_hbm(3) + vmem(4),
+        out_specs=vmem(1) + in_hbm(1),
         scratch_shapes=[
             pltpu.VMEM((slab_rows, piece), BF16),
             pltpu.VMEM((2, units, width), BF16),
             pltpu.VMEM((units, width), BF16),
             pltpu.VMEM((kept, width), BF16),
             pltpu.VMEM((kept, width), F32),
-            pltpu.SemaphoreType.DMA((1 + 2 * len(unit_chunks(units)),)),
+            pltpu.SemaphoreType.DMA((3 + 2 * len(unit_chunks(units)),)),
         ],
         compiler_params=pltpu.CompilerParams(vmem_limit_bytes=20 * MIB),
-    )(arrived, *pinned(expert_gate_up, expert_down), other_up, other_down)
+    )(arrived, *pinned(expert_gate_up, expert_down), other_up, other_down, keys, values)
     returned = exchange(leaving)
     if kv_count == 1:
         out_hidden = pl.pallas_call(

time: 47.4 us -> 48.3 us (1.019)
  blocking collectives: 18.2 us -> 30.9 us
  Pallas kernels: 21.2 us -> 15.9 us
  starting transfers between devices: 4.16 us -> 0.6 us
  waiting for transfers between devices: 1.54 us -> 0.01 us
  other arithmetic: 1.25 us -> 0 us
    all_to_all x1 -> x2, blocking collectives: 18.2 us -> 30.9 us  [exchange(): lax.all_to_all(array, 'req', split_axis=0, concat_axis=0, tiled=True, axi...]
    pallas_call x2 -> x1, Pallas kernels: 12.9 us -> 7.34 us  [body(): pl.pallas_call(functools.partial(expert_kernel, capacity), out_shape=[lik...]
    all_to_all x1 -> x0, starting transfers between devices: 3.56 us -> none  [exchange(): lax.all_to_all(array, 'req', split_axis=0, concat_axis=0, tiled=True, axi...]
    all_to_all x1 -> x0, waiting for transfers between devices: 1.53 us -> none  [exchange(): lax.all_to_all(array, 'req', split_axis=0, concat_axis=0, tiled=True, axi...]
    pallas_call x2 -> x0, other arithmetic: 1.25 us -> none  [body(): pl.pallas_call(functools.partial(attend_route_kernel, capacity), out_shap...]
  transfers between devices with their start and end apart: 3 -> 2, of which waited for: 1 -> 0; matrix products, arithmetic and copies ran while one was open for 3% -> 0% of each run, Pallas kernels for 30% -> 16%
where the time goes in v13:
time: 48.3 us; the launch traced here: 48.1 us
  blocking collectives  30.9 us (64%)
  Pallas kernels  15.9 us (33%)
  between operations  0.65 us (1%)
  starting transfers between devices  0.6 us (1%)
    all_to_all x2, blocking collectives, exchange(): lax.all_to_all(array, 'req', split_axis=0, concat_axis=0, tiled=True, axi...  30.9 us
    pallas_call x1, Pallas kernels, body(): pl.pallas_call(functools.partial(attend_route_kernel, capacity), out_shap...  7.79 us
    pallas_call x1, Pallas kernels, body(): pl.pallas_call(functools.partial(expert_kernel, capacity), out_shape=[lik...  7.34 us
  transfers between devices with their start and end apart: 2, of which 0 were waited for; matrix products, arithmetic and copies ran while one was open for 0% of the time, Pallas kernels for 16%

profile of v13, /device:TPU:0, one launch (start us, length us, event | category | flops | bytes accessed | tf_op | source)
XLA Modules:
  0.0 48.1 jit_solution(5216465601059928865)
XLA Ops:
  0.6 0.5 %collective-permute-start = (bf16[1,2,704,2048]{3,2,1,0:T(8,128)(2,1)}, bf16[1,2,704,2048]{3,2,1,0:T(8,128)(2,1)S(1)}, u32[]{:S(2)}, u32[]{:S(2)}) collective-permute-start(bf16[1,2,704,2048]{3,2,1,0:T(8,128)(2,1)} %own_up.1), channel_id=1, source_target_pairs={{0,1},{1,0},{2,3},{3,2},{4,5},{5,4},{6,7},{7,6},{8,9},{9,8},{10,11... | collective-permute-start | bytes 17301512 | tf_op jit(solution)/shard_map/ppermute | solution.py:292
  1.2 0.1 collective-permute-start.1
  1.2 7.8 %shard_map.147 = (bf16[104,32,4,128]{3,2,1,0:T(4,128)(2,1)S(1)}, bf16[104,32,4,128]{3,2,1,0:T(4,128)(2,1)S(1)}, bf16[8,2048]{1,0:T(8,128)(2,1)S(1)}, f32[1,8]{1,...) custom-call(s32[8,20]{1,0:T(8,128)} %refs_0_.1, s32[8]{0:T(128)} %refs_1_.1, ...), custom_call_target="tpu_custom_call" | custom-call | tf_op jit(solution)/shard_map/pallas_call | solution.py:319
  9.0 18.2 %all_to_all.10 = bf16[16,16,512]{2,1,0:T(8,128)(2,1)S(1)} all-to-all(bf16[16,16,512]{2,1,0:T(8,128)(2,1)S(1)} %bitcast.8), channel_id=1, replica_groups={{0,2,4,6,8,10,12,14,16,18,20,22,24,26,28,30},{1,3,5,7,9,11,13,15,17,19,..., dimensions={0} | all-to-all | bytes 524288 | tf_op jit(solution)/shard_map/all_to_all | solution.py:347
  27.2 0.0 collective-permute-done.1.other_down
  27.2 0.0 collective-permute-done.other_up
  27.2 7.3 %shard_map.148 = (bf16[256,512]{1,0:T(8,128)(2,1)S(1)}, bf16[104,32,4,256]{3,2,1,0:T(4,128)(2,1)}) custom-call(bf16[256,512]{1,0:T(8,128)(2,1)S(1)} %bitcast.6, bf16[1,2,704,2048]{3,2,1,0:T(8,128)(2,1)} %own_up.1, bf16[1,704,2048]{2,1,0:T(8,128)(2,1)} %own_down.1, bf16[1,2,704,2048]{3,2,1,0:T(8,128)(2,1)S(1)} %collective-permute-done.other_up, ...), custom_call_target="tpu_custom_call" | custom-call | tf_op jit(solution)/shard_map/pallas_call | solution.py:355
  34.6 12.7 %all_to_all.11 = bf16[16,16,512]{2,1,0:T(8,128)(2,1)S(1)} all-to-all(bf16[16,16,512]{2,1,0:T(8,128)(2,1)S(1)} %bitcast.9), channel_id=1, replica_groups={{0,2,4,6,8,10,12,14,16,18,20,22,24,26,28,30},{1,3,5,7,9,11,13,15,17,19,..., dimensions={0} | all-to-all | bytes 524288 | tf_op jit(solution)/shard_map/all_to_all | solution.py:347
  47.3 0.8 %shard_map.149 = bf16[8,2048]{1,0:T(8,128)(2,1)} custom-call(f32[8,256]{1,0:T(8,128)S(1)} %get-tuple-element.13.comb, bf16[256,512]{1,0:T(8,128)(2,1)S(1)} %bitcast.7, bf16[8,2048]{1,0:T(8,128)(2,1)S(1)} %get-tuple-element.18.mixed), custom_call_target="tpu_custom_call" | custom-call | tf_op jit(solution)/shard_map/pallas_call | solution.py:372
Async XLA Ops:
  0.6 26.6 %collective-permute-start = (bf16[1,2,704,2048]{3,2,1,0:T(8,128)(2,1)}, bf16[1,2,704,2048]{3,2,1,0:T(8,128)(2,1)S(1)}, u32[]{:S(2)}, u32[]{:S(2)}) collective-permute-start(bf16[1,2,704,2048]{3,2,1,0:T(8,128)(2,1)} %own_up.1), channel_id=1, source_target_pairs={{0,1},{1,0},{2,3},{3,2},{4,5},{5,4},{6,7},{7,6},{8,9},{9,8},{10,11... | collective-permute-start | bytes 17301512 | tf_op jit(solution)/shard_map/ppermute | solution.py:292
  1.2 26.1 %collective-permute-start.1 = (bf16[1,704,2048]{2,1,0:T(8,128)(2,1)}, bf16[1,704,2048]{2,1,0:T(8,128)(2,1)S(1)}, u32[]{:S(2)}, u32[]{:S(2)}) collective-permute-start(bf16[1,704,2048]{2,1,0:T(8,128)(2,1)} %own_down.1), channel_id=1, source_target_pairs={{0,1},{1,0},{2,3},{3,2},{4,5},{5,4},{6,7},{7,6},{8,9},{9,8},{10,11... | collective-permute-start | bytes 8650760 | tf_op jit(solution)/shard_map/ppermute | solution.py:293

commit v14 on v10

--- a/solution.py
+++ b/solution.py
@@ -47,10 +47,12 @@
         [(pool_half(pool, 0), keys), (pool_half(pool, 1), values), (weight, kept_weight)], sems, 4
     )
     later = copies(list(zip(refs[4:-2], small[4:])), sems, 7)
-    for copy in loads + [key_load, value_load] + later + [weight_load]:
+    for copy in loads + [key_load]:
         copy.start()
     for copy in loads:
         copy.wait()
+    for copy in [value_load, weight_load] + later:
+        copy.start()
     for h in range(heads):
         qs[pl.ds(h * requests, requests), :] = q_ref[:, pl.ds(h * head_dim, head_dim)].astype(F32)
     spots = [(table[r, lengths[r] // page_len], lengths[r] % page_len) for r in range(requests)]
@@ -89,20 +91,23 @@
     return projected
 
 
-def route(projected, hidden, gain, router, ids, mixed_ref, norms_ref, top_ref, slabs_ref, comb_ref, capacity, leave=None):
+def as_row(column):
+    shape = (column.shape[0],) * 2
+    return jnp.sum(jnp.where(iota(shape, 0) == iota(shape, 1), column, 0.0), axis=0, keepdims=True)
+
+
+def route(projected, hidden, gain, router, ids, mixed_ref, norms_ref, top_ref, packet_ref):
     requests, width = hidden.shape
     experts = router.shape[0]
-    parts = SLAB // capacity
-    piece = width // parts
-    slab_rows = experts * SLAB
     mixed = (hidden[...].astype(F32) + projected).astype(BF16)
     mixed_ref[...] = mixed
     mixed = mixed.astype(F32)
     norms = jnp.sqrt(jnp.mean(mixed * mixed, axis=1, keepdims=True) + 1e-06)
-    norms_ref[...] = norms
+    norms_ref[...] = as_row(norms)
     normed = (mixed / norms * gain[...].astype(F32).reshape(1, width)).astype(BF16)
+    packet_ref[:, :width] = normed
     logits = dot(normed, router[...], NT)
-    top_ref[...] = jnp.max(logits, axis=1, keepdims=True)
+    top_ref[...] = as_row(jnp.max(logits, axis=1, keepdims=True))
     column = iota((requests, experts), 1)
     named = column < 0
     for k in range(ids.shape[1]):
@@ -111,22 +116,45 @@
     weights = weights / jnp.sum(weights, axis=1, keepdims=True)
     earlier = (iota((requests, requests), 1) < iota((requests, requests), 0)).astype(F32)
     rank = dot(earlier, named.astype(F32))
-    place = jnp.where(named, rank, -1.0)
-    normed = normed.astype(F32)
-    stacked = jnp.concatenate([normed[:, p * piece : (p + 1) * piece] for p in range(parts)], axis=0)
+    fields = [jnp.where(named, rank, -1.0)] + split(weights)
+    spare = packet_ref.shape[1] - width - len(fields) * experts
+    if spare:
+        fields.append(jnp.zeros((requests, spare), F32))
+    packet_ref[:, width:] = jnp.concatenate(fields, axis=1).astype(BF16)
+
+
+def split(values):
+    pieces = []
+    for _ in range(3):
+        pieces.append(values.astype(BF16).astype(F32))
+        values = values - pieces[-1]
+    return pieces
+
+
+def dispatch_kernel(capacity, experts, own, partner, slabs_ref, comb_ref):
+    rows, piece = slabs_ref.shape
+    requests = own.shape[0]
+    tokens = 2 * requests
+    parts = SLAB // (2 * capacity)
+    width = parts * piece
+    first = lax.axis_index("req") // (lax.axis_size("req") // 2) * (rows // SLAB)
+    packet = jnp.concatenate([own[...].astype(F32), partner[...].astype(F32)], axis=0)
+    place = packet[:, width : width + experts]
+    source = iota(place.shape, 0) // requests * capacity
+    place = jnp.where(place >= 0.0, place + source.astype(F32), -1.0)
+    weights = sum(packet[:, width + i * experts : width + (i + 1) * experts] for i in (1, 2, 3))
+    stacked = jnp.concatenate([packet[:, p * piece : (p + 1) * piece] for p in range(parts)], axis=0)
     places = jnp.concatenate([place] * parts, axis=0)
-    shape = (slab_rows, parts * requests)
+    shape = (rows, parts * tokens)
     inner = iota(shape, 0) % SLAB
-    spread = (iota((slab_rows, experts), 0) // SLAB == iota((slab_rows, experts), 1)).astype(F32)
+    spread = (iota((rows, experts), 0) // SLAB + first == iota((rows, experts), 1)).astype(F32)
     picks = (dot(spread, places, NT) == (inner // parts).astype(F32)) & (
-        inner % parts == iota(shape, 1) // requests
+        inner % parts == iota(shape, 1) // tokens
     )
     slabs_ref[...] = dot(picks.astype(BF16), stacked.astype(BF16)).astype(BF16)
-    if leave is not None:
-        leave()
-    shape = (experts, slab_rows)
-    spread = (iota(shape, 1) // SLAB == iota(shape, 0)).astype(F32)
-    inner = iota((requests, slab_rows), 1) % SLAB
+    shape = (experts, rows)
+    spread = (iota(shape, 1) // SLAB + first == iota(shape, 0)).astype(F32)
+    inner = iota((tokens, rows), 1) % SLAB
     comb_ref[...] = jnp.where(
         dot(place, spread) == (inner // parts).astype(F32),
         dot(weights, spread, precision=lax.Precision.HIGHEST),
@@ -134,23 +162,21 @@
     )
 
 
-def attend_route_kernel(capacity, *refs):
-    inputs, (mixed, norms, top, slabs, comb) = refs[:10], refs[10:15]
-    small, scratch = refs[15:23], refs[23:]
-    keys, values, kept_slabs = scratch[:3]
-    projected = attend(inputs, keys, values, (small, scratch[3:]))
+def attend_route_kernel(*refs):
+    inputs, outputs = refs[:10], refs[10:14]
+    small, scratch = refs[14:22], refs[22:]
+    projected = attend(inputs, scratch[0], scratch[1], (small, scratch[2:]))
     hidden, gain, router, ids = small[4:]
-    leave = pltpu.make_async_copy(kept_slabs, slabs, scratch[-1].at[0])
-    route(projected, hidden, gain, router, ids, mixed, norms, top, kept_slabs, comb, capacity, leave.start)
-    leave.wait()
+    route(projected, hidden, gain, router, ids, *outputs)
 
 
 def attend_kernel(*refs):
-    attended, scratch = refs[6], refs[11:]
-    attended[...] = attend(refs[:6], scratch[0], scratch[1], (refs[7:11], scratch[2:]))
-
-
-def refresh_kernel(table, lengths, fresh, after, pool, new_pool, kept, sems):
+    projected, scratch = refs[6], refs[11:]
+    projected[...] = attend(refs[:6], scratch[0], scratch[1], (refs[7:11], scratch[2:]))
+
+
+def refresh_kernel(table, lengths, fresh, after, pool, new_pool, done, kept, sems):
+    done[...] = after[...]
     pages, page_len = kept.shape[:2]
     step = -(-pages // 4)
     spans = [pl.ds(start, min(step, pages - start)) for start in range(0, pages, step)]
@@ -168,15 +194,15 @@
         copy.wait()
 
 
-def route_kernel(capacity, projected, hidden, gain, router, ids, mixed, norms, top, slabs, comb):
-    route(projected[...], hidden, gain, router, ids, mixed, norms, top, slabs, comb, capacity)
+def route_kernel(projected, hidden, gain, router, ids, *outputs):
+    route(projected[...], hidden, gain, router, ids, *outputs)
 
 
 def unit_chunks(units):
     return [(start, min(256, units - start)) for start in range(0, units, 256)]
 
 
-def expert_kernel(capacity, arrived, own_up, own_down, other_up, other_down, slabs,
+def expert_kernel(slots, arrived, own_up, own_down, other_up, other_down, slabs, done,
                   slab_rows, kept_up, kept_down, rows, total, sems):
     units = kept_down.shape[0]
     arrive = pltpu.make_async_copy(arrived, slab_rows, sems.at[0])
@@ -189,11 +215,10 @@
             sems,
             1 + 2 * i,
         )))
-    for _, loads in chunks:
-        for copy in loads:
-            copy.start()
+    for copy in [copy for _, loads in chunks for copy in loads]:
+        copy.start()
     arrive.wait()
-    parts = SLAB // capacity
+    parts = SLAB // slots
     piece = slabs.shape[1]
     block = 128
     each = block // parts
@@ -223,37 +248,28 @@
         summed = total[pl.ds(i * each, each), :].astype(BF16)
         stacked = jnp.concatenate([summed[:, p * piece : (p + 1) * piece] for p in range(parts)], axis=0)
         slabs[pl.ds(i * block, block), :] = dot(unsort, stacked).astype(BF16)
-
-
-def gather_terms(comb, slabs, capacity):
-    parts = SLAB // capacity
-    requests = comb.shape[0]
-    weights = comb[...]
-    pieces = []
-    for _ in range(3):
-        piece = weights.astype(BF16).astype(F32)
-        weights = weights - piece
-        pieces.append(piece)
+    done[...] = jnp.zeros(done.shape, F32)
+
+
+def gather_kernel(slots, comb, slabs, stored, own, partner):
+    parts = SLAB // slots
+    tokens = comb.shape[0]
     part = iota(comb.shape, 1) % parts
+    pieces = split(comb[...])
     stacked = jnp.concatenate(
         [jnp.where(part == p, piece, 0.0) for p in range(parts) for piece in pieces], axis=0
     ).astype(BF16)
     terms = dot(stacked, slabs[...])
-    return jnp.concatenate(
-        [
-            sum(terms[(3 * p + i) * requests : (3 * p + i + 1) * requests] for i in range(3))
-            for p in range(parts)
-        ],
+    terms = jnp.concatenate(
+        [sum(terms[(3 * p + i) * tokens : (3 * p + i + 1) * tokens] for i in range(3)) for p in range(parts)],
         axis=1,
     )
-
-
-def combine_kernel(capacity, comb, slabs, mixed, out):
-    out[...] = (mixed[...].astype(F32) + gather_terms(comb, slabs, capacity)).astype(BF16)
-
-
-def gather_kernel(capacity, comb, slabs, out):
-    out[...] = gather_terms(comb, slabs, capacity).astype(BF16)
+    own[...] = terms[: tokens // 2]
+    partner[...] = terms[tokens // 2 :].astype(BF16)
+
+
+def finish_kernel(mixed, own, partner, out):
+    out[...] = (mixed[...].astype(F32) + own[...] + partner[...].astype(F32)).astype(BF16)
 
 
 def vmem(count):
@@ -299,11 +315,14 @@
     copies = req_count // experts
     chosen = expert_ids.shape[1]
     capacity = 2 * max(1, (requests * chosen + 2 * experts - 1) // (2 * experts))
-    parts = SLAB // capacity
-    piece = width // parts
-    slab_rows = experts * SLAB
-
-    same_part = [list(range(part, req_count, copies)) for part in range(copies)]
+    slots = 2 * capacity
+    piece = width // (SLAB // slots)
+    members = experts // 2
+    slab_rows = members * SLAB
+
+    far = req_count // 2
+    near = [list(range(base + part, base + far, copies)) for base in (0, far) for part in range(copies)]
+    across = [(index, (index + far) % req_count) for index in range(req_count)]
     swap = [(index, index ^ 1) for index in range(req_count)]
     other_up = lax.ppermute(expert_gate_up, "req", swap)
     other_down = lax.ppermute(expert_down, "req", swap)
@@ -326,19 +345,17 @@
     inputs += small(queries, fresh_key_value)
     routed_shapes = [
         like((requests, width)),
-        like((requests, 1), F32),
-        like((requests, 1), F32),
-        like((slab_rows, piece)),
-        like((requests, slab_rows), F32),
+        like((1, requests), F32),
+        like((1, requests), F32),
+        like((requests, width + -(-4 * experts // 128) * 128)),
     ]
     attend_params = pltpu.CompilerParams(vmem_limit_bytes=24 * MIB)
     if kv_count == 1:
-        attend_scratch.insert(2, pltpu.VMEM((slab_rows, piece), BF16))
-        mixed, norms, top, slabs, comb = pl.pallas_call(
-            functools.partial(attend_route_kernel, capacity),
+        mixed, norms, top, packet = pl.pallas_call(
+            attend_route_kernel,
             out_shape=routed_shapes,
             in_specs=in_hbm(10),
-            out_specs=vmem(3) + in_hbm(1) + vmem(1),
+            out_specs=vmem(4),
             scratch_shapes=inputs + small(hidden, norm_gain, router_weight, expert_ids) + attend_scratch,
             compiler_params=attend_params,
         )(*pinned(page_table, lengths, queries, fresh_key_value, hidden, norm_gain, router_weight, expert_ids,
@@ -353,38 +370,34 @@
             compiler_params=attend_params,
         )(*pinned(page_table, lengths, queries, fresh_key_value, kv_pool, out_weight))
         projected = lax.psum(projected, "kv")
-        mixed, norms, top, slabs, comb = pl.pallas_call(
-            functools.partial(route_kernel, capacity),
+        mixed, norms, top, packet = pl.pallas_call(
+            route_kernel,
             out_shape=routed_shapes,
             in_specs=vmem(5),
-            out_specs=vmem(5),
+            out_specs=vmem(4),
         )(projected, hidden, norm_gain, router_weight, expert_ids)
 
-    new_pool = pl.pallas_call(
-        refresh_kernel,
-        out_shape=like(kv_pool.shape),
-        in_specs=scalars(2) + vmem(1) + in_hbm(2),
-        out_specs=pl.BlockSpec(memory_space=pltpu.HBM),
-        scratch_shapes=[pltpu.VMEM(kv_pool.shape, BF16), pltpu.SemaphoreType.DMA((8,))],
-        compiler_params=pltpu.CompilerParams(vmem_limit_bytes=12 * MIB),
-        cost_estimate=pl.CostEstimate(flops=0, bytes_accessed=8 * kv_pool.size, transcendentals=0),
-    )(page_table, lengths, fresh_key_value, top, *pinned(kv_pool))
-
     def exchange(array):
-        array = array.reshape(experts, SLAB, piece)
-        array = lax.all_to_all(
-            array, "req", split_axis=0, concat_axis=0, tiled=True, axis_index_groups=same_part
-        )
+        array = array.reshape(members, SLAB, piece)
+        array = lax.all_to_all(array, "req", split_axis=0, concat_axis=0, tiled=True, axis_index_groups=near)
         return array.reshape(slab_rows, piece)
 
+    small_grant = pltpu.CompilerParams(vmem_limit_bytes=8 * MIB)
+    slabs, comb = pl.pallas_call(
+        functools.partial(dispatch_kernel, capacity, experts),
+        out_shape=[like((slab_rows, piece)), like((2 * requests, slab_rows), F32)],
+        in_specs=vmem(2),
+        out_specs=vmem(2),
+        compiler_params=small_grant,
+    )(packet, lax.ppermute(packet, "req", across))
     arrived = exchange(slabs)
-    kept = experts * capacity
+    kept = members * slots
     units = expert_down.shape[1]
-    leaving = pl.pallas_call(
-        functools.partial(expert_kernel, capacity),
-        out_shape=like((slab_rows, piece)),
+    leaving, done = pl.pallas_call(
+        functools.partial(expert_kernel, slots),
+        out_shape=[like((slab_rows, piece)), like((8, 128), F32)],
         in_specs=in_hbm(3) + vmem(2),
-        out_specs=pl.BlockSpec(memory_space=pltpu.VMEM),
+        out_specs=vmem(2),
         scratch_shapes=[
             pltpu.VMEM((slab_rows, piece), BF16),
             pltpu.VMEM((2, units, width), BF16),
@@ -395,22 +408,33 @@
         ],
         compiler_params=pltpu.CompilerParams(vmem_limit_bytes=20 * MIB),
     )(arrived, *pinned(expert_gate_up, expert_down), other_up, other_down)
-    returned = exchange(leaving)
+    new_pool, stored = pl.pallas_call(
+        refresh_kernel,
+        out_shape=[like(kv_pool.shape), like((8, 128), F32)],
+        in_specs=scalars(2) + vmem(2) + in_hbm(1),
+        out_specs=in_hbm(1) + vmem(1),
+        scratch_shapes=[pltpu.VMEM(kv_pool.shape, BF16), pltpu.SemaphoreType.DMA((8,))],
+        compiler_params=pltpu.CompilerParams(vmem_limit_bytes=12 * MIB),
+        cost_estimate=pl.CostEstimate(flops=0, bytes_accessed=8 * kv_pool.size, transcendentals=0),
+    )(page_table, lengths, fresh_key_value, done, *pinned(kv_pool))
+    own_sum, partner_sum = pl.pallas_call(
+        functools.partial(gather_kernel, slots),
+        out_shape=[like((requests, width), F32), like((requests, width))],
+        in_specs=vmem(3),
+        out_specs=vmem(2),
+        compiler_params=small_grant,
+    )(comb, exchange(leaving), stored)
+    crossed = lax.ppermute(partner_sum, "req", across)
     if kv_count == 1:
         out_hidden = pl.pallas_call(
-            functools.partial(combine_kernel, capacity),
+            finish_kernel,
             out_shape=like((requests, width)),
             in_specs=vmem(3),
             out_specs=pl.BlockSpec(memory_space=pltpu.VMEM),
-            compiler_params=pltpu.CompilerParams(vmem_limit_bytes=8 * MIB),
-        )(comb, returned, mixed)
+            compiler_params=small_grant,
+        )(mixed, own_sum, crossed)
     else:
-        routed = pl.pallas_call(
-            functools.partial(gather_kernel, capacity),
-            out_shape=like((requests, width)),
-            in_specs=vmem(2),
-            out_specs=pl.BlockSpec(memory_space=pltpu.VMEM),
-        )(comb, returned)
+        routed = (own_sum + crossed.astype(F32)).astype(BF16)
         routed = lax.psum(routed, "kv").astype(F32)
         out_hidden = (mixed.astype(F32) + routed).astype(BF16)
     return out_hidden, new_pool, norms.reshape(requests), top.reshape(requests)

time: 47.4 us -> 49.2 us (1.038)
  starting transfers between devices: 4.16 us -> 11 us
  blocking collectives: 18.2 us -> 11.5 us
  waiting for transfers between devices: 1.54 us -> 3.88 us
  other arithmetic: 1.25 us -> 0 us
  Pallas kernels: 21.2 us -> 21.8 us
    ppermute x0 -> x2, starting transfers between devices: none -> 7 us  [the longest x1 4.08 us: body(): lax.ppermute(packet, 'req', across)]
    all_to_all x1, blocking collectives: 18.2 us -> 11.5 us  [exchange(): lax.all_to_all(array, 'req', split_axis=0, concat_axis=0, tiled=True, axi...]
    ppermute x0 -> x2, waiting for transfers between devices: none -> 3.88 us  [the longest x1 1.96 us: body(): crossed = lax.ppermute(partner_sum, 'req', across)]
    all_to_all x1, waiting for transfers between devices: 1.53 us -> 0.01 us  [exchange(): lax.all_to_all(array, 'req', split_axis=0, concat_axis=0, tiled=True, axi...]
    pallas_call x2 -> x0, other arithmetic: 1.25 us -> none  [body(): pl.pallas_call(functools.partial(attend_route_kernel, capacity), out_shap...]
    pallas_call x4 -> x6, Pallas kernels: 21.2 us -> 21.8 us  [the longest x1 7.79 us: body(): pl.pallas_call(attend_route_kernel, out_shape=routed_shapes, in_specs=in_...]
  transfers between devices with their start and end apart: 3 -> 5, of which waited for: 1 -> 2; matrix products, arithmetic and copies ran while one was open for 3% -> 0% of each run, Pallas kernels for 30% -> 30%
where the time goes in v14:
time: 49.2 us; the launch traced here: 49 us
  Pallas kernels  21.8 us (44%)
  blocking collectives  11.5 us (23%)
  starting transfers between devices  11 us (22%)
  waiting for transfers between devices  3.88 us (8%)
  between operations  0.73 us (1%)
    all_to_all x1, blocking collectives, exchange(): lax.all_to_all(array, 'req', split_axis=0, concat_axis=0, tiled=True, axi...  11.5 us
    pallas_call x1, Pallas kernels, body(): pl.pallas_call(attend_route_kernel, out_shape=routed_shapes, in_specs=in_...  7.79 us
    pallas_call x1, Pallas kernels, body(): pl.pallas_call(refresh_kernel, out_shape=[like(kv_pool.shape), like((8, 1...  6.54 us
    pallas_call x1, Pallas kernels, body(): pl.pallas_call(functools.partial(expert_kernel, slots), out_shape=[like((...  6.35 us
    ppermute x1, starting transfers between devices, body(): lax.ppermute(packet, 'req', across)  4.08 us
    all_to_all x1, starting transfers between devices, exchange(): lax.all_to_all(array, 'req', split_axis=0, concat_axis=0, tiled=True, axi...  3.42 us
    ppermute x1, starting transfers between devices, body(): crossed = lax.ppermute(partner_sum, 'req', across)  2.92 us
    ppermute x1, waiting for transfers between devices, body(): crossed = lax.ppermute(partner_sum, 'req', across)  1.96 us
  transfers between devices with their start and end apart: 5, of which 2 were waited for; matrix products, arithmetic and copies ran while one was open for 0% of the time, Pallas kernels for 30%

profile of v14, /device:TPU:0, one launch (start us, length us, event | category | flops | bytes accessed | tf_op | source)
XLA Modules:
  0.0 49.0 jit_solution(3809773331877160983)
XLA Ops:
  0.6 0.5 %collective-permute-start.1 = (bf16[1,2,704,2048]{3,2,1,0:T(8,128)(2,1)}, bf16[1,2,704,2048]{3,2,1,0:T(8,128)(2,1)S(1)}, u32[]{:S(2)}, u32[]{:S(2)}) collective-permute-start(bf16[1,2,704,2048]{3,2,1,0:T(8,128)(2,1)} %own_up.1), channel_id=1, source_target_pairs={{0,1},{1,0},{2,3},{3,2},{4,5},{5,4},{6,7},{7,6},{8,9},{9,8},{10,11... | collective-permute-start | bytes 17301512 | tf_op jit(solution)/shard_map/ppermute | solution.py:327
  1.1 0.1 collective-permute-start.2
  1.2 7.8 %shard_map.147 = (bf16[8,2048]{1,0:T(8,128)(2,1)S(1)}, f32[1,8]{1,0:T(1,128)}, f32[1,8]{1,0:T(1,128)}, bf16[8,2176]{1,0:T(8,128)(2,1)S(1)}) custom-call(s32[8,20]{1,0:T(8,128)} %table.1, s32[8]{0:T(128)} %lengths.1, bf16[8,2048]{1,0:T(8,128)(2,1)} %refs_2_.1, bf16[8,4,256]{2,1,0:T(4,128)(2,1)} %fresh.1, bf16[8,2048]{1,0:T(8,128)(2,1)} %refs_4_.1, ...), custom_call_target="tpu_custom_call" | custom-call | tf_op jit(solution)/shard_map/pallas_call | solution.py:354
  9.0 4.1 %collective-permute-start = (bf16[8,2176]{1,0:T(8,128)(2,1)S(1)}, bf16[8,2176]{1,0:T(8,128)(2,1)S(1)}, u32[]{:S(2)}, u32[]{:S(2)}) collective-permute-start(bf16[8,2176]{1,0:T(8,128)(2,1)S(1)} %get-tuple-element.17.own), channel_id=1, source_target_pairs={{0,16},{1,17},{2,18},{3,19},{4,20},{5,21},{6,22},{7,23},{8,24},{9,... | collective-permute-start | bytes 104456 | tf_op jit(solution)/shard_map/ppermute | solution.py:392
  13.1 1.9 %collective-permute-done.partner = bf16[8,2176]{1,0:T(8,128)(2,1)S(1)} collective-permute-done((bf16[8,2176]{1,0:T(8,128)(2,1)S(1)}, bf16[8,2176]{1,0:T(8,128)(2,1)S(1)}, u32[]{:S(2)}, u32[]{:S(2)}) %collective-permute-start) | collective-permute-done | bytes 34848 | tf_op jit(solution)/shard_map/ppermute | solution.py:392
  15.0 0.4 shard_map.148
  15.4 11.5 %all_to_all.10 = bf16[8,16,1024]{2,1,0:T(8,128)(2,1)S(1)} all-to-all(bf16[8,16,1024]{2,1,0:T(8,128)(2,1)S(1)} %bitcast.8), channel_id=1, replica_groups={{0,2,4,6,8,10,12,14},{1,3,5,7,9,11,13,15},{16,18,20,22,24,26,28,30},{17..., dimensions={0} | all-to-all | bytes 524288 | tf_op jit(solution)/shard_map/all_to_all | solution.py:382
  26.9 0.0 collective-permute-done.2.other_down
  26.9 0.0 collective-permute-done.1.other_up
  26.9 0.0 copy-start
  26.9 0.0 copy-start.1
  26.9 0.0 copy-start.2
  26.9 6.3 %shard_map.149 = (bf16[128,1024]{1,0:T(8,128)(2,1)}, f32[8,128]{1,0:T(8,128)S(1)}) custom-call(bf16[128,1024]{1,0:T(8,128)(2,1)S(1)} %bitcast.6, bf16[1,2,704,2048]{3,2,1,0:T(8,128)(2,1)} %own_up.1, bf16[1,704,2048]{2,1,0:T(8,128)(2,1)} %own_down.1, bf16[1,2,704,2048]{3,2,1,0:T(8,128)(2,1)S(1)} %collective-permute-done.1.other_up, ...), custom_call_target="tpu_custom_call" | custom-call | tf_op jit(solution)/shard_map/pallas_call | solution.py:396
  33.2 3.4 %all-to-all-start.1 = ((bf16[8,16,1024]{2,1,0:T(8,128)(2,1)}), bf16[8,16,1024]{2,1,0:T(8,128)(2,1)S(1)}, u32[]{:S(2)}, u32[]{:S(2)}) async-start(bf16[8,16,1024]{2,1,0:T(8,128)(2,1)} %bitcast.2), calls=%async_computation.1 | async-start | bytes 524288 | tf_op jit(solution)/shard_map/all_to_all | solution.py:382
  36.7 0.0 copy-done
  36.7 0.0 copy-done.1
  36.7 0.0 copy-done.2
  36.7 6.5 %shard_map.150 = (bf16[104,32,4,256]{3,2,1,0:T(4,128)(2,1)}, f32[8,128]{1,0:T(8,128)S(1)}) custom-call(s32[8,20]{1,0:T(8,128)S(1)} %copy-done.1, s32[8]{0:T(128)S(1)} %copy-done.2, bf16[8,4,256]{2,1,0:T(4,128)(2,1)S(1)} %copy-done, f32[8,128]{1,0:T(8,128)S(1)} %get-tuple-element.21.after, bf16[104,32,4,256]{3,2,1,0:T(4,128)(2,1)} %pool.1), custom_call_target="tpu_custom_call" | custom-call | bytes 27262976 | tf_op jit(solution)/shard_map/pallas_call | solution.py:411
  43.3 0.0 all-to-all-done.1
  43.3 0.2 shard_map.151
  43.4 2.9 %collective-permute-start.3 = (bf16[8,2048]{1,0:T(8,128)(2,1)S(1)}, bf16[8,2048]{1,0:T(8,128)(2,1)S(1)}, u32[]{:S(2)}, u32[]{:S(2)}) collective-permute-start(bf16[8,2048]{1,0:T(8,128)(2,1)S(1)} %get-tuple-element.24), channel_id=1, source_target_pairs={{0,16},{1,17},{2,18},{3,19},{4,20},{5,21},{6,22},{7,23},{8,24},{9,... | collective-permute-start | bytes 98312 | tf_op jit(solution)/shard_map/ppermute | solution.py:427
  46.4 2.0 %collective-permute-done.3.partner = bf16[8,2048]{1,0:T(8,128)(2,1)S(1)} collective-permute-done((bf16[8,2048]{1,0:T(8,128)(2,1)S(1)}, bf16[8,2048]{1,0:T(8,128)(2,1)S(1)}, u32[]{:S(2)}, u32[]{:S(2)}) %collective-permute-start.3) | collective-permute-done | bytes 32800 | tf_op jit(solution)/shard_map/ppermute | solution.py:427
  48.3 0.6 %shard_map.152 = bf16[8,2048]{1,0:T(8,128)(2,1)} custom-call(bf16[8,2048]{1,0:T(8,128)(2,1)S(1)} %get-tuple-element.16.mixed, f32[8,2048]{1,0:T(8,128)S(1)} %get-tuple-element.23.own, bf16[8,2048]{1,0:T(8,128)(2,1)S(1)} %collective-permute-done.3.partner), custom_call_target="tpu_custom_call" | custom-call | tf_op jit(solution)/shard_map/pallas_call | solution.py:429
Async XLA Ops:
  0.6 26.2 %collective-permute-start.1 = (bf16[1,2,704,2048]{3,2,1,0:T(8,128)(2,1)}, bf16[1,2,704,2048]{3,2,1,0:T(8,128)(2,1)S(1)}, u32[]{:S(2)}, u32[]{:S(2)}) collective-permute-start(bf16[1,2,704,2048]{3,2,1,0:T(8,128)(2,1)} %own_up.1), channel_id=1, source_target_pairs={{0,1},{1,0},{2,3},{3,2},{4,5},{5,4},{6,7},{7,6},{8,9},{9,8},{10,11... | collective-permute-start | bytes 17301512 | tf_op jit(solution)/shard_map/ppermute | solution.py:327
  1.1 25.7 %collective-permute-start.2 = (bf16[1,704,2048]{2,1,0:T(8,128)(2,1)}, bf16[1,704,2048]{2,1,0:T(8,128)(2,1)S(1)}, u32[]{:S(2)}, u32[]{:S(2)}) collective-permute-start(bf16[1,704,2048]{2,1,0:T(8,128)(2,1)} %own_down.1), channel_id=1, source_target_pairs={{0,1},{1,0},{2,3},{3,2},{4,5},{5,4},{6,7},{7,6},{8,9},{9,8},{10,11... | collective-permute-start | bytes 8650760 | tf_op jit(solution)/shard_map/ppermute | solution.py:328
  9.0 6.0 %collective-permute-start = (bf16[8,2176]{1,0:T(8,128)(2,1)S(1)}, bf16[8,2176]{1,0:T(8,128)(2,1)S(1)}, u32[]{:S(2)}, u32[]{:S(2)}) collective-permute-start(bf16[8,2176]{1,0:T(8,128)(2,1)S(1)} %get-tuple-element.17.own), channel_id=1, source_target_pairs={{0,16},{1,17},{2,18},{3,19},{4,20},{5,21},{6,22},{7,23},{8,24},{9,... | collective-permute-start | bytes 104456 | tf_op jit(solution)/shard_map/ppermute | solution.py:392
  26.9 9.8 %copy-start = (bf16[8,4,256]{2,1,0:T(4,128)(2,1)S(1)}, bf16[8,4,256]{2,1,0:T(4,128)(2,1)}, u32[]{:S(2)}) copy-start(bf16[8,4,256]{2,1,0:T(4,128)(2,1)} %fresh.1) | copy-start | bytes 49156
  26.9 9.8 %copy-start.1 = (s32[8,20]{1,0:T(8,128)S(1)}, s32[8,20]{1,0:T(8,128)}, u32[]{:S(2)}) copy-start(s32[8,20]{1,0:T(8,128)} %table.1) | copy-start | bytes 1924
  26.9 9.8 %copy-start.2 = (s32[8]{0:T(128)S(1)}, s32[8]{0:T(128)}, u32[]{:S(2)}) copy-start(s32[8]{0:T(128)} %lengths.1) | copy-start | bytes 100
  33.2 10.0 %all-to-all-start.1 = ((bf16[8,16,1024]{2,1,0:T(8,128)(2,1)}), bf16[8,16,1024]{2,1,0:T(8,128)(2,1)S(1)}, u32[]{:S(2)}, u32[]{:S(2)}) async-start(bf16[8,16,1024]{2,1,0:T(8,128)(2,1)} %bitcast.2), calls=%async_computation.1 | async-start | bytes 524288 | tf_op jit(solution)/shard_map/all_to_all | solution.py:382
  43.4 4.9 %collective-permute-start.3 = (bf16[8,2048]{1,0:T(8,128)(2,1)S(1)}, bf16[8,2048]{1,0:T(8,128)(2,1)S(1)}, u32[]{:S(2)}, u32[]{:S(2)}) collective-permute-start(bf16[8,2048]{1,0:T(8,128)(2,1)S(1)} %get-tuple-element.24), channel_id=1, source_target_pairs={{0,16},{1,17},{2,18},{3,19},{4,20},{5,21},{6,22},{7,23},{8,24},{9,... | collective-permute-start | bytes 98312 | tf_op jit(solution)/shard_map/ppermute | solution.py:427

commit v15 on v12

--- a/solution.py
+++ b/solution.py
@@ -29,13 +29,17 @@
     return [pltpu.make_async_copy(src, dst, sems.at[first + i]) for i, (src, dst) in enumerate(pairs)]
 
 
+def group_turn(chips, part):
+    return chips * 9 // 16 if part % 2 else chips * 3 // 8
+
+
 def pool_half(array, i):
     head_dim = array.shape[3] // 2
     return array.at[:, :, :, pl.ds(i * head_dim, head_dim)]
 
 
 def attend(refs, keys, values, scratch):
-    small, (kept_weight, qs, att, probs, sums, sems) = scratch
+    small, (kept_weight, qs, att, scores, probs, sems) = scratch
     table, lengths, q_ref, fresh = small[:4]
     requests, max_pages = table.shape
     pages, page_len, heads_kv, head_dim = keys.shape
@@ -44,14 +48,17 @@
     page_rows = page_len * heads_kv
     pool, weight = refs[-2:]
     loads = copies(list(zip(refs[:4], small[:4])), sems)
-    key_load, value_load, weight_load = copies(
-        [(pool_half(pool, 0), keys), (pool_half(pool, 1), values), (weight, kept_weight)], sems, 4
-    )
-    later = copies(list(zip(refs[4:-2], small[4:])), sems, 7)
-    for copy in loads + [key_load, value_load] + later + [weight_load]:
+    key_load, value_load = copies([(pool_half(pool, 0), keys), (pool_half(pool, 1), values)], sems, 4)
+    later = copies(list(zip(refs[4:-2], small[4:])), sems, 6)
+    step = weight.shape[0] // 4
+    spans = [pl.ds(i * step, step) for i in range(4)]
+    weight_loads = copies([(weight.at[span], kept_weight.at[span]) for span in spans], sems, 10)
+    for copy in loads + [key_load]:
         copy.start()
     for copy in loads:
         copy.wait()
+    for copy in [value_load] + later + weight_loads[:1]:
+        copy.start()
     for h in range(heads):
         qs[pl.ds(h * requests, requests), :] = q_ref[:, pl.ds(h * head_dim, head_dim)].astype(F32)
     spots = [(table[r, lengths[r] // page_len], lengths[r] % page_len) for r in range(requests)]
@@ -62,43 +69,63 @@
     key_pages = keys.reshape(pages, page_rows, head_dim)
     value_pages = values.reshape(pages, page_rows, head_dim)
     columns = max_pages * page_rows
-    lane = iota((heads, columns), 1)
-    own_head = lane % heads_kv == iota((heads, columns), 0) // group
-    position = lane // heads_kv
     shared_columns = SHARED_PAGES * page_rows
+    rows = requests * heads
 
     def pages_of(array, r, first, last):
         return jnp.concatenate([array[table[r, j]] for j in range(first, last)], axis=0)
 
+    weight_loads[1].start()
     query = [qs[pl.ds(r, heads, stride=requests), :] for r in range(requests)]
-    shared = dot(jnp.concatenate(query, axis=0).astype(BF16), pages_of(key_pages, 0, 0, SHARED_PAGES), NT)
+    query_rows = jnp.concatenate(query, axis=0).astype(BF16)
+    scores[:, :shared_columns] = dot(query_rows, pages_of(key_pages, 0, 0, SHARED_PAGES), NT)
     for r in range(requests):
-        own = dot(query[r].astype(BF16), pages_of(key_pages, r, SHARED_PAGES, max_pages), NT)
-        scores = jnp.concatenate([shared[r * heads : (r + 1) * heads], own], axis=1)
-        scores = scores * (1.0 / math.sqrt(head_dim))
-        scores = jnp.where(own_head & (position <= lengths[r]), scores, -1e30)
-        exponent = jnp.exp(scores - jnp.max(scores, axis=1, keepdims=True))
-        sums[r] = jnp.broadcast_to(jnp.sum(exponent, axis=1, keepdims=True), (heads, head_dim))
-        probs[r] = exponent.astype(BF16)
+        scores[pl.ds(r * heads, heads), shared_columns:] = dot(
+            query[r].astype(BF16), pages_of(key_pages, r, SHARED_PAGES, max_pages), NT
+        )
+    lane = iota((heads, columns), 1)
+    own_head = (lane & (heads_kv - 1)) == iota((heads, columns), 0) // group
+    position = lane >> (heads_kv.bit_length() - 1)
+    masked = jnp.concatenate(
+        [
+            jnp.where(own_head & (position <= lengths[r]), scores[pl.ds(r * heads, heads), :], -1e30)
+            for r in range(requests)
+        ],
+        axis=0,
+    )
+    scale = 1.0 / math.sqrt(head_dim)
+    exponent = jnp.exp((masked - jnp.max(masked, axis=1, keepdims=True)) * scale)
+    sums = jnp.sum(exponent, axis=1, keepdims=True)
+    probs[...] = exponent.astype(BF16)
 
     value_load.wait()
+    for copy in weight_loads[2:]:
+        copy.start()
     for r, (page, slot) in enumerate(spots):
         values[page, slot] = fresh[r][:, head_dim:]
-    shared = dot(
-        probs[:, :, :shared_columns].reshape(requests * heads, shared_columns),
-        pages_of(value_pages, 0, 0, SHARED_PAGES),
-    )
+    shared = dot(probs[:, :shared_columns], pages_of(value_pages, 0, 0, SHARED_PAGES))
+    own = [
+        dot(probs[pl.ds(r * heads, heads), shared_columns:], pages_of(value_pages, r, SHARED_PAGES, max_pages))
+        for r in range(requests)
+    ]
+    mean = (shared + jnp.concatenate(own, axis=0)) / sums
     for r in range(requests):
-        own = dot(probs[r, :, shared_columns:], pages_of(value_pages, r, SHARED_PAGES, max_pages))
-        att[pl.ds(r, heads, stride=requests), :] = (shared[r * heads : (r + 1) * heads] + own) / sums[r]
+        att[pl.ds(r, heads, stride=requests), :] = mean[r * heads : (r + 1) * heads]
     attended = jnp.concatenate(
         [att[pl.ds(h * requests, requests), :] for h in range(heads)], axis=1
     ).astype(BF16)
-    weight_load.wait()
-    projected = dot(attended, kept_weight[...])
+    projected = 0.0
+    for i, copy in enumerate(weight_loads):
+        copy.wait()
+        projected = projected + dot(attended[:, i * step : (i + 1) * step], kept_weight[spans[i], :])
     for copy in later:
         copy.wait()
     return projected
+
+
+def as_row(column):
+    shape = (column.shape[0],) * 2
+    return jnp.sum(jnp.where(iota(shape, 0) == iota(shape, 1), column, 0.0), axis=0, keepdims=True)
 
 
 def route(projected, hidden, gain, router, ids, mixed_ref, norms_ref, top_ref, slabs_ref, comb_ref, capacity, leave=None):
@@ -107,20 +134,19 @@
     parts = SLAB // capacity
     piece = width // parts
     slab_rows = experts * SLAB
-    backwards = lax.axis_index("req") % 2 == 0
+    turns = jnp.where(lax.axis_index("req") % 2 == 0, group_turn(experts, 0), group_turn(experts, 1))
 
     def slab_expert(shape, dim):
-        slab = iota(shape, dim) // SLAB
-        return jnp.where(backwards, experts - 1 - slab, slab)
+        return (iota(shape, dim) // SLAB) ^ turns
 
     mixed = (hidden[...].astype(F32) + projected).astype(BF16)
     mixed_ref[...] = mixed
     mixed = mixed.astype(F32)
     norms = jnp.sqrt(jnp.mean(mixed * mixed, axis=1, keepdims=True) + 1e-06)
-    norms_ref[...] = norms
+    norms_ref[...] = as_row(norms)
     normed = (mixed / norms * gain[...].astype(F32).reshape(1, width)).astype(BF16)
     logits = dot(normed, router[...], NT)
-    top_ref[...] = jnp.max(logits, axis=1, keepdims=True)
+    top_ref[...] = as_row(jnp.max(logits, axis=1, keepdims=True))
     column = iota((requests, experts), 1)
     named = column < 0
     for k in range(ids.shape[1]):
@@ -176,12 +202,16 @@
     stores = copies([(kept.at[span], new_pool.at[span]) for span in spans], sems, len(spans))
     for copy in loads:
         copy.start()
-    for copy in loads:
-        copy.wait()
-    for r in range(table.shape[0]):
-        kept[table[r, lengths[r] // page_len], lengths[r] % page_len] = fresh[r]
-    for copy in stores:
-        copy.start()
+    spots = [(table[r, lengths[r] // page_len], lengths[r] % page_len) for r in range(table.shape[0])]
+    for i, (load, store) in enumerate(zip(loads, stores)):
+        load.wait()
+        for r, (page, slot) in enumerate(spots):
+
+            @pl.when((page >= i * step) & (page < (i + 1) * step))
+            def _():
+                kept[page, slot] = fresh[r]
+
+        store.start()
     for copy in stores:
         copy.wait()
 
@@ -191,7 +221,8 @@
 
 
 def unit_chunks(units):
-    return [(start, min(256, units - start)) for start in range(0, units, 256)]
+    whole = units // 256 * 256
+    return [(start, size) for start, size in ((0, whole), (whole, units - whole)) if size]
 
 
 def expert_kernel(capacity, arrived, own_up, own_down, other_up, other_down, slabs,
@@ -208,8 +239,7 @@
             1 + 2 * i,
         )))
     for _, loads in chunks:
-        for copy in loads:
-            copy.start()
+        loads[0].start()
     arrive.wait()
     parts = SLAB // capacity
     piece = slabs.shape[1]
@@ -227,14 +257,27 @@
     states = rows[...]
     steps = [(other_up.at[0], other_down.at[0], span, []) for span, _ in chunks]
     steps += [(kept_up, kept_down, span, loads) for span, loads in chunks]
-    for i, (gate_up, down, span, loads) in enumerate(steps):
-        for copy in loads:
-            copy.wait()
+
+    def add_down(i, activated):
+        _, down, span, loads = steps[i]
+        if loads:
+            loads[1].wait()
+        term = dot(activated, down[span, :])
+        total[...] = term if i == 0 else total[...] + term
+
+    activated = None
+    for i, (gate_up, _, span, loads) in enumerate(steps):
+        if loads:
+            loads[0].wait()
         gate = dot(states, gate_up[0, span, :], NT)
         up = dot(states, gate_up[1, span, :], NT)
+        if i == 0:
+            for _, loads in chunks:
+                loads[1].start()
+        else:
+            add_down(i - 1, activated)
         activated = (gate / (1.0 + jnp.exp(-gate)) * up).astype(BF16)
-        term = dot(activated, down[span, :])
-        total[...] = term if i == 0 else total[...] + term
+    add_down(len(steps) - 1, activated)
     slab_row, sorted_row = iota(shape, 0), iota(shape, 1)
     unsort = (slab_row == sorted_row % each * parts + sorted_row // each).astype(BF16)
     for i in range(blocks):
@@ -321,7 +364,9 @@
     piece = width // parts
     slab_rows = experts * SLAB
 
-    same_part = [list(range(part, req_count, copies))[:: 1 if part % 2 else -1] for part in range(copies)]
+    same_part = [
+        [(place ^ group_turn(experts, part)) * copies + part for place in range(experts)] for part in range(copies)
+    ]
     swap = [(index, index ^ 1) for index in range(req_count)]
     other_up = lax.ppermute(expert_gate_up, "req", swap)
     other_down = lax.ppermute(expert_down, "req", swap)
@@ -332,9 +377,9 @@
         pltpu.VMEM(out_weight.shape, BF16),
         pltpu.VMEM((heads * requests, head_dim), F32),
         pltpu.VMEM((heads * requests, head_dim), F32),
-        pltpu.VMEM((requests, heads, page_table.shape[1] * page_len * heads_kv), BF16),
-        pltpu.VMEM((requests, heads, head_dim), F32),
-        pltpu.SemaphoreType.DMA((11,)),
+        pltpu.VMEM((requests * heads, page_table.shape[1] * page_len * heads_kv), F32),
+        pltpu.VMEM((requests * heads, page_table.shape[1] * page_len * heads_kv), BF16),
+        pltpu.SemaphoreType.DMA((14,)),
     ]
 
     def small(*arrays):
@@ -344,8 +389,8 @@
     inputs += small(queries, fresh_key_value)
     routed_shapes = [
         like((requests, width)),
-        like((requests, 1), F32),
-        like((requests, 1), F32),
+        like((1, requests), F32),
+        like((1, requests), F32),
         like((slab_rows, piece)),
         like((requests, slab_rows), F32),
     ]

time: 48 us -> 44.9 us (0.935)
  starting transfers between devices: 7.7 us -> 5.73 us
  other arithmetic: 1.25 us -> 0 us
  waiting for transfers between devices: 0.01 us -> 0.87 us
  blocking collectives: 16.8 us -> 16.2 us
    all_to_all x1, starting transfers between devices: 7.1 us -> 5.13 us  [exchange(): lax.all_to_all(array, 'req', split_axis=0, concat_axis=0, tiled=True, axi...]
    pallas_call x2 -> x0, other arithmetic: 1.25 us -> none  [body(): pl.pallas_call(functools.partial(attend_route_kernel, capacity), out_shap...]
    all_to_all x1, waiting for transfers between devices: 0.01 us -> 0.86 us  [exchange(): lax.all_to_all(array, 'req', split_axis=0, concat_axis=0, tiled=True, axi...]
    pallas_call x1, Pallas kernels: 7.52 us -> 8.11 us  [body(): pl.pallas_call(functools.partial(attend_route_kernel, capacity), out_shap...]
    all_to_all x1, blocking collectives: 16.8 us -> 16.2 us  [exchange(): lax.all_to_all(array, 'req', split_axis=0, concat_axis=0, tiled=True, axi...]
    pallas_call x1, Pallas kernels: 6.37 us -> 5.87 us  [body(): pl.pallas_call(functools.partial(expert_kernel, capacity), out_shape=like...]
  transfers between devices with their start and end apart: 3 -> 3, of which waited for: 0 -> 1; matrix products, arithmetic and copies ran while one was open for 3% -> 0% of each run, Pallas kernels for 30% -> 32%
where the time goes in v15:
time: 44.9 us; the launch traced here: 44.5 us
  Pallas kernels  21 us (47%)
  blocking collectives  16.2 us (36%)
  starting transfers between devices  5.73 us (13%)
  waiting for transfers between devices  0.87 us (2%)
  between operations  0.71 us (2%)
    all_to_all x1, blocking collectives, exchange(): lax.all_to_all(array, 'req', split_axis=0, concat_axis=0, tiled=True, axi...  16.2 us
    pallas_call x1, Pallas kernels, body(): pl.pallas_call(functools.partial(attend_route_kernel, capacity), out_shap...  8.11 us
    pallas_call x1, Pallas kernels, body(): pl.pallas_call(refresh_kernel, out_shape=like(kv_pool.shape), in_specs=sc...  6.2 us
    pallas_call x1, Pallas kernels, body(): pl.pallas_call(functools.partial(expert_kernel, capacity), out_shape=like...  5.87 us
    all_to_all x1, starting transfers between devices, exchange(): lax.all_to_all(array, 'req', split_axis=0, concat_axis=0, tiled=True, axi...  5.13 us
  transfers between devices with their start and end apart: 3, of which 1 were waited for; matrix products, arithmetic and copies ran while one was open for 0% of the time, Pallas kernels for 32%

profile of v15, /device:TPU:0, one launch (start us, length us, event | category | flops | bytes accessed | tf_op | source)
XLA Modules:
  0.0 44.5 jit_solution(14468497922450844008)
XLA Ops:
  0.6 0.5 %collective-permute-start = (bf16[1,2,704,2048]{3,2,1,0:T(8,128)(2,1)}, bf16[1,2,704,2048]{3,2,1,0:T(8,128)(2,1)S(1)}, u32[]{:S(2)}, u32[]{:S(2)}) collective-permute-start(bf16[1,2,704,2048]{3,2,1,0:T(8,128)(2,1)} %own_up.1), channel_id=1, source_target_pairs={{0,1},{1,0},{2,3},{3,2},{4,5},{5,4},{6,7},{7,6},{8,9},{9,8},{10,11... | collective-permute-start | bytes 17301512 | tf_op jit(solution)/shard_map/ppermute | solution.py:371
  1.1 0.1 collective-permute-start.1
  1.2 8.1 %shard_map.147 = (bf16[8,2048]{1,0:T(8,128)(2,1)S(1)}, f32[1,8]{1,0:T(1,128)}, f32[1,8]{1,0:T(1,128)}, bf16[256,512]{1,0:T(8,128)(2,1)S(1)}, f32[8,256]{1,0:T(8,128)S(1)}) custom-call(s32[8,20]{1,0:T(8,128)} %table.1, s32[8]{0:T(128)} %lengths.1, bf16[8,2048]{1,0:T(8,128)(2,1)} %refs_2_.1, bf16[8,4,256]{2,1,0:T(4,128)(2,1)} %fresh.1, ...), custom_call_target="tpu_custom_call" | custom-call | tf_op jit(solution)/shard_map/pallas_call | solution.py:400
  9.3 16.2 %all_to_all.10 = bf16[16,16,512]{2,1,0:T(8,128)(2,1)S(1)} all-to-all(bf16[16,16,512]{2,1,0:T(8,128)(2,1)S(1)} %bitcast.8), channel_id=1, replica_groups={{12,14,8,10,4,6,0,2,28,30,24,26,20,22,16,18},{19,17,23,21,27,25,31,29,3..., dimensions={0} | all-to-all | bytes 524288 | tf_op jit(solution)/shard_map/all_to_all | solution.py:438
  25.6 0.0 collective-permute-done.1.other_down
  25.6 0.0 collective-permute-done.other_up
  25.6 0.0 copy-start
  25.6 0.0 copy-start.1
  25.6 0.0 copy-start.2
  25.6 0.0 copy-start.3
  25.6 5.9 %shard_map.148 = bf16[256,512]{1,0:T(8,128)(2,1)} custom-call(bf16[256,512]{1,0:T(8,128)(2,1)S(1)} %bitcast.6, bf16[1,2,704,2048]{3,2,1,0:T(8,128)(2,1)} %own_up.1, bf16[1,704,2048]{2,1,0:T(8,128)(2,1)} %own_down.1, bf16[1,2,704,2048]{3,2,1,0:T(8,128)(2,1)S(1)} %collective-permute-done.other_up, bf16[1,704,2048]{2,1,0:T(8,128)(2,1)S(1)} %collective-permute-done.1.other_down), custom_call_target="tpu_custom_call" | custom-call | tf_op jit(solution)/shard_map/pallas_call | solution.py:446
  31.5 5.1 %all-to-all-start.1 = ((bf16[16,16,512]{2,1,0:T(8,128)(2,1)}), bf16[16,16,512]{2,1,0:T(8,128)(2,1)S(1)}, u32[]{:S(2)}, u32[]{:S(2)}) async-start(bf16[16,16,512]{2,1,0:T(8,128)(2,1)} %bitcast.2), calls=%async_computation.1 | async-start | bytes 524288 | tf_op jit(solution)/shard_map/all_to_all | solution.py:438
  36.6 0.0 copy-done
  36.6 0.0 copy-done.1
  36.6 0.0 copy-done.2
  36.6 0.0 copy-done.3
  36.6 6.2 %shard_map.150 = bf16[104,32,4,256]{3,2,1,0:T(4,128)(2,1)} custom-call(s32[8,20]{1,0:T(8,128)S(1)} %copy-done.1, s32[8]{0:T(128)S(1)} %copy-done.2, bf16[8,4,256]{2,1,0:T(4,128)(2,1)S(1)} %copy-done, f32[1,8]{1,0:T(1,128)S(1)} %copy-done.3, bf16[104,32,4,256]{3,2,1,0:T(4,128)(2,1)} %pool.1), custom_call_target="tpu_custom_call" | custom-call | bytes 27262976 | tf_op jit(solution)/shard_map/pallas_call | solution.py:426
  42.9 0.9 %all-to-all-done.1 = bf16[16,16,512]{2,1,0:T(8,128)(2,1)S(1)} async-done(((bf16[16,16,512]{2,1,0:T(8,128)(2,1)}), bf16[16,16,512]{2,1,0:T(8,128)(2,1)S(1)}, u32[]{:S(2)}, u32[]{:S(2)}) %all-to-all-start.1) | async-done | bytes 262176 | tf_op jit(solution)/shard_map/all_to_all | solution.py:438
  43.7 0.8 %shard_map.149 = bf16[8,2048]{1,0:T(8,128)(2,1)} custom-call(f32[8,256]{1,0:T(8,128)S(1)} %get-tuple-element.9.comb, bf16[256,512]{1,0:T(8,128)(2,1)S(1)} %bitcast.7, bf16[8,2048]{1,0:T(8,128)(2,1)S(1)} %get-tuple-element.11.mixed), custom_call_target="tpu_custom_call" | custom-call | tf_op jit(solution)/shard_map/pallas_call | solution.py:463
Async XLA Ops:
  0.6 24.9 %collective-permute-start = (bf16[1,2,704,2048]{3,2,1,0:T(8,128)(2,1)}, bf16[1,2,704,2048]{3,2,1,0:T(8,128)(2,1)S(1)}, u32[]{:S(2)}, u32[]{:S(2)}) collective-permute-start(bf16[1,2,704,2048]{3,2,1,0:T(8,128)(2,1)} %own_up.1), channel_id=1, source_target_pairs={{0,1},{1,0},{2,3},{3,2},{4,5},{5,4},{6,7},{7,6},{8,9},{9,8},{10,11... | collective-permute-start | bytes 17301512 | tf_op jit(solution)/shard_map/ppermute | solution.py:371
  1.1 24.4 %collective-permute-start.1 = (bf16[1,704,2048]{2,1,0:T(8,128)(2,1)}, bf16[1,704,2048]{2,1,0:T(8,128)(2,1)S(1)}, u32[]{:S(2)}, u32[]{:S(2)}) collective-permute-start(bf16[1,704,2048]{2,1,0:T(8,128)(2,1)} %own_down.1), channel_id=1, source_target_pairs={{0,1},{1,0},{2,3},{3,2},{4,5},{5,4},{6,7},{7,6},{8,9},{9,8},{10,11... | collective-permute-start | bytes 8650760 | tf_op jit(solution)/shard_map/ppermute | solution.py:372
  25.6 11.0 %copy-start = (bf16[8,4,256]{2,1,0:T(4,128)(2,1)S(1)}, bf16[8,4,256]{2,1,0:T(4,128)(2,1)}, u32[]{:S(2)}) copy-start(bf16[8,4,256]{2,1,0:T(4,128)(2,1)} %fresh.1) | copy-start | bytes 49156
  25.6 11.1 %copy-start.1 = (s32[8,20]{1,0:T(8,128)S(1)}, s32[8,20]{1,0:T(8,128)}, u32[]{:S(2)}) copy-start(s32[8,20]{1,0:T(8,128)} %table.1) | copy-start | bytes 1924
  25.6 11.0 %copy-start.2 = (s32[8]{0:T(128)S(1)}, s32[8]{0:T(128)}, u32[]{:S(2)}) copy-start(s32[8]{0:T(128)} %lengths.1) | copy-start | bytes 100
  25.6 11.0 %copy-start.3 = (f32[1,8]{1,0:T(1,128)S(1)}, f32[1,8]{1,0:T(1,128)}, u32[]{:S(2)}) copy-start(f32[1,8]{1,0:T(1,128)} %get-tuple-element.12.after) | copy-start | bytes 100
  31.5 12.2 %all-to-all-start.1 = ((bf16[16,16,512]{2,1,0:T(8,128)(2,1)}), bf16[16,16,512]{2,1,0:T(8,128)(2,1)S(1)}, u32[]{:S(2)}, u32[]{:S(2)}) async-start(bf16[16,16,512]{2,1,0:T(8,128)(2,1)} %bitcast.2), calls=%async_computation.1 | async-start | bytes 524288 | tf_op jit(solution)/shard_map/all_to_all | solution.py:438

commit v16 on v15

--- a/solution.py
+++ b/solution.py
@@ -30,7 +30,7 @@
 
 
 def group_turn(chips, part):
-    return chips * 9 // 16 if part % 2 else chips * 3 // 8
+    return chips * 9 // 16 if part % 2 else chips * 11 // 16
 
 
 def pool_half(array, i):
@@ -48,22 +48,28 @@
     page_rows = page_len * heads_kv
     pool, weight = refs[-2:]
     loads = copies(list(zip(refs[:4], small[:4])), sems)
-    key_load, value_load = copies([(pool_half(pool, 0), keys), (pool_half(pool, 1), values)], sems, 4)
-    later = copies(list(zip(refs[4:-2], small[4:])), sems, 6)
-    step = weight.shape[0] // 4
-    spans = [pl.ds(i * step, step) for i in range(4)]
-    weight_loads = copies([(weight.at[span], kept_weight.at[span]) for span in spans], sems, 10)
-    for copy in loads + [key_load]:
+    page_step = -(-pages // 4)
+    page_spans = [pl.ds(first, min(page_step, pages - first)) for first in range(0, pages, page_step)]
+    key_loads, value_loads = [
+        copies(
+            [(pool_half(pool, i).at[span], kept.at[span]) for span in page_spans], sems, 4 + i * len(page_spans)
+        )
+        for i, kept in enumerate((keys, values))
+    ]
+    step = weight.shape[0] // 2
+    spans = [pl.ds(i * step, step) for i in range(2)]
+    weight_loads = copies([(weight.at[span], kept_weight.at[span]) for span in spans], sems, 12)
+    later = copies(list(zip(refs[4:-2], small[4:])), sems, 14)
+    for copy in loads + key_loads + value_loads + weight_loads + later:
         copy.start()
     for copy in loads:
         copy.wait()
-    for copy in [value_load] + later + weight_loads[:1]:
-        copy.start()
     for h in range(heads):
         qs[pl.ds(h * requests, requests), :] = q_ref[:, pl.ds(h * head_dim, head_dim)].astype(F32)
     spots = [(table[r, lengths[r] // page_len], lengths[r] % page_len) for r in range(requests)]
 
-    key_load.wait()
+    for copy in key_loads:
+        copy.wait()
     for r, (page, slot) in enumerate(spots):
         keys[page, slot] = fresh[r][:, :head_dim]
     key_pages = keys.reshape(pages, page_rows, head_dim)
@@ -75,7 +81,6 @@
     def pages_of(array, r, first, last):
         return jnp.concatenate([array[table[r, j]] for j in range(first, last)], axis=0)
 
-    weight_loads[1].start()
     query = [qs[pl.ds(r, heads, stride=requests), :] for r in range(requests)]
     query_rows = jnp.concatenate(query, axis=0).astype(BF16)
     scores[:, :shared_columns] = dot(query_rows, pages_of(key_pages, 0, 0, SHARED_PAGES), NT)
@@ -98,9 +103,8 @@
     sums = jnp.sum(exponent, axis=1, keepdims=True)
     probs[...] = exponent.astype(BF16)
 
-    value_load.wait()
-    for copy in weight_loads[2:]:
-        copy.start()
+    for copy in value_loads:
+        copy.wait()
     for r, (page, slot) in enumerate(spots):
         values[page, slot] = fresh[r][:, head_dim:]
     shared = dot(probs[:, :shared_columns], pages_of(value_pages, 0, 0, SHARED_PAGES))
@@ -379,7 +383,7 @@
         pltpu.VMEM((heads * requests, head_dim), F32),
         pltpu.VMEM((requests * heads, page_table.shape[1] * page_len * heads_kv), F32),
         pltpu.VMEM((requests * heads, page_table.shape[1] * page_len * heads_kv), BF16),
-        pltpu.SemaphoreType.DMA((14,)),
+        pltpu.SemaphoreType.DMA((18,)),
     ]
 
     def small(*arrays):

time: 44.9 us -> 44.9 us (level)
  starting transfers between devices: 5.73 us -> 8.27 us
  blocking collectives: 16.2 us -> 14.6 us
  waiting for transfers between devices: 0.87 us -> 0.01 us
    all_to_all x1, starting transfers between devices: 5.13 us -> 7.67 us  [exchange(): lax.all_to_all(array, 'req', split_axis=0, concat_axis=0, tiled=True, axi...]
    all_to_all x1, blocking collectives: 16.2 us -> 14.6 us  [exchange(): lax.all_to_all(array, 'req', split_axis=0, concat_axis=0, tiled=True, axi...]
    all_to_all x1, waiting for transfers between devices: 0.86 us -> 0.01 us  [exchange(): lax.all_to_all(array, 'req', split_axis=0, concat_axis=0, tiled=True, axi...]
  transfers between devices with their start and end apart: 3 -> 3, of which waited for: 1 -> 0; matrix products, arithmetic and copies ran while one was open for 0% -> 0% of each run, Pallas kernels for 32% -> 32%
where the time goes in v16:
time: 44.9 us; the launch traced here: 44.5 us
  Pallas kernels  21 us (47%)
  blocking collectives  14.6 us (33%)
  starting transfers between devices  8.27 us (18%)
  between operations  0.72 us (2%)
    all_to_all x1, blocking collectives, exchange(): lax.all_to_all(array, 'req', split_axis=0, concat_axis=0, tiled=True, axi...  14.6 us
    pallas_call x1, Pallas kernels, body(): pl.pallas_call(functools.partial(attend_route_kernel, capacity), out_shap...  8.07 us
    all_to_all x1, starting transfers between devices, exchange(): lax.all_to_all(array, 'req', split_axis=0, concat_axis=0, tiled=True, axi...  7.67 us
    pallas_call x1, Pallas kernels, body(): pl.pallas_call(refresh_kernel, out_shape=like(kv_pool.shape), in_specs=sc...  6.23 us
    pallas_call x1, Pallas kernels, body(): pl.pallas_call(functools.partial(expert_kernel, capacity), out_shape=like...  5.87 us
  transfers between devices with their start and end apart: 3, of which 0 were waited for; matrix products, arithmetic and copies ran while one was open for 0% of the time, Pallas kernels for 32%

profile of v16, /device:TPU:0, one launch (start us, length us, event | category | flops | bytes accessed | tf_op | source)
XLA Modules:
  0.0 44.5 jit_solution(5277059357798333020)
XLA Ops:
  0.6 0.5 %collective-permute-start = (bf16[1,2,704,2048]{3,2,1,0:T(8,128)(2,1)}, bf16[1,2,704,2048]{3,2,1,0:T(8,128)(2,1)S(1)}, u32[]{:S(2)}, u32[]{:S(2)}) collective-permute-start(bf16[1,2,704,2048]{3,2,1,0:T(8,128)(2,1)} %own_up.1), channel_id=1, source_target_pairs={{0,1},{1,0},{2,3},{3,2},{4,5},{5,4},{6,7},{7,6},{8,9},{9,8},{10,11... | collective-permute-start | bytes 17301512 | tf_op jit(solution)/shard_map/ppermute | solution.py:375
  1.1 0.1 collective-permute-start.1
  1.2 8.1 %shard_map.147 = (bf16[8,2048]{1,0:T(8,128)(2,1)S(1)}, f32[1,8]{1,0:T(1,128)}, f32[1,8]{1,0:T(1,128)}, bf16[256,512]{1,0:T(8,128)(2,1)S(1)}, f32[8,256]{1,0:T(8,128)S(1)}) custom-call(s32[8,20]{1,0:T(8,128)} %table.1, s32[8]{0:T(128)} %lengths.1, bf16[8,2048]{1,0:T(8,128)(2,1)} %refs_2_.1, bf16[8,4,256]{2,1,0:T(4,128)(2,1)} %fresh.1, ...), custom_call_target="tpu_custom_call" | custom-call | tf_op jit(solution)/shard_map/pallas_call | solution.py:404
  9.3 14.6 %all_to_all.10 = bf16[16,16,512]{2,1,0:T(8,128)(2,1)S(1)} all-to-all(bf16[16,16,512]{2,1,0:T(8,128)(2,1)S(1)} %bitcast.8), channel_id=1, replica_groups={{22,20,18,16,30,28,26,24,6,4,2,0,14,12,10,8},{19,17,23,21,27,25,31,29,3..., dimensions={0} | all-to-all | bytes 524288 | tf_op jit(solution)/shard_map/all_to_all | solution.py:442
  23.9 0.0 collective-permute-done.1.other_down
  23.9 0.0 collective-permute-done.other_up
  23.9 0.0 copy-start
  23.9 0.0 copy-start.1
  23.9 0.0 copy-start.2
  23.9 0.0 copy-start.3
  23.9 5.9 %shard_map.148 = bf16[256,512]{1,0:T(8,128)(2,1)} custom-call(bf16[256,512]{1,0:T(8,128)(2,1)S(1)} %bitcast.6, bf16[1,2,704,2048]{3,2,1,0:T(8,128)(2,1)} %own_up.1, bf16[1,704,2048]{2,1,0:T(8,128)(2,1)} %own_down.1, bf16[1,2,704,2048]{3,2,1,0:T(8,128)(2,1)S(1)} %collective-permute-done.other_up, bf16[1,704,2048]{2,1,0:T(8,128)(2,1)S(1)} %collective-permute-done.1.other_down), custom_call_target="tpu_custom_call" | custom-call | tf_op jit(solution)/shard_map/pallas_call | solution.py:450
  29.8 7.7 %all-to-all-start.1 = ((bf16[16,16,512]{2,1,0:T(8,128)(2,1)}), bf16[16,16,512]{2,1,0:T(8,128)(2,1)S(1)}, u32[]{:S(2)}, u32[]{:S(2)}) async-start(bf16[16,16,512]{2,1,0:T(8,128)(2,1)} %bitcast.2), calls=%async_computation.1 | async-start | bytes 524288 | tf_op jit(solution)/shard_map/all_to_all | solution.py:442
  37.5 0.0 copy-done
  37.5 0.0 copy-done.1
  37.5 0.0 copy-done.2
  37.5 0.0 copy-done.3
  37.5 6.2 %shard_map.150 = bf16[104,32,4,256]{3,2,1,0:T(4,128)(2,1)} custom-call(s32[8,20]{1,0:T(8,128)S(1)} %copy-done.1, s32[8]{0:T(128)S(1)} %copy-done.2, bf16[8,4,256]{2,1,0:T(4,128)(2,1)S(1)} %copy-done, f32[1,8]{1,0:T(1,128)S(1)} %copy-done.3, bf16[104,32,4,256]{3,2,1,0:T(4,128)(2,1)} %pool.1), custom_call_target="tpu_custom_call" | custom-call | bytes 27262976 | tf_op jit(solution)/shard_map/pallas_call | solution.py:430
  43.7 0.0 all-to-all-done.1
  43.8 0.8 %shard_map.149 = bf16[8,2048]{1,0:T(8,128)(2,1)} custom-call(f32[8,256]{1,0:T(8,128)S(1)} %get-tuple-element.9.comb, bf16[256,512]{1,0:T(8,128)(2,1)S(1)} %bitcast.7, bf16[8,2048]{1,0:T(8,128)(2,1)S(1)} %get-tuple-element.11.mixed), custom_call_target="tpu_custom_call" | custom-call | tf_op jit(solution)/shard_map/pallas_call | solution.py:467
Async XLA Ops:
  0.6 23.2 %collective-permute-start = (bf16[1,2,704,2048]{3,2,1,0:T(8,128)(2,1)}, bf16[1,2,704,2048]{3,2,1,0:T(8,128)(2,1)S(1)}, u32[]{:S(2)}, u32[]{:S(2)}) collective-permute-start(bf16[1,2,704,2048]{3,2,1,0:T(8,128)(2,1)} %own_up.1), channel_id=1, source_target_pairs={{0,1},{1,0},{2,3},{3,2},{4,5},{5,4},{6,7},{7,6},{8,9},{9,8},{10,11... | collective-permute-start | bytes 17301512 | tf_op jit(solution)/shard_map/ppermute | solution.py:375
  1.1 22.7 %collective-permute-start.1 = (bf16[1,704,2048]{2,1,0:T(8,128)(2,1)}, bf16[1,704,2048]{2,1,0:T(8,128)(2,1)S(1)}, u32[]{:S(2)}, u32[]{:S(2)}) collective-permute-start(bf16[1,704,2048]{2,1,0:T(8,128)(2,1)} %own_down.1), channel_id=1, source_target_pairs={{0,1},{1,0},{2,3},{3,2},{4,5},{5,4},{6,7},{7,6},{8,9},{9,8},{10,11... | collective-permute-start | bytes 8650760 | tf_op jit(solution)/shard_map/ppermute | solution.py:376
  23.9 13.6 %copy-start = (bf16[8,4,256]{2,1,0:T(4,128)(2,1)S(1)}, bf16[8,4,256]{2,1,0:T(4,128)(2,1)}, u32[]{:S(2)}) copy-start(bf16[8,4,256]{2,1,0:T(4,128)(2,1)} %fresh.1) | copy-start | bytes 49156
  23.9 13.6 %copy-start.1 = (s32[8,20]{1,0:T(8,128)S(1)}, s32[8,20]{1,0:T(8,128)}, u32[]{:S(2)}) copy-start(s32[8,20]{1,0:T(8,128)} %table.1) | copy-start | bytes 1924
  23.9 13.6 %copy-start.2 = (s32[8]{0:T(128)S(1)}, s32[8]{0:T(128)}, u32[]{:S(2)}) copy-start(s32[8]{0:T(128)} %lengths.1) | copy-start | bytes 100
  23.9 13.6 %copy-start.3 = (f32[1,8]{1,0:T(1,128)S(1)}, f32[1,8]{1,0:T(1,128)}, u32[]{:S(2)}) copy-start(f32[1,8]{1,0:T(1,128)} %get-tuple-element.12.after) | copy-start | bytes 100
  29.8 13.9 %all-to-all-start.1 = ((bf16[16,16,512]{2,1,0:T(8,128)(2,1)}), bf16[16,16,512]{2,1,0:T(8,128)(2,1)S(1)}, u32[]{:S(2)}, u32[]{:S(2)}) async-start(bf16[16,16,512]{2,1,0:T(8,128)(2,1)} %bitcast.2), calls=%async_computation.1 | async-start | bytes 524288 | tf_op jit(solution)/shard_map/all_to_all | solution.py:442

commit v17 on v16

--- a/solution.py
+++ b/solution.py
@@ -12,7 +12,6 @@
 F32 = jnp.float32
 NT = (((1,), (1,)), ((), ()))
 NN = (((1,), (0,)), ((), ()))
-SHARED_PAGES = 8
 SLAB = 16
 MIB = 1 << 20
 
@@ -30,7 +29,7 @@
 
 
 def group_turn(chips, part):
-    return chips * 9 // 16 if part % 2 else chips * 11 // 16
+    return chips * 9 // 16 if part % 2 else chips * 3 // 8
 
 
 def pool_half(array, i):
@@ -39,7 +38,7 @@
 
 
 def attend(refs, keys, values, scratch):
-    small, (kept_weight, qs, att, scores, probs, sems) = scratch
+    small, (kept_weight, qs, att, probs, sums, sems) = scratch
     table, lengths, q_ref, fresh = small[:4]
     requests, max_pages = table.shape
     pages, page_len, heads_kv, head_dim = keys.shape
@@ -75,46 +74,25 @@
     key_pages = keys.reshape(pages, page_rows, head_dim)
     value_pages = values.reshape(pages, page_rows, head_dim)
     columns = max_pages * page_rows
-    shared_columns = SHARED_PAGES * page_rows
-    rows = requests * heads
-
-    def pages_of(array, r, first, last):
-        return jnp.concatenate([array[table[r, j]] for j in range(first, last)], axis=0)
-
-    query = [qs[pl.ds(r, heads, stride=requests), :] for r in range(requests)]
-    query_rows = jnp.concatenate(query, axis=0).astype(BF16)
-    scores[:, :shared_columns] = dot(query_rows, pages_of(key_pages, 0, 0, SHARED_PAGES), NT)
-    for r in range(requests):
-        scores[pl.ds(r * heads, heads), shared_columns:] = dot(
-            query[r].astype(BF16), pages_of(key_pages, r, SHARED_PAGES, max_pages), NT
-        )
     lane = iota((heads, columns), 1)
     own_head = (lane & (heads_kv - 1)) == iota((heads, columns), 0) // group
-    position = lane >> (heads_kv.bit_length() - 1)
-    masked = jnp.concatenate(
-        [
-            jnp.where(own_head & (position <= lengths[r]), scores[pl.ds(r * heads, heads), :], -1e30)
-            for r in range(requests)
-        ],
-        axis=0,
-    )
-    scale = 1.0 / math.sqrt(head_dim)
-    exponent = jnp.exp((masked - jnp.max(masked, axis=1, keepdims=True)) * scale)
-    sums = jnp.sum(exponent, axis=1, keepdims=True)
-    probs[...] = exponent.astype(BF16)
+    position = jnp.where(own_head, lane >> (heads_kv.bit_length() - 1), columns)
+    scale = math.log2(math.e) / math.sqrt(head_dim)
+    for r in range(requests):
+        query = qs[pl.ds(r, heads, stride=requests), :].astype(BF16)
+        gathered = jnp.concatenate([key_pages[table[r, j]] for j in range(max_pages)], axis=0)
+        scores = jnp.where(position <= lengths[r], dot(query, gathered, NT), -1e30)
+        exponent = jnp.exp2((scores - jnp.max(scores, axis=1, keepdims=True)) * scale)
+        sums[r] = jnp.broadcast_to(jnp.sum(exponent, axis=1, keepdims=True), (heads, head_dim))
+        probs[r] = exponent.astype(BF16)
 
     for copy in value_loads:
         copy.wait()
     for r, (page, slot) in enumerate(spots):
         values[page, slot] = fresh[r][:, head_dim:]
-    shared = dot(probs[:, :shared_columns], pages_of(value_pages, 0, 0, SHARED_PAGES))
-    own = [
-        dot(probs[pl.ds(r * heads, heads), shared_columns:], pages_of(value_pages, r, SHARED_PAGES, max_pages))
-        for r in range(requests)
-    ]
-    mean = (shared + jnp.concatenate(own, axis=0)) / sums
     for r in range(requests):
-        att[pl.ds(r, heads, stride=requests), :] = mean[r * heads : (r + 1) * heads]
+        gathered = jnp.concatenate([value_pages[table[r, j]] for j in range(max_pages)], axis=0)
+        att[pl.ds(r, heads, stride=requests), :] = dot(probs[r], gathered) / sums[r]
     attended = jnp.concatenate(
         [att[pl.ds(h * requests, requests), :] for h in range(heads)], axis=1
     ).astype(BF16)
@@ -381,8 +359,8 @@
         pltpu.VMEM(out_weight.shape, BF16),
         pltpu.VMEM((heads * requests, head_dim), F32),
         pltpu.VMEM((heads * requests, head_dim), F32),
-        pltpu.VMEM((requests * heads, page_table.shape[1] * page_len * heads_kv), F32),
-        pltpu.VMEM((requests * heads, page_table.shape[1] * page_len * heads_kv), BF16),
+        pltpu.VMEM((requests, heads, page_table.shape[1] * page_len * heads_kv), BF16),
+        pltpu.VMEM((requests, heads, head_dim), F32),
         pltpu.SemaphoreType.DMA((18,)),
     ]
 

time: 44.9 us -> 44.8 us (level)
  starting transfers between devices: 8.27 us -> 5.73 us
  blocking collectives: 14.6 us -> 16.2 us
  waiting for transfers between devices: 0.01 us -> 0.84 us
    all_to_all x1, starting transfers between devices: 7.67 us -> 5.13 us  [exchange(): lax.all_to_all(array, 'req', split_axis=0, concat_axis=0, tiled=True, axi...]
    all_to_all x1, blocking collectives: 14.6 us -> 16.2 us  [exchange(): lax.all_to_all(array, 'req', split_axis=0, concat_axis=0, tiled=True, axi...]
    all_to_all x1, waiting for transfers between devices: 0.01 us -> 0.84 us  [exchange(): lax.all_to_all(array, 'req', split_axis=0, concat_axis=0, tiled=True, axi...]
  transfers between devices with their start and end apart: 3 -> 3, of which waited for: 0 -> 1; matrix products, arithmetic and copies ran while one was open for 0% -> 0% of each run, Pallas kernels for 32% -> 32%
where the time goes in v17:
time: 44.8 us; the launch traced here: 44.5 us
  Pallas kernels  21 us (47%)
  blocking collectives  16.2 us (36%)
  starting transfers between devices  5.73 us (13%)
  waiting for transfers between devices  0.84 us (2%)
  between operations  0.71 us (2%)
    all_to_all x1, blocking collectives, exchange(): lax.all_to_all(array, 'req', split_axis=0, concat_axis=0, tiled=True, axi...  16.2 us
    pallas_call x1, Pallas kernels, body(): pl.pallas_call(functools.partial(attend_route_kernel, capacity), out_shap...  8.07 us
    pallas_call x1, Pallas kernels, body(): pl.pallas_call(refresh_kernel, out_shape=like(kv_pool.shape), in_specs=sc...  6.23 us
    pallas_call x1, Pallas kernels, body(): pl.pallas_call(functools.partial(expert_kernel, capacity), out_shape=like...  5.87 us
    all_to_all x1, starting transfers between devices, exchange(): lax.all_to_all(array, 'req', split_axis=0, concat_axis=0, tiled=True, axi...  5.13 us
  transfers between devices with their start and end apart: 3, of which 1 were waited for; matrix products, arithmetic and copies ran while one was open for 0% of the time, Pallas kernels for 32%

profile of v17, /device:TPU:0, one launch (start us, length us, event | category | flops | bytes accessed | tf_op | source)
XLA Modules:
  0.0 44.5 jit_solution(6261233045464707291)
XLA Ops:
  0.6 0.5 %collective-permute-start = (bf16[1,2,704,2048]{3,2,1,0:T(8,128)(2,1)}, bf16[1,2,704,2048]{3,2,1,0:T(8,128)(2,1)S(1)}, u32[]{:S(2)}, u32[]{:S(2)}) collective-permute-start(bf16[1,2,704,2048]{3,2,1,0:T(8,128)(2,1)} %own_up.1), channel_id=1, source_target_pairs={{0,1},{1,0},{2,3},{3,2},{4,5},{5,4},{6,7},{7,6},{8,9},{9,8},{10,11... | collective-permute-start | bytes 17301512 | tf_op jit(solution)/shard_map/ppermute | solution.py:353
  1.1 0.1 collective-permute-start.1
  1.2 8.1 %shard_map.147 = (bf16[8,2048]{1,0:T(8,128)(2,1)S(1)}, f32[1,8]{1,0:T(1,128)}, f32[1,8]{1,0:T(1,128)}, bf16[256,512]{1,0:T(8,128)(2,1)S(1)}, f32[8,256]{1,0:T(8,128)S(1)}) custom-call(s32[8,20]{1,0:T(8,128)} %table.1, s32[8]{0:T(128)} %lengths.1, bf16[8,2048]{1,0:T(8,128)(2,1)} %refs_2_.1, bf16[8,4,256]{2,1,0:T(4,128)(2,1)} %fresh.1, ...), custom_call_target="tpu_custom_call" | custom-call | tf_op jit(solution)/shard_map/pallas_call | solution.py:382
  9.3 16.2 %all_to_all.10 = bf16[16,16,512]{2,1,0:T(8,128)(2,1)S(1)} all-to-all(bf16[16,16,512]{2,1,0:T(8,128)(2,1)S(1)} %bitcast.8), channel_id=1, replica_groups={{12,14,8,10,4,6,0,2,28,30,24,26,20,22,16,18},{19,17,23,21,27,25,31,29,3..., dimensions={0} | all-to-all | bytes 524288 | tf_op jit(solution)/shard_map/all_to_all | solution.py:420
  25.5 0.0 collective-permute-done.1.other_down
  25.5 0.0 collective-permute-done.other_up
  25.5 0.0 copy-start
  25.5 0.0 copy-start.1
  25.5 0.0 copy-start.2
  25.5 0.0 copy-start.3
  25.6 5.9 %shard_map.148 = bf16[256,512]{1,0:T(8,128)(2,1)} custom-call(bf16[256,512]{1,0:T(8,128)(2,1)S(1)} %bitcast.6, bf16[1,2,704,2048]{3,2,1,0:T(8,128)(2,1)} %own_up.1, bf16[1,704,2048]{2,1,0:T(8,128)(2,1)} %own_down.1, bf16[1,2,704,2048]{3,2,1,0:T(8,128)(2,1)S(1)} %collective-permute-done.other_up, bf16[1,704,2048]{2,1,0:T(8,128)(2,1)S(1)} %collective-permute-done.1.other_down), custom_call_target="tpu_custom_call" | custom-call | tf_op jit(solution)/shard_map/pallas_call | solution.py:428
  31.4 5.1 %all-to-all-start.1 = ((bf16[16,16,512]{2,1,0:T(8,128)(2,1)}), bf16[16,16,512]{2,1,0:T(8,128)(2,1)S(1)}, u32[]{:S(2)}, u32[]{:S(2)}) async-start(bf16[16,16,512]{2,1,0:T(8,128)(2,1)} %bitcast.2), calls=%async_computation.1 | async-start | bytes 524288 | tf_op jit(solution)/shard_map/all_to_all | solution.py:420
  36.6 0.0 copy-done
  36.6 0.0 copy-done.1
  36.6 0.0 copy-done.2
  36.6 0.0 copy-done.3
  36.6 6.2 %shard_map.150 = bf16[104,32,4,256]{3,2,1,0:T(4,128)(2,1)} custom-call(s32[8,20]{1,0:T(8,128)S(1)} %copy-done.1, s32[8]{0:T(128)S(1)} %copy-done.2, bf16[8,4,256]{2,1,0:T(4,128)(2,1)S(1)} %copy-done, f32[1,8]{1,0:T(1,128)S(1)} %copy-done.3, bf16[104,32,4,256]{3,2,1,0:T(4,128)(2,1)} %pool.1), custom_call_target="tpu_custom_call" | custom-call | bytes 27262976 | tf_op jit(solution)/shard_map/pallas_call | solution.py:408
  42.8 0.8 %all-to-all-done.1 = bf16[16,16,512]{2,1,0:T(8,128)(2,1)S(1)} async-done(((bf16[16,16,512]{2,1,0:T(8,128)(2,1)}), bf16[16,16,512]{2,1,0:T(8,128)(2,1)S(1)}, u32[]{:S(2)}, u32[]{:S(2)}) %all-to-all-start.1) | async-done | bytes 262176 | tf_op jit(solution)/shard_map/all_to_all | solution.py:420
  43.7 0.8 %shard_map.149 = bf16[8,2048]{1,0:T(8,128)(2,1)} custom-call(f32[8,256]{1,0:T(8,128)S(1)} %get-tuple-element.9.comb, bf16[256,512]{1,0:T(8,128)(2,1)S(1)} %bitcast.7, bf16[8,2048]{1,0:T(8,128)(2,1)S(1)} %get-tuple-element.11.mixed), custom_call_target="tpu_custom_call" | custom-call | tf_op jit(solution)/shard_map/pallas_call | solution.py:445
Async XLA Ops:
  0.6 24.9 %collective-permute-start = (bf16[1,2,704,2048]{3,2,1,0:T(8,128)(2,1)}, bf16[1,2,704,2048]{3,2,1,0:T(8,128)(2,1)S(1)}, u32[]{:S(2)}, u32[]{:S(2)}) collective-permute-start(bf16[1,2,704,2048]{3,2,1,0:T(8,128)(2,1)} %own_up.1), channel_id=1, source_target_pairs={{0,1},{1,0},{2,3},{3,2},{4,5},{5,4},{6,7},{7,6},{8,9},{9,8},{10,11... | collective-permute-start | bytes 17301512 | tf_op jit(solution)/shard_map/ppermute | solution.py:353
  1.1 24.4 %collective-permute-start.1 = (bf16[1,704,2048]{2,1,0:T(8,128)(2,1)}, bf16[1,704,2048]{2,1,0:T(8,128)(2,1)S(1)}, u32[]{:S(2)}, u32[]{:S(2)}) collective-permute-start(bf16[1,704,2048]{2,1,0:T(8,128)(2,1)} %own_down.1), channel_id=1, source_target_pairs={{0,1},{1,0},{2,3},{3,2},{4,5},{5,4},{6,7},{7,6},{8,9},{9,8},{10,11... | collective-permute-start | bytes 8650760 | tf_op jit(solution)/shard_map/ppermute | solution.py:354
  25.5 11.0 %copy-start = (bf16[8,4,256]{2,1,0:T(4,128)(2,1)S(1)}, bf16[8,4,256]{2,1,0:T(4,128)(2,1)}, u32[]{:S(2)}) copy-start(bf16[8,4,256]{2,1,0:T(4,128)(2,1)} %fresh.1) | copy-start | bytes 49156
  25.5 11.0 %copy-start.1 = (s32[8,20]{1,0:T(8,128)S(1)}, s32[8,20]{1,0:T(8,128)}, u32[]{:S(2)}) copy-start(s32[8,20]{1,0:T(8,128)} %table.1) | copy-start | bytes 1924
  25.5 11.0 %copy-start.2 = (s32[8]{0:T(128)S(1)}, s32[8]{0:T(128)}, u32[]{:S(2)}) copy-start(s32[8]{0:T(128)} %lengths.1) | copy-start | bytes 100
  25.5 11.0 %copy-start.3 = (f32[1,8]{1,0:T(1,128)S(1)}, f32[1,8]{1,0:T(1,128)}, u32[]{:S(2)}) copy-start(f32[1,8]{1,0:T(1,128)} %get-tuple-element.12.after) | copy-start | bytes 100
  31.4 12.2 %all-to-all-start.1 = ((bf16[16,16,512]{2,1,0:T(8,128)(2,1)}), bf16[16,16,512]{2,1,0:T(8,128)(2,1)S(1)}, u32[]{:S(2)}, u32[]{:S(2)}) async-start(bf16[16,16,512]{2,1,0:T(8,128)(2,1)} %bitcast.2), calls=%async_computation.1 | async-start | bytes 524288 | tf_op jit(solution)/shard_map/all_to_all | solution.py:420

commit v18 on v17

--- a/solution.py
+++ b/solution.py
@@ -12,6 +12,7 @@
 F32 = jnp.float32
 NT = (((1,), (1,)), ((), ()))
 NN = (((1,), (0,)), ((), ()))
+STATS = 128
 SLAB = 16
 MIB = 1 << 20
 
@@ -110,7 +111,7 @@
     return jnp.sum(jnp.where(iota(shape, 0) == iota(shape, 1), column, 0.0), axis=0, keepdims=True)
 
 
-def route(projected, hidden, gain, router, ids, mixed_ref, norms_ref, top_ref, slabs_ref, comb_ref, capacity, leave=None):
+def route(projected, hidden, gain, router, ids, mixed_ref, slabs_ref, comb_ref, capacity):
     requests, width = hidden.shape
     experts = router.shape[0]
     parts = SLAB // capacity
@@ -125,10 +126,9 @@
     mixed_ref[...] = mixed
     mixed = mixed.astype(F32)
     norms = jnp.sqrt(jnp.mean(mixed * mixed, axis=1, keepdims=True) + 1e-06)
-    norms_ref[...] = as_row(norms)
     normed = (mixed / norms * gain[...].astype(F32).reshape(1, width)).astype(BF16)
     logits = dot(normed, router[...], NT)
-    top_ref[...] = as_row(jnp.max(logits, axis=1, keepdims=True))
+    top = jnp.max(logits, axis=1, keepdims=True)
     column = iota((requests, experts), 1)
     named = column < 0
     for k in range(ids.shape[1]):
@@ -148,12 +148,12 @@
         inner % parts == iota(shape, 1) // requests
     )
     slabs_ref[...] = dot(picks.astype(BF16), stacked.astype(BF16)).astype(BF16)
-    if leave is not None:
-        leave()
     shape = (experts, slab_rows)
     spread = (slab_expert(shape, 1) == iota(shape, 0)).astype(F32)
     inner = iota((requests, slab_rows), 1) % SLAB
-    comb_ref[...] = jnp.where(
+    field = iota((requests, STATS), 1)
+    comb_ref[:, slab_rows:] = jnp.where(field == 0, norms, jnp.where(field == 1, top, 0.0))
+    comb_ref[:, :slab_rows] = jnp.where(
         dot(place, spread) == (inner // parts).astype(F32),
         dot(weights, spread, precision=lax.Precision.HIGHEST),
         0.0,
@@ -161,14 +161,11 @@
 
 
 def attend_route_kernel(capacity, *refs):
-    inputs, (mixed, norms, top, slabs, comb) = refs[:10], refs[10:15]
-    small, scratch = refs[15:23], refs[23:]
-    keys, values, kept_slabs = scratch[:3]
-    projected = attend(inputs, keys, values, (small, scratch[3:]))
+    inputs, (mixed, slabs, comb) = refs[:10], refs[10:13]
+    small, scratch = refs[13:21], refs[21:]
+    projected = attend(inputs, scratch[0], scratch[1], (small, scratch[2:]))
     hidden, gain, router, ids = small[4:]
-    leave = pltpu.make_async_copy(kept_slabs, slabs, scratch[-1].at[0])
-    route(projected, hidden, gain, router, ids, mixed, norms, top, kept_slabs, comb, capacity, leave.start)
-    leave.wait()
+    route(projected, hidden, gain, router, ids, mixed, slabs, comb, capacity)
 
 
 def attend_kernel(*refs):
@@ -198,8 +195,8 @@
         copy.wait()
 
 
-def route_kernel(capacity, projected, hidden, gain, router, ids, mixed, norms, top, slabs, comb):
-    route(projected[...], hidden, gain, router, ids, mixed, norms, top, slabs, comb, capacity)
+def route_kernel(capacity, projected, hidden, gain, router, ids, mixed, slabs, comb):
+    route(projected[...], hidden, gain, router, ids, mixed, slabs, comb, capacity)
 
 
 def unit_chunks(units):
@@ -268,16 +265,19 @@
         slabs[pl.ds(i * block, block), :] = dot(unsort, stacked).astype(BF16)
 
 
-def gather_terms(comb, slabs, capacity):
+def gather_terms(comb, slabs, norms, top, capacity):
     parts = SLAB // capacity
     requests = comb.shape[0]
-    weights = comb[...]
+    used = slabs.shape[0]
+    norms[...] = as_row(comb[:, used : used + 1])
+    top[...] = as_row(comb[:, used + 1 : used + 2])
+    weights = comb[:, :used]
     pieces = []
     for _ in range(3):
         piece = weights.astype(BF16).astype(F32)
         weights = weights - piece
         pieces.append(piece)
-    part = iota(comb.shape, 1) % parts
+    part = iota(weights.shape, 1) % parts
     stacked = jnp.concatenate(
         [jnp.where(part == p, piece, 0.0) for p in range(parts) for piece in pieces], axis=0
     ).astype(BF16)
@@ -291,12 +291,12 @@
     )
 
 
-def combine_kernel(capacity, comb, slabs, mixed, out):
-    out[...] = (mixed[...].astype(F32) + gather_terms(comb, slabs, capacity)).astype(BF16)
-
-
-def gather_kernel(capacity, comb, slabs, out):
-    out[...] = gather_terms(comb, slabs, capacity).astype(BF16)
+def combine_kernel(capacity, comb, slabs, mixed, out, norms, top):
+    out[...] = (mixed[...].astype(F32) + gather_terms(comb, slabs, norms, top, capacity)).astype(BF16)
+
+
+def gather_kernel(capacity, comb, slabs, out, norms, top):
+    out[...] = gather_terms(comb, slabs, norms, top, capacity).astype(BF16)
 
 
 def vmem(count):
@@ -369,21 +369,15 @@
 
     inputs = [pltpu.SMEM(page_table.shape, jnp.int32), pltpu.SMEM(lengths.shape, jnp.int32)]
     inputs += small(queries, fresh_key_value)
-    routed_shapes = [
-        like((requests, width)),
-        like((1, requests), F32),
-        like((1, requests), F32),
-        like((slab_rows, piece)),
-        like((requests, slab_rows), F32),
-    ]
+    routed_shapes = [like((requests, width)), like((slab_rows, piece)), like((requests, slab_rows + STATS), F32)]
+    final_shapes = [like((requests, width)), like((1, requests), F32), like((1, requests), F32)]
     attend_params = pltpu.CompilerParams(vmem_limit_bytes=24 * MIB)
     if kv_count == 1:
-        attend_scratch.insert(2, pltpu.VMEM((slab_rows, piece), BF16))
-        mixed, norms, top, slabs, comb = pl.pallas_call(
+        mixed, slabs, comb = pl.pallas_call(
             functools.partial(attend_route_kernel, capacity),
             out_shape=routed_shapes,
             in_specs=in_hbm(10),
-            out_specs=vmem(3) + in_hbm(1) + vmem(1),
+            out_specs=vmem(3),
             scratch_shapes=inputs + small(hidden, norm_gain, router_weight, expert_ids) + attend_scratch,
             compiler_params=attend_params,
         )(*pinned(page_table, lengths, queries, fresh_key_value, hidden, norm_gain, router_weight, expert_ids,
@@ -398,11 +392,11 @@
             compiler_params=attend_params,
         )(*pinned(page_table, lengths, queries, fresh_key_value, kv_pool, out_weight))
         projected = lax.psum(projected, "kv")
-        mixed, norms, top, slabs, comb = pl.pallas_call(
+        mixed, slabs, comb = pl.pallas_call(
             functools.partial(route_kernel, capacity),
             out_shape=routed_shapes,
             in_specs=vmem(5),
-            out_specs=vmem(5),
+            out_specs=vmem(3),
         )(projected, hidden, norm_gain, router_weight, expert_ids)
 
     new_pool = pl.pallas_call(
@@ -413,7 +407,7 @@
         scratch_shapes=[pltpu.VMEM(kv_pool.shape, BF16), pltpu.SemaphoreType.DMA((8,))],
         compiler_params=pltpu.CompilerParams(vmem_limit_bytes=12 * MIB),
         cost_estimate=pl.CostEstimate(flops=0, bytes_accessed=8 * kv_pool.size, transcendentals=0),
-    )(page_table, lengths, fresh_key_value, top, *pinned(kv_pool))
+    )(page_table, lengths, fresh_key_value, comb, *pinned(kv_pool))
 
     def exchange(array):
         array = array.reshape(experts, SLAB, piece)
@@ -442,19 +436,19 @@
     )(arrived, *pinned(expert_gate_up, expert_down), other_up, other_down)
     returned = exchange(leaving)
     if kv_count == 1:
-        out_hidden = pl.pallas_call(
+        out_hidden, norms, top = pl.pallas_call(
             functools.partial(combine_kernel, capacity),
-            out_shape=like((requests, width)),
+            out_shape=final_shapes,
             in_specs=vmem(3),
-            out_specs=pl.BlockSpec(memory_space=pltpu.VMEM),
+            out_specs=vmem(3),
             compiler_params=pltpu.CompilerParams(vmem_limit_bytes=8 * MIB),
         )(comb, returned, mixed)
     else:
-        routed = pl.pallas_call(
+        routed, norms, top = pl.pallas_call(
             functools.partial(gather_kernel, capacity),
-            out_shape=like((requests, width)),
+            out_shape=final_shapes,
             in_specs=vmem(2),
-            out_specs=pl.BlockSpec(memory_space=pltpu.VMEM),
+            out_specs=vmem(3),
         )(comb, returned)
         routed = lax.psum(routed, "kv").astype(F32)
         out_hidden = (mixed.astype(F32) + routed).astype(BF16)

time: 44.8 us -> 44.1 us (0.984)
  Pallas kernels: 21 us -> 20.3 us
    pallas_call x1, Pallas kernels: 8.07 us -> 7.41 us  [body(): pl.pallas_call(functools.partial(attend_route_kernel, capacity), out_shap...]
  transfers between devices with their start and end apart: 3 -> 3, of which waited for: 1 -> 1; matrix products, arithmetic and copies ran while one was open for 0% -> 0% of each run, Pallas kernels for 32% -> 31%
where the time goes in v18:
time: 44.1 us; the launch traced here: 43.8 us
  Pallas kernels  20.3 us (46%)
  blocking collectives  16.2 us (37%)
  starting transfers between devices  5.73 us (13%)
  waiting for transfers between devices  0.88 us (2%)
  between operations  0.7 us (2%)
    all_to_all x1, blocking collectives, exchange(): lax.all_to_all(array, 'req', split_axis=0, concat_axis=0, tiled=True, axi...  16.2 us
    pallas_call x1, Pallas kernels, body(): pl.pallas_call(functools.partial(attend_route_kernel, capacity), out_shap...  7.41 us
    pallas_call x1, Pallas kernels, body(): pl.pallas_call(refresh_kernel, out_shape=like(kv_pool.shape), in_specs=sc...  6.2 us
    pallas_call x1, Pallas kernels, body(): pl.pallas_call(functools.partial(expert_kernel, capacity), out_shape=like...  5.87 us
    all_to_all x1, starting transfers between devices, exchange(): lax.all_to_all(array, 'req', split_axis=0, concat_axis=0, tiled=True, axi...  5.13 us
  transfers between devices with their start and end apart: 3, of which 1 were waited for; matrix products, arithmetic and copies ran while one was open for 0% of the time, Pallas kernels for 31%

profile of v18, /device:TPU:0, one launch (start us, length us, event | category | flops | bytes accessed | tf_op | source)
XLA Modules:
  0.0 43.8 jit_solution(1407536008582957297)
XLA Ops:
  0.6 0.5 %collective-permute-start = (bf16[1,2,704,2048]{3,2,1,0:T(8,128)(2,1)}, bf16[1,2,704,2048]{3,2,1,0:T(8,128)(2,1)S(1)}, u32[]{:S(2)}, u32[]{:S(2)}) collective-permute-start(bf16[1,2,704,2048]{3,2,1,0:T(8,128)(2,1)} %own_up.1), channel_id=1, source_target_pairs={{0,1},{1,0},{2,3},{3,2},{4,5},{5,4},{6,7},{7,6},{8,9},{9,8},{10,11... | collective-permute-start | bytes 17301512 | tf_op jit(solution)/shard_map/ppermute | solution.py:353
  1.2 0.1 collective-permute-start.1
  1.2 7.4 %shard_map.147 = (bf16[8,2048]{1,0:T(8,128)(2,1)S(1)}, bf16[256,512]{1,0:T(8,128)(2,1)S(1)}, f32[8,384]{1,0:T(8,128)S(1)}) custom-call(s32[8,20]{1,0:T(8,128)} %table.1, s32[8]{0:T(128)} %lengths.1, bf16[8,2048]{1,0:T(8,128)(2,1)} %refs_2_.1, bf16[8,4,256]{2,1,0:T(4,128)(2,1)} %fresh.1, bf16[8,2048]{1,0:T(8,128)(2,1)} %refs_4_.1, bf16[2048]{0:T(1024)(128)(2,1)} %refs_5_.1, ...), custom_call_target="tpu_custom_call" | custom-call | tf_op jit(solution)/shard_map/pallas_call | solution.py:376
  8.7 16.2 %all_to_all.10 = bf16[16,16,512]{2,1,0:T(8,128)(2,1)S(1)} all-to-all(bf16[16,16,512]{2,1,0:T(8,128)(2,1)S(1)} %bitcast.8), channel_id=1, replica_groups={{12,14,8,10,4,6,0,2,28,30,24,26,20,22,16,18},{19,17,23,21,27,25,31,29,3..., dimensions={0} | all-to-all | bytes 524288 | tf_op jit(solution)/shard_map/all_to_all | solution.py:414
  24.9 0.0 collective-permute-done.1.other_down
  24.9 0.0 collective-permute-done.other_up
  24.9 0.0 copy-start
  24.9 0.0 copy-start.1
  24.9 0.0 copy-start.2
  24.9 5.9 %shard_map.148 = bf16[256,512]{1,0:T(8,128)(2,1)} custom-call(bf16[256,512]{1,0:T(8,128)(2,1)S(1)} %bitcast.6, bf16[1,2,704,2048]{3,2,1,0:T(8,128)(2,1)} %own_up.1, bf16[1,704,2048]{2,1,0:T(8,128)(2,1)} %own_down.1, bf16[1,2,704,2048]{3,2,1,0:T(8,128)(2,1)S(1)} %collective-permute-done.other_up, bf16[1,704,2048]{2,1,0:T(8,128)(2,1)S(1)} %collective-permute-done.1.other_down), custom_call_target="tpu_custom_call" | custom-call | tf_op jit(solution)/shard_map/pallas_call | solution.py:422
  30.8 5.1 %all-to-all-start.1 = ((bf16[16,16,512]{2,1,0:T(8,128)(2,1)}), bf16[16,16,512]{2,1,0:T(8,128)(2,1)S(1)}, u32[]{:S(2)}, u32[]{:S(2)}) async-start(bf16[16,16,512]{2,1,0:T(8,128)(2,1)} %bitcast.2), calls=%async_computation.1 | async-start | bytes 524288 | tf_op jit(solution)/shard_map/all_to_all | solution.py:414
  35.9 0.0 copy-done
  35.9 0.0 copy-done.1
  35.9 0.0 copy-done.2
  35.9 6.2 %shard_map.150 = bf16[104,32,4,256]{3,2,1,0:T(4,128)(2,1)} custom-call(s32[8,20]{1,0:T(8,128)S(1)} %copy-done.1, s32[8]{0:T(128)S(1)} %copy-done.2, bf16[8,4,256]{2,1,0:T(4,128)(2,1)S(1)} %copy-done, f32[8,384]{1,0:T(8,128)S(1)} %get-tuple-element.10.comb.after, bf16[104,32,4,256]{3,2,1,0:T(4,128)(2,1)} %pool.1), custom_call_target="tpu_custom_call" | custom-call | bytes 27262976 | tf_op jit(solution)/shard_map/pallas_call | solution.py:402
  42.1 0.9 %all-to-all-done.1 = bf16[16,16,512]{2,1,0:T(8,128)(2,1)S(1)} async-done(((bf16[16,16,512]{2,1,0:T(8,128)(2,1)}), bf16[16,16,512]{2,1,0:T(8,128)(2,1)S(1)}, u32[]{:S(2)}, u32[]{:S(2)}) %all-to-all-start.1) | async-done | bytes 262176 | tf_op jit(solution)/shard_map/all_to_all | solution.py:414
  43.0 0.8 %shard_map.149 = (bf16[8,2048]{1,0:T(8,128)(2,1)}, f32[1,8]{1,0:T(1,128)}, f32[1,8]{1,0:T(1,128)}) custom-call(f32[8,384]{1,0:T(8,128)S(1)} %get-tuple-element.10.comb.after, bf16[256,512]{1,0:T(8,128)(2,1)S(1)} %bitcast.7, bf16[8,2048]{1,0:T(8,128)(2,1)S(1)} %get-tuple-element.12.mixed), custom_call_target="tpu_custom_call" | custom-call | tf_op jit(solution)/shard_map/pallas_call | solution.py:439
Async XLA Ops:
  0.6 24.2 %collective-permute-start = (bf16[1,2,704,2048]{3,2,1,0:T(8,128)(2,1)}, bf16[1,2,704,2048]{3,2,1,0:T(8,128)(2,1)S(1)}, u32[]{:S(2)}, u32[]{:S(2)}) collective-permute-start(bf16[1,2,704,2048]{3,2,1,0:T(8,128)(2,1)} %own_up.1), channel_id=1, source_target_pairs={{0,1},{1,0},{2,3},{3,2},{4,5},{5,4},{6,7},{7,6},{8,9},{9,8},{10,11... | collective-permute-start | bytes 17301512 | tf_op jit(solution)/shard_map/ppermute | solution.py:353
  1.2 23.7 %collective-permute-start.1 = (bf16[1,704,2048]{2,1,0:T(8,128)(2,1)}, bf16[1,704,2048]{2,1,0:T(8,128)(2,1)S(1)}, u32[]{:S(2)}, u32[]{:S(2)}) collective-permute-start(bf16[1,704,2048]{2,1,0:T(8,128)(2,1)} %own_down.1), channel_id=1, source_target_pairs={{0,1},{1,0},{2,3},{3,2},{4,5},{5,4},{6,7},{7,6},{8,9},{9,8},{10,11... | collective-permute-start | bytes 8650760 | tf_op jit(solution)/shard_map/ppermute | solution.py:354
  24.9 11.0 %copy-start = (bf16[8,4,256]{2,1,0:T(4,128)(2,1)S(1)}, bf16[8,4,256]{2,1,0:T(4,128)(2,1)}, u32[]{:S(2)}) copy-start(bf16[8,4,256]{2,1,0:T(4,128)(2,1)} %fresh.1) | copy-start | bytes 49156
  24.9 11.0 %copy-start.1 = (s32[8,20]{1,0:T(8,128)S(1)}, s32[8,20]{1,0:T(8,128)}, u32[]{:S(2)}) copy-start(s32[8,20]{1,0:T(8,128)} %table.1) | copy-start | bytes 1924
  24.9 11.0 %copy-start.2 = (s32[8]{0:T(128)S(1)}, s32[8]{0:T(128)}, u32[]{:S(2)}) copy-start(s32[8]{0:T(128)} %lengths.1) | copy-start | bytes 100
  30.8 12.2 %all-to-all-start.1 = ((bf16[16,16,512]{2,1,0:T(8,128)(2,1)}), bf16[16,16,512]{2,1,0:T(8,128)(2,1)S(1)}, u32[]{:S(2)}, u32[]{:S(2)}) async-start(bf16[16,16,512]{2,1,0:T(8,128)(2,1)} %bitcast.2), calls=%async_computation.1 | async-start | bytes 524288 | tf_op jit(solution)/shard_map/all_to_all | solution.py:414

commit v19 on v18

--- a/solution.py
+++ b/solution.py
@@ -30,7 +30,7 @@
 
 
 def group_turn(chips, part):
-    return chips * 9 // 16 if part % 2 else chips * 3 // 8
+    return chips * 9 // 16 if part % 2 else chips // 4
 
 
 def pool_half(array, i):
@@ -56,11 +56,11 @@
         )
         for i, kept in enumerate((keys, values))
     ]
-    step = weight.shape[0] // 2
-    spans = [pl.ds(i * step, step) for i in range(2)]
+    step = weight.shape[0] // 4
+    spans = [pl.ds(i * step, step) for i in range(4)]
     weight_loads = copies([(weight.at[span], kept_weight.at[span]) for span in spans], sems, 12)
-    later = copies(list(zip(refs[4:-2], small[4:])), sems, 14)
-    for copy in loads + key_loads + value_loads + weight_loads + later:
+    later = copies(list(zip(refs[4:-2], small[4:])), sems, 16)
+    for copy in loads + key_loads + value_loads + weight_loads[:2] + later:
         copy.start()
     for copy in loads:
         copy.wait()
@@ -70,6 +70,7 @@
 
     for copy in key_loads:
         copy.wait()
+    weight_loads[2].start()
     for r, (page, slot) in enumerate(spots):
         keys[page, slot] = fresh[r][:, :head_dim]
     key_pages = keys.reshape(pages, page_rows, head_dim)
@@ -89,6 +90,7 @@
 
     for copy in value_loads:
         copy.wait()
+    weight_loads[3].start()
     for r, (page, slot) in enumerate(spots):
         values[page, slot] = fresh[r][:, head_dim:]
     for r in range(requests):
@@ -361,7 +363,7 @@
         pltpu.VMEM((heads * requests, head_dim), F32),
         pltpu.VMEM((requests, heads, page_table.shape[1] * page_len * heads_kv), BF16),
         pltpu.VMEM((requests, heads, head_dim), F32),
-        pltpu.SemaphoreType.DMA((18,)),
+        pltpu.SemaphoreType.DMA((20,)),
     ]
 
     def small(*arrays):

time: 44.1 us -> 44.5 us (level)
  waiting for transfers between devices: 0.88 us -> 1.4 us
    all_to_all x1, waiting for transfers between devices: 0.87 us -> 1.4 us  [exchange(): lax.all_to_all(array, 'req', split_axis=0, concat_axis=0, tiled=True, axi...]
where the time goes in v19:
time: 44.5 us; the launch traced here: 44.1 us
  Pallas kernels  20.4 us (46%)
  blocking collectives  16.2 us (36%)
  starting transfers between devices  5.36 us (12%)
  waiting for transfers between devices  1.4 us (3%)
  between operations  0.7 us (2%)
    all_to_all x1, blocking collectives, exchange(): lax.all_to_all(array, 'req', split_axis=0, concat_axis=0, tiled=True, axi...  16.2 us
    pallas_call x1, Pallas kernels, body(): pl.pallas_call(functools.partial(attend_route_kernel, capacity), out_shap...  7.55 us
    pallas_call x1, Pallas kernels, body(): pl.pallas_call(refresh_kernel, out_shape=like(kv_pool.shape), in_specs=sc...  6.23 us
    pallas_call x1, Pallas kernels, body(): pl.pallas_call(functools.partial(expert_kernel, capacity), out_shape=like...  5.87 us
    all_to_all x1, starting transfers between devices, exchange(): lax.all_to_all(array, 'req', split_axis=0, concat_axis=0, tiled=True, axi...  4.76 us
    all_to_all x1, waiting for transfers between devices, exchange(): lax.all_to_all(array, 'req', split_axis=0, concat_axis=0, tiled=True, axi...  1.4 us
  transfers between devices with their start and end apart: 3, of which 1 were waited for; matrix products, arithmetic and copies ran while one was open for 0% of the time, Pallas kernels for 31%

profile of v19, /device:TPU:0, one launch (start us, length us, event | category | flops | bytes accessed | tf_op | source)
XLA Modules:
  0.0 44.1 jit_solution(11762458741862739533)
XLA Ops:
  0.6 0.5 %collective-permute-start = (bf16[1,2,704,2048]{3,2,1,0:T(8,128)(2,1)}, bf16[1,2,704,2048]{3,2,1,0:T(8,128)(2,1)S(1)}, u32[]{:S(2)}, u32[]{:S(2)}) collective-permute-start(bf16[1,2,704,2048]{3,2,1,0:T(8,128)(2,1)} %own_up.1), channel_id=1, source_target_pairs={{0,1},{1,0},{2,3},{3,2},{4,5},{5,4},{6,7},{7,6},{8,9},{9,8},{10,11... | collective-permute-start | bytes 17301512 | tf_op jit(solution)/shard_map/ppermute | solution.py:355
  1.2 0.1 collective-permute-start.1
  1.2 7.5 %shard_map.147 = (bf16[8,2048]{1,0:T(8,128)(2,1)S(1)}, bf16[256,512]{1,0:T(8,128)(2,1)S(1)}, f32[8,384]{1,0:T(8,128)S(1)}) custom-call(s32[8,20]{1,0:T(8,128)} %table.1, s32[8]{0:T(128)} %lengths.1, bf16[8,2048]{1,0:T(8,128)(2,1)} %refs_2_.1, bf16[8,4,256]{2,1,0:T(4,128)(2,1)} %fresh.1, bf16[8,2048]{1,0:T(8,128)(2,1)} %refs_4_.1, bf16[2048]{0:T(1024)(128)(2,1)} %refs_5_.1, ...), custom_call_target="tpu_custom_call" | custom-call | tf_op jit(solution)/shard_map/pallas_call | solution.py:378
  8.8 16.2 %all_to_all.10 = bf16[16,16,512]{2,1,0:T(8,128)(2,1)S(1)} all-to-all(bf16[16,16,512]{2,1,0:T(8,128)(2,1)S(1)} %bitcast.8), channel_id=1, replica_groups={{8,10,12,14,0,2,4,6,24,26,28,30,16,18,20,22},{19,17,23,21,27,25,31,29,3..., dimensions={0} | all-to-all | bytes 524288 | tf_op jit(solution)/shard_map/all_to_all | solution.py:416
  25.0 0.0 collective-permute-done.1.other_down
  25.0 0.0 collective-permute-done.other_up
  25.0 0.0 copy-start
  25.0 0.0 copy-start.1
  25.0 0.0 copy-start.2
  25.0 5.9 %shard_map.148 = bf16[256,512]{1,0:T(8,128)(2,1)} custom-call(bf16[256,512]{1,0:T(8,128)(2,1)S(1)} %bitcast.6, bf16[1,2,704,2048]{3,2,1,0:T(8,128)(2,1)} %own_up.1, bf16[1,704,2048]{2,1,0:T(8,128)(2,1)} %own_down.1, bf16[1,2,704,2048]{3,2,1,0:T(8,128)(2,1)S(1)} %collective-permute-done.other_up, bf16[1,704,2048]{2,1,0:T(8,128)(2,1)S(1)} %collective-permute-done.1.other_down), custom_call_target="tpu_custom_call" | custom-call | tf_op jit(solution)/shard_map/pallas_call | solution.py:424
  30.9 4.8 %all-to-all-start.1 = ((bf16[16,16,512]{2,1,0:T(8,128)(2,1)}), bf16[16,16,512]{2,1,0:T(8,128)(2,1)S(1)}, u32[]{:S(2)}, u32[]{:S(2)}) async-start(bf16[16,16,512]{2,1,0:T(8,128)(2,1)} %bitcast.2), calls=%async_computation.1 | async-start | bytes 524288 | tf_op jit(solution)/shard_map/all_to_all | solution.py:416
  35.7 0.0 copy-done
  35.7 0.0 copy-done.1
  35.7 0.0 copy-done.2
  35.7 6.2 %shard_map.150 = bf16[104,32,4,256]{3,2,1,0:T(4,128)(2,1)} custom-call(s32[8,20]{1,0:T(8,128)S(1)} %copy-done.1, s32[8]{0:T(128)S(1)} %copy-done.2, bf16[8,4,256]{2,1,0:T(4,128)(2,1)S(1)} %copy-done, f32[8,384]{1,0:T(8,128)S(1)} %get-tuple-element.10.comb.after, bf16[104,32,4,256]{3,2,1,0:T(4,128)(2,1)} %pool.1), custom_call_target="tpu_custom_call" | custom-call | bytes 27262976 | tf_op jit(solution)/shard_map/pallas_call | solution.py:404
  41.9 1.4 %all-to-all-done.1 = bf16[16,16,512]{2,1,0:T(8,128)(2,1)S(1)} async-done(((bf16[16,16,512]{2,1,0:T(8,128)(2,1)}), bf16[16,16,512]{2,1,0:T(8,128)(2,1)S(1)}, u32[]{:S(2)}, u32[]{:S(2)}) %all-to-all-start.1) | async-done | bytes 262176 | tf_op jit(solution)/shard_map/all_to_all | solution.py:416
  43.3 0.8 %shard_map.149 = (bf16[8,2048]{1,0:T(8,128)(2,1)}, f32[1,8]{1,0:T(1,128)}, f32[1,8]{1,0:T(1,128)}) custom-call(f32[8,384]{1,0:T(8,128)S(1)} %get-tuple-element.10.comb.after, bf16[256,512]{1,0:T(8,128)(2,1)S(1)} %bitcast.7, bf16[8,2048]{1,0:T(8,128)(2,1)S(1)} %get-tuple-element.12.mixed), custom_call_target="tpu_custom_call" | custom-call | tf_op jit(solution)/shard_map/pallas_call | solution.py:441
Async XLA Ops:
  0.6 24.4 %collective-permute-start = (bf16[1,2,704,2048]{3,2,1,0:T(8,128)(2,1)}, bf16[1,2,704,2048]{3,2,1,0:T(8,128)(2,1)S(1)}, u32[]{:S(2)}, u32[]{:S(2)}) collective-permute-start(bf16[1,2,704,2048]{3,2,1,0:T(8,128)(2,1)} %own_up.1), channel_id=1, source_target_pairs={{0,1},{1,0},{2,3},{3,2},{4,5},{5,4},{6,7},{7,6},{8,9},{9,8},{10,11... | collective-permute-start | bytes 17301512 | tf_op jit(solution)/shard_map/ppermute | solution.py:355
  1.2 23.9 %collective-permute-start.1 = (bf16[1,704,2048]{2,1,0:T(8,128)(2,1)}, bf16[1,704,2048]{2,1,0:T(8,128)(2,1)S(1)}, u32[]{:S(2)}, u32[]{:S(2)}) collective-permute-start(bf16[1,704,2048]{2,1,0:T(8,128)(2,1)} %own_down.1), channel_id=1, source_target_pairs={{0,1},{1,0},{2,3},{3,2},{4,5},{5,4},{6,7},{7,6},{8,9},{9,8},{10,11... | collective-permute-start | bytes 8650760 | tf_op jit(solution)/shard_map/ppermute | solution.py:356
  25.0 10.7 %copy-start = (bf16[8,4,256]{2,1,0:T(4,128)(2,1)S(1)}, bf16[8,4,256]{2,1,0:T(4,128)(2,1)}, u32[]{:S(2)}) copy-start(bf16[8,4,256]{2,1,0:T(4,128)(2,1)} %fresh.1) | copy-start | bytes 49156
  25.0 10.7 %copy-start.1 = (s32[8,20]{1,0:T(8,128)S(1)}, s32[8,20]{1,0:T(8,128)}, u32[]{:S(2)}) copy-start(s32[8,20]{1,0:T(8,128)} %table.1) | copy-start | bytes 1924
  25.0 10.7 %copy-start.2 = (s32[8]{0:T(128)S(1)}, s32[8]{0:T(128)}, u32[]{:S(2)}) copy-start(s32[8]{0:T(128)} %lengths.1) | copy-start | bytes 100
  30.9 12.4 %all-to-all-start.1 = ((bf16[16,16,512]{2,1,0:T(8,128)(2,1)}), bf16[16,16,512]{2,1,0:T(8,128)(2,1)S(1)}, u32[]{:S(2)}, u32[]{:S(2)}) async-start(bf16[16,16,512]{2,1,0:T(8,128)(2,1)} %bitcast.2), calls=%async_computation.1 | async-start | bytes 524288 | tf_op jit(solution)/shard_map/all_to_all | solution.py:416

commit v20 on v18

--- a/solution.py
+++ b/solution.py
@@ -30,7 +30,7 @@
 
 
 def group_turn(chips, part):
-    return chips * 9 // 16 if part % 2 else chips * 3 // 8
+    return chips * 9 // 16 if part % 2 else chips * 7 // 16
 
 
 def pool_half(array, i):
@@ -38,7 +38,7 @@
     return array.at[:, :, :, pl.ds(i * head_dim, head_dim)]
 
 
-def attend(refs, keys, values, scratch):
+def attend(refs, keys, values, scratch, prepare):
     small, (kept_weight, qs, att, probs, sums, sems) = scratch
     table, lengths, q_ref, fresh = small[:4]
     requests, max_pages = table.shape
@@ -87,6 +87,9 @@
         sums[r] = jnp.broadcast_to(jnp.sum(exponent, axis=1, keepdims=True), (heads, head_dim))
         probs[r] = exponent.astype(BF16)
 
+    for copy in later:
+        copy.wait()
+    prepared = prepare()
     for copy in value_loads:
         copy.wait()
     for r, (page, slot) in enumerate(spots):
@@ -101,9 +104,7 @@
     for i, copy in enumerate(weight_loads):
         copy.wait()
         projected = projected + dot(attended[:, i * step : (i + 1) * step], kept_weight[spans[i], :])
-    for copy in later:
-        copy.wait()
-    return projected
+    return projected, prepared
 
 
 def as_row(column):
@@ -111,35 +112,29 @@
     return jnp.sum(jnp.where(iota(shape, 0) == iota(shape, 1), column, 0.0), axis=0, keepdims=True)
 
 
-def route(projected, hidden, gain, router, ids, mixed_ref, slabs_ref, comb_ref, capacity):
-    requests, width = hidden.shape
-    experts = router.shape[0]
+def split(values):
+    pieces = []
+    for _ in range(3):
+        pieces.append(values.astype(BF16).astype(F32))
+        values = values - pieces[-1]
+    return pieces
+
+
+def plan(ids, requests, experts, slab_rows, capacity):
     parts = SLAB // capacity
-    piece = width // parts
-    slab_rows = experts * SLAB
     turns = jnp.where(lax.axis_index("req") % 2 == 0, group_turn(experts, 0), group_turn(experts, 1))
 
     def slab_expert(shape, dim):
         return (iota(shape, dim) // SLAB) ^ turns
 
-    mixed = (hidden[...].astype(F32) + projected).astype(BF16)
-    mixed_ref[...] = mixed
-    mixed = mixed.astype(F32)
-    norms = jnp.sqrt(jnp.mean(mixed * mixed, axis=1, keepdims=True) + 1e-06)
-    normed = (mixed / norms * gain[...].astype(F32).reshape(1, width)).astype(BF16)
-    logits = dot(normed, router[...], NT)
-    top = jnp.max(logits, axis=1, keepdims=True)
     column = iota((requests, experts), 1)
     named = column < 0
     for k in range(ids.shape[1]):
         named = named | (ids[:, k : k + 1] == column)
-    weights = jnp.where(named, jnp.exp(logits), 0.0)
-    weights = weights / jnp.sum(weights, axis=1, keepdims=True)
+    named = named.astype(F32)
     earlier = (iota((requests, requests), 1) < iota((requests, requests), 0)).astype(F32)
-    rank = dot(earlier, named.astype(F32))
-    place = jnp.where(named, rank, -1.0)
-    normed = normed.astype(F32)
-    stacked = jnp.concatenate([normed[:, p * piece : (p + 1) * piece] for p in range(parts)], axis=0)
+    rank = dot(earlier, named)
+    place = jnp.where(named > 0.0, rank, -1.0)
     places = jnp.concatenate([place] * parts, axis=0)
     shape = (slab_rows, parts * requests)
     inner = iota(shape, 0) % SLAB
@@ -147,30 +142,53 @@
     picks = (dot(spread, places, NT) == (inner // parts).astype(F32)) & (
         inner % parts == iota(shape, 1) // requests
     )
-    slabs_ref[...] = dot(picks.astype(BF16), stacked.astype(BF16)).astype(BF16)
     shape = (experts, slab_rows)
     spread = (slab_expert(shape, 1) == iota(shape, 0)).astype(F32)
     inner = iota((requests, slab_rows), 1) % SLAB
+    holds = (dot(place, spread) == (inner // parts).astype(F32)).astype(F32)
+    return named, picks.astype(BF16), spread.astype(BF16), holds
+
+
+def route(projected, planned, hidden, gain, router, mixed_ref, slabs_ref, comb_ref, capacity):
+    named, picks, spread, holds = planned
+    requests, width = hidden.shape
+    parts = SLAB // capacity
+    piece = width // parts
+    slab_rows = slabs_ref.shape[0]
+    mixed = (hidden[...].astype(F32) + projected).astype(BF16)
+    mixed_ref[...] = mixed
+    mixed = mixed.astype(F32)
+    norms = jnp.sqrt(jnp.mean(mixed * mixed, axis=1, keepdims=True) + 1e-06)
+    normed = (mixed / norms * gain[...].astype(F32).reshape(1, width)).astype(BF16)
+    wide = normed.astype(F32)
+    stacked = jnp.concatenate([wide[:, p * piece : (p + 1) * piece] for p in range(parts)], axis=0)
+    slabs_ref[...] = dot(picks, stacked.astype(BF16)).astype(BF16)
+    logits = dot(normed, router[...], NT)
+    top = jnp.max(logits, axis=1, keepdims=True)
+    weights = jnp.where(named > 0.0, jnp.exp(logits), 0.0)
+    weights = weights / jnp.sum(weights, axis=1, keepdims=True)
+    spread_weights = dot(jnp.concatenate(split(weights), axis=0).astype(BF16), spread)
+    spread_weights = sum(spread_weights[i * requests : (i + 1) * requests] for i in range(3))
     field = iota((requests, STATS), 1)
     comb_ref[:, slab_rows:] = jnp.where(field == 0, norms, jnp.where(field == 1, top, 0.0))
-    comb_ref[:, :slab_rows] = jnp.where(
-        dot(place, spread) == (inner // parts).astype(F32),
-        dot(weights, spread, precision=lax.Precision.HIGHEST),
-        0.0,
-    )
+    comb_ref[:, :slab_rows] = jnp.where(holds > 0.0, spread_weights, 0.0)
 
 
 def attend_route_kernel(capacity, *refs):
     inputs, (mixed, slabs, comb) = refs[:10], refs[10:13]
     small, scratch = refs[13:21], refs[21:]
-    projected = attend(inputs, scratch[0], scratch[1], (small, scratch[2:]))
     hidden, gain, router, ids = small[4:]
-    route(projected, hidden, gain, router, ids, mixed, slabs, comb, capacity)
+
+    def prepare():
+        return plan(ids, ids.shape[0], router.shape[0], slabs.shape[0], capacity)
+
+    projected, planned = attend(inputs, scratch[0], scratch[1], (small, scratch[2:]), prepare)
+    route(projected, planned, hidden, gain, router, mixed, slabs, comb, capacity)
 
 
 def attend_kernel(*refs):
-    attended, scratch = refs[6], refs[11:]
-    attended[...] = attend(refs[:6], scratch[0], scratch[1], (refs[7:11], scratch[2:]))
+    projected, scratch = refs[6], refs[11:]
+    projected[...] = attend(refs[:6], scratch[0], scratch[1], (refs[7:11], scratch[2:]), lambda: None)[0]
 
 
 def refresh_kernel(table, lengths, fresh, after, pool, new_pool, kept, sems):
@@ -196,7 +214,8 @@
 
 
 def route_kernel(capacity, projected, hidden, gain, router, ids, mixed, slabs, comb):
-    route(projected[...], hidden, gain, router, ids, mixed, slabs, comb, capacity)
+    planned = plan(ids, ids.shape[0], router.shape[0], slabs.shape[0], capacity)
+    route(projected[...], planned, hidden, gain, router, mixed, slabs, comb, capacity)
 
 
 def unit_chunks(units):

time: 44.1 us -> 46 us (1.043)
  Pallas kernels: 20.3 us -> 21.9 us
    pallas_call x1, Pallas kernels: 7.41 us -> 9 us  [body(): pl.pallas_call(functools.partial(attend_route_kernel, capacity), out_shap...]
    all_to_all x1, starting transfers between devices: 5.13 us -> 5.59 us  [exchange(): lax.all_to_all(array, 'req', split_axis=0, concat_axis=0, tiled=True, axi...]
  transfers between devices with their start and end apart: 3 -> 3, of which waited for: 1 -> 1; matrix products, arithmetic and copies ran while one was open for 0% -> 0% of each run, Pallas kernels for 31% -> 33%
where the time goes in v20:
time: 46 us; the launch traced here: 45.6 us
  Pallas kernels  21.9 us (48%)
  blocking collectives  16.2 us (35%)
  starting transfers between devices  6.19 us (13%)
  between operations  0.7 us (2%)
  waiting for transfers between devices  0.65 us (1%)
    all_to_all x1, blocking collectives, exchange(): lax.all_to_all(array, 'req', split_axis=0, concat_axis=0, tiled=True, axi...  16.2 us
    pallas_call x1, Pallas kernels, body(): pl.pallas_call(functools.partial(attend_route_kernel, capacity), out_shap...  9 us
    pallas_call x1, Pallas kernels, body(): pl.pallas_call(refresh_kernel, out_shape=like(kv_pool.shape), in_specs=sc...  6.2 us
    pallas_call x1, Pallas kernels, body(): pl.pallas_call(functools.partial(expert_kernel, capacity), out_shape=like...  5.87 us
    all_to_all x1, starting transfers between devices, exchange(): lax.all_to_all(array, 'req', split_axis=0, concat_axis=0, tiled=True, axi...  5.59 us
  transfers between devices with their start and end apart: 3, of which 1 were waited for; matrix products, arithmetic and copies ran while one was open for 0% of the time, Pallas kernels for 33%

profile of v20, /device:TPU:0, one launch (start us, length us, event | category | flops | bytes accessed | tf_op | source)
XLA Modules:
  0.0 45.6 jit_solution(510642466664854143)
XLA Ops:
  0.6 0.5 %collective-permute-start = (bf16[1,2,704,2048]{3,2,1,0:T(8,128)(2,1)}, bf16[1,2,704,2048]{3,2,1,0:T(8,128)(2,1)S(1)}, u32[]{:S(2)}, u32[]{:S(2)}) collective-permute-start(bf16[1,2,704,2048]{3,2,1,0:T(8,128)(2,1)} %own_up.1), channel_id=1, source_target_pairs={{0,1},{1,0},{2,3},{3,2},{4,5},{5,4},{6,7},{7,6},{8,9},{9,8},{10,11... | collective-permute-start | bytes 17301512 | tf_op jit(solution)/shard_map/ppermute | solution.py:372
  1.2 0.1 collective-permute-start.1
  1.2 9.0 %shard_map.147 = (bf16[8,2048]{1,0:T(8,128)(2,1)S(1)}, bf16[256,512]{1,0:T(8,128)(2,1)S(1)}, f32[8,384]{1,0:T(8,128)S(1)}) custom-call(s32[8,20]{1,0:T(8,128)} %table.1, s32[8]{0:T(128)} %lengths.1, bf16[8,2048]{1,0:T(8,128)(2,1)} %refs_2_.1, bf16[8,4,256]{2,1,0:T(4,128)(2,1)} %fresh.1, bf16[8,2048]{1,0:T(8,128)(2,1)} %refs_4_.1, bf16[2048]{0:T(1024)(128)(2,1)} %refs_5_.1, ...), custom_call_target="tpu_custom_call" | custom-call | tf_op jit(solution)/shard_map/pallas_call | solution.py:395
  10.2 16.2 %all_to_all.10 = bf16[16,16,512]{2,1,0:T(8,128)(2,1)S(1)} all-to-all(bf16[16,16,512]{2,1,0:T(8,128)(2,1)S(1)} %bitcast.8), channel_id=1, replica_groups={{14,12,10,8,6,4,2,0,30,28,26,24,22,20,18,16},{19,17,23,21,27,25,31,29,3..., dimensions={0} | all-to-all | bytes 524288 | tf_op jit(solution)/shard_map/all_to_all | solution.py:433
  26.4 0.0 collective-permute-done.1.other_down
  26.5 0.0 collective-permute-done.other_up
  26.5 0.0 copy-start
  26.5 0.0 copy-start.1
  26.5 0.0 copy-start.2
  26.5 5.9 %shard_map.148 = bf16[256,512]{1,0:T(8,128)(2,1)} custom-call(bf16[256,512]{1,0:T(8,128)(2,1)S(1)} %bitcast.6, bf16[1,2,704,2048]{3,2,1,0:T(8,128)(2,1)} %own_up.1, bf16[1,704,2048]{2,1,0:T(8,128)(2,1)} %own_down.1, bf16[1,2,704,2048]{3,2,1,0:T(8,128)(2,1)S(1)} %collective-permute-done.other_up, bf16[1,704,2048]{2,1,0:T(8,128)(2,1)S(1)} %collective-permute-done.1.other_down), custom_call_target="tpu_custom_call" | custom-call | tf_op jit(solution)/shard_map/pallas_call | solution.py:441
  32.4 5.6 %all-to-all-start.1 = ((bf16[16,16,512]{2,1,0:T(8,128)(2,1)}), bf16[16,16,512]{2,1,0:T(8,128)(2,1)S(1)}, u32[]{:S(2)}, u32[]{:S(2)}) async-start(bf16[16,16,512]{2,1,0:T(8,128)(2,1)} %bitcast.2), calls=%async_computation.1 | async-start | bytes 524288 | tf_op jit(solution)/shard_map/all_to_all | solution.py:433
  38.0 0.0 copy-done
  38.0 0.0 copy-done.1
  38.0 0.0 copy-done.2
  38.0 6.2 %shard_map.150 = bf16[104,32,4,256]{3,2,1,0:T(4,128)(2,1)} custom-call(s32[8,20]{1,0:T(8,128)S(1)} %copy-done.1, s32[8]{0:T(128)S(1)} %copy-done.2, bf16[8,4,256]{2,1,0:T(4,128)(2,1)S(1)} %copy-done, f32[8,384]{1,0:T(8,128)S(1)} %get-tuple-element.10.comb.after, bf16[104,32,4,256]{3,2,1,0:T(4,128)(2,1)} %pool.1), custom_call_target="tpu_custom_call" | custom-call | bytes 27262976 | tf_op jit(solution)/shard_map/pallas_call | solution.py:421
  44.2 0.6 %all-to-all-done.1 = bf16[16,16,512]{2,1,0:T(8,128)(2,1)S(1)} async-done(((bf16[16,16,512]{2,1,0:T(8,128)(2,1)}), bf16[16,16,512]{2,1,0:T(8,128)(2,1)S(1)}, u32[]{:S(2)}, u32[]{:S(2)}) %all-to-all-start.1) | async-done | bytes 262176 | tf_op jit(solution)/shard_map/all_to_all | solution.py:433
  44.8 0.8 %shard_map.149 = (bf16[8,2048]{1,0:T(8,128)(2,1)}, f32[1,8]{1,0:T(1,128)}, f32[1,8]{1,0:T(1,128)}) custom-call(f32[8,384]{1,0:T(8,128)S(1)} %get-tuple-element.10.comb.after, bf16[256,512]{1,0:T(8,128)(2,1)S(1)} %bitcast.7, bf16[8,2048]{1,0:T(8,128)(2,1)S(1)} %get-tuple-element.12.mixed), custom_call_target="tpu_custom_call" | custom-call | tf_op jit(solution)/shard_map/pallas_call | solution.py:458
Async XLA Ops:
  0.6 25.8 %collective-permute-start = (bf16[1,2,704,2048]{3,2,1,0:T(8,128)(2,1)}, bf16[1,2,704,2048]{3,2,1,0:T(8,128)(2,1)S(1)}, u32[]{:S(2)}, u32[]{:S(2)}) collective-permute-start(bf16[1,2,704,2048]{3,2,1,0:T(8,128)(2,1)} %own_up.1), channel_id=1, source_target_pairs={{0,1},{1,0},{2,3},{3,2},{4,5},{5,4},{6,7},{7,6},{8,9},{9,8},{10,11... | collective-permute-start | bytes 17301512 | tf_op jit(solution)/shard_map/ppermute | solution.py:372
  1.2 25.3 %collective-permute-start.1 = (bf16[1,704,2048]{2,1,0:T(8,128)(2,1)}, bf16[1,704,2048]{2,1,0:T(8,128)(2,1)S(1)}, u32[]{:S(2)}, u32[]{:S(2)}) collective-permute-start(bf16[1,704,2048]{2,1,0:T(8,128)(2,1)} %own_down.1), channel_id=1, source_target_pairs={{0,1},{1,0},{2,3},{3,2},{4,5},{5,4},{6,7},{7,6},{8,9},{9,8},{10,11... | collective-permute-start | bytes 8650760 | tf_op jit(solution)/shard_map/ppermute | solution.py:373
  26.5 11.5 %copy-start = (bf16[8,4,256]{2,1,0:T(4,128)(2,1)S(1)}, bf16[8,4,256]{2,1,0:T(4,128)(2,1)}, u32[]{:S(2)}) copy-start(bf16[8,4,256]{2,1,0:T(4,128)(2,1)} %fresh.1) | copy-start | bytes 49156
  26.5 11.5 %copy-start.1 = (s32[8,20]{1,0:T(8,128)S(1)}, s32[8,20]{1,0:T(8,128)}, u32[]{:S(2)}) copy-start(s32[8,20]{1,0:T(8,128)} %table.1) | copy-start | bytes 1924
  26.5 11.5 %copy-start.2 = (s32[8]{0:T(128)S(1)}, s32[8]{0:T(128)}, u32[]{:S(2)}) copy-start(s32[8]{0:T(128)} %lengths.1) | copy-start | bytes 100
  32.4 12.5 %all-to-all-start.1 = ((bf16[16,16,512]{2,1,0:T(8,128)(2,1)}), bf16[16,16,512]{2,1,0:T(8,128)(2,1)S(1)}, u32[]{:S(2)}, u32[]{:S(2)}) async-start(bf16[16,16,512]{2,1,0:T(8,128)(2,1)} %bitcast.2), calls=%async_computation.1 | async-start | bytes 524288 | tf_op jit(solution)/shard_map/all_to_all | solution.py:433

commit v21 on v20

--- a/solution.py
+++ b/solution.py
@@ -30,7 +30,7 @@
 
 
 def group_turn(chips, part):
-    return chips * 9 // 16 if part % 2 else chips * 7 // 16
+    return chips * 9 // 16 if part % 2 else chips * 3 // 8
 
 
 def pool_half(array, i):
@@ -60,7 +60,7 @@
     spans = [pl.ds(i * step, step) for i in range(2)]
     weight_loads = copies([(weight.at[span], kept_weight.at[span]) for span in spans], sems, 12)
     later = copies(list(zip(refs[4:-2], small[4:])), sems, 14)
-    for copy in loads + key_loads + value_loads + weight_loads + later:
+    for copy in loads + later + key_loads + value_loads + weight_loads:
         copy.start()
     for copy in loads:
         copy.wait()
@@ -68,6 +68,9 @@
         qs[pl.ds(h * requests, requests), :] = q_ref[:, pl.ds(h * head_dim, head_dim)].astype(F32)
     spots = [(table[r, lengths[r] // page_len], lengths[r] % page_len) for r in range(requests)]
 
+    for copy in later:
+        copy.wait()
+    prepared = prepare()
     for copy in key_loads:
         copy.wait()
     for r, (page, slot) in enumerate(spots):
@@ -87,9 +90,6 @@
         sums[r] = jnp.broadcast_to(jnp.sum(exponent, axis=1, keepdims=True), (heads, head_dim))
         probs[r] = exponent.astype(BF16)
 
-    for copy in later:
-        copy.wait()
-    prepared = prepare()
     for copy in value_loads:
         copy.wait()
     for r, (page, slot) in enumerate(spots):

time: 46 us -> 44.2 us (0.961)
  Pallas kernels: 21.9 us -> 20.3 us
    pallas_call x1, Pallas kernels: 9 us -> 7.44 us  [body(): pl.pallas_call(functools.partial(attend_route_kernel, capacity), out_shap...]
    all_to_all x1, starting transfers between devices: 5.59 us -> 5.13 us  [exchange(): lax.all_to_all(array, 'req', split_axis=0, concat_axis=0, tiled=True, axi...]
  transfers between devices with their start and end apart: 3 -> 3, of which waited for: 1 -> 1; matrix products, arithmetic and copies ran while one was open for 0% -> 0% of each run, Pallas kernels for 33% -> 31%
where the time goes in v21:
time: 44.2 us; the launch traced here: 43.8 us
  Pallas kernels  20.3 us (46%)
  blocking collectives  16.2 us (37%)
  starting transfers between devices  5.73 us (13%)
  waiting for transfers between devices  0.85 us (2%)
  between operations  0.7 us (2%)
    all_to_all x1, blocking collectives, exchange(): lax.all_to_all(array, 'req', split_axis=0, concat_axis=0, tiled=True, axi...  16.2 us
    pallas_call x1, Pallas kernels, body(): pl.pallas_call(functools.partial(attend_route_kernel, capacity), out_shap...  7.44 us
    pallas_call x1, Pallas kernels, body(): pl.pallas_call(refresh_kernel, out_shape=like(kv_pool.shape), in_specs=sc...  6.23 us
    pallas_call x1, Pallas kernels, body(): pl.pallas_call(functools.partial(expert_kernel, capacity), out_shape=like...  5.87 us
    all_to_all x1, starting transfers between devices, exchange(): lax.all_to_all(array, 'req', split_axis=0, concat_axis=0, tiled=True, axi...  5.13 us
  transfers between devices with their start and end apart: 3, of which 1 were waited for; matrix products, arithmetic and copies ran while one was open for 0% of the time, Pallas kernels for 31%

profile of v21, /device:TPU:0, one launch (start us, length us, event | category | flops | bytes accessed | tf_op | source)
XLA Modules:
  0.0 43.8 jit_solution(10196279088554845064)
XLA Ops:
  0.6 0.5 %collective-permute-start = (bf16[1,2,704,2048]{3,2,1,0:T(8,128)(2,1)}, bf16[1,2,704,2048]{3,2,1,0:T(8,128)(2,1)S(1)}, u32[]{:S(2)}, u32[]{:S(2)}) collective-permute-start(bf16[1,2,704,2048]{3,2,1,0:T(8,128)(2,1)} %own_up.1), channel_id=1, source_target_pairs={{0,1},{1,0},{2,3},{3,2},{4,5},{5,4},{6,7},{7,6},{8,9},{9,8},{10,11... | collective-permute-start | bytes 17301512 | tf_op jit(solution)/shard_map/ppermute | solution.py:372
  1.2 0.1 collective-permute-start.1
  1.2 7.4 %shard_map.147 = (bf16[8,2048]{1,0:T(8,128)(2,1)S(1)}, bf16[256,512]{1,0:T(8,128)(2,1)S(1)}, f32[8,384]{1,0:T(8,128)S(1)}) custom-call(s32[8,20]{1,0:T(8,128)} %table.1, s32[8]{0:T(128)} %lengths.1, bf16[8,2048]{1,0:T(8,128)(2,1)} %refs_2_.1, bf16[8,4,256]{2,1,0:T(4,128)(2,1)} %fresh.1, bf16[8,2048]{1,0:T(8,128)(2,1)} %refs_4_.1, bf16[2048]{0:T(1024)(128)(2,1)} %refs_5_.1, ...), custom_call_target="tpu_custom_call" | custom-call | tf_op jit(solution)/shard_map/pallas_call | solution.py:395
  8.7 16.2 %all_to_all.10 = bf16[16,16,512]{2,1,0:T(8,128)(2,1)S(1)} all-to-all(bf16[16,16,512]{2,1,0:T(8,128)(2,1)S(1)} %bitcast.8), channel_id=1, replica_groups={{12,14,8,10,4,6,0,2,28,30,24,26,20,22,16,18},{19,17,23,21,27,25,31,29,3..., dimensions={0} | all-to-all | bytes 524288 | tf_op jit(solution)/shard_map/all_to_all | solution.py:433
  24.9 0.0 collective-permute-done.1.other_down
  24.9 0.0 collective-permute-done.other_up
  24.9 0.0 copy-start
  24.9 0.0 copy-start.1
  24.9 0.0 copy-start.2
  24.9 5.9 %shard_map.148 = bf16[256,512]{1,0:T(8,128)(2,1)} custom-call(bf16[256,512]{1,0:T(8,128)(2,1)S(1)} %bitcast.6, bf16[1,2,704,2048]{3,2,1,0:T(8,128)(2,1)} %own_up.1, bf16[1,704,2048]{2,1,0:T(8,128)(2,1)} %own_down.1, bf16[1,2,704,2048]{3,2,1,0:T(8,128)(2,1)S(1)} %collective-permute-done.other_up, bf16[1,704,2048]{2,1,0:T(8,128)(2,1)S(1)} %collective-permute-done.1.other_down), custom_call_target="tpu_custom_call" | custom-call | tf_op jit(solution)/shard_map/pallas_call | solution.py:441
  30.8 5.1 %all-to-all-start.1 = ((bf16[16,16,512]{2,1,0:T(8,128)(2,1)}), bf16[16,16,512]{2,1,0:T(8,128)(2,1)S(1)}, u32[]{:S(2)}, u32[]{:S(2)}) async-start(bf16[16,16,512]{2,1,0:T(8,128)(2,1)} %bitcast.2), calls=%async_computation.1 | async-start | bytes 524288 | tf_op jit(solution)/shard_map/all_to_all | solution.py:433
  35.9 0.0 copy-done
  35.9 0.0 copy-done.1
  35.9 0.0 copy-done.2
  36.0 6.2 %shard_map.150 = bf16[104,32,4,256]{3,2,1,0:T(4,128)(2,1)} custom-call(s32[8,20]{1,0:T(8,128)S(1)} %copy-done.1, s32[8]{0:T(128)S(1)} %copy-done.2, bf16[8,4,256]{2,1,0:T(4,128)(2,1)S(1)} %copy-done, f32[8,384]{1,0:T(8,128)S(1)} %get-tuple-element.10.comb.after, bf16[104,32,4,256]{3,2,1,0:T(4,128)(2,1)} %pool.1), custom_call_target="tpu_custom_call" | custom-call | bytes 27262976 | tf_op jit(solution)/shard_map/pallas_call | solution.py:421
  42.2 0.8 %all-to-all-done.1 = bf16[16,16,512]{2,1,0:T(8,128)(2,1)S(1)} async-done(((bf16[16,16,512]{2,1,0:T(8,128)(2,1)}), bf16[16,16,512]{2,1,0:T(8,128)(2,1)S(1)}, u32[]{:S(2)}, u32[]{:S(2)}) %all-to-all-start.1) | async-done | bytes 262176 | tf_op jit(solution)/shard_map/all_to_all | solution.py:433
  43.0 0.8 %shard_map.149 = (bf16[8,2048]{1,0:T(8,128)(2,1)}, f32[1,8]{1,0:T(1,128)}, f32[1,8]{1,0:T(1,128)}) custom-call(f32[8,384]{1,0:T(8,128)S(1)} %get-tuple-element.10.comb.after, bf16[256,512]{1,0:T(8,128)(2,1)S(1)} %bitcast.7, bf16[8,2048]{1,0:T(8,128)(2,1)S(1)} %get-tuple-element.12.mixed), custom_call_target="tpu_custom_call" | custom-call | tf_op jit(solution)/shard_map/pallas_call | solution.py:458
Async XLA Ops:
  0.6 24.3 %collective-permute-start = (bf16[1,2,704,2048]{3,2,1,0:T(8,128)(2,1)}, bf16[1,2,704,2048]{3,2,1,0:T(8,128)(2,1)S(1)}, u32[]{:S(2)}, u32[]{:S(2)}) collective-permute-start(bf16[1,2,704,2048]{3,2,1,0:T(8,128)(2,1)} %own_up.1), channel_id=1, source_target_pairs={{0,1},{1,0},{2,3},{3,2},{4,5},{5,4},{6,7},{7,6},{8,9},{9,8},{10,11... | collective-permute-start | bytes 17301512 | tf_op jit(solution)/shard_map/ppermute | solution.py:372
  1.2 23.7 %collective-permute-start.1 = (bf16[1,704,2048]{2,1,0:T(8,128)(2,1)}, bf16[1,704,2048]{2,1,0:T(8,128)(2,1)S(1)}, u32[]{:S(2)}, u32[]{:S(2)}) collective-permute-start(bf16[1,704,2048]{2,1,0:T(8,128)(2,1)} %own_down.1), channel_id=1, source_target_pairs={{0,1},{1,0},{2,3},{3,2},{4,5},{5,4},{6,7},{7,6},{8,9},{9,8},{10,11... | collective-permute-start | bytes 8650760 | tf_op jit(solution)/shard_map/ppermute | solution.py:373
  24.9 11.0 %copy-start = (bf16[8,4,256]{2,1,0:T(4,128)(2,1)S(1)}, bf16[8,4,256]{2,1,0:T(4,128)(2,1)}, u32[]{:S(2)}) copy-start(bf16[8,4,256]{2,1,0:T(4,128)(2,1)} %fresh.1) | copy-start | bytes 49156
  24.9 11.0 %copy-start.1 = (s32[8,20]{1,0:T(8,128)S(1)}, s32[8,20]{1,0:T(8,128)}, u32[]{:S(2)}) copy-start(s32[8,20]{1,0:T(8,128)} %table.1) | copy-start | bytes 1924
  24.9 11.0 %copy-start.2 = (s32[8]{0:T(128)S(1)}, s32[8]{0:T(128)}, u32[]{:S(2)}) copy-start(s32[8]{0:T(128)} %lengths.1) | copy-start | bytes 100
  30.8 12.2 %all-to-all-start.1 = ((bf16[16,16,512]{2,1,0:T(8,128)(2,1)}), bf16[16,16,512]{2,1,0:T(8,128)(2,1)S(1)}, u32[]{:S(2)}, u32[]{:S(2)}) async-start(bf16[16,16,512]{2,1,0:T(8,128)(2,1)} %bitcast.2), calls=%async_computation.1 | async-start | bytes 524288 | tf_op jit(solution)/shard_map/all_to_all | solution.py:433

commit v22 on v18

--- a/solution.py
+++ b/solution.py
@@ -29,8 +29,8 @@
     return [pltpu.make_async_copy(src, dst, sems.at[first + i]) for i, (src, dst) in enumerate(pairs)]
 
 
-def group_turn(chips, part):
-    return chips * 9 // 16 if part % 2 else chips * 3 // 8
+def chip_at(position, chips, part):
+    return position ^ (chips * 9 // 16) if part % 2 else (position + chips * 5 // 16) % chips
 
 
 def pool_half(array, i):
@@ -117,10 +117,11 @@
     parts = SLAB // capacity
     piece = width // parts
     slab_rows = experts * SLAB
-    turns = jnp.where(lax.axis_index("req") % 2 == 0, group_turn(experts, 0), group_turn(experts, 1))
+    even = lax.axis_index("req") % 2 == 0
 
     def slab_expert(shape, dim):
-        return (iota(shape, dim) // SLAB) ^ turns
+        slab = iota(shape, dim) // SLAB
+        return jnp.where(even, chip_at(slab, experts, 0), chip_at(slab, experts, 1))
 
     mixed = (hidden[...].astype(F32) + projected).astype(BF16)
     mixed_ref[...] = mixed
@@ -347,7 +348,7 @@
     slab_rows = experts * SLAB
 
     same_part = [
-        [(place ^ group_turn(experts, part)) * copies + part for place in range(experts)] for part in range(copies)
+        [chip_at(place, experts, part) * copies + part for place in range(experts)] for part in range(copies)
     ]
     swap = [(index, index ^ 1) for index in range(req_count)]
     other_up = lax.ppermute(expert_gate_up, "req", swap)

time: 44.1 us -> 44.2 us (level)
  blocking collectives: 16.2 us -> 15.7 us
  starting transfers between devices: 5.73 us -> 6.23 us
    all_to_all x1, blocking collectives: 16.2 us -> 15.7 us  [exchange(): lax.all_to_all(array, 'req', split_axis=0, concat_axis=0, tiled=True, axi...]
    all_to_all x1, starting transfers between devices: 5.13 us -> 5.63 us  [exchange(): lax.all_to_all(array, 'req', split_axis=0, concat_axis=0, tiled=True, axi...]
where the time goes in v22:
time: 44.2 us; the launch traced here: 43.8 us
  Pallas kernels  20.3 us (46%)
  blocking collectives  15.7 us (36%)
  starting transfers between devices  6.23 us (14%)
  waiting for transfers between devices  0.85 us (2%)
  between operations  0.7 us (2%)
    all_to_all x1, blocking collectives, exchange(): lax.all_to_all(array, 'req', split_axis=0, concat_axis=0, tiled=True, axi...  15.7 us
    pallas_call x1, Pallas kernels, body(): pl.pallas_call(functools.partial(attend_route_kernel, capacity), out_shap...  7.42 us
    pallas_call x1, Pallas kernels, body(): pl.pallas_call(refresh_kernel, out_shape=like(kv_pool.shape), in_specs=sc...  6.23 us
    pallas_call x1, Pallas kernels, body(): pl.pallas_call(functools.partial(expert_kernel, capacity), out_shape=like...  5.87 us
    all_to_all x1, starting transfers between devices, exchange(): lax.all_to_all(array, 'req', split_axis=0, concat_axis=0, tiled=True, axi...  5.63 us
  transfers between devices with their start and end apart: 3, of which 1 were waited for; matrix products, arithmetic and copies ran while one was open for 0% of the time, Pallas kernels for 31%

profile of v22, /device:TPU:0, one launch (start us, length us, event | category | flops | bytes accessed | tf_op | source)
XLA Modules:
  0.0 43.8 jit_solution(10323575362629948705)
XLA Ops:
  0.6 0.5 %collective-permute-start = (bf16[1,2,704,2048]{3,2,1,0:T(8,128)(2,1)}, bf16[1,2,704,2048]{3,2,1,0:T(8,128)(2,1)S(1)}, u32[]{:S(2)}, u32[]{:S(2)}) collective-permute-start(bf16[1,2,704,2048]{3,2,1,0:T(8,128)(2,1)} %own_up.1), channel_id=1, source_target_pairs={{0,1},{1,0},{2,3},{3,2},{4,5},{5,4},{6,7},{7,6},{8,9},{9,8},{10,11... | collective-permute-start | bytes 17301512 | tf_op jit(solution)/shard_map/ppermute | solution.py:354
  1.2 0.1 collective-permute-start.1
  1.2 7.4 %shard_map.147 = (bf16[8,2048]{1,0:T(8,128)(2,1)S(1)}, bf16[256,512]{1,0:T(8,128)(2,1)S(1)}, f32[8,384]{1,0:T(8,128)S(1)}) custom-call(s32[8,20]{1,0:T(8,128)} %table.1, s32[8]{0:T(128)} %lengths.1, bf16[8,2048]{1,0:T(8,128)(2,1)} %refs_2_.1, bf16[8,4,256]{2,1,0:T(4,128)(2,1)} %fresh.1, bf16[8,2048]{1,0:T(8,128)(2,1)} %refs_4_.1, bf16[2048]{0:T(1024)(128)(2,1)} %refs_5_.1, ...), custom_call_target="tpu_custom_call" | custom-call | tf_op jit(solution)/shard_map/pallas_call | solution.py:377
  8.7 15.7 %all_to_all.10 = bf16[16,16,512]{2,1,0:T(8,128)(2,1)S(1)} all-to-all(bf16[16,16,512]{2,1,0:T(8,128)(2,1)S(1)} %bitcast.8), channel_id=1, replica_groups={{10,12,14,16,18,20,22,24,26,28,30,0,2,4,6,8},{19,17,23,21,27,25,31,29,3..., dimensions={0} | all-to-all | bytes 524288 | tf_op jit(solution)/shard_map/all_to_all | solution.py:415
  24.4 0.0 collective-permute-done.1.other_down
  24.4 0.0 collective-permute-done.other_up
  24.4 0.0 copy-start
  24.4 0.0 copy-start.1
  24.4 0.0 copy-start.2
  24.4 5.9 %shard_map.148 = bf16[256,512]{1,0:T(8,128)(2,1)} custom-call(bf16[256,512]{1,0:T(8,128)(2,1)S(1)} %bitcast.6, bf16[1,2,704,2048]{3,2,1,0:T(8,128)(2,1)} %own_up.1, bf16[1,704,2048]{2,1,0:T(8,128)(2,1)} %own_down.1, bf16[1,2,704,2048]{3,2,1,0:T(8,128)(2,1)S(1)} %collective-permute-done.other_up, bf16[1,704,2048]{2,1,0:T(8,128)(2,1)S(1)} %collective-permute-done.1.other_down), custom_call_target="tpu_custom_call" | custom-call | tf_op jit(solution)/shard_map/pallas_call | solution.py:423
  30.3 5.6 %all-to-all-start.1 = ((bf16[16,16,512]{2,1,0:T(8,128)(2,1)}), bf16[16,16,512]{2,1,0:T(8,128)(2,1)S(1)}, u32[]{:S(2)}, u32[]{:S(2)}) async-start(bf16[16,16,512]{2,1,0:T(8,128)(2,1)} %bitcast.2), calls=%async_computation.1 | async-start | bytes 524288 | tf_op jit(solution)/shard_map/all_to_all | solution.py:415
  35.9 0.0 copy-done
  35.9 0.0 copy-done.1
  35.9 0.0 copy-done.2
  35.9 6.2 %shard_map.150 = bf16[104,32,4,256]{3,2,1,0:T(4,128)(2,1)} custom-call(s32[8,20]{1,0:T(8,128)S(1)} %copy-done.1, s32[8]{0:T(128)S(1)} %copy-done.2, bf16[8,4,256]{2,1,0:T(4,128)(2,1)S(1)} %copy-done, f32[8,384]{1,0:T(8,128)S(1)} %get-tuple-element.10.comb.after, bf16[104,32,4,256]{3,2,1,0:T(4,128)(2,1)} %pool.1), custom_call_target="tpu_custom_call" | custom-call | bytes 27262976 | tf_op jit(solution)/shard_map/pallas_call | solution.py:403
  42.2 0.8 %all-to-all-done.1 = bf16[16,16,512]{2,1,0:T(8,128)(2,1)S(1)} async-done(((bf16[16,16,512]{2,1,0:T(8,128)(2,1)}), bf16[16,16,512]{2,1,0:T(8,128)(2,1)S(1)}, u32[]{:S(2)}, u32[]{:S(2)}) %all-to-all-start.1) | async-done | bytes 262176 | tf_op jit(solution)/shard_map/all_to_all | solution.py:415
  43.0 0.8 %shard_map.149 = (bf16[8,2048]{1,0:T(8,128)(2,1)}, f32[1,8]{1,0:T(1,128)}, f32[1,8]{1,0:T(1,128)}) custom-call(f32[8,384]{1,0:T(8,128)S(1)} %get-tuple-element.10.comb.after, bf16[256,512]{1,0:T(8,128)(2,1)S(1)} %bitcast.7, bf16[8,2048]{1,0:T(8,128)(2,1)S(1)} %get-tuple-element.12.mixed), custom_call_target="tpu_custom_call" | custom-call | tf_op jit(solution)/shard_map/pallas_call | solution.py:440
Async XLA Ops:
  0.6 23.7 %collective-permute-start = (bf16[1,2,704,2048]{3,2,1,0:T(8,128)(2,1)}, bf16[1,2,704,2048]{3,2,1,0:T(8,128)(2,1)S(1)}, u32[]{:S(2)}, u32[]{:S(2)}) collective-permute-start(bf16[1,2,704,2048]{3,2,1,0:T(8,128)(2,1)} %own_up.1), channel_id=1, source_target_pairs={{0,1},{1,0},{2,3},{3,2},{4,5},{5,4},{6,7},{7,6},{8,9},{9,8},{10,11... | collective-permute-start | bytes 17301512 | tf_op jit(solution)/shard_map/ppermute | solution.py:354
  1.2 23.2 %collective-permute-start.1 = (bf16[1,704,2048]{2,1,0:T(8,128)(2,1)}, bf16[1,704,2048]{2,1,0:T(8,128)(2,1)S(1)}, u32[]{:S(2)}, u32[]{:S(2)}) collective-permute-start(bf16[1,704,2048]{2,1,0:T(8,128)(2,1)} %own_down.1), channel_id=1, source_target_pairs={{0,1},{1,0},{2,3},{3,2},{4,5},{5,4},{6,7},{7,6},{8,9},{9,8},{10,11... | collective-permute-start | bytes 8650760 | tf_op jit(solution)/shard_map/ppermute | solution.py:355
  24.4 11.5 %copy-start = (bf16[8,4,256]{2,1,0:T(4,128)(2,1)S(1)}, bf16[8,4,256]{2,1,0:T(4,128)(2,1)}, u32[]{:S(2)}) copy-start(bf16[8,4,256]{2,1,0:T(4,128)(2,1)} %fresh.1) | copy-start | bytes 49156
  24.4 11.5 %copy-start.1 = (s32[8,20]{1,0:T(8,128)S(1)}, s32[8,20]{1,0:T(8,128)}, u32[]{:S(2)}) copy-start(s32[8,20]{1,0:T(8,128)} %table.1) | copy-start | bytes 1924
  24.4 11.5 %copy-start.2 = (s32[8]{0:T(128)S(1)}, s32[8]{0:T(128)}, u32[]{:S(2)}) copy-start(s32[8]{0:T(128)} %lengths.1) | copy-start | bytes 100
  30.3 12.7 %all-to-all-start.1 = ((bf16[16,16,512]{2,1,0:T(8,128)(2,1)}), bf16[16,16,512]{2,1,0:T(8,128)(2,1)S(1)}, u32[]{:S(2)}, u32[]{:S(2)}) async-start(bf16[16,16,512]{2,1,0:T(8,128)(2,1)} %bitcast.2), calls=%async_computation.1 | async-start | bytes 524288 | tf_op jit(solution)/shard_map/all_to_all | solution.py:415

commit v23 on v22

--- a/solution.py
+++ b/solution.py
@@ -30,7 +30,7 @@
 
 
 def chip_at(position, chips, part):
-    return position ^ (chips * 9 // 16) if part % 2 else (position + chips * 5 // 16) % chips
+    return (position + chips * (9 if part % 2 else 5) // 16) % chips
 
 
 def pool_half(array, i):

time: 44.2 us -> 44.2 us (level)
  no operation moved by 1% of the time
where the time goes in v23:
time: 44.2 us; the launch traced here: 43.8 us
  Pallas kernels  20.3 us (46%)
  blocking collectives  15.7 us (36%)
  starting transfers between devices  6.23 us (14%)
  waiting for transfers between devices  0.87 us (2%)
  between operations  0.7 us (2%)
    all_to_all x1, blocking collectives, exchange(): lax.all_to_all(array, 'req', split_axis=0, concat_axis=0, tiled=True, axi...  15.7 us
    pallas_call x1, Pallas kernels, body(): pl.pallas_call(functools.partial(attend_route_kernel, capacity), out_shap...  7.42 us
    pallas_call x1, Pallas kernels, body(): pl.pallas_call(refresh_kernel, out_shape=like(kv_pool.shape), in_specs=sc...  6.2 us
    pallas_call x1, Pallas kernels, body(): pl.pallas_call(functools.partial(expert_kernel, capacity), out_shape=like...  5.87 us
    all_to_all x1, starting transfers between devices, exchange(): lax.all_to_all(array, 'req', split_axis=0, concat_axis=0, tiled=True, axi...  5.63 us
  transfers between devices with their start and end apart: 3, of which 1 were waited for; matrix products, arithmetic and copies ran while one was open for 0% of the time, Pallas kernels for 31%

profile of v23, /device:TPU:0, one launch (start us, length us, event | category | flops | bytes accessed | tf_op | source)
XLA Modules:
  0.0 43.8 jit_solution(415668653439818274)
XLA Ops:
  0.6 0.5 %collective-permute-start = (bf16[1,2,704,2048]{3,2,1,0:T(8,128)(2,1)}, bf16[1,2,704,2048]{3,2,1,0:T(8,128)(2,1)S(1)}, u32[]{:S(2)}, u32[]{:S(2)}) collective-permute-start(bf16[1,2,704,2048]{3,2,1,0:T(8,128)(2,1)} %own_up.1), channel_id=1, source_target_pairs={{0,1},{1,0},{2,3},{3,2},{4,5},{5,4},{6,7},{7,6},{8,9},{9,8},{10,11... | collective-permute-start | bytes 17301512 | tf_op jit(solution)/shard_map/ppermute | solution.py:354
  1.2 0.1 collective-permute-start.1
  1.2 7.4 %shard_map.147 = (bf16[8,2048]{1,0:T(8,128)(2,1)S(1)}, bf16[256,512]{1,0:T(8,128)(2,1)S(1)}, f32[8,384]{1,0:T(8,128)S(1)}) custom-call(s32[8,20]{1,0:T(8,128)} %table.1, s32[8]{0:T(128)} %lengths.1, bf16[8,2048]{1,0:T(8,128)(2,1)} %refs_2_.1, bf16[8,4,256]{2,1,0:T(4,128)(2,1)} %fresh.1, bf16[8,2048]{1,0:T(8,128)(2,1)} %refs_4_.1, bf16[2048]{0:T(1024)(128)(2,1)} %refs_5_.1, ...), custom_call_target="tpu_custom_call" | custom-call | tf_op jit(solution)/shard_map/pallas_call | solution.py:377
  8.7 15.7 %all_to_all.10 = bf16[16,16,512]{2,1,0:T(8,128)(2,1)S(1)} all-to-all(bf16[16,16,512]{2,1,0:T(8,128)(2,1)S(1)} %bitcast.8), channel_id=1, replica_groups={{10,12,14,16,18,20,22,24,26,28,30,0,2,4,6,8},{19,21,23,25,27,29,31,1,3,..., dimensions={0} | all-to-all | bytes 524288 | tf_op jit(solution)/shard_map/all_to_all | solution.py:415
  24.4 0.0 collective-permute-done.1.other_down
  24.4 0.0 collective-permute-done.other_up
  24.4 0.0 copy-start
  24.4 0.0 copy-start.1
  24.4 0.0 copy-start.2
  24.4 5.9 %shard_map.148 = bf16[256,512]{1,0:T(8,128)(2,1)} custom-call(bf16[256,512]{1,0:T(8,128)(2,1)S(1)} %bitcast.6, bf16[1,2,704,2048]{3,2,1,0:T(8,128)(2,1)} %own_up.1, bf16[1,704,2048]{2,1,0:T(8,128)(2,1)} %own_down.1, bf16[1,2,704,2048]{3,2,1,0:T(8,128)(2,1)S(1)} %collective-permute-done.other_up, bf16[1,704,2048]{2,1,0:T(8,128)(2,1)S(1)} %collective-permute-done.1.other_down), custom_call_target="tpu_custom_call" | custom-call | tf_op jit(solution)/shard_map/pallas_call | solution.py:423
  30.3 5.6 %all-to-all-start.1 = ((bf16[16,16,512]{2,1,0:T(8,128)(2,1)}), bf16[16,16,512]{2,1,0:T(8,128)(2,1)S(1)}, u32[]{:S(2)}, u32[]{:S(2)}) async-start(bf16[16,16,512]{2,1,0:T(8,128)(2,1)} %bitcast.2), calls=%async_computation.1 | async-start | bytes 524288 | tf_op jit(solution)/shard_map/all_to_all | solution.py:415
  35.9 0.0 copy-done
  35.9 0.0 copy-done.1
  35.9 0.0 copy-done.2
  35.9 6.2 %shard_map.150 = bf16[104,32,4,256]{3,2,1,0:T(4,128)(2,1)} custom-call(s32[8,20]{1,0:T(8,128)S(1)} %copy-done.1, s32[8]{0:T(128)S(1)} %copy-done.2, bf16[8,4,256]{2,1,0:T(4,128)(2,1)S(1)} %copy-done, f32[8,384]{1,0:T(8,128)S(1)} %get-tuple-element.10.comb.after, bf16[104,32,4,256]{3,2,1,0:T(4,128)(2,1)} %pool.1), custom_call_target="tpu_custom_call" | custom-call | bytes 27262976 | tf_op jit(solution)/shard_map/pallas_call | solution.py:403
  42.1 0.9 %all-to-all-done.1 = bf16[16,16,512]{2,1,0:T(8,128)(2,1)S(1)} async-done(((bf16[16,16,512]{2,1,0:T(8,128)(2,1)}), bf16[16,16,512]{2,1,0:T(8,128)(2,1)S(1)}, u32[]{:S(2)}, u32[]{:S(2)}) %all-to-all-start.1) | async-done | bytes 262176 | tf_op jit(solution)/shard_map/all_to_all | solution.py:415
  43.0 0.8 %shard_map.149 = (bf16[8,2048]{1,0:T(8,128)(2,1)}, f32[1,8]{1,0:T(1,128)}, f32[1,8]{1,0:T(1,128)}) custom-call(f32[8,384]{1,0:T(8,128)S(1)} %get-tuple-element.10.comb.after, bf16[256,512]{1,0:T(8,128)(2,1)S(1)} %bitcast.7, bf16[8,2048]{1,0:T(8,128)(2,1)S(1)} %get-tuple-element.12.mixed), custom_call_target="tpu_custom_call" | custom-call | tf_op jit(solution)/shard_map/pallas_call | solution.py:440
Async XLA Ops:
  0.6 23.7 %collective-permute-start = (bf16[1,2,704,2048]{3,2,1,0:T(8,128)(2,1)}, bf16[1,2,704,2048]{3,2,1,0:T(8,128)(2,1)S(1)}, u32[]{:S(2)}, u32[]{:S(2)}) collective-permute-start(bf16[1,2,704,2048]{3,2,1,0:T(8,128)(2,1)} %own_up.1), channel_id=1, source_target_pairs={{0,1},{1,0},{2,3},{3,2},{4,5},{5,4},{6,7},{7,6},{8,9},{9,8},{10,11... | collective-permute-start | bytes 17301512 | tf_op jit(solution)/shard_map/ppermute | solution.py:354
  1.2 23.2 %collective-permute-start.1 = (bf16[1,704,2048]{2,1,0:T(8,128)(2,1)}, bf16[1,704,2048]{2,1,0:T(8,128)(2,1)S(1)}, u32[]{:S(2)}, u32[]{:S(2)}) collective-permute-start(bf16[1,704,2048]{2,1,0:T(8,128)(2,1)} %own_down.1), channel_id=1, source_target_pairs={{0,1},{1,0},{2,3},{3,2},{4,5},{5,4},{6,7},{7,6},{8,9},{9,8},{10,11... | collective-permute-start | bytes 8650760 | tf_op jit(solution)/shard_map/ppermute | solution.py:355
  24.4 11.5 %copy-start = (bf16[8,4,256]{2,1,0:T(4,128)(2,1)S(1)}, bf16[8,4,256]{2,1,0:T(4,128)(2,1)}, u32[]{:S(2)}) copy-start(bf16[8,4,256]{2,1,0:T(4,128)(2,1)} %fresh.1) | copy-start | bytes 49156
  24.4 11.5 %copy-start.1 = (s32[8,20]{1,0:T(8,128)S(1)}, s32[8,20]{1,0:T(8,128)}, u32[]{:S(2)}) copy-start(s32[8,20]{1,0:T(8,128)} %table.1) | copy-start | bytes 1924
  24.4 11.5 %copy-start.2 = (s32[8]{0:T(128)S(1)}, s32[8]{0:T(128)}, u32[]{:S(2)}) copy-start(s32[8]{0:T(128)} %lengths.1) | copy-start | bytes 100
  30.3 12.7 %all-to-all-start.1 = ((bf16[16,16,512]{2,1,0:T(8,128)(2,1)}), bf16[16,16,512]{2,1,0:T(8,128)(2,1)S(1)}, u32[]{:S(2)}, u32[]{:S(2)}) async-start(bf16[16,16,512]{2,1,0:T(8,128)(2,1)} %bitcast.2), calls=%async_computation.1 | async-start | bytes 524288 | tf_op jit(solution)/shard_map/all_to_all | solution.py:415
